TPU v7x, 256 devices: a whole 4x4x8 slice. The times are simulated.
256 devices in a mesh: mem: 4 (over z_lo, core), tile: 64 (over x, y, z_hi).
Axes of the slice: x: 4, y: 4, z: 8 (z_hi: 4, z_lo: 2; z = z_hi * 2 + z_lo), core: 2. Of those that a mesh axis runs over, the one named last changes fastest.
Arguments:
- alpha: bfloat16 [80, 512, 32, 128], P('mem', 'tile'), may hold values from -0.8984375 to 0.8984375
- ensemble: bfloat16 [80, 3, 512, 32, 128], P('mem', None, 'tile'), may hold values from -6 to 6
- loc_vert: bfloat16 [128, 128], replicated, may hold values from -0.25 to 1.5, as said below
- obs_col: int32 [64, 2048], P('tile'), may hold values from 0 to 1023
- obs_lev: int32 [64, 2048], P('tile'), may hold values from 0 to 127
- obs_count: int32 [64], P('tile'), may hold values from 512 to 2048
- innovation: float32 [64, 2048], P('tile'), may hold values from -6 to 6
- obs_weight: float32 [64, 2048], P('tile'), may hold values from 1 to 8
Outputs:
- gradient: float32 [80, 512, 32, 128], P('mem', 'tile')
Inputs may be any that keep to these rules, and one draw needn't show every extreme that they name: `loc_vert`: a square root of the vertical localization, applied along levels.
All inputs are finite; a program needn't handle non-finite values.
Results may differ from a plain program's by a relative error of at most 0.0019.
Values sent between devices are 32-bit elements; how exact they have to be, the bound alone decides.
No kernel may reach another device: no remote copies, remote signals or barrier semaphores. Data moves between devices by JAX's collectives and lax.ppermute only.
A program may use at most 64 MiB of HBM per device.

v0:
```python
import jax
import jax.numpy as jnp
from jax import lax
from jax.sharding import PartitionSpec as P

V = 3
NS = 2


def padded_2(block, sides, width):
    for axis, dim in sides:
        count = lax.axis_size(axis)
        forward = [(i, i + 1) for i in range(count - 1)]
        backward = [(target, source) for source, target in forward]
        low = lax.ppermute(
            lax.slice_in_dim(block, block.shape[dim] - width, None, axis=dim), axis, forward
        )
        high = lax.ppermute(lax.slice_in_dim(block, 0, width, axis=dim), axis, backward)
        block = jnp.concatenate([low, block, high], axis=dim)
    return block


def copy_for_each(array, axis):
    copies = jnp.broadcast_to(array, (lax.axis_size(axis), *array.shape))
    return lax.all_to_all(copies, axis, split_axis=0, concat_axis=0, tiled=True)


def of_everyone(array, axis):
    everything = copy_for_each(array, axis)
    return jnp.sum(everything, axis=0)


def widen(field, axis):
    pads = [(1, 1) if dim == axis else (0, 0) for dim in range(field.ndim)]
    return jnp.pad(field, pads)


def spread(padded, axis):
    length = padded.shape[axis] - 2
    before = lax.slice_in_dim(padded, 0, length, axis=axis)
    middle = lax.slice_in_dim(padded, 1, length + 1, axis=axis)
    after = lax.slice_in_dim(padded, 2, length + 2, axis=axis)
    return 0.25 * before + 0.5 * middle + 0.25 * after


def refine(padded, axis):
    length = padded.shape[axis] - 2
    before = lax.slice_in_dim(padded, 0, length, axis=axis)
    middle = lax.slice_in_dim(padded, 1, length + 1, axis=axis)
    after = lax.slice_in_dim(padded, 2, length + 2, axis=axis)
    evens = 0.75 * middle + 0.25 * before
    odds = 0.75 * middle + 0.25 * after
    stacked = jnp.stack([evens, odds], axis=axis + 1)
    shape = list(middle.shape)
    shape[axis] = 2 * length
    return stacked.reshape(shape)


def coarsen(padded, axis):
    length = padded.shape[axis] - 2
    first = lax.slice_in_dim(padded, 0, length, 2, axis=axis)
    second = lax.slice_in_dim(padded, 1, length + 1, 2, axis=axis)
    third = lax.slice_in_dim(padded, 2, length + 2, 2, axis=axis)
    fourth = lax.slice_in_dim(padded, 3, length + 2, 2, axis=axis)
    return 0.25 * first + 0.75 * second + 0.75 * third + 0.25 * fourth


def smooth(field, forward):
    rows = field.shape[1]
    if forward:
        padded = padded_2(field, (("tile", 1),), NS)
    else:
        padded = padded_2(field, (("tile", 1),), NS)
    global_row = lax.axis_index("tile") * rows - NS + jnp.arange(rows + 2 * NS, dtype=jnp.int32)
    inside = (global_row >= 0) & (global_row < rows * lax.axis_size("tile"))
    for sweep in range(NS):
        padded = spread(widen(padded, 1), 1)
        padded = spread(widen(padded, 2), 2)
        padded = jnp.where(inside[None, :, None, None], padded, jnp.zeros_like(padded))
    return padded[:, NS : NS + rows]


def on_device(alpha, ensemble, loc_vert, obs_col, obs_lev, obs_count, innovation, obs_weight):
    lifted = smooth(jnp.dot(alpha, loc_vert.T, preferred_element_type=jnp.float32), True).astype(
        jnp.bfloat16
    )
    partial_inc = jnp.einsum(
        "kvyxl,kyxl->vyxl", ensemble, lifted, preferred_element_type=jnp.float32
    )
    increment = of_everyone(partial_inc, "mem")
    padded = padded_2(increment, (("tile", 1),), 1)
    fine = refine(widen(refine(padded, 1), 2), 2)
    fine_rows = fine.shape[1]
    fine_cols = fine.shape[2]
    share = fine.shape[3]
    flat = fine.reshape(V, fine_rows * fine_cols, share)
    column = obs_col[0]
    level = obs_lev[0]
    slots = column.shape[0]
    variable = jnp.arange(slots, dtype=jnp.int32) % V
    level_hot = (level[:, None] == jnp.arange(share, dtype=jnp.int32)[None, :]).astype(jnp.float32)
    picked = flat[variable, column]
    value = jnp.sum(picked * level_hot, axis=1)
    live = jnp.arange(slots, dtype=jnp.int32) < obs_count[0]
    weighted = jnp.where(live, obs_weight[0] * (value - innovation[0]), jnp.zeros_like(value))
    spread_back = weighted[:, None] * level_hot
    fine_adjoint = (
        jnp.zeros((V, fine_rows * fine_cols, share), jnp.float32)
        .at[variable, column]
        .add(spread_back)
    )
    fine_adjoint = fine_adjoint.reshape(V, fine_rows, fine_cols, share)
    fine_padded = padded_2(fine_adjoint, (("tile", 1),), 1)
    coarse_adjoint = coarsen(widen(coarsen(fine_padded, 1), 2), 2)
    back = jnp.einsum("kvyxl,vyxl->kyxl", ensemble.astype(jnp.float32), coarse_adjoint)
    back = smooth(back, False)
    return alpha.astype(jnp.float32) + jnp.dot(
        back, loc_vert.astype(jnp.float32), precision=lax.Precision.HIGHEST
    )


def solution(mesh):
    in_specs = (
        P("mem", "tile", None, None),
        P("mem", None, "tile", None, None),
        P(),
        P("tile", None),
        P("tile", None),
        P("tile"),
        P("tile", None),
        P("tile", None),
    )
    out_specs = P("mem", "tile", None, None)
    return jax.shard_map(
        on_device, mesh=mesh, in_specs=in_specs, out_specs=out_specs, check_vma=False
    )
```

profile of v0, /device:TPU:6, one launch (start us, length us, event | category | flops | bytes accessed | tf_op | source)
XLA Modules:
  0.0 182.0 jit_solution(14909957979446069382)
XLA Ops:
  0.8 1.8 fusion.64
  2.6 1.0 fusion.70
  3.5 5.2 %collective-permute-start = (f32[20,2,32,128]{3,2,1,0:T(8,128)}, f32[20,2,32,128]{3,2,1,0:T(8,128)}, u32[]{:S(2)}, u32[]{:S(2)}) collective-permute-start(f32[20,2,32,128]{3,2,1,0:T(8,128)} %get-tuple-element.11), channel_id=1, source_target_pairs={{0,1},{1,2},{2,3},{3,4},{4,5},{5,6},{6,7},{7,8},{8,9},{9,10},{10,1... | collective-permute-start | bytes 1966088 | tf_op jit(solution)/shard_map/ppermute | solution.py:15
  8.7 7.7 %collective-permute-start.1 = (f32[20,2,32,128]{3,2,1,0:T(8,128)S(1)}, f32[20,2,32,128]{3,2,1,0:T(8,128)}, u32[]{:S(2)}, u32[]{:S(2)}) collective-permute-start(f32[20,2,32,128]{3,2,1,0:T(8,128)S(1)} %get-tuple-element.12), channel_id=1, source_target_pairs={{1,0},{2,1},{3,2},{4,3},{5,4},{6,5},{7,6},{8,7},{9,8},{10,9},{11,1... | collective-permute-start | bytes 1966088 | tf_op jit(solution)/shard_map/ppermute | solution.py:18
  16.5 18.9 %collective-permute-done = f32[20,2,32,128]{3,2,1,0:T(8,128)} collective-permute-done((f32[20,2,32,128]{3,2,1,0:T(8,128)}, f32[20,2,32,128]{3,2,1,0:T(8,128)}, u32[]{:S(2)}, u32[]{:S(2)}) %collective-permute-start) | collective-permute-done | bytes 655392 | tf_op jit(solution)/shard_map/ppermute | solution.py:15
  35.4 8.3 %collective-permute-done.1 = f32[20,2,32,128]{3,2,1,0:T(8,128)} collective-permute-done((f32[20,2,32,128]{3,2,1,0:T(8,128)S(1)}, f32[20,2,32,128]{3,2,1,0:T(8,128)}, u32[]{:S(2)}, u32[]{:S(2)}) %collective-permute-start.1) | collective-permute-done | bytes 655392 | tf_op jit(solution)/shard_map/ppermute | solution.py:18
  43.7 1.9 %pad_maximum_fusion = f32[20,12,32,128]{3,2,1,0:T(8,128)S(1)} fusion(f32[20,2,32,128]{3,2,1,0:T(8,128)} %collective-permute-done.1, f32[20,8,32,128]{3,2,1,0:T(8,128)S(1)} %fusion.64, f32[20,2,32,128]{3,2,1,0:T(8,128)} %collective-permute-done), kind=kLoop, calls=%fused_computation.52 | loop fusion | flops 1966080 | bytes 7864320 | tf_op jit(solution)/shard_map/concatenate | solution.py:19
  46.2 1.3 fusion.19
  47.5 0.9 fusion.6
  48.4 1.5 pad_slice_fusion.5
  49.9 1.2 bitcast_convert_fusion
  51.1 0.9 copy-done.1
  52.0 0.9 multiply_reduce_fusion.1
  53.0 1.3 broadcast_in_dim.38
  54.4 3.6 %all-to-all-start = ((f32[4,3,8,32,128]{4,3,2,1,0:T(8,128)}), f32[4,3,8,32,128]{4,3,2,1,0:T(8,128)S(1)}, u32[]{:S(2)}, u32[]{:S(2)}) async-start(f32[4,3,8,32,128]{4,3,2,1,0:T(8,128)} %broadcast_in_dim.38), calls=%async_computation | async-start | bytes 3145728 | tf_op jit(solution)/shard_map/all_to_all | solution.py:25
  58.2 19.7 %all-to-all-done = f32[4,3,8,32,128]{4,3,2,1,0:T(8,128)S(1)} async-done(((f32[4,3,8,32,128]{4,3,2,1,0:T(8,128)}), f32[4,3,8,32,128]{4,3,2,1,0:T(8,128)S(1)}, u32[]{:S(2)}, u32[]{:S(2)}) %all-to-all-start) | async-done | bytes 1572896 | tf_op jit(solution)/shard_map/all_to_all | solution.py:25
  78.2 5.6 %collective-permute-start.2 = (f32[3,1,32,128]{3,2,1,0:T(8,128)S(1)}, f32[3,1,32,128]{3,2,1,0:T(8,128)S(1)}, u32[]{:S(2)}, u32[]{:S(2)}) collective-permute-start(f32[3,1,32,128]{3,2,1,0:T(8,128)S(1)} %get-tuple-element.19), channel_id=1, source_target_pairs={{0,1},{1,2},{2,3},{3,4},{4,5},{5,6},{6,7},{7,8},{8,9},{9,10},{10,1... | collective-permute-start | bytes 147464 | tf_op jit(solution)/shard_map/ppermute | solution.py:15
  83.8 5.5 %collective-permute-start.3 = (f32[3,1,32,128]{3,2,1,0:T(8,128)S(1)}, f32[3,1,32,128]{3,2,1,0:T(8,128)S(1)}, u32[]{:S(2)}, u32[]{:S(2)}) collective-permute-start(f32[3,1,32,128]{3,2,1,0:T(8,128)S(1)} %get-tuple-element.20), channel_id=1, source_target_pairs={{1,0},{2,1},{3,2},{4,3},{5,4},{6,5},{7,6},{8,7},{9,8},{10,9},{11,1... | collective-permute-start | bytes 147464 | tf_op jit(solution)/shard_map/ppermute | solution.py:18
  90.0 1.1 collective-permute-done.3
  91.8 1.4 copy.19
  93.2 13.0 %gather_fusion = f32[2048,128]{1,0:T(8,128)S(1)} fusion(f32[3,1024,128]{2,1,0:T(8,128)S(1)} %bitcast.40, s32[2048]{0:T(1024)S(1)} %bitcast.39), kind=kCustom, calls=%fused_computation | custom fusion | bytes 2113536 | tf_op jit(solution)/shard_map/gather | solution.py:102
  106.9 13.1 %scatter_custom_fusion = f32[3072,128]{1,0:T(8,128)S(1)} fusion(s32[2048]{0:T(1024)S(1)} %broadcast_select_fusion, f32[]{:T(128)} %constant.16.clone.1, f32[2048]{0:T(1024)S(1)} %multiply_select_fusion, s32[2048]{0:T(1024)S(1)} %bitcast.49), kind=kCustom, calls=%fused_computation.70 | custom fusion | flops 786432 | bytes 1590272
  120.1 3.7 %collective-permute-start.4 = (f32[3,1,64,128]{3,2,1,0:T(8,128)S(1)}, f32[3,1,64,128]{3,2,1,0:T(8,128)S(1)}, u32[]{:S(2)}, u32[]{:S(2)}) collective-permute-start(f32[3,1,64,128]{3,2,1,0:T(8,128)S(1)} %get-tuple-element.13), channel_id=1, source_target_pairs={{0,1},{1,2},{2,3},{3,4},{4,5},{5,6},{6,7},{7,8},{8,9},{9,10},{10,1... | collective-permute-start | bytes 294920 | tf_op jit(solution)/shard_map/ppermute | solution.py:15
  123.8 7.7 %collective-permute-start.5 = (f32[3,1,64,128]{3,2,1,0:T(8,128)S(1)}, f32[3,1,64,128]{3,2,1,0:T(8,128)S(1)}, u32[]{:S(2)}, u32[]{:S(2)}) collective-permute-start(f32[3,1,64,128]{3,2,1,0:T(8,128)S(1)} %get-tuple-element.14), channel_id=1, source_target_pairs={{1,0},{2,1},{3,2},{4,3},{5,4},{6,5},{7,6},{8,7},{9,8},{10,9},{11,1... | collective-permute-start | bytes 294920 | tf_op jit(solution)/shard_map/ppermute | solution.py:18
  131.5 1.4 collective-permute-done.4
  132.9 1.3 collective-permute-done.5
  135.7 3.4 %multiply_reduce_fusion = f32[8,32,128,20]{2,1,0,3:T(8,128)S(1)} fusion(f32[8,32,128,3]{2,1,0,3:T(8,128)S(1)} %add_bitcast_fusion, bf16[20,3,8,32,128]{4,3,2,1,0:T(8,128)(2,1)} %param.9), kind=kLoop, calls=%fused_computation.2 | loop fusion | flops 5242880 | bytes 6946816 | tf_op jit(solution)/shard_map/kvyxl,vyxl->kyxl/dot_general | solution.py:115
  139.2 1.9 %collective-permute-start.6 = (f32[20,2,32,128]{3,2,1,0:T(8,128)S(1)}, f32[20,2,32,128]{3,2,1,0:T(8,128)S(1)}, u32[]{:S(2)}, u32[]{:S(2)}) collective-permute-start(f32[20,2,32,128]{3,2,1,0:T(8,128)S(1)} %get-tuple-element.9), channel_id=1, source_target_pairs={{0,1},{1,2},{2,3},{3,4},{4,5},{5,6},{6,7},{7,8},{8,9},{9,10},{10,1... | collective-permute-start | bytes 1966088 | tf_op jit(solution)/shard_map/ppermute | solution.py:15
  141.1 9.7 %collective-permute-start.7 = (f32[20,2,32,128]{3,2,1,0:T(8,128)S(1)}, f32[20,2,32,128]{3,2,1,0:T(8,128)S(1)}, u32[]{:S(2)}, u32[]{:S(2)}) collective-permute-start(f32[20,2,32,128]{3,2,1,0:T(8,128)S(1)} %get-tuple-element.10), channel_id=1, source_target_pairs={{1,0},{2,1},{3,2},{4,3},{5,4},{6,5},{7,6},{8,7},{9,8},{10,9},{11,1... | collective-permute-start | bytes 1966088 | tf_op jit(solution)/shard_map/ppermute | solution.py:18
  150.8 23.9 %collective-permute-done.6 = f32[20,2,32,128]{3,2,1,0:T(8,128)S(1)} collective-permute-done((f32[20,2,32,128]{3,2,1,0:T(8,128)S(1)}, f32[20,2,32,128]{3,2,1,0:T(8,128)S(1)}, u32[]{:S(2)}, u32[]{:S(2)}) %collective-permute-start.6) | collective-permute-done | bytes 655392 | tf_op jit(solution)/shard_map/ppermute | solution.py:15
  175.8 1.3 fusion.24
  178.4 3.6 %convert_add_fusion = f32[20,8,32,128]{3,2,1,0:T(8,128)} fusion(bf16[20,8,32,128]{3,2,1,0:T(8,128)(2,1)S(1)} %copy-done.2, f32[20,12,32,128]{3,2,1,0:T(8,128)S(1)} %fusion.14, pred[12]{0:T(512)(128)(4,1)S(1)} %compare_and_fusion, bf16[128,128]{1,0:T(8,128)(2,1)S(1)} %copy-done), kind=kOutput, calls=%fused_computation.62 | convolution fusion | flops 1013841920 | bytes 7897100 | tf_op jit(solution)/shard_map/dot_general | solution.py:117
  (48 shorter events, 7.1 us)
Async XLA Ops:
  0.0 0.8 copy-start
  3.5 31.8 %collective-permute-start = (f32[20,2,32,128]{3,2,1,0:T(8,128)}, f32[20,2,32,128]{3,2,1,0:T(8,128)}, u32[]{:S(2)}, u32[]{:S(2)}) collective-permute-start(f32[20,2,32,128]{3,2,1,0:T(8,128)} %get-tuple-element.11), channel_id=1, source_target_pairs={{0,1},{1,2},{2,3},{3,4},{4,5},{5,6},{6,7},{7,8},{8,9},{9,10},{10,1... | collective-permute-start | bytes 1966088 | tf_op jit(solution)/shard_map/ppermute | solution.py:15
  8.7 35.0 %collective-permute-start.1 = (f32[20,2,32,128]{3,2,1,0:T(8,128)S(1)}, f32[20,2,32,128]{3,2,1,0:T(8,128)}, u32[]{:S(2)}, u32[]{:S(2)}) collective-permute-start(f32[20,2,32,128]{3,2,1,0:T(8,128)S(1)} %get-tuple-element.12), channel_id=1, source_target_pairs={{1,0},{2,1},{3,2},{4,3},{5,4},{6,5},{7,6},{8,7},{9,8},{10,9},{11,1... | collective-permute-start | bytes 1966088 | tf_op jit(solution)/shard_map/ppermute | solution.py:18
  49.9 2.1 %copy-start.1 = (bf16[20,3,8,32,128]{4,3,2,1,0:T(8,128)(2,1)S(1)}, bf16[20,3,8,32,128]{4,3,2,1,0:T(8,128)(2,1)}, u32[]{:S(2)}) copy-start(bf16[20,3,8,32,128]{4,3,2,1,0:T(8,128)(2,1)} %param.9) | copy-start | bytes 11796484
  53.0 5.0 %copy-start.4 = (s32[1,2048]{1,0:T(1,128)S(1)}, s32[1,2048]{1,0:T(1,128)}, u32[]{:S(2)}) copy-start(s32[1,2048]{1,0:T(1,128)} %param.11) | copy-start | bytes 24580
  53.0 5.0 %copy-start.8 = (s32[2]{0:T(128)S(1)}, s32[2]{0:T(128)}, u32[]{:S(2)}) copy-start(s32[2]{0:T(128)} %constant.75) | copy-start | bytes 28
  53.0 5.1 %copy-start.7 = (s32[2]{0:T(128)S(1)}, s32[2]{0:T(128)}, u32[]{:S(2)}) copy-start(s32[2]{0:T(128)} %constant.78) | copy-start | bytes 28
  54.4 23.6 %all-to-all-start = ((f32[4,3,8,32,128]{4,3,2,1,0:T(8,128)}), f32[4,3,8,32,128]{4,3,2,1,0:T(8,128)S(1)}, u32[]{:S(2)}, u32[]{:S(2)}) async-start(f32[4,3,8,32,128]{4,3,2,1,0:T(8,128)} %broadcast_in_dim.38), calls=%async_computation | async-start | bytes 3145728 | tf_op jit(solution)/shard_map/all_to_all | solution.py:25
  78.2 11.8 %collective-permute-start.2 = (f32[3,1,32,128]{3,2,1,0:T(8,128)S(1)}, f32[3,1,32,128]{3,2,1,0:T(8,128)S(1)}, u32[]{:S(2)}, u32[]{:S(2)}) collective-permute-start(f32[3,1,32,128]{3,2,1,0:T(8,128)S(1)} %get-tuple-element.19), channel_id=1, source_target_pairs={{0,1},{1,2},{2,3},{3,4},{4,5},{5,6},{6,7},{7,8},{8,9},{9,10},{10,1... | collective-permute-start | bytes 147464 | tf_op jit(solution)/shard_map/ppermute | solution.py:15
  83.8 7.3 %collective-permute-start.3 = (f32[3,1,32,128]{3,2,1,0:T(8,128)S(1)}, f32[3,1,32,128]{3,2,1,0:T(8,128)S(1)}, u32[]{:S(2)}, u32[]{:S(2)}) collective-permute-start(f32[3,1,32,128]{3,2,1,0:T(8,128)S(1)} %get-tuple-element.20), channel_id=1, source_target_pairs={{1,0},{2,1},{3,2},{4,3},{5,4},{6,5},{7,6},{8,7},{9,8},{10,9},{11,1... | collective-permute-start | bytes 147464 | tf_op jit(solution)/shard_map/ppermute | solution.py:18
  93.2 13.1 %copy-start.3 = (s32[1,2048]{1,0:T(1,128)S(1)}, s32[1,2048]{1,0:T(1,128)}, u32[]{:S(2)}) copy-start(s32[1,2048]{1,0:T(1,128)} %param.12) | copy-start | bytes 24580
  93.2 13.7 %copy-start.5 = (f32[1,2048]{1,0:T(1,128)S(1)}, f32[1,2048]{1,0:T(1,128)}, u32[]{:S(2)}) copy-start(f32[1,2048]{1,0:T(1,128)} %param.15) | copy-start | bytes 24580
  93.2 13.7 %copy-start.6 = (f32[1,2048]{1,0:T(1,128)S(1)}, f32[1,2048]{1,0:T(1,128)}, u32[]{:S(2)}) copy-start(f32[1,2048]{1,0:T(1,128)} %param.14) | copy-start | bytes 24580
  120.1 12.8 %collective-permute-start.4 = (f32[3,1,64,128]{3,2,1,0:T(8,128)S(1)}, f32[3,1,64,128]{3,2,1,0:T(8,128)S(1)}, u32[]{:S(2)}, u32[]{:S(2)}) collective-permute-start(f32[3,1,64,128]{3,2,1,0:T(8,128)S(1)} %get-tuple-element.13), channel_id=1, source_target_pairs={{0,1},{1,2},{2,3},{3,4},{4,5},{5,6},{6,7},{7,8},{8,9},{9,10},{10,1... | collective-permute-start | bytes 294920 | tf_op jit(solution)/shard_map/ppermute | solution.py:15
  123.8 10.4 %collective-permute-start.5 = (f32[3,1,64,128]{3,2,1,0:T(8,128)S(1)}, f32[3,1,64,128]{3,2,1,0:T(8,128)S(1)}, u32[]{:S(2)}, u32[]{:S(2)}) collective-permute-start(f32[3,1,64,128]{3,2,1,0:T(8,128)S(1)} %get-tuple-element.14), channel_id=1, source_target_pairs={{1,0},{2,1},{3,2},{4,3},{5,4},{6,5},{7,6},{8,7},{9,8},{10,9},{11,1... | collective-permute-start | bytes 294920 | tf_op jit(solution)/shard_map/ppermute | solution.py:18
  139.2 35.5 %collective-permute-start.6 = (f32[20,2,32,128]{3,2,1,0:T(8,128)S(1)}, f32[20,2,32,128]{3,2,1,0:T(8,128)S(1)}, u32[]{:S(2)}, u32[]{:S(2)}) collective-permute-start(f32[20,2,32,128]{3,2,1,0:T(8,128)S(1)} %get-tuple-element.9), channel_id=1, source_target_pairs={{0,1},{1,2},{2,3},{3,4},{4,5},{5,6},{6,7},{7,8},{8,9},{9,10},{10,1... | collective-permute-start | bytes 1966088 | tf_op jit(solution)/shard_map/ppermute | solution.py:15
  141.1 33.6 %collective-permute-start.7 = (f32[20,2,32,128]{3,2,1,0:T(8,128)S(1)}, f32[20,2,32,128]{3,2,1,0:T(8,128)S(1)}, u32[]{:S(2)}, u32[]{:S(2)}) collective-permute-start(f32[20,2,32,128]{3,2,1,0:T(8,128)S(1)} %get-tuple-element.10), channel_id=1, source_target_pairs={{1,0},{2,1},{3,2},{4,3},{5,4},{6,5},{7,6},{8,7},{9,8},{10,9},{11,1... | collective-permute-start | bytes 1966088 | tf_op jit(solution)/shard_map/ppermute | solution.py:18
  177.1 1.3 copy-start.2
where the time goes:
time: 183 us; the launch traced here: 182 us
  waiting for transfers between devices  74.6 us (41%)
  starting transfers between devices  50.6 us (28%)
  other arithmetic  28.4 us (16%)
  local copies, waits for them, and re-layouts  21.8 us (12%)
  matrix products  5.4 us (3%)
    ppermute x4, waiting for transfers between devices, padded_2(): lax.ppermute(lax.slice_in_dim(block, block.shape[dim] - width, None, axis...  44.2 us
    ppermute x4, starting transfers between devices, padded_2(): lax.ppermute(lax.slice_in_dim(block, 0, width, axis=dim), axis, backward)  30.6 us
    all_to_all x1, waiting for transfers between devices, copy_for_each(): return lax.all_to_all(copies, axis, split_axis=0, concat_axis=0, tiled=True)  19.7 us
    ppermute x4, starting transfers between devices, padded_2(): lax.ppermute(lax.slice_in_dim(block, block.shape[dim] - width, None, axis...  16.4 us
    unnamed x7, other arithmetic  15.6 us
    gather x1, local copies, waits for them, and re-layouts, on_device(): picked = flat[variable, column]  13 us
    ppermute x4, waiting for transfers between devices, padded_2(): lax.ppermute(lax.slice_in_dim(block, 0, width, axis=dim), axis, backward)  10.7 us
  transfers between devices with their start and end apart: 9, of which 7 were waited for; matrix products, arithmetic and copies ran while one was open for 0% of the time, Pallas kernels for 0%

commit v1 on v0

v1 whole, which is shorter than its diff:
```python
import jax
import jax.numpy as jnp
from jax import lax
from jax.experimental import pallas as pl
from jax.experimental.pallas import tpu as pltpu
from jax.sharding import PartitionSpec as P

V = 3
F32 = jnp.float32
BF16 = jnp.bfloat16
SLOTS = 768
GROUP = 4

TILES = 64
EVEN = [(i, i ^ 1) for i in range(TILES)]
ODD = [(i, ((i - 1) ^ 1) + 1) for i in range(1, TILES - 1)] + [(0, TILES - 1), (TILES - 1, 0)]


def nn(a, b):
    return lax.dot_general(a, b, (((1,), (0,)), ((), ())), preferred_element_type=F32)


def nt(a, b):
    return lax.dot_general(a, b, (((1,), (1,)), ((), ())), preferred_element_type=F32)


def tn(a, b):
    return lax.dot_general(a, b, (((0,), (0,)), ((), ())), preferred_element_type=F32)


def halves(x):
    high = x.astype(BF16)
    low = (x - high.astype(F32)).astype(BF16)
    return high, low


def lift(smoothed, loc):
    high, low = halves(smoothed)
    return nt(high, loc) + nt(low, loc)


def call(kernel, out, grid=None, ins=None, outs=None, scratch=(), aliases=None, cost=1000000):
    vmem = pl.BlockSpec(memory_space=pltpu.VMEM)
    kw = {}
    if grid is not None:
        kw["grid"] = grid
    return pl.pallas_call(
        kernel,
        out_shape=out,
        in_specs=ins,
        out_specs=outs if outs is not None else jax.tree.map(lambda o: vmem, out),
        scratch_shapes=scratch,
        input_output_aliases=aliases or {},
        compiler_params=pltpu.CompilerParams(vmem_limit_bytes=24 * 1024 * 1024),
        cost_estimate=pl.CostEstimate(flops=cost, bytes_accessed=cost, transcendentals=0),
        **kw,
    )


def sds(*shape, dtype=F32):
    return jax.ShapeDtypeStruct(shape, dtype)


def own_kernel(alpha_ref, ens_ref, smat_ref, loc_ref, inner_ref, edge_ref):
    @pl.when(pl.program_id(0) == 0)
    def _():
        inner_ref[...] = jnp.zeros_like(inner_ref)

    smat = smat_ref[...]
    loc = loc_ref[...]
    total = [inner_ref[v] for v in range(V)]
    for k in range(GROUP):
        full = lift(nn(smat, alpha_ref[k]), loc)
        edge_ref[k, :64] = full[:64]
        edge_ref[k, 64:] = full[192:]
        lifted = full[64:192].astype(BF16).astype(F32)
        for v in range(V):
            total[v] = total[v] + ens_ref[k, v, 64:192].astype(F32) * lifted
    for v in range(V):
        inner_ref[v] = total[v]


def own_part(alpha, ensemble, smat, loc):
    members = alpha.shape[0]
    return call(
        own_kernel,
        (sds(V, 128, 128), sds(members, 128, 128)),
        grid=(members // GROUP,),
        ins=[
            pl.BlockSpec((GROUP, 256, 128), lambda i: (i, 0, 0)),
            pl.BlockSpec((GROUP, V, 256, 128), lambda i: (i, 0, 0, 0)),
            pl.BlockSpec((256, 256), lambda i: (0, 0)),
            pl.BlockSpec((128, 128), lambda i: (0, 0)),
        ],
        outs=(
            pl.BlockSpec((V, 128, 128), lambda i: (0, 0, 0)),
            pl.BlockSpec((GROUP, 128, 128), lambda i: (i, 0, 0)),
        ),
        cost=20000000,
    )(alpha, ensemble, smat, loc)


def edge_kernel(where_ref, e_ref, o_ref, own_ref, low_ref, high_ref, hmat_ref, loc_ref, inner_ref, inc_ref, se_ref, so_ref):
    step = pl.program_id(0)

    @pl.when(step == 0)
    def _():
        zeros = jnp.zeros((64, 128), F32)
        for v in range(V):
            inc_ref[v, :64] = zeros
            inc_ref[v, 64:192] = inner_ref[v]
            inc_ref[v, 192:] = zeros

    hmat = hmat_ref[...]
    loc = loc_ref[...]
    low = [inc_ref[v, :64] for v in range(V)]
    high = [inc_ref[v, 192:] for v in range(V)]
    for k in range(GROUP):
        halo = jnp.concatenate([e_ref[k].astype(BF16), o_ref[k].astype(BF16)], axis=0)
        lifted = (own_ref[k] + lift(nn(hmat, halo), loc)).astype(BF16).astype(F32)
        for v in range(V):
            low[v] = low[v] + low_ref[k, v, 0].astype(F32) * lifted[:64]
            high[v] = high[v] + high_ref[k, v, 0].astype(F32) * lifted[64:]
    for v in range(V):
        inc_ref[v, :64] = low[v]
        inc_ref[v, 192:] = high[v]

    @pl.when(step == pl.num_programs(0) - 1)
    def _():
        for v in range(V):
            se_ref[v] = inc_ref[v, pl.ds(pl.multiple_of(where_ref[0], 32), 32)]
            so_ref[v] = inc_ref[v, pl.ds(pl.multiple_of(where_ref[1], 32), 32)]


def edge_part(where, from_even, from_odd, own, quarters, hmat, loc, inner):
    members = own.shape[0]
    return call(
        edge_kernel,
        (sds(V, 256, 128), sds(V, 32, 128), sds(V, 32, 128)),
        grid=(members // GROUP,),
        ins=[
            pl.BlockSpec(memory_space=pltpu.SMEM),
            pl.BlockSpec((GROUP, 64, 128), lambda i: (i, 0, 0)),
            pl.BlockSpec((GROUP, 64, 128), lambda i: (i, 0, 0)),
            pl.BlockSpec((GROUP, 128, 128), lambda i: (i, 0, 0)),
            pl.BlockSpec((GROUP, V, 1, 64, 128), lambda i: (i, 0, 0, 0, 0)),
            pl.BlockSpec((GROUP, V, 1, 64, 128), lambda i: (i, 0, 3, 0, 0)),
            pl.BlockSpec((128, 128), lambda i: (0, 0)),
            pl.BlockSpec((128, 128), lambda i: (0, 0)),
            pl.BlockSpec((V, 128, 128), lambda i: (0, 0, 0)),
        ],
        outs=(
            pl.BlockSpec((V, 256, 128), lambda i: (0, 0, 0)),
            pl.BlockSpec((V, 32, 128), lambda i: (0, 0, 0)),
            pl.BlockSpec((V, 32, 128), lambda i: (0, 0, 0)),
        ),
    )(where, from_even, from_odd, own, quarters, quarters, hmat, loc, inner)


def tent(distance):
    return jnp.maximum(1.0 - jnp.abs(distance), 0.0)


def weights_kernel(where_ref, own_ref, e_ref, o_ref, wown_ref, wnear_ref):
    even_row = where_ref[2].astype(F32)
    odd_row = where_ref[3].astype(F32)
    odd_there = where_ref[4].astype(F32)
    cell = lax.broadcasted_iota(jnp.int32, (32, SLOTS), 0).astype(F32)

    def columns(code):
        row = jnp.floor(code * (1.0 / 64.0))
        column = code - 64.0 * row
        return row, tent(cell - (column * 0.5 - 0.25))

    for v in range(V):
        row, across = columns(own_ref[0, v : v + 1, :])
        middle = row * 0.5 - 0.25
        for r in range(8):
            wown_ref[v, 32 * r : 32 * r + 32] = (tent(r - middle) * across).astype(BF16)
        wown_ref[v, 256:288] = (tent(even_row - middle) * across).astype(BF16)
        wown_ref[v, 288:320] = (tent(odd_row - middle) * odd_there * across).astype(BF16)
        for n, ref in enumerate((e_ref, o_ref)):
            row, across = columns(ref[0, v : v + 1, :])
            wnear_ref[n, v, :32] = (0.25 * across).astype(BF16)
            wnear_ref[n, v, 32:] = (0.75 * across).astype(BF16)


def weights(where, own, even, odd):
    vmem = pl.BlockSpec(memory_space=pltpu.VMEM)
    return call(
        weights_kernel,
        (sds(V, 320, SLOTS, dtype=BF16), sds(2, V, 64, SLOTS, dtype=BF16)),
        ins=[pl.BlockSpec(memory_space=pltpu.SMEM), vmem, vmem, vmem],
        cost=5000000,
    )(where, own, even, odd)


def values_kernel(where_ref, inc_ref, e_ref, o_ref, wown_ref, wnear_ref, lev_ref, out_ref):
    level = lax.broadcasted_iota(jnp.int32, (128, SLOTS), 0).astype(F32)

    def pick(cells, weight, row):
        both = jnp.concatenate(halves(cells), axis=1)
        at_all = tn(both, weight)
        at_all = at_all[:128] + at_all[128:]
        hot = level == lev_ref[row : row + 1, :]
        out_ref[row : row + 1, :] = jnp.sum(jnp.where(hot, at_all, 0.0), axis=0, keepdims=True)

    for v in range(V):
        pick(jnp.concatenate([inc_ref[v], e_ref[v], o_ref[v]], axis=0), wown_ref[v], v)
        for n, ref in enumerate((e_ref, o_ref)):
            mine = inc_ref[v, pl.ds(pl.multiple_of(where_ref[n], 32), 32)]
            pick(jnp.concatenate([mine, ref[v]], axis=0), wnear_ref[n, v], 3 * n + 3 + v)


def values(where, inc, even, odd, wown, wnear, lev):
    vmem = pl.BlockSpec(memory_space=pltpu.VMEM)
    return call(
        values_kernel,
        sds(9, SLOTS),
        ins=[pl.BlockSpec(memory_space=pltpu.SMEM)] + [vmem] * 6,
        outs=vmem,
    )(where, inc, even, odd, wown, wnear, lev)


def adjoint_kernel(where_ref, v0, v1, v2, v3, innov_ref, weight_ref, lev_ref, wown_ref, wnear_ref, ens_ref, c_ref, se_ref, so_ref, near, sems):
    members = se_ref.shape[0]
    copies = [
        pltpu.make_async_copy(ens_ref.at[:, :, pl.ds(3 * n, 1)], near.at[:, :, pl.ds(n, 1)], sems.at[n])
        for n in range(2)
    ]
    for copy in copies:
        copy.start()
    level = lax.broadcasted_iota(jnp.int32, (128, SLOTS), 0).astype(F32)
    value = v0[...] + v1[...] + v2[...] + v3[...]
    weighted = weight_ref[...] * (value - innov_ref[...])

    def place(weight, row):
        hot = level == lev_ref[row : row + 1, :]
        spread = jnp.where(hot, weighted[row : row + 1, :], 0.0)
        both = jnp.concatenate(halves(spread), axis=0)
        out = nt(weight, both)
        return out[:, :128] + out[:, 128:]

    for v in range(V):
        c_ref[v] = place(wown_ref[v, :256], v)
        for n in range(2):
            rows = pl.ds(pl.multiple_of(where_ref[n], 32), 32)
            c_ref[v, rows] = c_ref[v, rows] + place(wnear_ref[n, v, :32], 3 * n + 3 + v)
    for copy in copies:
        copy.wait()
    odd_strip = where_ref[5]
    for n, ref in enumerate((se_ref, so_ref)):
        side = (1 - odd_strip) if n == 0 else odd_strip
        start = pl.multiple_of(192 * side, 64)
        adj = [c_ref[v, pl.ds(start, 64)] for v in range(V)]

        @pl.loop(0, members)
        def _(k):
            total = near[k, 0, side].astype(F32) * adj[0]
            for v in range(1, V):
                total = total + near[k, v, side].astype(F32) * adj[v]
            ref[k] = total


def adjoint(where, vals, innov, weight, lev, wown, wnear, quarters):
    members = quarters.shape[0]
    vmem = pl.BlockSpec(memory_space=pltpu.VMEM)
    return call(
        adjoint_kernel,
        (sds(V, 256, 128), sds(members, 64, 128), sds(members, 64, 128)),
        ins=[pl.BlockSpec(memory_space=pltpu.SMEM)] + [vmem] * 9 + [pl.BlockSpec(memory_space=pl.ANY)],
        scratch=[pltpu.VMEM((members, V, 2, 64, 128), BF16), pltpu.SemaphoreType.DMA((2,))],
    )(where, *vals, innov, weight, lev, wown, wnear, quarters)


def drop(smoothed, loc):
    high, low = halves(smoothed)
    return nn(high, loc) + nn(low, loc)


def smooth(matrix, field):
    both = jnp.concatenate(halves(field), axis=1)
    out = nn(matrix, both)
    return out[:, :128] + out[:, 128:]


def back_kernel(alpha_ref, ens_ref, c_ref, smat_ref, loc_ref, out_ref, edge_ref):
    smat = smat_ref[...]
    loc = loc_ref[...]
    for k in range(GROUP):
        back = ens_ref[k, 0].astype(F32) * c_ref[0]
        for v in range(1, V):
            back = back + ens_ref[k, v].astype(F32) * c_ref[v]
        full = alpha_ref[k].astype(F32) + drop(smooth(smat, back), loc)
        out_ref[k] = full
        edge_ref[k, :64] = full[:64]
        edge_ref[k, 64:] = full[192:]


def back_part(alpha, ensemble, c, smat, loc):
    members = alpha.shape[0]
    return call(
        back_kernel,
        (sds(members, 256, 128), sds(members, 128, 128)),
        grid=(members // GROUP,),
        ins=[
            pl.BlockSpec((GROUP, 256, 128), lambda i: (i, 0, 0)),
            pl.BlockSpec((GROUP, V, 256, 128), lambda i: (i, 0, 0, 0)),
            pl.BlockSpec((V, 256, 128), lambda i: (0, 0, 0)),
            pl.BlockSpec((256, 256), lambda i: (0, 0)),
            pl.BlockSpec((128, 128), lambda i: (0, 0)),
        ],
        outs=(
            pl.BlockSpec((GROUP, 256, 128), lambda i: (i, 0, 0)),
            pl.BlockSpec((GROUP, 128, 128), lambda i: (i, 0, 0)),
        ),
        cost=20000000,
    )(alpha, ensemble, c, smat, loc)


def last_kernel(e_ref, o_ref, edge_ref, hmat_ref, loc_ref, unused_ref, out_ref, held):
    side = pl.program_id(1)

    @pl.when(side == 0)
    def _():
        hmat = hmat_ref[...]
        loc = loc_ref[...]
        for k in range(GROUP):
            halo = jnp.concatenate([e_ref[k], o_ref[k]], axis=0)
            full = edge_ref[k] + drop(smooth(hmat, halo), loc)
            out_ref[k, 0] = full[:64]
            held[k] = full[64:]

    @pl.when(side == 1)
    def _():
        out_ref[:, 0] = held[...]


def last_part(from_even, from_odd, edge, hmat, loc, out):
    members = edge.shape[0]
    return call(
        last_kernel,
        sds(members, 4, 64, 128),
        grid=(members // GROUP, 2),
        ins=[
            pl.BlockSpec((GROUP, 64, 128), lambda i, j: (i, 0, 0)),
            pl.BlockSpec((GROUP, 64, 128), lambda i, j: (i, 0, 0)),
            pl.BlockSpec((GROUP, 128, 128), lambda i, j: (i, 0, 0)),
            pl.BlockSpec((128, 128), lambda i, j: (0, 0)),
            pl.BlockSpec((128, 128), lambda i, j: (0, 0)),
            pl.BlockSpec(memory_space=pl.ANY),
        ],
        outs=pl.BlockSpec((GROUP, 1, 64, 128), lambda i, j: (i, 3 * j, 0, 0)),
        scratch=[pltpu.VMEM((GROUP, 64, 128), F32)],
        aliases={5: 0},
    )(from_even, from_odd, edge, hmat, loc, out)


def stencil(gap):
    gap = jnp.abs(gap)
    return jnp.where(gap == 0, 6.0, jnp.where(gap == 1, 4.0, jnp.where(gap == 2, 1.0, 0.0)))


def matrices(tile, tiles, even):
    def across(i, j):
        gap = stencil(i - j)
        return jnp.where((i == j) & ((i == 0) | (i == 31)), 5.0, gap)

    i = lax.broadcasted_iota(jnp.int32, (256, 256), 0)
    j = lax.broadcasted_iota(jnp.int32, (256, 256), 1)
    ri, rj = i // 32, j // 32
    ends = ((ri == 0) & (tile == 0)) | ((ri == 7) & (tile == tiles - 1))
    down = jnp.where((ri == rj) & ends, 5.0, stencil(ri - rj))
    smat = (down * across(i % 32, j % 32) * (1.0 / 256.0)).astype(BF16)
    i = lax.broadcasted_iota(jnp.int32, (128, 128), 0)
    j = lax.broadcasted_iota(jnp.int32, (128, 128), 1)
    ri = i // 32
    ri = jnp.where(ri < 2, ri, ri + 4)
    is_even = j < 64
    above = is_even == even
    rj = jnp.where(above, 8, -2) + (j // 32) % 2
    there = is_even | ((tile > 0) & (tile < tiles - 1))
    hmat = jnp.where(there, stencil(ri - rj), 0.0) * across(i % 32, j % 32) * (1.0 / 256.0)
    return smat, hmat.astype(BF16)


def swap_even(x):
    return lax.ppermute(x, "tile", EVEN)


def swap_odd(x):
    return lax.ppermute(x, "tile", ODD)


def by_variable(x):
    return jnp.pad(x, (0, V * SLOTS - x.shape[0])).reshape(SLOTS, V).T


def on_device(alpha, ensemble, loc_vert, obs_col, obs_lev, obs_count, innovation, obs_weight):
    members = alpha.shape[0]
    tile = lax.axis_index("tile")
    tiles = lax.axis_size("tile")
    even = tile % 2 == 0
    odd_there = (tile > 0) & (tile < tiles - 1)

    high, low = alpha[:, 6:], alpha[:, :2]
    to_even = jnp.where(even, high, low).astype(F32).reshape(members, 64, 128)
    to_odd = jnp.where(even, low, high).astype(F32).reshape(members, 64, 128)
    from_even = swap_even(to_even)
    from_odd = swap_odd(to_odd)

    live = jnp.arange(obs_col.shape[1], dtype=jnp.int32) < obs_count[0]
    own_obs = jnp.stack(
        [
            by_variable(obs_col[0].astype(F32)),
            by_variable(obs_lev[0].astype(F32)),
            by_variable(innovation[0]),
            by_variable(jnp.where(live, obs_weight[0], 0.0)),
        ]
    )
    even_obs = swap_even(own_obs)
    odd_obs = swap_odd(own_obs)
    even_on = jnp.where(even, even_obs[0] < 64.0, even_obs[0] >= 960.0)
    odd_on = jnp.where(even, odd_obs[0] >= 960.0, odd_obs[0] < 64.0) & odd_there
    lev = jnp.concatenate([own_obs[1], even_obs[1], odd_obs[1]])
    innov = jnp.concatenate([own_obs[2], even_obs[2], odd_obs[2]])
    weight = jnp.concatenate(
        [own_obs[3], jnp.where(even_on, even_obs[3], 0.0), jnp.where(odd_on, odd_obs[3], 0.0)]
    )
    at_even = jnp.where(even, 7 * 32, 0)
    at_odd = jnp.where(even, 0, 7 * 32)
    where = jnp.stack(
        [
            at_even,
            at_odd,
            jnp.where(even, 8, -1),
            jnp.where(even, -1, 8),
            odd_there.astype(jnp.int32),
            tile % 2,
        ]
    ).astype(jnp.int32)
    smat, hmat = matrices(tile, tiles, even)

    flat = alpha.reshape(members, 256, 128)
    flat_ens = ensemble.reshape(members, V, 256, 128)
    quarters = ensemble.reshape(members, V, 4, 64, 128)
    inner, own_edge = own_part(flat, flat_ens, smat, loc_vert)
    wown, wnear = weights(where, own_obs, even_obs, odd_obs)
    inc, inc_even, inc_odd = edge_part(where, from_even, from_odd, own_edge, quarters, hmat, loc_vert, inner)
    near_even = swap_even(inc_even)
    near_odd = swap_odd(inc_odd)
    mine = values(where, inc, near_even, near_odd, wown, wnear, lev)
    size = lax.axis_size("mem")
    vals = [mine] + [
        lax.ppermute(mine, "mem", [(i, (i + shift) % size) for i in range(size)]) for shift in range(1, size)
    ]
    c, back_even, back_odd = adjoint(where, vals, innov, weight, lev, wown, wnear, quarters)
    halo_even = swap_even(back_even)
    halo_odd = swap_odd(back_odd)
    out, out_edge = back_part(flat, flat_ens, c, smat, loc_vert)
    out = last_part(halo_even, halo_odd, out_edge, hmat, loc_vert, out.reshape(members, 4, 64, 128))
    return out.reshape(members, 8, 32, 128)


def solution(mesh):
    in_specs = (
        P("mem", "tile", None, None),
        P("mem", None, "tile", None, None),
        P(),
        P("tile", None),
        P("tile", None),
        P("tile"),
        P("tile", None),
        P("tile", None),
    )
    out_specs = P("mem", "tile", None, None)
    return jax.shard_map(
        on_device, mesh=mesh, in_specs=in_specs, out_specs=out_specs, check_vma=False
    )
```

time: 183 us -> 122 us (0.67)
  the two profiles are of different devices: /device:TPU:6 before, /device:TPU:32 now
where the time goes in v1:
time: 122 us; the launch traced here: 121 us
  waiting for transfers between devices  73.8 us (60%)
  Pallas kernels  22 us (18%)
  starting transfers between devices  15.3 us (13%)
  other arithmetic  4.89 us (4%)
  local copies, waits for them, and re-layouts  4.66 us (4%)
    ppermute x4, waiting for transfers between devices, swap_even(): return lax.ppermute(x, 'tile', EVEN)  49.5 us
    ppermute x4, waiting for transfers between devices, swap_odd(): return lax.ppermute(x, 'tile', ODD)  20.1 us
    ppermute x4, starting transfers between devices, swap_odd(): return lax.ppermute(x, 'tile', ODD)  11.6 us
    pallas_call x1, Pallas kernels, last_part(): call(last_kernel, sds(members, 4, 64, 128), grid=(members // GROUP, 2), i...  5.38 us
    pallas_call x1, Pallas kernels, back_part(): call(back_kernel, (sds(members, 256, 128), sds(members, 128, 128)), grid=...  4.67 us
    ppermute x3, waiting for transfers between devices, on_device(): lax.ppermute(mine, 'mem', [(i, (i + shift) % size) for i in range(size)])  4.16 us
    pallas_call x1, Pallas kernels, edge_part(): call(edge_kernel, (sds(V, 256, 128), sds(V, 32, 128), sds(V, 32, 128)), g...  3.71 us
    ppermute x4, starting transfers between devices, swap_even(): return lax.ppermute(x, 'tile', EVEN)  3.11 us
  transfers between devices with their start and end apart: 11, of which 9 were waited for; matrix products, arithmetic and copies ran while one was open for 2% of the time, Pallas kernels for 7%

profile of v1, /device:TPU:32, one launch (start us, length us, event | category | flops | bytes accessed | tf_op | source)
XLA Modules:
  0.0 121.5 jit_solution(83521381579512822)
XLA Ops:
  0.7 0.7 convert_element_type.28
  1.4 0.7 fusion.26
  2.1 0.7 convert_element_type.30
  2.8 0.7 pad.15
  3.5 0.3 reshape.68
  3.9 0.3 reshape.67
  4.4 0.3 reshape.66
  4.8 0.3 reshape.69
  5.3 10.1 %collective-permute-start.5 = (f32[4,3,768]{2,1,0:T(4,128)S(1)}, f32[4,3,768]{2,1,0:T(4,128)S(1)}, u32[]{:S(2)}, u32[]{:S(2)}) collective-permute-start(f32[4,3,768]{2,1,0:T(4,128)S(1)} %pad_maximum_fusion.own_ref), channel_id=1, source_target_pairs={{1,2},{2,1},{3,4},{4,3},{5,6},{6,5},{7,8},{8,7},{9,10},{10,9},{11,... | collective-permute-start | bytes 110600 | tf_op jit(solution)/shard_map/ppermute | solution.py:392
  15.5 0.9 bitcast_convert_fusion.1
  16.4 2.9 %collective-permute-start = (f32[20,64,128]{2,1,0:T(8,128)}, f32[20,64,128]{2,1,0:T(8,128)S(1)}, u32[]{:S(2)}, u32[]{:S(2)}) collective-permute-start(f32[20,64,128]{2,1,0:T(8,128)} %bitcast_convert_fusion.1), channel_id=1, source_target_pairs={{0,1},{1,0},{2,3},{3,2},{4,5},{5,4},{6,7},{7,6},{8,9},{9,8},{10,11... | collective-permute-start | bytes 1966088 | tf_op jit(solution)/shard_map/ppermute | solution.py:388
  19.3 0.9 bitcast_convert_fusion
  20.4 0.6 multiply_convert_fusion.smat_ref
  21.3 2.1 %copy-done = bf16[20,3,8,32,128]{4,3,2,1,0:T(8,128)(2,1)S(1)} copy-done((bf16[20,3,8,32,128]{4,3,2,1,0:T(8,128)(2,1)S(1)}, bf16[20,3,8,32,128]{4,3,2,1,0:T(8,128)(2,1)}, u32[]{:S(2)}) %copy-start) | copy-done | bytes 3932184
  23.4 2.9 %shard_map.82 = (f32[3,128,128]{2,1,0:T(8,128)S(1)}, f32[20,128,128]{2,1,0:T(8,128)S(1)}) custom-call(bf16[20,256,128]{2,1,0:T(8,128)(2,1)S(1)} %bitcast.52, bf16[20,3,256,128]{3,2,1,0:T(8,128)(2,1)S(1)} %bitcast.47, bf16[256,256]{1,0:T(8,128)(2,1)S(1)} %multiply_convert_fusion.smat_ref, bf16[128,128]{1,0:T(8,128)(2,1)S(1)} %copy-done.3), custom_call_target="tpu_custom_call" | custom-call | flops 20000000 | bytes 20000000 | tf_op jit(solution)/shard_map/pallas_call | solution.py:85
  26.4 21.4 %collective-permute-done.e_ref = f32[20,64,128]{2,1,0:T(8,128)S(1)} collective-permute-done((f32[20,64,128]{2,1,0:T(8,128)}, f32[20,64,128]{2,1,0:T(8,128)S(1)}, u32[]{:S(2)}, u32[]{:S(2)}) %collective-permute-start) | collective-permute-done | bytes 655392 | tf_op jit(solution)/shard_map/ppermute | solution.py:388
  47.8 8.7 %collective-permute-done.1.o_ref = f32[20,64,128]{2,1,0:T(8,128)S(1)} collective-permute-done((f32[20,64,128]{2,1,0:T(8,128)}, f32[20,64,128]{2,1,0:T(8,128)S(1)}, u32[]{:S(2)}, u32[]{:S(2)}) %collective-permute-start.1) | collective-permute-done | bytes 655392 | tf_op jit(solution)/shard_map/ppermute | solution.py:392
  56.5 3.7 %shard_map.83 = (f32[3,256,128]{2,1,0:T(8,128)S(1)}, f32[3,32,128]{2,1,0:T(8,128)S(1)}, f32[3,32,128]{2,1,0:T(8,128)S(1)}) custom-call(s32[6]{0:T(128)S(1)} %stack.46.where_ref, f32[20,64,128]{2,1,0:T(8,128)S(1)} %collective-permute-done.e_ref, f32[20,64,128]{2,1,0:T(8,128)S(1)} %collective-permute-done.1.o_ref, ...), custom_call_target="tpu_custom_call" | custom-call | flops 1000000 | bytes 1000000 | tf_op jit(solution)/shard_map/pallas_call | solution.py:137
  60.3 0.5 collective-permute-start.3
  60.8 0.9 shard_map.84
  61.8 3.5 %collective-permute-done.2.e_ref = f32[3,32,128]{2,1,0:T(8,128)S(1)} collective-permute-done((f32[3,32,128]{2,1,0:T(8,128)S(1)}, f32[3,32,128]{2,1,0:T(8,128)S(1)}, u32[]{:S(2)}, u32[]{:S(2)}) %collective-permute-start.2) | collective-permute-done | bytes 49184 | tf_op jit(solution)/shard_map/ppermute | solution.py:388
  65.3 5.6 %collective-permute-done.3.o_ref = f32[3,32,128]{2,1,0:T(8,128)S(1)} collective-permute-done((f32[3,32,128]{2,1,0:T(8,128)S(1)}, f32[3,32,128]{2,1,0:T(8,128)S(1)}, u32[]{:S(2)}, u32[]{:S(2)}) %collective-permute-start.3) | collective-permute-done | bytes 49184 | tf_op jit(solution)/shard_map/ppermute | solution.py:392
  70.9 2.0 %shard_map.85.v0 = f32[9,768]{1,0:T(8,128)S(1)} custom-call(s32[6]{0:T(128)S(1)} %stack.46.where_ref, f32[3,256,128]{2,1,0:T(8,128)S(1)} %get-tuple-element.19.inc_ref, f32[3,32,128]{2,1,0:T(8,128)S(1)} %collective-permute-done.2.e_ref, f32[3,32,128]{2,1,0:T(8,128)S(1)} %collective-permute-done.3.o_ref, bf16[3,320,768]{2,1,0:T(8,128)(2,1)S(1)} %get-tuple-element.22.wown_ref, ...), custom_call_target="tpu_custom_call" | custom-call | flops 1000000 | bytes 1000000 | tf_op jit(solution)/shard_map/pallas_call | solution.py:217
  73.1 0.4 collective-permute-start.6
  73.5 1.4 %collective-permute-done.8.v3 = f32[9,768]{1,0:T(8,128)S(1)} collective-permute-done((f32[9,768]{1,0:T(8,128)S(1)}, f32[9,768]{1,0:T(8,128)S(1)}, u32[]{:S(2)}, u32[]{:S(2)}) %collective-permute-start.8) | collective-permute-done | bytes 27680 | tf_op jit(solution)/shard_map/ppermute | solution.py:455
  74.9 2.7 %collective-permute-done.7.v2 = f32[9,768]{1,0:T(8,128)S(1)} collective-permute-done((f32[9,768]{1,0:T(8,128)S(1)}, f32[9,768]{1,0:T(8,128)S(1)}, u32[]{:S(2)}, u32[]{:S(2)}) %collective-permute-start.7) | collective-permute-done | bytes 27680 | tf_op jit(solution)/shard_map/ppermute | solution.py:455
  77.7 2.4 %shard_map.86 = (f32[3,256,128]{2,1,0:T(8,128)S(1)}, f32[20,64,128]{2,1,0:T(8,128)S(1)}, f32[20,64,128]{2,1,0:T(8,128)S(1)}) custom-call(s32[6]{0:T(128)S(1)} %stack.46.where_ref, f32[9,768]{1,0:T(8,128)S(1)} %shard_map.85.v0, f32[9,768]{1,0:T(8,128)S(1)} %collective-permute-done.6.v1, f32[9,768]{1,0:T(8,128)S(1)} %collective-permute-done.7.v2, ...), custom_call_target="tpu_custom_call" | custom-call | flops 1000000 | bytes 1000000 | tf_op jit(solution)/shard_map/pallas_call | solution.py:268
  80.2 0.9 collective-permute-start.10
  81.1 4.7 %shard_map.87 = (f32[20,256,128]{2,1,0:T(8,128)}, f32[20,128,128]{2,1,0:T(8,128)S(1)}) custom-call(bf16[20,256,128]{2,1,0:T(8,128)(2,1)S(1)} %bitcast.53, bf16[20,3,256,128]{3,2,1,0:T(8,128)(2,1)S(1)} %bitcast.51, f32[3,256,128]{2,1,0:T(8,128)S(1)} %get-tuple-element.26.c_ref, bf16[256,256]{1,0:T(8,128)(2,1)S(1)} %multiply_convert_fusion.smat_ref, ...), custom_call_target="tpu_custom_call" | custom-call | flops 20000000 | bytes 20000000 | tf_op jit(solution)/shard_map/pallas_call | solution.py:302
  85.8 24.5 %collective-permute-done.9.e_ref = f32[20,64,128]{2,1,0:T(8,128)S(1)} collective-permute-done((f32[20,64,128]{2,1,0:T(8,128)S(1)}, f32[20,64,128]{2,1,0:T(8,128)S(1)}, u32[]{:S(2)}, u32[]{:S(2)}) %collective-permute-start.9) | collective-permute-done | bytes 655392 | tf_op jit(solution)/shard_map/ppermute | solution.py:388
  110.3 5.8 %collective-permute-done.10.o_ref = f32[20,64,128]{2,1,0:T(8,128)S(1)} collective-permute-done((f32[20,64,128]{2,1,0:T(8,128)S(1)}, f32[20,64,128]{2,1,0:T(8,128)S(1)}, u32[]{:S(2)}, u32[]{:S(2)}) %collective-permute-start.10) | collective-permute-done | bytes 655392 | tf_op jit(solution)/shard_map/ppermute | solution.py:392
  116.1 5.4 %shard_map.88 = f32[20,4,64,128]{3,2,1,0:T(8,128)} custom-call(f32[20,64,128]{2,1,0:T(8,128)S(1)} %collective-permute-done.9.e_ref, f32[20,64,128]{2,1,0:T(8,128)S(1)} %collective-permute-done.10.o_ref, f32[20,128,128]{2,1,0:T(8,128)S(1)} %get-tuple-element.27.edge_ref, ...), custom_call_target="tpu_custom_call", output_to_operand_aliasing={{}: (5, {})} | custom-call | flops 1000000 | bytes 1000000 | tf_op jit(solution)/shard_map/pallas_call | solution.py:341
  (39 shorter events, 1.6 us)
Async XLA Ops:
  3.8 11.7 %copy-start.2 = (bf16[20,8,32,128]{3,2,1,0:T(8,128)(2,1)S(1)}, bf16[20,8,32,128]{3,2,1,0:T(8,128)(2,1)}, u32[]{:S(2)}) copy-start(bf16[20,8,32,128]{3,2,1,0:T(8,128)(2,1)} %param.8) | copy-start | bytes 3932164
  5.3 21.0 %collective-permute-start.5 = (f32[4,3,768]{2,1,0:T(4,128)S(1)}, f32[4,3,768]{2,1,0:T(4,128)S(1)}, u32[]{:S(2)}, u32[]{:S(2)}) collective-permute-start(f32[4,3,768]{2,1,0:T(4,128)S(1)} %pad_maximum_fusion.own_ref), channel_id=1, source_target_pairs={{1,2},{2,1},{3,4},{4,3},{5,6},{6,5},{7,8},{8,7},{9,10},{10,9},{11,... | collective-permute-start | bytes 110600 | tf_op jit(solution)/shard_map/ppermute | solution.py:392
  15.4 10.9 %collective-permute-start.4 = (f32[4,3,768]{2,1,0:T(4,128)S(1)}, f32[4,3,768]{2,1,0:T(4,128)S(1)}, u32[]{:S(2)}, u32[]{:S(2)}) collective-permute-start(f32[4,3,768]{2,1,0:T(4,128)S(1)} %pad_maximum_fusion.own_ref), channel_id=1, source_target_pairs={{0,1},{1,0},{2,3},{3,2},{4,5},{5,4},{6,7},{7,6},{8,9},{9,8},{10,11... | collective-permute-start | bytes 110600 | tf_op jit(solution)/shard_map/ppermute | solution.py:388
  15.4 5.9 %copy-start.3 = (bf16[128,128]{1,0:T(8,128)(2,1)S(1)}, bf16[128,128]{1,0:T(8,128)(2,1)}, u32[]{:S(2)}) copy-start(bf16[128,128]{1,0:T(8,128)(2,1)} %loc_ref.7) | copy-start | bytes 98308
  16.4 31.4 %collective-permute-start = (f32[20,64,128]{2,1,0:T(8,128)}, f32[20,64,128]{2,1,0:T(8,128)S(1)}, u32[]{:S(2)}, u32[]{:S(2)}) collective-permute-start(f32[20,64,128]{2,1,0:T(8,128)} %bitcast_convert_fusion.1), channel_id=1, source_target_pairs={{0,1},{1,0},{2,3},{3,2},{4,5},{5,4},{6,7},{7,6},{8,9},{9,8},{10,11... | collective-permute-start | bytes 1966088 | tf_op jit(solution)/shard_map/ppermute | solution.py:388
  20.2 36.3 %collective-permute-start.1 = (f32[20,64,128]{2,1,0:T(8,128)}, f32[20,64,128]{2,1,0:T(8,128)S(1)}, u32[]{:S(2)}, u32[]{:S(2)}) collective-permute-start(f32[20,64,128]{2,1,0:T(8,128)} %bitcast_convert_fusion), channel_id=1, source_target_pairs={{1,2},{2,1},{3,4},{4,3},{5,6},{6,5},{7,8},{8,7},{9,10},{10,9},{11,... | collective-permute-start | bytes 1966088 | tf_op jit(solution)/shard_map/ppermute | solution.py:392
  21.3 2.1 %copy-start = (bf16[20,3,8,32,128]{4,3,2,1,0:T(8,128)(2,1)S(1)}, bf16[20,3,8,32,128]{4,3,2,1,0:T(8,128)(2,1)}, u32[]{:S(2)}) copy-start(bf16[20,3,8,32,128]{4,3,2,1,0:T(8,128)(2,1)} %param.9) | copy-start | bytes 11796484
  23.4 33.1 %copy-start.1 = (bf16[20,3,8,32,128]{4,3,2,1,0:T(8,128)(2,1)S(1)}, bf16[20,3,8,32,128]{4,3,2,1,0:T(8,128)(2,1)}, u32[]{:S(2)}) copy-start(bf16[20,3,8,32,128]{4,3,2,1,0:T(8,128)(2,1)} %param.9) | copy-start | bytes 11796484
  60.2 5.1 %collective-permute-start.2 = (f32[3,32,128]{2,1,0:T(8,128)S(1)}, f32[3,32,128]{2,1,0:T(8,128)S(1)}, u32[]{:S(2)}, u32[]{:S(2)}) collective-permute-start(f32[3,32,128]{2,1,0:T(8,128)S(1)} %get-tuple-element.20), channel_id=1, source_target_pairs={{0,1},{1,0},{2,3},{3,2},{4,5},{5,4},{6,7},{7,6},{8,9},{9,8},{10,11... | collective-permute-start | bytes 147464 | tf_op jit(solution)/shard_map/ppermute | solution.py:388
  60.3 10.6 %collective-permute-start.3 = (f32[3,32,128]{2,1,0:T(8,128)S(1)}, f32[3,32,128]{2,1,0:T(8,128)S(1)}, u32[]{:S(2)}, u32[]{:S(2)}) collective-permute-start(f32[3,32,128]{2,1,0:T(8,128)S(1)} %get-tuple-element.21), channel_id=1, source_target_pairs={{1,2},{2,1},{3,4},{4,3},{5,6},{6,5},{7,8},{8,7},{9,10},{10,9},{11,... | collective-permute-start | bytes 147464 | tf_op jit(solution)/shard_map/ppermute | solution.py:392
  72.9 2.0 %collective-permute-start.8 = (f32[9,768]{1,0:T(8,128)S(1)}, f32[9,768]{1,0:T(8,128)S(1)}, u32[]{:S(2)}, u32[]{:S(2)}) collective-permute-start(f32[9,768]{1,0:T(8,128)S(1)} %shard_map.85.v0), channel_id=1, source_target_pairs={{0,192},{64,0},{128,64},{192,128},{1,193},{65,1},{129,65},{193,129... | collective-permute-start | bytes 82952 | tf_op jit(solution)/shard_map/ppermute | solution.py:455
  73.0 4.6 %collective-permute-start.7 = (f32[9,768]{1,0:T(8,128)S(1)}, f32[9,768]{1,0:T(8,128)S(1)}, u32[]{:S(2)}, u32[]{:S(2)}) collective-permute-start(f32[9,768]{1,0:T(8,128)S(1)} %shard_map.85.v0), channel_id=1, source_target_pairs={{0,128},{64,192},{128,0},{192,64},{1,129},{65,193},{129,1},{193,65... | collective-permute-start | bytes 82952 | tf_op jit(solution)/shard_map/ppermute | solution.py:455
  73.1 4.6 %collective-permute-start.6 = (f32[9,768]{1,0:T(8,128)S(1)}, f32[9,768]{1,0:T(8,128)S(1)}, u32[]{:S(2)}, u32[]{:S(2)}) collective-permute-start(f32[9,768]{1,0:T(8,128)S(1)} %shard_map.85.v0), channel_id=1, source_target_pairs={{0,64},{64,128},{128,192},{192,0},{1,65},{65,129},{129,193},{193,1... | collective-permute-start | bytes 82952 | tf_op jit(solution)/shard_map/ppermute | solution.py:455
  80.1 30.2 %collective-permute-start.9 = (f32[20,64,128]{2,1,0:T(8,128)S(1)}, f32[20,64,128]{2,1,0:T(8,128)S(1)}, u32[]{:S(2)}, u32[]{:S(2)}) collective-permute-start(f32[20,64,128]{2,1,0:T(8,128)S(1)} %get-tuple-element.24), channel_id=1, source_target_pairs={{0,1},{1,0},{2,3},{3,2},{4,5},{5,4},{6,7},{7,6},{8,9},{9,8},{10,11... | collective-permute-start | bytes 1966088 | tf_op jit(solution)/shard_map/ppermute | solution.py:388
  80.2 35.9 %collective-permute-start.10 = (f32[20,64,128]{2,1,0:T(8,128)S(1)}, f32[20,64,128]{2,1,0:T(8,128)S(1)}, u32[]{:S(2)}, u32[]{:S(2)}) collective-permute-start(f32[20,64,128]{2,1,0:T(8,128)S(1)} %get-tuple-element.25), channel_id=1, source_target_pairs={{1,2},{2,1},{3,4},{4,3},{5,6},{6,5},{7,8},{8,7},{9,10},{10,9},{11,... | collective-permute-start | bytes 1966088 | tf_op jit(solution)/shard_map/ppermute | solution.py:392

commit v2 on v1

v2 whole, which is shorter than its diff:
```python
import functools

import jax
import jax.numpy as jnp
from jax import lax
from jax.experimental import pallas as pl
from jax.experimental.pallas import tpu as pltpu
from jax.sharding import PartitionSpec as P

V = 3
F32 = jnp.float32
BF16 = jnp.bfloat16
SLOTS = 768
GROUP = 4
PAIRS = 10

TILES = 64
EVEN = [(i, i ^ 1) for i in range(TILES)]
ODD = [(i, ((i - 1) ^ 1) + 1) for i in range(1, TILES - 1)] + [(0, TILES - 1), (TILES - 1, 0)]


def nn(a, b):
    return lax.dot_general(a, b, (((1,), (0,)), ((), ())), preferred_element_type=F32)


def nt(a, b):
    return lax.dot_general(a, b, (((1,), (1,)), ((), ())), preferred_element_type=F32)


def tn(a, b):
    return lax.dot_general(a, b, (((0,), (0,)), ((), ())), preferred_element_type=F32)


def halves(x):
    high = x.astype(BF16)
    low = (x - high.astype(F32)).astype(BF16)
    return high, low


def lift(smoothed, loc):
    high, low = halves(smoothed)
    return nt(high, loc) + nt(low, loc)


def call(kernel, out, grid=None, ins=None, outs=None, scratch=(), aliases=None, cost=1000000):
    vmem = pl.BlockSpec(memory_space=pltpu.VMEM)
    kw = {}
    if grid is not None:
        kw["grid"] = grid
    return pl.pallas_call(
        kernel,
        out_shape=out,
        in_specs=ins,
        out_specs=outs if outs is not None else jax.tree.map(lambda o: vmem, out),
        scratch_shapes=scratch,
        input_output_aliases=aliases or {},
        compiler_params=pltpu.CompilerParams(vmem_limit_bytes=24 * 1024 * 1024),
        cost_estimate=pl.CostEstimate(flops=cost, bytes_accessed=cost, transcendentals=0),
        **kw,
    )


def sds(*shape, dtype=F32):
    return jax.ShapeDtypeStruct(shape, dtype)


ANY = pl.BlockSpec(memory_space=pl.ANY)
SMEM = pl.BlockSpec(memory_space=pltpu.SMEM)
VMEM = pl.BlockSpec(memory_space=pltpu.VMEM)


def smooth(matrix, field):
    both = jnp.concatenate(halves(field), axis=1)
    out = nn(matrix, both)
    return out[:, :128] + out[:, 128:]


def twice(loc):
    zeros = jnp.zeros_like(loc)
    return jnp.concatenate(
        [jnp.concatenate([loc, zeros], axis=1), jnp.concatenate([zeros, loc], axis=1)], axis=0
    )


def edge_levels(first, second, both, odd, e_ref, o_ref, p):
    out = nt(jnp.concatenate([first, second], axis=1), both)
    low, high = out[:64], out[64:]
    e_ref[p] = jnp.where(odd, low, high)
    o_ref[p] = jnp.where(odd, high, low)


def send_kernel(where_ref, low_ref, high_ref, loc_ref, e_ref, o_ref, token_ref):
    odd = where_ref[5] == 1
    both = twice(loc_ref[:64])
    for p in range(PAIRS):
        members = [jnp.concatenate([low_ref[m, p, 0], high_ref[m, p, 0]], axis=0) for m in range(2)]
        edge_levels(*members, both, odd, e_ref, o_ref, p)
    token_ref[...] = jnp.zeros_like(token_ref)


def send_part(where, quarters, loc):
    edge = lambda q: pl.BlockSpec((2, PAIRS, 1, 64, 128), lambda i: (0, 0, q, 0, 0))
    flat = pl.BlockSpec((PAIRS, 64, 128), lambda i: (0, 0, 0))
    return call(
        send_kernel,
        (sds(PAIRS, 64, 128), sds(PAIRS, 64, 128), sds(8, 128)),
        grid=(1,),
        ins=[SMEM, edge(0), edge(3), pl.BlockSpec((128, 128), lambda i: (0, 0))],
        outs=(flat, flat, pl.BlockSpec((8, 128), lambda i: (0, 0))),
    )(where, quarters, quarters, loc)


def packed(first, second, h):
    return jnp.concatenate([first[:, 64 * h : 64 * h + 64], second[:, 64 * h : 64 * h + 64]], axis=1)


def own_kernel(where_ref, alpha_ref, ens_ref, loc_ref, after_ref, inner_ref, la_ref, lb_ref, xa_ref, xb_ref, smat_ref, hmat_ref, token_ref, eb_ref, ob_ref):
    @pl.when(pl.program_id(0) == 0)
    def _():
        inner_ref[...] = jnp.zeros_like(inner_ref)
        token_ref[...] = jnp.zeros_like(token_ref)
        smat, hmat = matrices(where_ref[6], TILES, where_ref[5] == 0)
        smat_ref[...] = smat
        hmat_ref[...] = hmat

    smat = smat_ref[...]
    loc = loc_ref[...]
    total = [inner_ref[v] for v in range(V)]
    odd = where_ref[5] == 1
    both = twice(loc[64:])
    for p in range(2):
        members = [jnp.concatenate([alpha_ref[m, p, :64], alpha_ref[m, p, 192:]], axis=0) for m in range(2)]
        edge_levels(*members, both, odd, eb_ref, ob_ref, p)
        edges = []
        for m in range(2):
            full = lift(nn(smat, alpha_ref[m, p]), loc)
            edges.append(jnp.concatenate([full[:64], full[192:]], axis=0))
            lifted = full[64:192].astype(BF16).astype(F32)
            for v in range(V):
                total[v] = total[v] + ens_ref[m, p, v, 64:192].astype(F32) * lifted
        for h, (l_ref, x_ref) in enumerate(((la_ref, xa_ref), (lb_ref, xb_ref))):
            l_ref[p] = packed(edges[0], edges[1], h)
            for v in range(V):
                for side in range(2):
                    rows = slice(192 * side, 192 * side + 64)
                    x_ref[p, v, 64 * side : 64 * side + 64] = packed(ens_ref[0, p, v, rows], ens_ref[1, p, v, rows], h)
    for v in range(V):
        inner_ref[v] = total[v]


def own_part(where, alpha, ensemble, loc, after):
    whole = lambda *shape: pl.BlockSpec(shape, lambda i: (0,) * len(shape))
    fields = pl.BlockSpec((2, 128, 128), lambda i: (i, 0, 0))
    members = pl.BlockSpec((2, V, 128, 128), lambda i: (i, 0, 0, 0))
    return call(
        own_kernel,
        (
            sds(V, 128, 128),
            sds(PAIRS, 128, 128),
            sds(PAIRS, 128, 128),
            sds(PAIRS, V, 128, 128, dtype=BF16),
            sds(PAIRS, V, 128, 128, dtype=BF16),
            sds(256, 256, dtype=BF16),
            sds(128, 128, dtype=BF16),
            sds(8, 128),
            sds(PAIRS, 64, 128),
            sds(PAIRS, 64, 128),
        ),
        grid=(PAIRS // 2,),
        ins=[
            SMEM,
            pl.BlockSpec((2, 2, 256, 128), lambda i: (0, i, 0, 0)),
            pl.BlockSpec((2, 2, V, 256, 128), lambda i: (0, i, 0, 0, 0)),
            whole(128, 128),
            whole(8, 128),
        ],
        outs=(
            whole(V, 128, 128),
            fields,
            fields,
            members,
            members,
            whole(256, 256),
            whole(128, 128),
            whole(8, 128),
            pl.BlockSpec((2, 64, 128), lambda i: (i, 0, 0)),
            pl.BlockSpec((2, 64, 128), lambda i: (i, 0, 0)),
        ),
    )(where, alpha, ensemble, loc, after)


def pass_kernel(obs_ref, after_ref, out_ref):
    out_ref[...] = obs_ref[...]


def pass_on(obs, after):
    return call(pass_kernel, sds(*obs.shape), ins=[VMEM, VMEM], outs=VMEM)(obs, after)


def edge_kernel(h, where_ref, e_ref, o_ref, own_ref, x_ref, hmat_ref, loc_ref, inner_ref, after_ref, inc_ref, se_ref, so_ref):
    hmat = hmat_ref[...]
    total = [jnp.zeros((128, 128), F32) for v in range(V)]
    for p in range(PAIRS):
        halo = jnp.concatenate([e_ref[p], o_ref[p]], axis=0)
        lifted = (own_ref[p] + smooth(hmat, halo)).astype(BF16).astype(F32)
        for v in range(V):
            total[v] = total[v] + x_ref[p, v].astype(F32) * lifted
    for v in range(V):
        edges = total[v][:, :64] + total[v][:, 64:]
        inc_ref[v, :64] = edges[:64]
        inc_ref[v, 64:192] = inner_ref[v][:, 64 * h : 64 * h + 64]
        inc_ref[v, 192:] = edges[64:]
        for n, ref in enumerate((se_ref, so_ref)):
            row = inc_ref[v, pl.ds(pl.multiple_of(where_ref[n], 32), 32)]
            ref[v] = jnp.concatenate([row[:16], row[16:]], axis=1)


def edge_part(h, where, from_even, from_odd, own, x, hmat, loc, inner, after):
    return call(
        functools.partial(edge_kernel, h),
        (sds(V, 256, 64), sds(V, 16, 128), sds(V, 16, 128)),
        ins=[SMEM] + [VMEM] * 8,
        outs=(VMEM,) * 3,
    )(where, from_even, from_odd, own, x, hmat, loc, inner, after)


def tent(distance):
    return jnp.maximum(1.0 - jnp.abs(distance), 0.0)


def weights_kernel(where_ref, own_ref, e_ref, o_ref, wown_ref, wnear_ref):
    even_row = where_ref[2].astype(F32)
    odd_row = where_ref[3].astype(F32)
    odd_there = where_ref[4].astype(F32)
    cell = lax.broadcasted_iota(jnp.int32, (32, SLOTS), 0).astype(F32)

    def columns(code):
        row = jnp.floor(code * (1.0 / 64.0))
        column = code - 64.0 * row
        return row, tent(cell - (column * 0.5 - 0.25))

    for v in range(V):
        row, across = columns(own_ref[0, v : v + 1, :])
        middle = row * 0.5 - 0.25
        for r in range(8):
            wown_ref[v, 32 * r : 32 * r + 32] = (tent(r - middle) * across).astype(BF16)
        wown_ref[v, 256:288] = (tent(even_row - middle) * across).astype(BF16)
        wown_ref[v, 288:320] = (tent(odd_row - middle) * odd_there * across).astype(BF16)
        for n, ref in enumerate((e_ref, o_ref)):
            row, across = columns(ref[0, v : v + 1, :])
            wnear_ref[n, v, :32] = (0.25 * across).astype(BF16)
            wnear_ref[n, v, 32:] = (0.75 * across).astype(BF16)


def weights(where, own, even, odd):
    vmem = pl.BlockSpec(memory_space=pltpu.VMEM)
    return call(
        weights_kernel,
        (sds(V, 320, SLOTS, dtype=BF16), sds(2, V, 64, SLOTS, dtype=BF16)),
        ins=[pl.BlockSpec(memory_space=pltpu.SMEM), vmem, vmem, vmem],
        cost=5000000,
    )(where, own, even, odd)


def values_kernel(h, where_ref, inc_ref, e_ref, o_ref, wown_ref, wnear_ref, lev_ref, after_ref, out_ref):
    level = lax.broadcasted_iota(jnp.int32, (64, SLOTS), 0).astype(F32) + 64.0 * h

    def pick(cells, weight, row):
        both = jnp.concatenate(halves(cells), axis=1)
        at_all = tn(both, weight)
        at_all = at_all[:64] + at_all[64:]
        hot = level == lev_ref[row : row + 1, :]
        out_ref[row : row + 1, :] = jnp.sum(jnp.where(hot, at_all, 0.0), axis=0, keepdims=True)

    for v in range(V):
        near = []
        for ref in (e_ref, o_ref):
            row = ref[v]
            near.append(jnp.concatenate([row[:, :64], row[:, 64:]], axis=0))
        pick(jnp.concatenate([inc_ref[v]] + near, axis=0), wown_ref[v], v)
        for n in range(2):
            mine = inc_ref[v, pl.ds(pl.multiple_of(where_ref[n], 32), 32)]
            pick(jnp.concatenate([mine, near[n]], axis=0), wnear_ref[n, v], 3 * n + 3 + v)


def values(h, where, inc, even, odd, wown, wnear, lev, after):
    return call(
        functools.partial(values_kernel, h),
        sds(9, SLOTS),
        ins=[SMEM] + [VMEM] * 7,
        outs=VMEM,
    )(where, inc, even, odd, wown, wnear, lev, after)


def adjoint_kernel(h, where_ref, v0, v1, v2, v3, innov_ref, weight_ref, lev_ref, wown_ref, wnear_ref, x_ref, after_ref, c_ref, se_ref, so_ref):
    level = lax.broadcasted_iota(jnp.int32, (64, SLOTS), 0).astype(F32) + 64.0 * h
    value = v0[...] + v1[...] + v2[...] + v3[...]
    weighted = weight_ref[...] * (value - innov_ref[...])

    def place(weight, row):
        hot = level == lev_ref[row : row + 1, :]
        spread = jnp.where(hot, weighted[row : row + 1, :], 0.0)
        both = jnp.concatenate(halves(spread), axis=0)
        out = nt(weight, both)
        return out[:, :64] + out[:, 64:]

    adj = []
    for v in range(V):
        c_ref[v] = place(wown_ref[v, :256], v)
        for n in range(2):
            rows = pl.ds(pl.multiple_of(where_ref[n], 32), 32)
            c_ref[v, rows] = c_ref[v, rows] + place(wnear_ref[n, v, :32], 3 * n + 3 + v)
        edges = jnp.concatenate([c_ref[v, :64], c_ref[v, 192:]], axis=0)
        adj.append(jnp.concatenate([edges, edges], axis=1))
    odd = where_ref[5] == 1
    for p in range(PAIRS):
        total = x_ref[p, 0].astype(F32) * adj[0]
        for v in range(1, V):
            total = total + x_ref[p, v].astype(F32) * adj[v]
        low, high = total[:64], total[64:]
        se_ref[p] = jnp.where(odd, low, high)
        so_ref[p] = jnp.where(odd, high, low)


def adjoint(h, where, vals, innov, weight, lev, wown, wnear, x, after):
    return call(
        functools.partial(adjoint_kernel, h),
        (sds(V, 256, 64), sds(PAIRS, 64, 128), sds(PAIRS, 64, 128)),
        ins=[SMEM] + [VMEM] * 11,
        outs=(VMEM,) * 3,
    )(where, *vals, innov, weight, lev, wown, wnear, x, after)


def drop(smoothed, loc):
    high, low = halves(smoothed)
    return nn(high, loc) + nn(low, loc)


def back_kernel(alpha_ref, ens_ref, ca_ref, cb_ref, smat_ref, loc_ref, out_ref, edge_ref, c_ref):
    @pl.when(pl.program_id(0) == 0)
    def _():
        for v in range(V):
            c_ref[v] = jnp.concatenate([ca_ref[v], cb_ref[v]], axis=1)

    smat = smat_ref[...]
    loc = loc_ref[...]
    for k in range(GROUP):
        back = ens_ref[k, 0].astype(F32) * c_ref[0]
        for v in range(1, V):
            back = back + ens_ref[k, v].astype(F32) * c_ref[v]
        full = alpha_ref[k].astype(F32) + drop(smooth(smat, back), loc)
        out_ref[k] = full
        edge_ref[k, :64] = full[:64]
        edge_ref[k, 64:] = full[192:]


def back_part(alpha, ensemble, ca, cb, smat, loc):
    members = alpha.shape[0]
    half = pl.BlockSpec((V, 256, 64), lambda i: (0, 0, 0))
    return call(
        back_kernel,
        (sds(members, 256, 128), sds(members, 128, 128)),
        grid=(members // GROUP,),
        ins=[
            pl.BlockSpec((GROUP, 256, 128), lambda i: (i, 0, 0)),
            pl.BlockSpec((GROUP, V, 256, 128), lambda i: (i, 0, 0, 0)),
            half,
            half,
            pl.BlockSpec((256, 256), lambda i: (0, 0)),
            pl.BlockSpec((128, 128), lambda i: (0, 0)),
        ],
        outs=(
            pl.BlockSpec((GROUP, 256, 128), lambda i: (i, 0, 0)),
            pl.BlockSpec((GROUP, 128, 128), lambda i: (i, 0, 0)),
        ),
        scratch=[pltpu.VMEM((V, 256, 128), F32)],
    )(alpha, ensemble, ca, cb, smat, loc)


def halo_terms(e_ref, o_ref, hmat, loc, p):
    halo = jnp.concatenate([e_ref[p], o_ref[p]], axis=0)
    return drop(smooth(hmat, halo), loc)


def first_kernel(e_ref, o_ref, edge_ref, hmat_ref, loc_ref, out_ref):
    hmat = hmat_ref[...]
    loc = twice(loc_ref[:64])
    for p in range(PAIRS):
        terms = halo_terms(e_ref, o_ref, hmat, loc, p)
        out_ref[p] = edge_ref[p] + terms[:, :128]
        out_ref[p + PAIRS] = edge_ref[p + PAIRS] + terms[:, 128:]


def first_part(from_even, from_odd, edge, hmat, loc):
    return call(first_kernel, sds(*edge.shape), ins=[VMEM] * 5, outs=VMEM)(from_even, from_odd, edge, hmat, loc)


def last_kernel(e_ref, o_ref, edge_ref, hmat_ref, loc_ref, unused_ref, out_ref, held, sems):
    hmat = hmat_ref[...]
    loc = twice(loc_ref[64:])
    copies = []
    for p in range(PAIRS):
        terms = halo_terms(e_ref, o_ref, hmat, loc, p)
        for m in range(2):
            full = edge_ref[p + m * PAIRS] + terms[:, 128 * m : 128 * m + 128]
            held[m, p, 0] = full[:64]
            held[m, p, 1] = full[64:]
        if p % 2:
            group = pl.ds(p - 1, 2)
            for side in range(2):
                copies.append(
                    pltpu.make_async_copy(
                        held.at[:, group, side], out_ref.at[:, group, 3 * side], sems.at[p // 2, side]
                    )
                )
                copies[-1].start()
    for copy in copies:
        copy.wait()


def last_part(from_even, from_odd, edge, hmat, loc, out):
    return call(
        last_kernel,
        sds(*out.shape),
        ins=[VMEM] * 5 + [ANY],
        outs=ANY,
        scratch=[pltpu.VMEM((2, PAIRS, 2, 64, 128), F32), pltpu.SemaphoreType.DMA((PAIRS // 2, 2))],
        aliases={5: 0},
    )(from_even, from_odd, edge, hmat, loc, out)


def stencil(gap):
    gap = jnp.abs(gap)
    return jnp.where(gap == 0, 6.0, jnp.where(gap == 1, 4.0, jnp.where(gap == 2, 1.0, 0.0)))


def matrices(tile, tiles, even):
    def across(i, j):
        gap = stencil(i - j)
        return jnp.where((i == j) & ((i == 0) | (i == 31)), 5.0, gap)

    i = lax.broadcasted_iota(jnp.int32, (256, 256), 0)
    j = lax.broadcasted_iota(jnp.int32, (256, 256), 1)
    ri, rj = i // 32, j // 32
    ends = ((ri == 0) & (tile == 0)) | ((ri == 7) & (tile == tiles - 1))
    down = jnp.where((ri == rj) & ends, 5.0, stencil(ri - rj))
    smat = (down * across(i % 32, j % 32) * (1.0 / 256.0)).astype(BF16)
    i = lax.broadcasted_iota(jnp.int32, (128, 128), 0)
    j = lax.broadcasted_iota(jnp.int32, (128, 128), 1)
    ri = i // 32
    ri = jnp.where(ri < 2, ri, ri + 4)
    is_even = j < 64
    above = is_even == even
    rj = jnp.where(above, 8, -2) + (j // 32) % 2
    there = is_even | ((tile > 0) & (tile < tiles - 1))
    hmat = jnp.where(there, stencil(ri - rj), 0.0) * across(i % 32, j % 32) * (1.0 / 256.0)
    return smat, hmat.astype(BF16)


def swap_even(x):
    return lax.ppermute(x, "tile", EVEN)


def swap_odd(x):
    return lax.ppermute(x, "tile", ODD)


def round_mem(mine):
    size = lax.axis_size("mem")
    return [mine] + [
        lax.ppermute(mine, "mem", [(i, (i + shift) % size) for i in range(size)]) for shift in range(1, size)
    ]


def by_variable(x):
    return jnp.pad(x, (0, V * SLOTS - x.shape[0])).reshape(SLOTS, V).T


def on_device(alpha, ensemble, loc_vert, obs_col, obs_lev, obs_count, innovation, obs_weight):
    members = alpha.shape[0]
    tile = lax.axis_index("tile")
    tiles = lax.axis_size("tile")
    even = tile % 2 == 0
    odd_there = (tile > 0) & (tile < tiles - 1)
    where = jnp.stack(
        [
            jnp.where(even, 7 * 32, 0),
            jnp.where(even, 0, 7 * 32),
            jnp.where(even, 8, -1),
            jnp.where(even, -1, 8),
            odd_there.astype(jnp.int32),
            tile % 2,
            tile,
        ]
    ).astype(jnp.int32)

    send_ea, send_oa, token = send_part(where, alpha.reshape(2, PAIRS, 4, 64, 128), loc_vert)
    ea, oa = swap_even(send_ea), swap_odd(send_oa)
    inner, la, lb, xa, xb, smat, hmat, token, send_eb, send_ob = own_part(
        where,
        alpha.reshape(2, PAIRS, 256, 128),
        ensemble.reshape(2, PAIRS, V, 256, 128),
        loc_vert,
        token,
    )
    eb, ob = swap_even(send_eb), swap_odd(send_ob)

    token, obs_col, obs_lev, obs_count, innovation, obs_weight = lax.optimization_barrier(
        (token, obs_col, obs_lev, obs_count, innovation, obs_weight)
    )
    live = jnp.arange(obs_col.shape[1], dtype=jnp.int32) < obs_count[0]
    own_obs = jnp.stack(
        [
            by_variable(obs_col[0].astype(F32) + token[0, 0]),
            by_variable(obs_lev[0].astype(F32)),
            by_variable(innovation[0]),
            by_variable(jnp.where(live, obs_weight[0], 0.0)),
        ]
    )
    own_obs = pass_on(own_obs, ea)
    even_obs = swap_even(own_obs)
    odd_obs = swap_odd(own_obs)
    even_on = jnp.where(even, even_obs[0] < 64.0, even_obs[0] >= 960.0)
    odd_on = jnp.where(even, odd_obs[0] >= 960.0, odd_obs[0] < 64.0) & odd_there
    lev = jnp.concatenate([own_obs[1], even_obs[1], odd_obs[1]])
    innov = jnp.concatenate([own_obs[2], even_obs[2], odd_obs[2]])
    weight = jnp.concatenate(
        [own_obs[3], jnp.where(even_on, even_obs[3], 0.0), jnp.where(odd_on, odd_obs[3], 0.0)]
    )

    inc_a, se_a, so_a = edge_part(0, where, ea, oa, la, xa, hmat, loc_vert, inner, own_obs)
    near_a = swap_even(se_a), swap_odd(so_a)
    wown, wnear = weights(where, own_obs, even_obs, odd_obs)
    mine_a = values(0, where, inc_a, *near_a, wown, wnear, lev, inc_a)
    vals_a = round_mem(mine_a)

    inc_b, se_b, so_b = edge_part(1, where, eb, ob, lb, xb, hmat, loc_vert, inner, mine_a)
    near_b = swap_even(se_b), swap_odd(so_b)

    c_a, back_ea, back_oa = adjoint(0, where, vals_a, innov, weight, lev, wown, wnear, xa, se_b)
    halo_ea, halo_oa = swap_even(back_ea), swap_odd(back_oa)

    mine_b = values(1, where, inc_b, *near_b, wown, wnear, lev, back_ea)
    vals_b = round_mem(mine_b)
    c_b, back_eb, back_ob = adjoint(1, where, vals_b, innov, weight, lev, wown, wnear, xb, mine_b)
    halo_eb, halo_ob = swap_even(back_eb), swap_odd(back_ob)

    out, edge = back_part(
        alpha.reshape(members, 256, 128), ensemble.reshape(members, V, 256, 128), c_a, c_b, smat, loc_vert
    )
    edge = first_part(halo_ea, halo_oa, edge, hmat, loc_vert)
    out = last_part(halo_eb, halo_ob, edge, hmat, loc_vert, out.reshape(2, PAIRS, 4, 64, 128))
    return out.reshape(members, 8, 32, 128)


def solution(mesh):
    in_specs = (
        P("mem", "tile", None, None),
        P("mem", None, "tile", None, None),
        P(),
        P("tile", None),
        P("tile", None),
        P("tile"),
        P("tile", None),
        P("tile", None),
    )
    out_specs = P("mem", "tile", None, None)
    return jax.shard_map(
        on_device, mesh=mesh, in_specs=in_specs, out_specs=out_specs, check_vma=False
    )
```

time: 122 us -> 124 us (1.016)
  the two profiles are of different devices: /device:TPU:32 before, /device:TPU:33 now
where the time goes in v2:
time: 124 us
  starting transfers between devices  57.8 us (47%)
  Pallas kernels  26.2 us (21%)
  local copies, waits for them, and re-layouts  21.7 us (18%)
  waiting for transfers between devices  15.6 us (13%)
  other arithmetic  1.39 us (1%)
    ppermute x7, starting transfers between devices, swap_odd(): return lax.ppermute(x, 'tile', ODD)  44 us
    ppermute x7, waiting for transfers between devices, swap_odd(): return lax.ppermute(x, 'tile', ODD)  14.4 us
    reshape x8, local copies, waits for them, and re-layouts, by_variable(): return jnp.pad(x, (0, V * SLOTS - x.shape[0])).reshape(SLOTS, V).T  12.6 us
    ppermute x6, starting transfers between devices, round_mem(): lax.ppermute(mine, 'mem', [(i, (i + shift) % size) for i in range(size)])  8.27 us
    unnamed x28, local copies, waits for them, and re-layouts  6.78 us
    ppermute x7, starting transfers between devices, swap_even(): return lax.ppermute(x, 'tile', EVEN)  5.51 us
    pallas_call x1, Pallas kernels, own_part(): call(own_kernel, (sds(V, 128, 128), sds(PAIRS, 128, 128), sds(PAIRS, 128,...  5.22 us
    pallas_call x1, Pallas kernels, back_part(): call(back_kernel, (sds(members, 256, 128), sds(members, 128, 128)), grid=...  4.88 us
  transfers between devices with their start and end apart: 20, of which 4 were waited for; matrix products, arithmetic and copies ran while one was open for 13% of the time, Pallas kernels for 16%

profile of v2, /device:TPU:33, one launch (start us, length us, event | category | flops | bytes accessed | tf_op | source)
XLA Modules:
  0.0 123.7 jit_solution(10849365990818657933)
XLA Ops:
  0.1 1.3 %copy-done = bf16[20,8,32,128]{3,2,1,0:T(8,128)(2,1)S(1)} copy-done((bf16[20,8,32,128]{3,2,1,0:T(8,128)(2,1)S(1)}, bf16[20,8,32,128]{3,2,1,0:T(8,128)(2,1)}, u32[]{:S(2)}) %copy-start) | copy-done | bytes 1310744
  2.2 1.8 %shard_map.82 = (f32[10,64,128]{2,1,0:T(8,128)}, f32[10,64,128]{2,1,0:T(8,128)}, f32[8,128]{1,0:T(8,128)S(1)}) custom-call(s32[7]{0:T(128)S(1)} %stack.50.where_ref, bf16[2,10,4,64,128]{4,3,2,1,0:T(8,128)(2,1)S(1)} %bitcast.51, bf16[2,10,4,64,128]{4,3,2,1,0:T(8,128)(2,1)S(1)} %bitcast.52, bf16[128,128]{1,0:T(8,128)(2,1)S(1)} %copy-done.4), custom_call_target="tpu_custom_call" | custom-call | flops 1000000 | bytes 1000000 | tf_op jit(solution)/shard_map/pallas_call | solution.py:104
  3.9 3.0 %collective-permute-start.2 = (f32[10,64,128]{2,1,0:T(8,128)}, f32[10,64,128]{2,1,0:T(8,128)S(1)}, u32[]{:S(2)}, u32[]{:S(2)}) collective-permute-start(f32[10,64,128]{2,1,0:T(8,128)} %get-tuple-element.47), channel_id=1, source_target_pairs={{0,1},{1,0},{2,3},{3,2},{4,5},{5,4},{6,7},{7,6},{8,9},{9,8},{10,11... | collective-permute-start | bytes 983048 | tf_op jit(solution)/shard_map/ppermute | solution.py:461
  6.9 7.9 %collective-permute-start.3 = (f32[10,64,128]{2,1,0:T(8,128)}, f32[10,64,128]{2,1,0:T(8,128)}, u32[]{:S(2)}, u32[]{:S(2)}) collective-permute-start(f32[10,64,128]{2,1,0:T(8,128)} %get-tuple-element.48), channel_id=1, source_target_pairs={{1,2},{2,1},{3,4},{4,3},{5,6},{6,5},{7,8},{8,7},{9,10},{10,9},{11,... | collective-permute-start | bytes 983048 | tf_op jit(solution)/shard_map/ppermute | solution.py:465
  14.9 2.1 %copy-done.2 = bf16[20,3,8,32,128]{4,3,2,1,0:T(8,128)(2,1)S(1)} copy-done((bf16[20,3,8,32,128]{4,3,2,1,0:T(8,128)(2,1)S(1)}, bf16[20,3,8,32,128]{4,3,2,1,0:T(8,128)(2,1)}, u32[]{:S(2)}) %copy-start.2) | copy-done | bytes 3932184
  17.0 5.2 %shard_map.83 = (f32[3,128,128]{2,1,0:T(8,128)S(1)}, f32[10,128,128]{2,1,0:T(8,128)S(1)}, f32[10,128,128]{2,1,0:T(8,128)S(1)}, bf16[10,3,128,128]{3,2,1,0:T(8,12...) custom-call(s32[7]{0:T(128)S(1)} %stack.50.where_ref, ...), custom_call_target="tpu_custom_call" | custom-call | flops 1000000 | bytes 1000000 | tf_op jit(solution)/shard_map/pallas_call | solution.py:155
  30.6 1.7 %reshape.59 = f32[768,3]{1,0:T(8,128)} reshape(f32[2304]{0:T(1024)} %pad.14) | data formatting | bytes 18432 | tf_op jit(solution)/shard_map/reshape | solution.py:476
  32.3 1.7 %copy.11 = f32[768,3]{0,1:T(4,128)} copy(f32[768,3]{1,0:T(8,128)} %reshape.59) | data formatting | bytes 18432 | tf_op jit(solution)/shard_map/reshape | solution.py:476
  34.1 1.7 %reshape.61 = f32[768,3]{1,0:T(8,128)} reshape(f32[2304]{0:T(1024)} %pad.16) | data formatting | bytes 18432 | tf_op jit(solution)/shard_map/reshape | solution.py:476
  35.8 1.7 %copy.13 = f32[768,3]{0,1:T(4,128)} copy(f32[768,3]{1,0:T(8,128)} %reshape.61) | data formatting | bytes 18432 | tf_op jit(solution)/shard_map/reshape | solution.py:476
  37.5 1.7 %reshape.58 = f32[768,3]{1,0:T(8,128)} reshape(f32[2304]{0:T(1024)} %pad.13) | data formatting | bytes 18432 | tf_op jit(solution)/shard_map/reshape | solution.py:476
  39.3 1.7 %copy.10 = f32[768,3]{0,1:T(4,128)} copy(f32[768,3]{1,0:T(8,128)} %reshape.58) | data formatting | bytes 18432 | tf_op jit(solution)/shard_map/reshape | solution.py:476
  41.8 6.7 %collective-permute-start.7 = (f32[4,3,768]{2,1,0:T(4,128)S(1)}, f32[4,3,768]{2,1,0:T(4,128)S(1)}, u32[]{:S(2)}, u32[]{:S(2)}) collective-permute-start(f32[4,3,768]{2,1,0:T(4,128)S(1)} %shard_map.84.after_ref.own_ref), channel_id=1, source_target_pairs={{1,2},{2,1},{3,4},{4,3},{5,6},{6,5},{7,8},{8,7},{9,10},{10,9},{11,... | collective-permute-start | bytes 110600 | tf_op jit(solution)/shard_map/ppermute | solution.py:465
  49.6 1.6 %shard_map.85 = (f32[3,256,64]{2,1,0:T(8,128)S(1)}, f32[3,16,128]{2,1,0:T(8,128)S(1)}, f32[3,16,128]{2,1,0:T(8,128)S(1)}) custom-call(s32[7]{0:T(128)S(1)} %stack.50.where_ref, f32[10,64,128]{2,1,0:T(8,128)S(1)} %collective-permute-done.2.after_ref.e_ref, f32[10,64,128]{2,1,0:T(8,128)} %collective-permute-done.3.o_ref, f32[10,128,128]{2,1,0:T(8,128)S(1)} %copy-done.7, ...), custom_call_target="tpu_custom_call" | custom-call | flops 1000000 | bytes 1000000 | tf_op jit(solution)/shard_map/pallas_call | solution.py:219
  51.1 2.4 %collective-permute-start.4 = (f32[3,16,128]{2,1,0:T(8,128)S(1)}, f32[3,16,128]{2,1,0:T(8,128)S(1)}, u32[]{:S(2)}, u32[]{:S(2)}) collective-permute-start(f32[3,16,128]{2,1,0:T(8,128)S(1)} %get-tuple-element.59), channel_id=1, source_target_pairs={{0,1},{1,0},{2,3},{3,2},{4,5},{5,4},{6,7},{7,6},{8,9},{9,8},{10,11... | collective-permute-start | bytes 73736 | tf_op jit(solution)/shard_map/ppermute | solution.py:461
  53.6 4.2 %collective-permute-start.5 = (f32[3,16,128]{2,1,0:T(8,128)S(1)}, f32[3,16,128]{2,1,0:T(8,128)S(1)}, u32[]{:S(2)}, u32[]{:S(2)}) collective-permute-start(f32[3,16,128]{2,1,0:T(8,128)S(1)} %get-tuple-element.60), channel_id=1, source_target_pairs={{1,2},{2,1},{3,4},{4,3},{5,6},{6,5},{7,8},{8,7},{9,10},{10,9},{11,... | collective-permute-start | bytes 73736 | tf_op jit(solution)/shard_map/ppermute | solution.py:465
  58.8 3.7 %collective-permute-done.5.o_ref = f32[3,16,128]{2,1,0:T(8,128)S(1)} collective-permute-done((f32[3,16,128]{2,1,0:T(8,128)S(1)}, f32[3,16,128]{2,1,0:T(8,128)S(1)}, u32[]{:S(2)}, u32[]{:S(2)}) %collective-permute-start.5) | collective-permute-done | bytes 24608 | tf_op jit(solution)/shard_map/ppermute | solution.py:465
  62.6 1.6 %shard_map.87.after_ref.v0 = f32[9,768]{1,0:T(8,128)S(1)} custom-call(s32[7]{0:T(128)S(1)} %stack.50.where_ref, f32[3,256,64]{2,1,0:T(8,128)S(1)} %get-tuple-element.58.inc_ref.after_ref, f32[3,16,128]{2,1,0:T(8,128)S(1)} %collective-permute-done.4.e_ref, f32[3,16,128]{2,1,0:T(8,128)S(1)} %collective-permute-done.5.o_ref, ...), custom_call_target="tpu_custom_call" | custom-call | flops 1000000 | bytes 1000000 | tf_op jit(solution)/shard_map/pallas_call | solution.py:287
  64.2 3.7 %collective-permute-start.12 = (f32[9,768]{1,0:T(8,128)S(1)}, f32[9,768]{1,0:T(8,128)S(1)}, u32[]{:S(2)}, u32[]{:S(2)}) collective-permute-start(f32[9,768]{1,0:T(8,128)S(1)} %shard_map.87.after_ref.v0), channel_id=1, source_target_pairs={{0,192},{64,0},{128,64},{192,128},{1,193},{65,1},{129,65},{193,129... | collective-permute-start | bytes 82952 | tf_op jit(solution)/shard_map/ppermute | solution.py:471
  69.6 1.6 %shard_map.88 = (f32[3,256,64]{2,1,0:T(8,128)S(1)}, f32[3,16,128]{2,1,0:T(8,128)S(1)}, f32[3,16,128]{2,1,0:T(8,128)S(1)}) custom-call(s32[7]{0:T(128)S(1)} %stack.50.where_ref, f32[10,64,128]{2,1,0:T(8,128)S(1)} %collective-permute-done.e_ref, f32[10,64,128]{2,1,0:T(8,128)} %collective-permute-done.1.o_ref, f32[10,128,128]{2,1,0:T(8,128)S(1)} %get-tuple-element.43.own_ref, ...), custom_call_target="tpu_custom_call" | custom-call | flops 1000000 | bytes 1000000 | tf_op jit(solution)/shard_map/pallas_call | solution.py:219
  71.2 4.8 %collective-permute-start.9 = (f32[3,16,128]{2,1,0:T(8,128)S(1)}, f32[3,16,128]{2,1,0:T(8,128)S(1)}, u32[]{:S(2)}, u32[]{:S(2)}) collective-permute-start(f32[3,16,128]{2,1,0:T(8,128)S(1)} %get-tuple-element.65), channel_id=1, source_target_pairs={{1,2},{2,1},{3,4},{4,3},{5,6},{6,5},{7,8},{8,7},{9,10},{10,9},{11,... | collective-permute-start | bytes 73736 | tf_op jit(solution)/shard_map/ppermute | solution.py:465
  76.1 1.6 %shard_map.89 = (f32[3,256,64]{2,1,0:T(8,128)S(1)}, f32[10,64,128]{2,1,0:T(8,128)S(1)}, f32[10,64,128]{2,1,0:T(8,128)S(1)}) custom-call(s32[7]{0:T(128)S(1)} %stack.50.where_ref, f32[9,768]{1,0:T(8,128)S(1)} %shard_map.87.after_ref.v0, f32[9,768]{1,0:T(8,128)S(1)} %collective-permute-done.10.v1, f32[9,768]{1,0:T(8,128)S(1)} %collective-permute-done.11.v2, ...), custom_call_target="tpu_custom_call" | custom-call | flops 1000000 | bytes 1000000 | tf_op jit(solution)/shard_map/pallas_call | solution.py:326
  77.7 3.1 %collective-permute-done.9.o_ref = f32[3,16,128]{2,1,0:T(8,128)S(1)} collective-permute-done((f32[3,16,128]{2,1,0:T(8,128)S(1)}, f32[3,16,128]{2,1,0:T(8,128)S(1)}, u32[]{:S(2)}, u32[]{:S(2)}) %collective-permute-start.9) | collective-permute-done | bytes 24608 | tf_op jit(solution)/shard_map/ppermute | solution.py:465
  80.8 1.6 %shard_map.90.v0.after_ref = f32[9,768]{1,0:T(8,128)S(1)} custom-call(s32[7]{0:T(128)S(1)} %stack.50.where_ref, f32[3,256,64]{2,1,0:T(8,128)S(1)} %get-tuple-element.63.inc_ref, f32[3,16,128]{2,1,0:T(8,128)S(1)} %collective-permute-done.8.e_ref, f32[3,16,128]{2,1,0:T(8,128)S(1)} %collective-permute-done.9.o_ref, ...), custom_call_target="tpu_custom_call" | custom-call | flops 1000000 | bytes 1000000 | tf_op jit(solution)/shard_map/pallas_call | solution.py:287
  83.8 1.5 %collective-permute-start.13 = (f32[9,768]{1,0:T(8,128)S(1)}, f32[9,768]{1,0:T(8,128)S(1)}, u32[]{:S(2)}, u32[]{:S(2)}) collective-permute-start(f32[9,768]{1,0:T(8,128)S(1)} %shard_map.90.v0.after_ref), channel_id=1, source_target_pairs={{0,64},{64,128},{128,192},{192,0},{1,65},{65,129},{129,193},{193,1... | collective-permute-start | bytes 82952 | tf_op jit(solution)/shard_map/ppermute | solution.py:471
  85.3 4.4 %collective-permute-start.19 = (f32[10,64,128]{2,1,0:T(8,128)S(1)}, f32[10,64,128]{2,1,0:T(8,128)S(1)}, u32[]{:S(2)}, u32[]{:S(2)}) collective-permute-start(f32[10,64,128]{2,1,0:T(8,128)S(1)} %get-tuple-element.69), channel_id=1, source_target_pairs={{1,2},{2,1},{3,4},{4,3},{5,6},{6,5},{7,8},{8,7},{9,10},{10,9},{11,... | collective-permute-start | bytes 983048 | tf_op jit(solution)/shard_map/ppermute | solution.py:465
  89.7 1.6 %shard_map.91 = (f32[3,256,64]{2,1,0:T(8,128)S(1)}, f32[10,64,128]{2,1,0:T(8,128)S(1)}, f32[10,64,128]{2,1,0:T(8,128)S(1)}) custom-call(s32[7]{0:T(128)S(1)} %stack.50.where_ref, f32[9,768]{1,0:T(8,128)S(1)} %shard_map.90.v0.after_ref, f32[9,768]{1,0:T(8,128)S(1)} %collective-permute-done.13.v1, f32[9,768]{1,0:T(8,128)S(1)} %collective-permute-done.14.v2, ...), custom_call_target="tpu_custom_call" | custom-call | flops 1000000 | bytes 1000000 | tf_op jit(solution)/shard_map/pallas_call | solution.py:326
  91.5 14.7 %collective-permute-start.17 = (f32[10,64,128]{2,1,0:T(8,128)S(1)}, f32[10,64,128]{2,1,0:T(8,128)S(1)}, u32[]{:S(2)}, u32[]{:S(2)}) collective-permute-start(f32[10,64,128]{2,1,0:T(8,128)S(1)} %get-tuple-element.68), channel_id=1, source_target_pairs={{1,2},{2,1},{3,4},{4,3},{5,6},{6,5},{7,8},{8,7},{9,10},{10,9},{11,... | collective-permute-start | bytes 983048 | tf_op jit(solution)/shard_map/ppermute | solution.py:465
  106.2 4.9 %shard_map.92 = (f32[20,256,128]{2,1,0:T(8,128)}, f32[20,128,128]{2,1,0:T(8,128)S(1)}) custom-call(bf16[20,256,128]{2,1,0:T(8,128)(2,1)S(1)} %bitcast.54, bf16[20,3,256,128]{3,2,1,0:T(8,128)(2,1)S(1)} %bitcast.56, f32[3,256,64]{2,1,0:T(8,128)S(1)} %get-tuple-element.70.ca_ref, f32[3,256,64]{2,1,0:T(8,128)S(1)} %get-tuple-element.71.cb_ref, ...), custom_call_target="tpu_custom_call" | custom-call | flops 1000000 | bytes 1000000 | tf_op jit(solution)/shard_map/pallas_call | solution.py:360
  111.1 1.2 shard_map.93.edge_ref
  113.4 7.5 %collective-permute-done.17.o_ref = f32[10,64,128]{2,1,0:T(8,128)S(1)} collective-permute-done((f32[10,64,128]{2,1,0:T(8,128)S(1)}, f32[10,64,128]{2,1,0:T(8,128)S(1)}, u32[]{:S(2)}, u32[]{:S(2)}) %collective-permute-start.17) | collective-permute-done | bytes 327712 | tf_op jit(solution)/shard_map/ppermute | solution.py:465
  121.0 2.6 %shard_map.94 = f32[2,10,4,64,128]{4,3,2,1,0:T(8,128)} custom-call(f32[10,64,128]{2,1,0:T(8,128)S(1)} %collective-permute-done.16.e_ref, f32[10,64,128]{2,1,0:T(8,128)S(1)} %collective-permute-done.17.o_ref, f32[20,128,128]{2,1,0:T(8,128)S(1)} %shard_map.93.edge_ref, ...), custom_call_target="tpu_custom_call", output_to_operand_aliasing={{}: (5, {})} | custom-call | flops 1000000 | bytes 1000000 | tf_op jit(solution)/shard_map/pallas_call | solution.py:422
  (72 shorter events, 15.8 us)
Async XLA Ops:
  0.1 1.3 %copy-start = (bf16[20,8,32,128]{3,2,1,0:T(8,128)(2,1)S(1)}, bf16[20,8,32,128]{3,2,1,0:T(8,128)(2,1)}, u32[]{:S(2)}) copy-start(bf16[20,8,32,128]{3,2,1,0:T(8,128)(2,1)} %param.8) | copy-start | bytes 3932164
  3.9 37.8 %collective-permute-start.2 = (f32[10,64,128]{2,1,0:T(8,128)}, f32[10,64,128]{2,1,0:T(8,128)S(1)}, u32[]{:S(2)}, u32[]{:S(2)}) collective-permute-start(f32[10,64,128]{2,1,0:T(8,128)} %get-tuple-element.47), channel_id=1, source_target_pairs={{0,1},{1,0},{2,3},{3,2},{4,5},{5,4},{6,7},{7,6},{8,9},{9,8},{10,11... | collective-permute-start | bytes 983048 | tf_op jit(solution)/shard_map/ppermute | solution.py:461
  6.9 41.6 %collective-permute-start.3 = (f32[10,64,128]{2,1,0:T(8,128)}, f32[10,64,128]{2,1,0:T(8,128)}, u32[]{:S(2)}, u32[]{:S(2)}) collective-permute-start(f32[10,64,128]{2,1,0:T(8,128)} %get-tuple-element.48), channel_id=1, source_target_pairs={{1,2},{2,1},{3,4},{4,3},{5,6},{6,5},{7,8},{8,7},{9,10},{10,9},{11,... | collective-permute-start | bytes 983048 | tf_op jit(solution)/shard_map/ppermute | solution.py:465
  14.9 2.1 %copy-start.2 = (bf16[20,3,8,32,128]{4,3,2,1,0:T(8,128)(2,1)S(1)}, bf16[20,3,8,32,128]{4,3,2,1,0:T(8,128)(2,1)}, u32[]{:S(2)}) copy-start(bf16[20,3,8,32,128]{4,3,2,1,0:T(8,128)(2,1)} %param.9) | copy-start | bytes 11796484
  17.0 9.0 %copy-start.10 = (s32[1,2048]{1,0:T(1,128)S(1)}, s32[1,2048]{1,0:T(1,128)}, u32[]{:S(2)}) copy-start(s32[1,2048]{1,0:T(1,128)} %param.11) | copy-start | bytes 24580
  17.0 10.2 %copy-start.11 = (f32[1,2048]{1,0:T(1,128)S(1)}, f32[1,2048]{1,0:T(1,128)}, u32[]{:S(2)}) copy-start(f32[1,2048]{1,0:T(1,128)} %param.15) | copy-start | bytes 24580
  17.0 10.8 %copy-start.12 = (s32[1,2048]{1,0:T(1,128)S(1)}, s32[1,2048]{1,0:T(1,128)}, u32[]{:S(2)}) copy-start(s32[1,2048]{1,0:T(1,128)} %param.12) | copy-start | bytes 24580
  17.0 11.4 %copy-start.13 = (f32[1,2048]{1,0:T(1,128)S(1)}, f32[1,2048]{1,0:T(1,128)}, u32[]{:S(2)}) copy-start(f32[1,2048]{1,0:T(1,128)} %param.14) | copy-start | bytes 24580
  22.2 0.8 copy-start.6
  23.7 45.9 %collective-permute-start = (f32[10,64,128]{2,1,0:T(8,128)}, f32[10,64,128]{2,1,0:T(8,128)S(1)}, u32[]{:S(2)}, u32[]{:S(2)}) collective-permute-start(f32[10,64,128]{2,1,0:T(8,128)} %get-tuple-element.41), channel_id=1, source_target_pairs={{0,1},{1,0},{2,3},{3,2},{4,5},{5,4},{6,7},{7,6},{8,9},{9,8},{10,11... | collective-permute-start | bytes 983048 | tf_op jit(solution)/shard_map/ppermute | solution.py:461
  23.7 45.9 %collective-permute-start.1 = (f32[10,64,128]{2,1,0:T(8,128)}, f32[10,64,128]{2,1,0:T(8,128)}, u32[]{:S(2)}, u32[]{:S(2)}) collective-permute-start(f32[10,64,128]{2,1,0:T(8,128)} %get-tuple-element.42), channel_id=1, source_target_pairs={{1,2},{2,1},{3,4},{4,3},{5,6},{6,5},{7,8},{8,7},{9,10},{10,9},{11,... | collective-permute-start | bytes 983048 | tf_op jit(solution)/shard_map/ppermute | solution.py:465
  30.6 17.9 %copy-start.5 = (bf16[128,128]{1,0:T(8,128)(2,1)S(1)}, bf16[128,128]{1,0:T(8,128)(2,1)}, u32[]{:S(2)}) copy-start(bf16[128,128]{1,0:T(8,128)(2,1)} %loc_ref.13) | copy-start | bytes 98308
  41.8 11.8 %collective-permute-start.7 = (f32[4,3,768]{2,1,0:T(4,128)S(1)}, f32[4,3,768]{2,1,0:T(4,128)S(1)}, u32[]{:S(2)}, u32[]{:S(2)}) collective-permute-start(f32[4,3,768]{2,1,0:T(4,128)S(1)} %shard_map.84.after_ref.own_ref), channel_id=1, source_target_pairs={{1,2},{2,1},{3,4},{4,3},{5,6},{6,5},{7,8},{8,7},{9,10},{10,9},{11,... | collective-permute-start | bytes 110600 | tf_op jit(solution)/shard_map/ppermute | solution.py:465
  48.5 9.4 %collective-permute-start.6 = (f32[4,3,768]{2,1,0:T(4,128)S(1)}, f32[4,3,768]{2,1,0:T(4,128)S(1)}, u32[]{:S(2)}, u32[]{:S(2)}) collective-permute-start(f32[4,3,768]{2,1,0:T(4,128)S(1)} %shard_map.84.after_ref.own_ref), channel_id=1, source_target_pairs={{0,1},{1,0},{2,3},{3,2},{4,5},{5,4},{6,7},{7,6},{8,9},{9,8},{10,11... | collective-permute-start | bytes 110600 | tf_op jit(solution)/shard_map/ppermute | solution.py:461
  48.5 1.1 copy-start.7
  51.1 7.7 %collective-permute-start.4 = (f32[3,16,128]{2,1,0:T(8,128)S(1)}, f32[3,16,128]{2,1,0:T(8,128)S(1)}, u32[]{:S(2)}, u32[]{:S(2)}) collective-permute-start(f32[3,16,128]{2,1,0:T(8,128)S(1)} %get-tuple-element.59), channel_id=1, source_target_pairs={{0,1},{1,0},{2,3},{3,2},{4,5},{5,4},{6,7},{7,6},{8,9},{9,8},{10,11... | collective-permute-start | bytes 73736 | tf_op jit(solution)/shard_map/ppermute | solution.py:461
  53.6 9.0 %collective-permute-start.5 = (f32[3,16,128]{2,1,0:T(8,128)S(1)}, f32[3,16,128]{2,1,0:T(8,128)S(1)}, u32[]{:S(2)}, u32[]{:S(2)}) collective-permute-start(f32[3,16,128]{2,1,0:T(8,128)S(1)} %get-tuple-element.60), channel_id=1, source_target_pairs={{1,2},{2,1},{3,4},{4,3},{5,6},{6,5},{7,8},{8,7},{9,10},{10,9},{11,... | collective-permute-start | bytes 73736 | tf_op jit(solution)/shard_map/ppermute | solution.py:465
  64.2 11.8 %collective-permute-start.12 = (f32[9,768]{1,0:T(8,128)S(1)}, f32[9,768]{1,0:T(8,128)S(1)}, u32[]{:S(2)}, u32[]{:S(2)}) collective-permute-start(f32[9,768]{1,0:T(8,128)S(1)} %shard_map.87.after_ref.v0), channel_id=1, source_target_pairs={{0,192},{64,0},{128,64},{192,128},{1,193},{65,1},{129,65},{193,129... | collective-permute-start | bytes 82952 | tf_op jit(solution)/shard_map/ppermute | solution.py:471
  67.9 8.2 %collective-permute-start.11 = (f32[9,768]{1,0:T(8,128)S(1)}, f32[9,768]{1,0:T(8,128)S(1)}, u32[]{:S(2)}, u32[]{:S(2)}) collective-permute-start(f32[9,768]{1,0:T(8,128)S(1)} %shard_map.87.after_ref.v0), channel_id=1, source_target_pairs={{0,128},{64,192},{128,0},{192,64},{1,129},{65,193},{129,1},{193,65... | collective-permute-start | bytes 82952 | tf_op jit(solution)/shard_map/ppermute | solution.py:471
  68.5 7.5 %collective-permute-start.10 = (f32[9,768]{1,0:T(8,128)S(1)}, f32[9,768]{1,0:T(8,128)S(1)}, u32[]{:S(2)}, u32[]{:S(2)}) collective-permute-start(f32[9,768]{1,0:T(8,128)S(1)} %shard_map.87.after_ref.v0), channel_id=1, source_target_pairs={{0,64},{64,128},{128,192},{192,0},{1,65},{65,129},{129,193},{193,1... | collective-permute-start | bytes 82952 | tf_op jit(solution)/shard_map/ppermute | solution.py:471
  71.2 9.6 %collective-permute-start.9 = (f32[3,16,128]{2,1,0:T(8,128)S(1)}, f32[3,16,128]{2,1,0:T(8,128)S(1)}, u32[]{:S(2)}, u32[]{:S(2)}) collective-permute-start(f32[3,16,128]{2,1,0:T(8,128)S(1)} %get-tuple-element.65), channel_id=1, source_target_pairs={{1,2},{2,1},{3,4},{4,3},{5,6},{6,5},{7,8},{8,7},{9,10},{10,9},{11,... | collective-permute-start | bytes 73736 | tf_op jit(solution)/shard_map/ppermute | solution.py:465
  76.0 4.8 %collective-permute-start.8 = (f32[3,16,128]{2,1,0:T(8,128)S(1)}, f32[3,16,128]{2,1,0:T(8,128)S(1)}, u32[]{:S(2)}, u32[]{:S(2)}) collective-permute-start(f32[3,16,128]{2,1,0:T(8,128)S(1)} %get-tuple-element.64.after_ref), channel_id=1, source_target_pairs={{0,1},{1,0},{2,3},{3,2},{4,5},{5,4},{6,7},{7,6},{8,9},{9,8},{10,11... | collective-permute-start | bytes 73736 | tf_op jit(solution)/shard_map/ppermute | solution.py:461
  80.8 25.4 %copy-start.3 = (bf16[20,3,8,32,128]{4,3,2,1,0:T(8,128)(2,1)S(1)}, bf16[20,3,8,32,128]{4,3,2,1,0:T(8,128)(2,1)}, u32[]{:S(2)}) copy-start(bf16[20,3,8,32,128]{4,3,2,1,0:T(8,128)(2,1)} %param.9) | copy-start | bytes 11796484
  82.5 7.3 %collective-permute-start.15 = (f32[9,768]{1,0:T(8,128)S(1)}, f32[9,768]{1,0:T(8,128)S(1)}, u32[]{:S(2)}, u32[]{:S(2)}) collective-permute-start(f32[9,768]{1,0:T(8,128)S(1)} %shard_map.90.v0.after_ref), channel_id=1, source_target_pairs={{0,192},{64,0},{128,64},{192,128},{1,193},{65,1},{129,65},{193,129... | collective-permute-start | bytes 82952 | tf_op jit(solution)/shard_map/ppermute | solution.py:471
  83.0 6.7 %collective-permute-start.14 = (f32[9,768]{1,0:T(8,128)S(1)}, f32[9,768]{1,0:T(8,128)S(1)}, u32[]{:S(2)}, u32[]{:S(2)}) collective-permute-start(f32[9,768]{1,0:T(8,128)S(1)} %shard_map.90.v0.after_ref), channel_id=1, source_target_pairs={{0,128},{64,192},{128,0},{192,64},{1,129},{65,193},{129,1},{193,65... | collective-permute-start | bytes 82952 | tf_op jit(solution)/shard_map/ppermute | solution.py:471
  83.8 5.9 %collective-permute-start.13 = (f32[9,768]{1,0:T(8,128)S(1)}, f32[9,768]{1,0:T(8,128)S(1)}, u32[]{:S(2)}, u32[]{:S(2)}) collective-permute-start(f32[9,768]{1,0:T(8,128)S(1)} %shard_map.90.v0.after_ref), channel_id=1, source_target_pairs={{0,64},{64,128},{128,192},{192,0},{1,65},{65,129},{129,193},{193,1... | collective-permute-start | bytes 82952 | tf_op jit(solution)/shard_map/ppermute | solution.py:471
  85.3 25.8 %collective-permute-start.18 = (f32[10,64,128]{2,1,0:T(8,128)S(1)}, f32[10,64,128]{2,1,0:T(8,128)S(1)}, u32[]{:S(2)}, u32[]{:S(2)}) collective-permute-start(f32[10,64,128]{2,1,0:T(8,128)S(1)} %get-tuple-element.66.after_ref), channel_id=1, source_target_pairs={{0,1},{1,0},{2,3},{3,2},{4,5},{5,4},{6,7},{7,6},{8,9},{9,8},{10,11... | collective-permute-start | bytes 983048 | tf_op jit(solution)/shard_map/ppermute | solution.py:461
  85.3 20.9 %copy-start.1 = (bf16[20,8,32,128]{3,2,1,0:T(8,128)(2,1)S(1)}, bf16[20,8,32,128]{3,2,1,0:T(8,128)(2,1)}, u32[]{:S(2)}) copy-start(bf16[20,8,32,128]{3,2,1,0:T(8,128)(2,1)} %param.8) | copy-start | bytes 3932164
  85.3 20.9 %copy-start.9 = (bf16[256,256]{1,0:T(8,128)(2,1)S(1)}, bf16[256,256]{1,0:T(8,128)(2,1)}, u32[]{:S(2)}) copy-start(bf16[256,256]{1,0:T(8,128)(2,1)} %copy-done.8) | copy-start | bytes 393220
  85.3 25.8 %collective-permute-start.19 = (f32[10,64,128]{2,1,0:T(8,128)S(1)}, f32[10,64,128]{2,1,0:T(8,128)S(1)}, u32[]{:S(2)}, u32[]{:S(2)}) collective-permute-start(f32[10,64,128]{2,1,0:T(8,128)S(1)} %get-tuple-element.69), channel_id=1, source_target_pairs={{1,2},{2,1},{3,4},{4,3},{5,6},{6,5},{7,8},{8,7},{9,10},{10,9},{11,... | collective-permute-start | bytes 983048 | tf_op jit(solution)/shard_map/ppermute | solution.py:465
  91.4 22.1 %collective-permute-start.16 = (f32[10,64,128]{2,1,0:T(8,128)S(1)}, f32[10,64,128]{2,1,0:T(8,128)S(1)}, u32[]{:S(2)}, u32[]{:S(2)}) collective-permute-start(f32[10,64,128]{2,1,0:T(8,128)S(1)} %get-tuple-element.67), channel_id=1, source_target_pairs={{0,1},{1,0},{2,3},{3,2},{4,5},{5,4},{6,7},{7,6},{8,9},{9,8},{10,11... | collective-permute-start | bytes 983048 | tf_op jit(solution)/shard_map/ppermute | solution.py:461
  91.5 29.5 %collective-permute-start.17 = (f32[10,64,128]{2,1,0:T(8,128)S(1)}, f32[10,64,128]{2,1,0:T(8,128)S(1)}, u32[]{:S(2)}, u32[]{:S(2)}) collective-permute-start(f32[10,64,128]{2,1,0:T(8,128)S(1)} %get-tuple-element.68), channel_id=1, source_target_pairs={{1,2},{2,1},{3,4},{4,3},{5,6},{6,5},{7,8},{8,7},{9,10},{10,9},{11,... | collective-permute-start | bytes 983048 | tf_op jit(solution)/shard_map/ppermute | solution.py:465
  (2 other events, 1.4 us)

commit v3 on v2

--- a/solution.py
+++ b/solution.py
@@ -54,7 +54,7 @@
         out_specs=outs if outs is not None else jax.tree.map(lambda o: vmem, out),
         scratch_shapes=scratch,
         input_output_aliases=aliases or {},
-        compiler_params=pltpu.CompilerParams(vmem_limit_bytes=24 * 1024 * 1024),
+        compiler_params=pltpu.CompilerParams(vmem_limit_bytes=16 * 1024 * 1024),
         cost_estimate=pl.CostEstimate(flops=cost, bytes_accessed=cost, transcendentals=0),
         **kw,
     )
@@ -189,12 +189,40 @@
     )(where, alpha, ensemble, loc, after)
 
 
-def pass_kernel(obs_ref, after_ref, out_ref):
-    out_ref[...] = obs_ref[...]
-
-
-def pass_on(obs, after):
-    return call(pass_kernel, sds(*obs.shape), ins=[VMEM, VMEM], outs=VMEM)(obs, after)
+def obs_kernel(count_ref, col_ref, lev_ref, innov_ref, weight_ref, after_ref, out_ref):
+    slots = col_ref.shape[1]
+    live = lax.broadcasted_iota(jnp.int32, (1, slots), 1) < count_ref[0]
+    rows = []
+    for field in (
+        col_ref[...].astype(F32),
+        lev_ref[...].astype(F32),
+        innov_ref[...],
+        jnp.where(live, weight_ref[...], 0.0),
+    ):
+        field = jnp.concatenate([field, jnp.zeros((1, V * SLOTS - slots), F32)], axis=1)
+        rows += [field[:, 384 * a : 384 * a + 384] for a in range(6)]
+    rest = jnp.concatenate(rows, axis=0)
+    i = lax.broadcasted_iota(jnp.int32, (384, 384), 0)
+    j = lax.broadcasted_iota(jnp.int32, (384, 384), 1)
+    order = (i == 3 * (j % 128) + j // 128).astype(F32).astype(BF16)
+    total = jnp.zeros((24, 384), F32)
+    for piece in range(3):
+        part = rest.astype(BF16)
+        rest = rest - part.astype(F32)
+        total = total + nn(part, order)
+    for f in range(4):
+        for a in range(6):
+            for v in range(V):
+                out_ref[f, v : v + 1, 128 * a : 128 * a + 128] = total[6 * f + a : 6 * f + a + 1, 128 * v : 128 * v + 128]
+
+
+def observations(count, col, lev, innov, weight, after):
+    return call(
+        obs_kernel,
+        sds(4, V, SLOTS),
+        ins=[SMEM] + [VMEM] * 5,
+        outs=VMEM,
+    )(count, col, lev, innov, weight, after)
 
 
 def edge_kernel(h, where_ref, e_ref, o_ref, own_ref, x_ref, hmat_ref, loc_ref, inner_ref, after_ref, inc_ref, se_ref, so_ref):
@@ -228,7 +256,7 @@
     return jnp.maximum(1.0 - jnp.abs(distance), 0.0)
 
 
-def weights_kernel(where_ref, own_ref, e_ref, o_ref, wown_ref, wnear_ref):
+def weights_kernel(where_ref, own_ref, e_ref, o_ref, wown_ref, wnear_ref, lev_ref, innov_ref, weight_ref):
     even_row = where_ref[2].astype(F32)
     odd_row = where_ref[3].astype(F32)
     odd_there = where_ref[4].astype(F32)
@@ -250,13 +278,31 @@
             row, across = columns(ref[0, v : v + 1, :])
             wnear_ref[n, v, :32] = (0.25 * across).astype(BF16)
             wnear_ref[n, v, 32:] = (0.75 * across).astype(BF16)
+    is_odd = where_ref[5]
+    for n, ref in enumerate((own_ref, e_ref, o_ref)):
+        rows = slice(3 * n, 3 * n + 3)
+        lev_ref[rows] = ref[1]
+        innov_ref[rows] = ref[2]
+        if n == 0:
+            weight_ref[rows] = ref[3]
+        else:
+            first = is_odd == (0 if n == 1 else 1)
+            at_edge = jnp.where(first, ref[0], 1023.0 - ref[0]) < 64.0
+            there = at_edge & ((n == 1) | (where_ref[4] == 1))
+            weight_ref[rows] = jnp.where(there, ref[3], 0.0)
 
 
 def weights(where, own, even, odd):
     vmem = pl.BlockSpec(memory_space=pltpu.VMEM)
     return call(
         weights_kernel,
-        (sds(V, 320, SLOTS, dtype=BF16), sds(2, V, 64, SLOTS, dtype=BF16)),
+        (
+            sds(V, 320, SLOTS, dtype=BF16),
+            sds(2, V, 64, SLOTS, dtype=BF16),
+            sds(9, SLOTS),
+            sds(9, SLOTS),
+            sds(9, SLOTS),
+        ),
         ins=[pl.BlockSpec(memory_space=pltpu.SMEM), vmem, vmem, vmem],
         cost=5000000,
     )(where, own, even, odd)
@@ -472,10 +518,6 @@
     ]
 
 
-def by_variable(x):
-    return jnp.pad(x, (0, V * SLOTS - x.shape[0])).reshape(SLOTS, V).T
-
-
 def on_device(alpha, ensemble, loc_vert, obs_col, obs_lev, obs_count, innovation, obs_weight):
     members = alpha.shape[0]
     tile = lax.axis_index("tile")
@@ -505,32 +547,13 @@
     )
     eb, ob = swap_even(send_eb), swap_odd(send_ob)
 
-    token, obs_col, obs_lev, obs_count, innovation, obs_weight = lax.optimization_barrier(
-        (token, obs_col, obs_lev, obs_count, innovation, obs_weight)
-    )
-    live = jnp.arange(obs_col.shape[1], dtype=jnp.int32) < obs_count[0]
-    own_obs = jnp.stack(
-        [
-            by_variable(obs_col[0].astype(F32) + token[0, 0]),
-            by_variable(obs_lev[0].astype(F32)),
-            by_variable(innovation[0]),
-            by_variable(jnp.where(live, obs_weight[0], 0.0)),
-        ]
-    )
-    own_obs = pass_on(own_obs, ea)
+    own_obs = observations(obs_count, obs_col, obs_lev, innovation, obs_weight, token)
     even_obs = swap_even(own_obs)
     odd_obs = swap_odd(own_obs)
-    even_on = jnp.where(even, even_obs[0] < 64.0, even_obs[0] >= 960.0)
-    odd_on = jnp.where(even, odd_obs[0] >= 960.0, odd_obs[0] < 64.0) & odd_there
-    lev = jnp.concatenate([own_obs[1], even_obs[1], odd_obs[1]])
-    innov = jnp.concatenate([own_obs[2], even_obs[2], odd_obs[2]])
-    weight = jnp.concatenate(
-        [own_obs[3], jnp.where(even_on, even_obs[3], 0.0), jnp.where(odd_on, odd_obs[3], 0.0)]
-    )
 
     inc_a, se_a, so_a = edge_part(0, where, ea, oa, la, xa, hmat, loc_vert, inner, own_obs)
     near_a = swap_even(se_a), swap_odd(so_a)
-    wown, wnear = weights(where, own_obs, even_obs, odd_obs)
+    wown, wnear, lev, innov, weight = weights(where, own_obs, even_obs, odd_obs)
     mine_a = values(0, where, inc_a, *near_a, wown, wnear, lev, inc_a)
     vals_a = round_mem(mine_a)
 

time: 124 us -> 116 us (0.935)
  local copies, waits for them, and re-layouts: 21.7 us -> 4.3 us
  starting transfers between devices: 57.8 us -> 66.3 us
  waiting for transfers between devices: 15.6 us -> 20.4 us
  Pallas kernels: 26.2 us -> 24.1 us
  other arithmetic: 1.39 us -> 0 us
    reshape x8 -> x0, local copies, waits for them, and re-layouts: 12.6 us -> none  [by_variable(): return jnp.pad(x, (0, V * SLOTS - x.shape[0])).reshape(SLOTS, V).T]
    ppermute x7, starting transfers between devices: 44 us -> 51.4 us  [swap_odd(): return lax.ppermute(x, 'tile', ODD)]
    ppermute x7, waiting for transfers between devices: 14.4 us -> 18.5 us  [swap_odd(): return lax.ppermute(x, 'tile', ODD)]
    unnamed x28 -> x20, local copies, waits for them, and re-layouts: 6.78 us -> 4.21 us
    pad x4 -> x0, local copies, waits for them, and re-layouts: 1.79 us -> none  [by_variable(): return jnp.pad(x, (0, V * SLOTS - x.shape[0])).reshape(SLOTS, V).T]
  transfers between devices with their start and end apart: 20 -> 20, of which waited for: 4 -> 5; matrix products, arithmetic and copies ran while one was open for 13% -> 0% of each run, Pallas kernels for 16% -> 16%
where the time goes in v3:
time: 116 us
  starting transfers between devices  66.3 us (57%)
  Pallas kernels  24.1 us (21%)
  waiting for transfers between devices  20.4 us (18%)
  local copies, waits for them, and re-layouts  4.3 us (4%)
    ppermute x7, starting transfers between devices, swap_odd(): return lax.ppermute(x, 'tile', ODD)  51.4 us
    ppermute x7, waiting for transfers between devices, swap_odd(): return lax.ppermute(x, 'tile', ODD)  18.5 us
    ppermute x6, starting transfers between devices, round_mem(): lax.ppermute(mine, 'mem', [(i, (i + shift) % size) for i in range(size)])  8.86 us
    ppermute x7, starting transfers between devices, swap_even(): return lax.ppermute(x, 'tile', EVEN)  6.05 us
    pallas_call x1, Pallas kernels, back_part(): call(back_kernel, (sds(members, 256, 128), sds(members, 128, 128)), grid=...  4.8 us
    pallas_call x1, Pallas kernels, own_part(): call(own_kernel, (sds(V, 128, 128), sds(PAIRS, 128, 128), sds(PAIRS, 128,...  4.58 us
    unnamed x20, local copies, waits for them, and re-layouts  4.21 us
    pallas_call x2, Pallas kernels, values(): call(functools.partial(values_kernel, h), sds(9, SLOTS), ins=[SMEM] + [VM...  3.28 us
  transfers between devices with their start and end apart: 20, of which 5 were waited for; matrix products, arithmetic and copies ran while one was open for 0% of the time, Pallas kernels for 16%

profile of v3, /device:TPU:33, one launch (start us, length us, event | category | flops | bytes accessed | tf_op | source)
XLA Modules:
  0.0 116.0 jit_solution(5883111891040158832)
XLA Ops:
  0.1 1.3 %copy-done = bf16[20,8,32,128]{3,2,1,0:T(8,128)(2,1)S(1)} copy-done((bf16[20,8,32,128]{3,2,1,0:T(8,128)(2,1)S(1)}, bf16[20,8,32,128]{3,2,1,0:T(8,128)(2,1)}, u32[]{:S(2)}) %copy-start) | copy-done | bytes 1310744
  1.4 0.8 copy-done.4
  2.2 0.9 shard_map.82
  3.0 3.1 %collective-permute-start.2 = (f32[10,64,128]{2,1,0:T(8,128)S(1)}, f32[10,64,128]{2,1,0:T(8,128)S(1)}, u32[]{:S(2)}, u32[]{:S(2)}) collective-permute-start(f32[10,64,128]{2,1,0:T(8,128)S(1)} %get-tuple-element.44), channel_id=1, source_target_pairs={{0,1},{1,0},{2,3},{3,2},{4,5},{5,4},{6,7},{7,6},{8,9},{9,8},{10,11... | collective-permute-start | bytes 983048 | tf_op jit(solution)/shard_map/ppermute | solution.py:507
  6.1 7.9 %collective-permute-start.3 = (f32[10,64,128]{2,1,0:T(8,128)S(1)}, f32[10,64,128]{2,1,0:T(8,128)S(1)}, u32[]{:S(2)}, u32[]{:S(2)}) collective-permute-start(f32[10,64,128]{2,1,0:T(8,128)S(1)} %get-tuple-element.45), channel_id=1, source_target_pairs={{1,2},{2,1},{3,4},{4,3},{5,6},{6,5},{7,8},{8,7},{9,10},{10,9},{11,... | collective-permute-start | bytes 983048 | tf_op jit(solution)/shard_map/ppermute | solution.py:511
  14.1 2.1 %copy-done.2 = bf16[20,3,8,32,128]{4,3,2,1,0:T(8,128)(2,1)S(1)} copy-done((bf16[20,3,8,32,128]{4,3,2,1,0:T(8,128)(2,1)S(1)}, bf16[20,3,8,32,128]{4,3,2,1,0:T(8,128)(2,1)}, u32[]{:S(2)}) %copy-start.2) | copy-done | bytes 3932184
  16.2 4.6 %shard_map.83 = (f32[3,128,128]{2,1,0:T(8,128)S(1)}, f32[10,128,128]{2,1,0:T(8,128)S(1)}, f32[10,128,128]{2,1,0:T(8,128)S(1)}, bf16[10,3,128,128]{3,2,1,0:T(8,12...) custom-call(s32[7]{0:T(128)S(1)} %stack.35.where_ref, ...), custom_call_target="tpu_custom_call" | custom-call | flops 1000000 | bytes 1000000 | tf_op jit(solution)/shard_map/pallas_call | solution.py:155
  20.9 1.2 %collective-permute-start.1 = (f32[10,64,128]{2,1,0:T(8,128)S(1)}, f32[10,64,128]{2,1,0:T(8,128)S(1)}, u32[]{:S(2)}, u32[]{:S(2)}) collective-permute-start(f32[10,64,128]{2,1,0:T(8,128)S(1)} %get-tuple-element.39), channel_id=1, source_target_pairs={{1,2},{2,1},{3,4},{4,3},{5,6},{6,5},{7,8},{8,7},{9,10},{10,9},{11,... | collective-permute-start | bytes 983048 | tf_op jit(solution)/shard_map/ppermute | solution.py:511
  23.1 6.8 %collective-permute-start.7 = (f32[4,3,768]{2,1,0:T(4,128)S(1)}, f32[4,3,768]{2,1,0:T(4,128)S(1)}, u32[]{:S(2)}, u32[]{:S(2)}) collective-permute-start(f32[4,3,768]{2,1,0:T(4,128)S(1)} %shard_map.84.after_ref.own_ref), channel_id=1, source_target_pairs={{1,2},{2,1},{3,4},{4,3},{5,6},{6,5},{7,8},{8,7},{9,10},{10,9},{11,... | collective-permute-start | bytes 110600 | tf_op jit(solution)/shard_map/ppermute | solution.py:511
  29.9 1.1 shard_map.85
  31.0 2.4 %collective-permute-start.4 = (f32[3,16,128]{2,1,0:T(8,128)S(1)}, f32[3,16,128]{2,1,0:T(8,128)S(1)}, u32[]{:S(2)}, u32[]{:S(2)}) collective-permute-start(f32[3,16,128]{2,1,0:T(8,128)S(1)} %get-tuple-element.50), channel_id=1, source_target_pairs={{0,1},{1,0},{2,3},{3,2},{4,5},{5,4},{6,7},{7,6},{8,9},{9,8},{10,11... | collective-permute-start | bytes 73736 | tf_op jit(solution)/shard_map/ppermute | solution.py:507
  33.4 9.3 %collective-permute-done.7.o_ref = f32[4,3,768]{2,1,0:T(4,128)S(1)} collective-permute-done((f32[4,3,768]{2,1,0:T(4,128)S(1)}, f32[4,3,768]{2,1,0:T(4,128)S(1)}, u32[]{:S(2)}, u32[]{:S(2)}) %collective-permute-start.7) | collective-permute-done | bytes 36896 | tf_op jit(solution)/shard_map/ppermute | solution.py:511
  42.8 8.5 %collective-permute-start.5 = (f32[3,16,128]{2,1,0:T(8,128)S(1)}, f32[3,16,128]{2,1,0:T(8,128)S(1)}, u32[]{:S(2)}, u32[]{:S(2)}) collective-permute-start(f32[3,16,128]{2,1,0:T(8,128)S(1)} %get-tuple-element.51), channel_id=1, source_target_pairs={{1,2},{2,1},{3,4},{4,3},{5,6},{6,5},{7,8},{8,7},{9,10},{10,9},{11,... | collective-permute-start | bytes 73736 | tf_op jit(solution)/shard_map/ppermute | solution.py:511
  51.3 0.9 shard_map.86
  52.5 1.6 %shard_map.87.after_ref.v0 = f32[9,768]{1,0:T(8,128)S(1)} custom-call(s32[7]{0:T(128)S(1)} %stack.35.where_ref, f32[3,256,64]{2,1,0:T(8,128)S(1)} %get-tuple-element.49.inc_ref.after_ref, f32[3,16,128]{2,1,0:T(8,128)S(1)} %collective-permute-done.4.e_ref, f32[3,16,128]{2,1,0:T(8,128)S(1)} %collective-permute-done.5.o_ref, ...), custom_call_target="tpu_custom_call" | custom-call | flops 1000000 | bytes 1000000 | tf_op jit(solution)/shard_map/pallas_call | solution.py:333
  54.2 1.4 %collective-permute-start.12 = (f32[9,768]{1,0:T(8,128)S(1)}, f32[9,768]{1,0:T(8,128)S(1)}, u32[]{:S(2)}, u32[]{:S(2)}) collective-permute-start(f32[9,768]{1,0:T(8,128)S(1)} %shard_map.87.after_ref.v0), channel_id=1, source_target_pairs={{0,192},{64,0},{128,64},{192,128},{1,193},{65,1},{129,65},{193,129... | collective-permute-start | bytes 82952 | tf_op jit(solution)/shard_map/ppermute | solution.py:517
  55.6 3.3 %collective-permute-start.11 = (f32[9,768]{1,0:T(8,128)S(1)}, f32[9,768]{1,0:T(8,128)S(1)}, u32[]{:S(2)}, u32[]{:S(2)}) collective-permute-start(f32[9,768]{1,0:T(8,128)S(1)} %shard_map.87.after_ref.v0), channel_id=1, source_target_pairs={{0,128},{64,192},{128,0},{192,64},{1,129},{65,193},{129,1},{193,65... | collective-permute-start | bytes 82952 | tf_op jit(solution)/shard_map/ppermute | solution.py:517
  58.9 0.4 collective-permute-start.10
  59.2 1.1 shard_map.88
  60.4 7.3 %collective-permute-start.9 = (f32[3,16,128]{2,1,0:T(8,128)S(1)}, f32[3,16,128]{2,1,0:T(8,128)S(1)}, u32[]{:S(2)}, u32[]{:S(2)}) collective-permute-start(f32[3,16,128]{2,1,0:T(8,128)S(1)} %get-tuple-element.57), channel_id=1, source_target_pairs={{1,2},{2,1},{3,4},{4,3},{5,6},{6,5},{7,8},{8,7},{9,10},{10,9},{11,... | collective-permute-start | bytes 73736 | tf_op jit(solution)/shard_map/ppermute | solution.py:511
  67.7 1.6 %shard_map.89 = (f32[3,256,64]{2,1,0:T(8,128)S(1)}, f32[10,64,128]{2,1,0:T(8,128)S(1)}, f32[10,64,128]{2,1,0:T(8,128)S(1)}) custom-call(s32[7]{0:T(128)S(1)} %stack.35.where_ref, f32[9,768]{1,0:T(8,128)S(1)} %shard_map.87.after_ref.v0, f32[9,768]{1,0:T(8,128)S(1)} %collective-permute-done.10.v1, f32[9,768]{1,0:T(8,128)S(1)} %collective-permute-done.11.v2, ...), custom_call_target="tpu_custom_call" | custom-call | flops 1000000 | bytes 1000000 | tf_op jit(solution)/shard_map/pallas_call | solution.py:372
  69.5 1.9 %collective-permute-done.8.e_ref = f32[3,16,128]{2,1,0:T(8,128)S(1)} collective-permute-done((f32[3,16,128]{2,1,0:T(8,128)S(1)}, f32[3,16,128]{2,1,0:T(8,128)S(1)}, u32[]{:S(2)}, u32[]{:S(2)}) %collective-permute-start.8) | collective-permute-done | bytes 24608 | tf_op jit(solution)/shard_map/ppermute | solution.py:507
  71.3 1.6 %shard_map.90.v0.after_ref = f32[9,768]{1,0:T(8,128)S(1)} custom-call(s32[7]{0:T(128)S(1)} %stack.35.where_ref, f32[3,256,64]{2,1,0:T(8,128)S(1)} %get-tuple-element.55.inc_ref, f32[3,16,128]{2,1,0:T(8,128)S(1)} %collective-permute-done.8.e_ref, f32[3,16,128]{2,1,0:T(8,128)S(1)} %collective-permute-done.9.o_ref, ...), custom_call_target="tpu_custom_call" | custom-call | flops 1000000 | bytes 1000000 | tf_op jit(solution)/shard_map/pallas_call | solution.py:333
  73.0 1.9 %collective-permute-start.15 = (f32[9,768]{1,0:T(8,128)S(1)}, f32[9,768]{1,0:T(8,128)S(1)}, u32[]{:S(2)}, u32[]{:S(2)}) collective-permute-start(f32[9,768]{1,0:T(8,128)S(1)} %shard_map.90.v0.after_ref), channel_id=1, source_target_pairs={{0,192},{64,0},{128,64},{192,128},{1,193},{65,1},{129,65},{193,129... | collective-permute-start | bytes 82952 | tf_op jit(solution)/shard_map/ppermute | solution.py:517
  75.1 1.6 %collective-permute-start.13 = (f32[9,768]{1,0:T(8,128)S(1)}, f32[9,768]{1,0:T(8,128)S(1)}, u32[]{:S(2)}, u32[]{:S(2)}) collective-permute-start(f32[9,768]{1,0:T(8,128)S(1)} %shard_map.90.v0.after_ref), channel_id=1, source_target_pairs={{0,64},{64,128},{128,192},{192,0},{1,65},{65,129},{129,193},{193,1... | collective-permute-start | bytes 82952 | tf_op jit(solution)/shard_map/ppermute | solution.py:517
  77.1 5.0 %collective-permute-start.19 = (f32[10,64,128]{2,1,0:T(8,128)S(1)}, f32[10,64,128]{2,1,0:T(8,128)S(1)}, u32[]{:S(2)}, u32[]{:S(2)}) collective-permute-start(f32[10,64,128]{2,1,0:T(8,128)S(1)} %get-tuple-element.63), channel_id=1, source_target_pairs={{1,2},{2,1},{3,4},{4,3},{5,6},{6,5},{7,8},{8,7},{9,10},{10,9},{11,... | collective-permute-start | bytes 983048 | tf_op jit(solution)/shard_map/ppermute | solution.py:511
  82.1 1.6 %shard_map.91 = (f32[3,256,64]{2,1,0:T(8,128)S(1)}, f32[10,64,128]{2,1,0:T(8,128)S(1)}, f32[10,64,128]{2,1,0:T(8,128)S(1)}) custom-call(s32[7]{0:T(128)S(1)} %stack.35.where_ref, f32[9,768]{1,0:T(8,128)S(1)} %shard_map.90.v0.after_ref, f32[9,768]{1,0:T(8,128)S(1)} %collective-permute-done.13.v1, f32[9,768]{1,0:T(8,128)S(1)} %collective-permute-done.14.v2, ...), custom_call_target="tpu_custom_call" | custom-call | flops 1000000 | bytes 1000000 | tf_op jit(solution)/shard_map/pallas_call | solution.py:372
  83.8 14.7 %collective-permute-start.17 = (f32[10,64,128]{2,1,0:T(8,128)S(1)}, f32[10,64,128]{2,1,0:T(8,128)S(1)}, u32[]{:S(2)}, u32[]{:S(2)}) collective-permute-start(f32[10,64,128]{2,1,0:T(8,128)S(1)} %get-tuple-element.62), channel_id=1, source_target_pairs={{1,2},{2,1},{3,4},{4,3},{5,6},{6,5},{7,8},{8,7},{9,10},{10,9},{11,... | collective-permute-start | bytes 983048 | tf_op jit(solution)/shard_map/ppermute | solution.py:511
  98.5 4.8 %shard_map.92 = (f32[20,256,128]{2,1,0:T(8,128)}, f32[20,128,128]{2,1,0:T(8,128)S(1)}) custom-call(bf16[20,256,128]{2,1,0:T(8,128)(2,1)S(1)} %bitcast.17, bf16[20,3,256,128]{3,2,1,0:T(8,128)(2,1)S(1)} %bitcast.19, f32[3,256,64]{2,1,0:T(8,128)S(1)} %get-tuple-element.64.ca_ref, f32[3,256,64]{2,1,0:T(8,128)S(1)} %get-tuple-element.65.cb_ref, ...), custom_call_target="tpu_custom_call" | custom-call | flops 1000000 | bytes 1000000 | tf_op jit(solution)/shard_map/pallas_call | solution.py:406
  103.3 1.2 %shard_map.93.edge_ref = f32[20,128,128]{2,1,0:T(8,128)S(1)} custom-call(f32[10,64,128]{2,1,0:T(8,128)S(1)} %collective-permute-done.18.e_ref, f32[10,64,128]{2,1,0:T(8,128)S(1)} %collective-permute-done.19.o_ref, f32[20,128,128]{2,1,0:T(8,128)S(1)} %get-tuple-element.67.edge_ref, bf16[128,128]{1,0:T(8,128)(2,1)S(1)} %get-tuple-element.42.hmat_ref, ...), custom_call_target="tpu_custom_call" | custom-call | flops 1000000 | bytes 1000000 | tf_op jit(solution)/shard_map/pallas_call | solution.py:441
  104.5 8.7 %collective-permute-done.17.o_ref = f32[10,64,128]{2,1,0:T(8,128)S(1)} collective-permute-done((f32[10,64,128]{2,1,0:T(8,128)S(1)}, f32[10,64,128]{2,1,0:T(8,128)S(1)}, u32[]{:S(2)}, u32[]{:S(2)}) %collective-permute-start.17) | collective-permute-done | bytes 327712 | tf_op jit(solution)/shard_map/ppermute | solution.py:511
  113.3 2.6 %shard_map.94 = f32[2,10,4,64,128]{4,3,2,1,0:T(8,128)} custom-call(f32[10,64,128]{2,1,0:T(8,128)S(1)} %collective-permute-done.16.e_ref, f32[10,64,128]{2,1,0:T(8,128)S(1)} %collective-permute-done.17.o_ref, f32[20,128,128]{2,1,0:T(8,128)S(1)} %shard_map.93.edge_ref, ...), custom_call_target="tpu_custom_call", output_to_operand_aliasing={{}: (5, {})} | custom-call | flops 1000000 | bytes 1000000 | tf_op jit(solution)/shard_map/pallas_call | solution.py:468
  (42 shorter events, 1.7 us)
Async XLA Ops:
  0.1 1.3 %copy-start = (bf16[20,8,32,128]{3,2,1,0:T(8,128)(2,1)S(1)}, bf16[20,8,32,128]{3,2,1,0:T(8,128)(2,1)}, u32[]{:S(2)}) copy-start(bf16[20,8,32,128]{3,2,1,0:T(8,128)(2,1)} %param.8) | copy-start | bytes 3932164
  1.4 0.8 copy-start.4
  3.0 26.8 %collective-permute-start.2 = (f32[10,64,128]{2,1,0:T(8,128)S(1)}, f32[10,64,128]{2,1,0:T(8,128)S(1)}, u32[]{:S(2)}, u32[]{:S(2)}) collective-permute-start(f32[10,64,128]{2,1,0:T(8,128)S(1)} %get-tuple-element.44), channel_id=1, source_target_pairs={{0,1},{1,0},{2,3},{3,2},{4,5},{5,4},{6,7},{7,6},{8,9},{9,8},{10,11... | collective-permute-start | bytes 983048 | tf_op jit(solution)/shard_map/ppermute | solution.py:507
  6.1 23.8 %collective-permute-start.3 = (f32[10,64,128]{2,1,0:T(8,128)S(1)}, f32[10,64,128]{2,1,0:T(8,128)S(1)}, u32[]{:S(2)}, u32[]{:S(2)}) collective-permute-start(f32[10,64,128]{2,1,0:T(8,128)S(1)} %get-tuple-element.45), channel_id=1, source_target_pairs={{1,2},{2,1},{3,4},{4,3},{5,6},{6,5},{7,8},{8,7},{9,10},{10,9},{11,... | collective-permute-start | bytes 983048 | tf_op jit(solution)/shard_map/ppermute | solution.py:511
  14.1 2.1 %copy-start.2 = (bf16[20,3,8,32,128]{4,3,2,1,0:T(8,128)(2,1)S(1)}, bf16[20,3,8,32,128]{4,3,2,1,0:T(8,128)(2,1)}, u32[]{:S(2)}) copy-start(bf16[20,3,8,32,128]{4,3,2,1,0:T(8,128)(2,1)} %param.9) | copy-start | bytes 11796484
  16.2 6.5 %copy-start.6 = (s32[1,2048]{1,0:T(1,128)S(1)}, s32[1,2048]{1,0:T(1,128)}, u32[]{:S(2)}) copy-start(s32[1,2048]{1,0:T(1,128)} %col_ref.1) | copy-start | bytes 24580
  16.2 6.5 %copy-start.7 = (s32[1,2048]{1,0:T(1,128)S(1)}, s32[1,2048]{1,0:T(1,128)}, u32[]{:S(2)}) copy-start(s32[1,2048]{1,0:T(1,128)} %lev_ref.1) | copy-start | bytes 24580
  16.2 6.5 %copy-start.8 = (f32[1,2048]{1,0:T(1,128)S(1)}, f32[1,2048]{1,0:T(1,128)}, u32[]{:S(2)}) copy-start(f32[1,2048]{1,0:T(1,128)} %innov_ref.1) | copy-start | bytes 24580
  16.2 6.6 %copy-start.9 = (f32[1,2048]{1,0:T(1,128)S(1)}, f32[1,2048]{1,0:T(1,128)}, u32[]{:S(2)}) copy-start(f32[1,2048]{1,0:T(1,128)} %weight_ref.1) | copy-start | bytes 24580
  20.8 38.5 %collective-permute-start = (f32[10,64,128]{2,1,0:T(8,128)S(1)}, f32[10,64,128]{2,1,0:T(8,128)S(1)}, u32[]{:S(2)}, u32[]{:S(2)}) collective-permute-start(f32[10,64,128]{2,1,0:T(8,128)S(1)} %get-tuple-element.38), channel_id=1, source_target_pairs={{0,1},{1,0},{2,3},{3,2},{4,5},{5,4},{6,7},{7,6},{8,9},{9,8},{10,11... | collective-permute-start | bytes 983048 | tf_op jit(solution)/shard_map/ppermute | solution.py:507
  20.9 38.4 %collective-permute-start.1 = (f32[10,64,128]{2,1,0:T(8,128)S(1)}, f32[10,64,128]{2,1,0:T(8,128)S(1)}, u32[]{:S(2)}, u32[]{:S(2)}) collective-permute-start(f32[10,64,128]{2,1,0:T(8,128)S(1)} %get-tuple-element.39), channel_id=1, source_target_pairs={{1,2},{2,1},{3,4},{4,3},{5,6},{6,5},{7,8},{8,7},{9,10},{10,9},{11,... | collective-permute-start | bytes 983048 | tf_op jit(solution)/shard_map/ppermute | solution.py:511
  23.1 19.7 %collective-permute-start.7 = (f32[4,3,768]{2,1,0:T(4,128)S(1)}, f32[4,3,768]{2,1,0:T(4,128)S(1)}, u32[]{:S(2)}, u32[]{:S(2)}) collective-permute-start(f32[4,3,768]{2,1,0:T(4,128)S(1)} %shard_map.84.after_ref.own_ref), channel_id=1, source_target_pairs={{1,2},{2,1},{3,4},{4,3},{5,6},{6,5},{7,8},{8,7},{9,10},{10,9},{11,... | collective-permute-start | bytes 110600 | tf_op jit(solution)/shard_map/ppermute | solution.py:511
  29.9 21.4 %collective-permute-start.6 = (f32[4,3,768]{2,1,0:T(4,128)S(1)}, f32[4,3,768]{2,1,0:T(4,128)S(1)}, u32[]{:S(2)}, u32[]{:S(2)}) collective-permute-start(f32[4,3,768]{2,1,0:T(4,128)S(1)} %shard_map.84.after_ref.own_ref), channel_id=1, source_target_pairs={{0,1},{1,0},{2,3},{3,2},{4,5},{5,4},{6,7},{7,6},{8,9},{9,8},{10,11... | collective-permute-start | bytes 110600 | tf_op jit(solution)/shard_map/ppermute | solution.py:507
  31.0 21.3 %collective-permute-start.4 = (f32[3,16,128]{2,1,0:T(8,128)S(1)}, f32[3,16,128]{2,1,0:T(8,128)S(1)}, u32[]{:S(2)}, u32[]{:S(2)}) collective-permute-start(f32[3,16,128]{2,1,0:T(8,128)S(1)} %get-tuple-element.50), channel_id=1, source_target_pairs={{0,1},{1,0},{2,3},{3,2},{4,5},{5,4},{6,7},{7,6},{8,9},{9,8},{10,11... | collective-permute-start | bytes 73736 | tf_op jit(solution)/shard_map/ppermute | solution.py:507
  42.8 9.7 %collective-permute-start.5 = (f32[3,16,128]{2,1,0:T(8,128)S(1)}, f32[3,16,128]{2,1,0:T(8,128)S(1)}, u32[]{:S(2)}, u32[]{:S(2)}) collective-permute-start(f32[3,16,128]{2,1,0:T(8,128)S(1)} %get-tuple-element.51), channel_id=1, source_target_pairs={{1,2},{2,1},{3,4},{4,3},{5,6},{6,5},{7,8},{8,7},{9,10},{10,9},{11,... | collective-permute-start | bytes 73736 | tf_op jit(solution)/shard_map/ppermute | solution.py:511
  54.2 13.5 %collective-permute-start.12 = (f32[9,768]{1,0:T(8,128)S(1)}, f32[9,768]{1,0:T(8,128)S(1)}, u32[]{:S(2)}, u32[]{:S(2)}) collective-permute-start(f32[9,768]{1,0:T(8,128)S(1)} %shard_map.87.after_ref.v0), channel_id=1, source_target_pairs={{0,192},{64,0},{128,64},{192,128},{1,193},{65,1},{129,65},{193,129... | collective-permute-start | bytes 82952 | tf_op jit(solution)/shard_map/ppermute | solution.py:517
  55.6 12.0 %collective-permute-start.11 = (f32[9,768]{1,0:T(8,128)S(1)}, f32[9,768]{1,0:T(8,128)S(1)}, u32[]{:S(2)}, u32[]{:S(2)}) collective-permute-start(f32[9,768]{1,0:T(8,128)S(1)} %shard_map.87.after_ref.v0), channel_id=1, source_target_pairs={{0,128},{64,192},{128,0},{192,64},{1,129},{65,193},{129,1},{193,65... | collective-permute-start | bytes 82952 | tf_op jit(solution)/shard_map/ppermute | solution.py:517
  58.9 8.8 %collective-permute-start.10 = (f32[9,768]{1,0:T(8,128)S(1)}, f32[9,768]{1,0:T(8,128)S(1)}, u32[]{:S(2)}, u32[]{:S(2)}) collective-permute-start(f32[9,768]{1,0:T(8,128)S(1)} %shard_map.87.after_ref.v0), channel_id=1, source_target_pairs={{0,64},{64,128},{128,192},{192,0},{1,65},{65,129},{129,193},{193,1... | collective-permute-start | bytes 82952 | tf_op jit(solution)/shard_map/ppermute | solution.py:517
  60.4 9.1 %collective-permute-start.9 = (f32[3,16,128]{2,1,0:T(8,128)S(1)}, f32[3,16,128]{2,1,0:T(8,128)S(1)}, u32[]{:S(2)}, u32[]{:S(2)}) collective-permute-start(f32[3,16,128]{2,1,0:T(8,128)S(1)} %get-tuple-element.57), channel_id=1, source_target_pairs={{1,2},{2,1},{3,4},{4,3},{5,6},{6,5},{7,8},{8,7},{9,10},{10,9},{11,... | collective-permute-start | bytes 73736 | tf_op jit(solution)/shard_map/ppermute | solution.py:511
  67.6 3.7 %collective-permute-start.8 = (f32[3,16,128]{2,1,0:T(8,128)S(1)}, f32[3,16,128]{2,1,0:T(8,128)S(1)}, u32[]{:S(2)}, u32[]{:S(2)}) collective-permute-start(f32[3,16,128]{2,1,0:T(8,128)S(1)} %get-tuple-element.56.after_ref), channel_id=1, source_target_pairs={{0,1},{1,0},{2,3},{3,2},{4,5},{5,4},{6,7},{7,6},{8,9},{9,8},{10,11... | collective-permute-start | bytes 73736 | tf_op jit(solution)/shard_map/ppermute | solution.py:507
  71.3 27.2 %copy-start.3 = (bf16[20,3,8,32,128]{4,3,2,1,0:T(8,128)(2,1)S(1)}, bf16[20,3,8,32,128]{4,3,2,1,0:T(8,128)(2,1)}, u32[]{:S(2)}) copy-start(bf16[20,3,8,32,128]{4,3,2,1,0:T(8,128)(2,1)} %param.9) | copy-start | bytes 11796484
  73.0 9.1 %collective-permute-start.15 = (f32[9,768]{1,0:T(8,128)S(1)}, f32[9,768]{1,0:T(8,128)S(1)}, u32[]{:S(2)}, u32[]{:S(2)}) collective-permute-start(f32[9,768]{1,0:T(8,128)S(1)} %shard_map.90.v0.after_ref), channel_id=1, source_target_pairs={{0,192},{64,0},{128,64},{192,128},{1,193},{65,1},{129,65},{193,129... | collective-permute-start | bytes 82952 | tf_op jit(solution)/shard_map/ppermute | solution.py:517
  74.8 7.2 %collective-permute-start.14 = (f32[9,768]{1,0:T(8,128)S(1)}, f32[9,768]{1,0:T(8,128)S(1)}, u32[]{:S(2)}, u32[]{:S(2)}) collective-permute-start(f32[9,768]{1,0:T(8,128)S(1)} %shard_map.90.v0.after_ref), channel_id=1, source_target_pairs={{0,128},{64,192},{128,0},{192,64},{1,129},{65,193},{129,1},{193,65... | collective-permute-start | bytes 82952 | tf_op jit(solution)/shard_map/ppermute | solution.py:517
  75.1 6.9 %collective-permute-start.13 = (f32[9,768]{1,0:T(8,128)S(1)}, f32[9,768]{1,0:T(8,128)S(1)}, u32[]{:S(2)}, u32[]{:S(2)}) collective-permute-start(f32[9,768]{1,0:T(8,128)S(1)} %shard_map.90.v0.after_ref), channel_id=1, source_target_pairs={{0,64},{64,128},{128,192},{192,0},{1,65},{65,129},{129,193},{193,1... | collective-permute-start | bytes 82952 | tf_op jit(solution)/shard_map/ppermute | solution.py:517
  76.7 26.6 %collective-permute-start.18 = (f32[10,64,128]{2,1,0:T(8,128)S(1)}, f32[10,64,128]{2,1,0:T(8,128)S(1)}, u32[]{:S(2)}, u32[]{:S(2)}) collective-permute-start(f32[10,64,128]{2,1,0:T(8,128)S(1)} %get-tuple-element.60.after_ref), channel_id=1, source_target_pairs={{0,1},{1,0},{2,3},{3,2},{4,5},{5,4},{6,7},{7,6},{8,9},{9,8},{10,11... | collective-permute-start | bytes 983048 | tf_op jit(solution)/shard_map/ppermute | solution.py:507
  77.1 21.4 %copy-start.1 = (bf16[20,8,32,128]{3,2,1,0:T(8,128)(2,1)S(1)}, bf16[20,8,32,128]{3,2,1,0:T(8,128)(2,1)}, u32[]{:S(2)}) copy-start(bf16[20,8,32,128]{3,2,1,0:T(8,128)(2,1)} %param.8) | copy-start | bytes 3932164
  77.1 26.2 %collective-permute-start.19 = (f32[10,64,128]{2,1,0:T(8,128)S(1)}, f32[10,64,128]{2,1,0:T(8,128)S(1)}, u32[]{:S(2)}, u32[]{:S(2)}) collective-permute-start(f32[10,64,128]{2,1,0:T(8,128)S(1)} %get-tuple-element.63), channel_id=1, source_target_pairs={{1,2},{2,1},{3,4},{4,3},{5,6},{6,5},{7,8},{8,7},{9,10},{10,9},{11,... | collective-permute-start | bytes 983048 | tf_op jit(solution)/shard_map/ppermute | solution.py:511
  83.7 20.8 %collective-permute-start.16 = (f32[10,64,128]{2,1,0:T(8,128)S(1)}, f32[10,64,128]{2,1,0:T(8,128)S(1)}, u32[]{:S(2)}, u32[]{:S(2)}) collective-permute-start(f32[10,64,128]{2,1,0:T(8,128)S(1)} %get-tuple-element.61), channel_id=1, source_target_pairs={{0,1},{1,0},{2,3},{3,2},{4,5},{5,4},{6,7},{7,6},{8,9},{9,8},{10,11... | collective-permute-start | bytes 983048 | tf_op jit(solution)/shard_map/ppermute | solution.py:507
  83.8 29.5 %collective-permute-start.17 = (f32[10,64,128]{2,1,0:T(8,128)S(1)}, f32[10,64,128]{2,1,0:T(8,128)S(1)}, u32[]{:S(2)}, u32[]{:S(2)}) collective-permute-start(f32[10,64,128]{2,1,0:T(8,128)S(1)} %get-tuple-element.62), channel_id=1, source_target_pairs={{1,2},{2,1},{3,4},{4,3},{5,6},{6,5},{7,8},{8,7},{9,10},{10,9},{11,... | collective-permute-start | bytes 983048 | tf_op jit(solution)/shard_map/ppermute | solution.py:511
  98.5 4.8 %copy-start.5 = (bf16[128,128]{1,0:T(8,128)(2,1)S(1)}, bf16[128,128]{1,0:T(8,128)(2,1)}, u32[]{:S(2)}) copy-start(bf16[128,128]{1,0:T(8,128)(2,1)} %loc_ref.13) | copy-start | bytes 98308

commit v4 on v3

v4 whole, which is shorter than its diff:
```python
import jax
import jax.numpy as jnp
from jax import lax
from jax.experimental import pallas as pl
from jax.experimental.pallas import tpu as pltpu
from jax.sharding import PartitionSpec as P

V = 3
F32 = jnp.float32
BF16 = jnp.bfloat16
SLOTS = 768
GROUP = 4

TILES = 64
EVEN = [(i, i ^ 1) for i in range(TILES)]
ODD = [(i, ((i - 1) ^ 1) + 1) for i in range(1, TILES - 1)] + [(0, TILES - 1), (TILES - 1, 0)]

MEMS = 4
FIRST = [(TILES * m + a, TILES * m + b) for m in range(MEMS) for a, b in (EVEN if m < MEMS // 2 else ODD)]
SECOND = [(TILES * m + a, TILES * m + b) for m in range(MEMS) for a, b in (ODD if m < MEMS // 2 else EVEN)]


def nn(a, b):
    return lax.dot_general(a, b, (((1,), (0,)), ((), ())), preferred_element_type=F32)


def nt(a, b):
    return lax.dot_general(a, b, (((1,), (1,)), ((), ())), preferred_element_type=F32)


def tn(a, b):
    return lax.dot_general(a, b, (((0,), (0,)), ((), ())), preferred_element_type=F32)


def halves(x):
    high = x.astype(BF16)
    low = (x - high.astype(F32)).astype(BF16)
    return high, low


def lift(smoothed, loc):
    high, low = halves(smoothed)
    return nt(high, loc) + nt(low, loc)


def call(kernel, out, grid=None, ins=None, outs=None, scratch=(), aliases=None, cost=1000000):
    vmem = pl.BlockSpec(memory_space=pltpu.VMEM)
    kw = {}
    if grid is not None:
        kw["grid"] = grid
    return pl.pallas_call(
        kernel,
        out_shape=out,
        in_specs=ins,
        out_specs=outs if outs is not None else jax.tree.map(lambda o: vmem, out),
        scratch_shapes=scratch,
        input_output_aliases=aliases or {},
        compiler_params=pltpu.CompilerParams(vmem_limit_bytes=16 * 1024 * 1024),
        cost_estimate=pl.CostEstimate(flops=cost, bytes_accessed=cost, transcendentals=0),
        **kw,
    )


def sds(*shape, dtype=F32):
    return jax.ShapeDtypeStruct(shape, dtype)


ANY = pl.BlockSpec(memory_space=pl.ANY)
SMEM = pl.BlockSpec(memory_space=pltpu.SMEM)
VMEM = pl.BlockSpec(memory_space=pltpu.VMEM)


def smooth(matrix, field):
    both = jnp.concatenate(halves(field), axis=1)
    out = nn(matrix, both)
    return out[:, :128] + out[:, 128:]


def send_kernel(where_ref, quarters_ref, first_ref, second_ref, token_ref, edges, sems):
    copies = [pltpu.make_async_copy(quarters_ref.at[:, 3 * n], edges.at[n], sems.at[n]) for n in range(2)]
    for copy in copies:
        copy.start()
    token_ref[...] = jnp.zeros_like(token_ref)
    for copy in copies:
        copy.wait()
    low = where_ref[7]
    first_ref[...] = edges[1 - low].astype(F32)
    second_ref[...] = edges[low].astype(F32)


def send_part(where, quarters):
    members = quarters.shape[0]
    return call(
        send_kernel,
        (sds(members, 64, 128), sds(members, 64, 128), sds(8, 128)),
        ins=[SMEM, ANY],
        outs=(VMEM,) * 3,
        scratch=[pltpu.VMEM((2, members, 64, 128), BF16), pltpu.SemaphoreType.DMA((2,))],
    )(where, quarters)


def own_kernel(where_ref, alpha_ref, ens_ref, loc_ref, after_ref, inner_ref, edge_ref, x_ref, smat_ref, hmat_ref, token_ref):
    @pl.when(pl.program_id(0) == 0)
    def _():
        inner_ref[...] = jnp.zeros_like(inner_ref)
        token_ref[...] = jnp.zeros_like(token_ref)
        smat, hmat = matrices(where_ref[6], TILES, where_ref[7] == 0)
        smat_ref[...] = smat
        hmat_ref[...] = hmat

    smat = smat_ref[...]
    loc = loc_ref[...]
    total = [inner_ref[v] for v in range(V)]
    for k in range(GROUP):
        full = lift(nn(smat, alpha_ref[k]), loc)
        edge_ref[k, :64] = full[:64]
        edge_ref[k, 64:] = full[192:]
        lifted = full[64:192].astype(BF16).astype(F32)
        for v in range(V):
            total[v] = total[v] + ens_ref[k, v, 64:192].astype(F32) * lifted
            x_ref[k, v, :64] = ens_ref[k, v, :64]
            x_ref[k, v, 64:] = ens_ref[k, v, 192:]
    for v in range(V):
        inner_ref[v] = total[v]


def own_part(where, alpha, ensemble, loc, after):
    members = alpha.shape[0]
    whole = lambda *shape: pl.BlockSpec(shape, lambda i: (0,) * len(shape))
    return call(
        own_kernel,
        (
            sds(V, 128, 128),
            sds(members, 128, 128),
            sds(members, V, 128, 128, dtype=BF16),
            sds(256, 256, dtype=BF16),
            sds(128, 128, dtype=BF16),
            sds(8, 128),
        ),
        grid=(members // GROUP,),
        ins=[
            SMEM,
            pl.BlockSpec((GROUP, 256, 128), lambda i: (i, 0, 0)),
            pl.BlockSpec((GROUP, V, 256, 128), lambda i: (i, 0, 0, 0)),
            whole(128, 128),
            whole(8, 128),
        ],
        outs=(
            whole(V, 128, 128),
            pl.BlockSpec((GROUP, 128, 128), lambda i: (i, 0, 0)),
            pl.BlockSpec((GROUP, V, 128, 128), lambda i: (i, 0, 0, 0)),
            whole(256, 256),
            whole(128, 128),
            whole(8, 128),
        ),
    )(where, alpha, ensemble, loc, after)


def obs_kernel(count_ref, col_ref, lev_ref, innov_ref, weight_ref, after_ref, out_ref):
    slots = col_ref.shape[1]
    live = lax.broadcasted_iota(jnp.int32, (1, slots), 1) < count_ref[0]
    rows = []
    for field in (
        col_ref[...].astype(F32),
        lev_ref[...].astype(F32),
        innov_ref[...],
        jnp.where(live, weight_ref[...], 0.0),
    ):
        field = jnp.concatenate([field, jnp.zeros((1, V * SLOTS - slots), F32)], axis=1)
        rows += [field[:, 384 * a : 384 * a + 384] for a in range(6)]
    rest = jnp.concatenate(rows, axis=0)
    i = lax.broadcasted_iota(jnp.int32, (384, 384), 0)
    j = lax.broadcasted_iota(jnp.int32, (384, 384), 1)
    order = (i == 3 * (j % 128) + j // 128).astype(F32).astype(BF16)
    total = jnp.zeros((24, 384), F32)
    for piece in range(3):
        part = rest.astype(BF16)
        rest = rest - part.astype(F32)
        total = total + nn(part, order)
    for f in range(4):
        for a in range(6):
            for v in range(V):
                row = 6 * (V * f + v) + a
                out_ref[row : row + 1] = total[6 * f + a : 6 * f + a + 1, 128 * v : 128 * v + 128]


def observations(count, col, lev, innov, weight, after):
    return call(
        obs_kernel,
        sds(4 * V * SLOTS // 128, 128),
        ins=[SMEM] + [VMEM] * 5,
        outs=VMEM,
    )(count, col, lev, innov, weight, after)


def edge_kernel(where_ref, first_ref, second_ref, own_ref, x_ref, hmat_ref, loc_ref, inner_ref, after_even, after_odd, inc_ref, se_ref, so_ref):
    hmat = hmat_ref[...]
    loc = loc_ref[...]
    total = [jnp.zeros((128, 128), F32) for v in range(V)]
    for k in range(own_ref.shape[0]):
        halo = jnp.concatenate([first_ref[k].astype(BF16), second_ref[k].astype(BF16)], axis=0)
        lifted = (own_ref[k] + lift(nn(hmat, halo), loc)).astype(BF16).astype(F32)
        for v in range(V):
            total[v] = total[v] + x_ref[k, v].astype(F32) * lifted
    for v in range(V):
        inc_ref[v, :64] = total[v][:64]
        inc_ref[v, 64:192] = inner_ref[v]
        inc_ref[v, 192:] = total[v][64:]
        for n, ref in enumerate((se_ref, so_ref)):
            ref[v] = inc_ref[v, pl.ds(pl.multiple_of(where_ref[n], 32), 32)]


def edge_part(where, first, second, own, x, hmat, loc, inner, *after):
    return call(
        edge_kernel,
        (sds(V, 256, 128), sds(V, 32, 128), sds(V, 32, 128)),
        ins=[SMEM] + [VMEM] * 9,
        outs=(VMEM,) * 3,
    )(where, first, second, own, x, hmat, loc, inner, *after)


def tent(distance):
    return jnp.maximum(1.0 - jnp.abs(distance), 0.0)


def weights_kernel(where_ref, own_ref, e_ref, o_ref, wown_ref, wnear_ref, lev_ref, innov_ref, weight_ref):
    even_row = where_ref[2].astype(F32)
    odd_row = where_ref[3].astype(F32)
    odd_there = where_ref[4].astype(F32)
    cell = lax.broadcasted_iota(jnp.int32, (32, SLOTS), 0).astype(F32)

    def line(ref, field, v):
        at = 6 * (V * field + v)
        return jnp.concatenate([ref[at + a : at + a + 1] for a in range(6)], axis=1)

    def columns(code):
        row = jnp.floor(code * (1.0 / 64.0))
        column = code - 64.0 * row
        return row, tent(cell - (column * 0.5 - 0.25))

    for v in range(V):
        row, across = columns(line(own_ref, 0, v))
        middle = row * 0.5 - 0.25
        for r in range(8):
            wown_ref[v, 32 * r : 32 * r + 32] = (tent(r - middle) * across).astype(BF16)
        wown_ref[v, 256:288] = (tent(even_row - middle) * across).astype(BF16)
        wown_ref[v, 288:320] = (tent(odd_row - middle) * odd_there * across).astype(BF16)
        for n, ref in enumerate((e_ref, o_ref)):
            row, across = columns(line(ref, 0, v))
            wnear_ref[n, v, :32] = (0.25 * across).astype(BF16)
            wnear_ref[n, v, 32:] = (0.75 * across).astype(BF16)
    is_odd = where_ref[5]
    for n, ref in enumerate((own_ref, e_ref, o_ref)):
        for v in range(V):
            row = slice(3 * n + v, 3 * n + v + 1)
            lev_ref[row] = line(ref, 1, v)
            innov_ref[row] = line(ref, 2, v)
            weight = line(ref, 3, v)
            if n > 0:
                code = line(ref, 0, v)
                first = is_odd == (0 if n == 1 else 1)
                at_edge = jnp.where(first, code, 1023.0 - code) < 64.0
                there = at_edge & ((n == 1) | (where_ref[4] == 1))
                weight = jnp.where(there, weight, 0.0)
            weight_ref[row] = weight


def weights(where, own, even, odd):
    vmem = pl.BlockSpec(memory_space=pltpu.VMEM)
    return call(
        weights_kernel,
        (
            sds(V, 320, SLOTS, dtype=BF16),
            sds(2, V, 64, SLOTS, dtype=BF16),
            sds(9, SLOTS),
            sds(9, SLOTS),
            sds(9, SLOTS),
        ),
        ins=[pl.BlockSpec(memory_space=pltpu.SMEM), vmem, vmem, vmem],
        cost=5000000,
    )(where, own, even, odd)


def picker(lev_ref):
    level = lax.broadcasted_iota(jnp.int32, (128, SLOTS), 0).astype(F32)

    def pick(cells, weight, row):
        both = jnp.concatenate(halves(cells), axis=1)
        at_all = tn(both, weight)
        at_all = at_all[:128] + at_all[128:]
        hot = level == lev_ref[row : row + 1, :]
        return jnp.sum(jnp.where(hot, at_all, 0.0), axis=0, keepdims=True)

    return pick


def mine_kernel(where_ref, inc_ref, wown_ref, wnear_ref, lev_ref, out_ref):
    pick = picker(lev_ref)
    for v in range(V):
        out_ref[v : v + 1] = pick(inc_ref[v], wown_ref[v, :256], v)
        for n in range(2):
            cells = inc_ref[v, pl.ds(pl.multiple_of(where_ref[n], 32), 32)]
            row = 3 * n + 3 + v
            out_ref[row : row + 1] = pick(cells, wnear_ref[n, v, :32], row)


def mine_part(where, inc, wown, wnear, lev):
    return call(
        mine_kernel,
        sds(9, SLOTS),
        ins=[SMEM] + [VMEM] * 4,
        outs=VMEM,
    )(where, inc, wown, wnear, lev)


def values_kernel(mine_ref, e_ref, o_ref, wown_ref, wnear_ref, lev_ref, out_ref):
    pick = picker(lev_ref)

    def put(row, more):
        line = mine_ref[row : row + 1] + more
        for a in range(6):
            out_ref[6 * row + a : 6 * row + a + 1] = line[:, 128 * a : 128 * a + 128]

    for v in range(V):
        put(v, pick(jnp.concatenate([e_ref[v], o_ref[v]], axis=0), wown_ref[v, 256:], v))
        for n, ref in enumerate((e_ref, o_ref)):
            row = 3 * n + 3 + v
            put(row, pick(ref[v], wnear_ref[n, v, 32:], row))


def values(mine, even, odd, wown, wnear, lev):
    return call(
        values_kernel,
        sds(9 * SLOTS // 128, 128),
        ins=[VMEM] * 6,
        outs=VMEM,
    )(mine, even, odd, wown, wnear, lev)


def adjoint_kernel(where_ref, v0, v1, v2, v3, innov_ref, weight_ref, lev_ref, wown_ref, wnear_ref, x_ref, c_ref, first_ref, second_ref):
    level = lax.broadcasted_iota(jnp.int32, (128, SLOTS), 0).astype(F32)
    value = v0[...] + v1[...] + v2[...] + v3[...]

    def place(weight, row):
        line = jnp.concatenate([value[6 * row + a : 6 * row + a + 1] for a in range(6)], axis=1)
        weighted = weight_ref[row : row + 1] * (line - innov_ref[row : row + 1])
        hot = level == lev_ref[row : row + 1, :]
        spread = jnp.where(hot, weighted, 0.0)
        both = jnp.concatenate(halves(spread), axis=0)
        out = nt(weight, both)
        return out[:, :128] + out[:, 128:]

    adj = []
    for v in range(V):
        c_ref[v] = place(wown_ref[v, :256], v)
        for n in range(2):
            rows = pl.ds(pl.multiple_of(where_ref[n], 32), 32)
            c_ref[v, rows] = c_ref[v, rows] + place(wnear_ref[n, v, :32], 3 * n + 3 + v)
        adj.append(jnp.concatenate([c_ref[v, :64], c_ref[v, 192:]], axis=0))
    first_low = where_ref[7] == 1
    for k in range(first_ref.shape[0]):
        total = x_ref[k, 0].astype(F32) * adj[0]
        for v in range(1, V):
            total = total + x_ref[k, v].astype(F32) * adj[v]
        low, high = total[:64], total[64:]
        first_ref[k] = jnp.where(first_low, low, high)
        second_ref[k] = jnp.where(first_low, high, low)


def adjoint(where, vals, innov, weight, lev, wown, wnear, x):
    members = x.shape[0]
    return call(
        adjoint_kernel,
        (sds(V, 256, 128), sds(members, 64, 128), sds(members, 64, 128)),
        ins=[SMEM] + [VMEM] * 10,
        outs=(VMEM,) * 3,
    )(where, *vals, innov, weight, lev, wown, wnear, x)


def drop(smoothed, loc):
    high, low = halves(smoothed)
    return nn(high, loc) + nn(low, loc)


def back_kernel(alpha_ref, ens_ref, c_ref, smat_ref, loc_ref, out_ref, edge_ref):
    smat = smat_ref[...]
    loc = loc_ref[...]
    for k in range(GROUP):
        back = ens_ref[k, 0].astype(F32) * c_ref[0]
        for v in range(1, V):
            back = back + ens_ref[k, v].astype(F32) * c_ref[v]
        full = alpha_ref[k].astype(F32) + drop(smooth(smat, back), loc)
        out_ref[k] = full
        edge_ref[k, :64] = full[:64]
        edge_ref[k, 64:] = full[192:]


def back_part(alpha, ensemble, c, smat, loc):
    members = alpha.shape[0]
    return call(
        back_kernel,
        (sds(members, 256, 128), sds(members, 128, 128)),
        grid=(members // GROUP,),
        ins=[
            pl.BlockSpec((GROUP, 256, 128), lambda i: (i, 0, 0)),
            pl.BlockSpec((GROUP, V, 256, 128), lambda i: (i, 0, 0, 0)),
            pl.BlockSpec((V, 256, 128), lambda i: (0, 0, 0)),
            pl.BlockSpec((256, 256), lambda i: (0, 0)),
            pl.BlockSpec((128, 128), lambda i: (0, 0)),
        ],
        outs=(
            pl.BlockSpec((GROUP, 256, 128), lambda i: (i, 0, 0)),
            pl.BlockSpec((GROUP, 128, 128), lambda i: (i, 0, 0)),
        ),
    )(alpha, ensemble, c, smat, loc)


def last_kernel(first_ref, second_ref, edge_ref, hmat_ref, loc_ref, unused_ref, out_ref, held, sems):
    members = edge_ref.shape[0]
    hmat = hmat_ref[...]
    loc = loc_ref[...]
    copies = []
    for g in range(members // GROUP):
        for k in range(g * GROUP, (g + 1) * GROUP):
            halo = jnp.concatenate([first_ref[k], second_ref[k]], axis=0)
            full = edge_ref[k] + drop(smooth(hmat, halo), loc)
            held[k, 0] = full[:64]
            held[k, 1] = full[64:]
        group = pl.ds(g * GROUP, GROUP)
        for side in range(2):
            copies.append(
                pltpu.make_async_copy(held.at[group, side], out_ref.at[group, 3 * side], sems.at[g, side])
            )
            copies[-1].start()
    for copy in copies:
        copy.wait()


def last_part(first, second, edge, hmat, loc, out):
    members = edge.shape[0]
    return call(
        last_kernel,
        sds(members, 4, 64, 128),
        ins=[VMEM] * 5 + [ANY],
        outs=ANY,
        scratch=[pltpu.VMEM((members, 2, 64, 128), F32), pltpu.SemaphoreType.DMA((members // GROUP, 2))],
        aliases={5: 0},
    )(first, second, edge, hmat, loc, out)


def stencil(gap):
    gap = jnp.abs(gap)
    return jnp.where(gap == 0, 6.0, jnp.where(gap == 1, 4.0, jnp.where(gap == 2, 1.0, 0.0)))


def matrices(tile, tiles, first_high):
    def across(i, j):
        gap = stencil(i - j)
        return jnp.where((i == j) & ((i == 0) | (i == 31)), 5.0, gap)

    i = lax.broadcasted_iota(jnp.int32, (256, 256), 0)
    j = lax.broadcasted_iota(jnp.int32, (256, 256), 1)
    ri, rj = i // 32, j // 32
    ends = ((ri == 0) & (tile == 0)) | ((ri == 7) & (tile == tiles - 1))
    down = jnp.where((ri == rj) & ends, 5.0, stencil(ri - rj))
    smat = (down * across(i % 32, j % 32) * (1.0 / 256.0)).astype(BF16)
    i = lax.broadcasted_iota(jnp.int32, (128, 128), 0)
    j = lax.broadcasted_iota(jnp.int32, (128, 128), 1)
    ri = i // 32
    ri = jnp.where(ri < 2, ri, ri + 4)
    above = (j < 64) == first_high
    rj = jnp.where(above, 8, -2) + (j // 32) % 2
    there = (above & (tile < tiles - 1)) | (jnp.logical_not(above) & (tile > 0))
    hmat = jnp.where(there, stencil(ri - rj), 0.0) * across(i % 32, j % 32) * (1.0 / 256.0)
    return smat, hmat.astype(BF16)


def swap_even(x):
    return lax.ppermute(x, "tile", EVEN)


def swap_odd(x):
    return lax.ppermute(x, "tile", ODD)


def swap_first(x):
    return lax.ppermute(x, ("mem", "tile"), FIRST)


def swap_second(x):
    return lax.ppermute(x, ("mem", "tile"), SECOND)


def round_mem(mine):
    size = lax.axis_size("mem")
    return [mine] + [
        lax.ppermute(mine, "mem", [(i, (i + shift) % size) for i in range(size)]) for shift in range(1, size)
    ]


def on_device(alpha, ensemble, loc_vert, obs_col, obs_lev, obs_count, innovation, obs_weight):
    members = alpha.shape[0]
    tile = lax.axis_index("tile")
    tiles = lax.axis_size("tile")
    even = tile % 2 == 0
    first_low = (tile + lax.axis_index("mem") // (MEMS // 2)) % 2
    where = jnp.stack(
        [
            jnp.where(even, 7 * 32, 0),
            jnp.where(even, 0, 7 * 32),
            jnp.where(even, 8, -1),
            jnp.where(even, -1, 8),
            ((tile > 0) & (tile < tiles - 1)).astype(jnp.int32),
            tile % 2,
            tile,
            first_low,
        ]
    ).astype(jnp.int32)
    flat = alpha.reshape(members, 256, 128)
    flat_ens = ensemble.reshape(members, V, 256, 128)

    send_first, send_second, token = send_part(where, alpha.reshape(members, 4, 64, 128))
    first, second = swap_first(send_first), swap_second(send_second)
    inner, own_edge, x, smat, hmat, token = own_part(where, flat, flat_ens, loc_vert, token)
    own_obs = observations(obs_count, obs_col, obs_lev, innovation, obs_weight, token)
    even_obs = swap_even(own_obs)
    odd_obs = swap_odd(own_obs)

    inc, se, so = edge_part(where, first, second, own_edge, x, hmat, loc_vert, inner, even_obs, odd_obs)
    near_even, near_odd = swap_even(se), swap_odd(so)
    wown, wnear, lev, innov, weight = weights(where, own_obs, even_obs, odd_obs)
    mine = mine_part(where, inc, wown, wnear, lev)
    vals = round_mem(values(mine, near_even, near_odd, wown, wnear, lev))
    c, back_first, back_second = adjoint(where, vals, innov, weight, lev, wown, wnear, x)
    halo_first, halo_second = swap_first(back_first), swap_second(back_second)
    out, edge = back_part(flat, flat_ens, c, smat, loc_vert)
    out = last_part(halo_first, halo_second, edge, hmat, loc_vert, out.reshape(members, 4, 64, 128))
    return out.reshape(members, 8, 32, 128)


def solution(mesh):
    in_specs = (
        P("mem", "tile", None, None),
        P("mem", None, "tile", None, None),
        P(),
        P("tile", None),
        P("tile", None),
        P("tile"),
        P("tile", None),
        P("tile", None),
    )
    out_specs = P("mem", "tile", None, None)
    return jax.shard_map(
        on_device, mesh=mesh, in_specs=in_specs, out_specs=out_specs, check_vma=False
    )
```

time: 116 us -> 105 us (0.905)
  the two profiles are of different devices: /device:TPU:33 before, /device:TPU:32 now
where the time goes in v4:
time: 105 us
  waiting for transfers between devices  55.6 us (53%)
  starting transfers between devices  23.8 us (23%)
  Pallas kernels  20.2 us (19%)
  local copies, waits for them, and re-layouts  4.3 us (4%)
    ppermute x2, waiting for transfers between devices, swap_odd(): return lax.ppermute(x, 'tile', ODD)  25.3 us
    ppermute x2, waiting for transfers between devices, swap_first(): return lax.ppermute(x, ('mem', 'tile'), FIRST)  23.9 us
    ppermute x2, starting transfers between devices, swap_first(): return lax.ppermute(x, ('mem', 'tile'), FIRST)  17.7 us
    pallas_call x1, Pallas kernels, back_part(): call(back_kernel, (sds(members, 256, 128), sds(members, 128, 128)), grid=...  4.71 us
    unnamed x20, local copies, waits for them, and re-layouts  4.21 us
    ppermute x2, starting transfers between devices, swap_odd(): return lax.ppermute(x, 'tile', ODD)  3.9 us
    pallas_call x1, Pallas kernels, own_part(): call(own_kernel, (sds(V, 128, 128), sds(members, 128, 128), sds(members,...  3.79 us
    ppermute x3, waiting for transfers between devices, round_mem(): lax.ppermute(mine, 'mem', [(i, (i + shift) % size) for i in range(size)])  3.25 us
  transfers between devices with their start and end apart: 11, of which 9 were waited for; matrix products, arithmetic and copies ran while one was open for 0% of the time, Pallas kernels for 11%

profile of v4, /device:TPU:32, one launch (start us, length us, event | category | flops | bytes accessed | tf_op | source)
XLA Modules:
  0.0 104.7 jit_solution(16535584943637042399)
XLA Ops:
  0.0 0.1 stack.39.where_ref
  0.1 1.3 %copy-done.2 = bf16[20,8,32,128]{3,2,1,0:T(8,128)(2,1)S(1)} copy-done((bf16[20,8,32,128]{3,2,1,0:T(8,128)(2,1)S(1)}, bf16[20,8,32,128]{3,2,1,0:T(8,128)(2,1)}, u32[]{:S(2)}) %copy-start.2) | copy-done | bytes 1310744
  1.4 0.7 shard_map.82
  2.1 10.1 %collective-permute-start = (f32[20,64,128]{2,1,0:T(8,128)S(1)}, f32[20,64,128]{2,1,0:T(8,128)S(1)}, u32[]{:S(2)}, u32[]{:S(2)}) collective-permute-start(f32[20,64,128]{2,1,0:T(8,128)S(1)} %get-tuple-element.27), channel_id=1, source_target_pairs={{0,1},{1,0},{2,3},{3,2},{4,5},{5,4},{6,7},{7,6},{8,9},{9,8},{10,11... | collective-permute-start | bytes 1966088 | tf_op jit(solution)/shard_map/ppermute | solution.py:487
  12.9 2.1 %copy-done = bf16[20,3,8,32,128]{4,3,2,1,0:T(8,128)(2,1)S(1)} copy-done((bf16[20,3,8,32,128]{4,3,2,1,0:T(8,128)(2,1)S(1)}, bf16[20,3,8,32,128]{4,3,2,1,0:T(8,128)(2,1)}, u32[]{:S(2)}) %copy-start) | copy-done | bytes 3932184
  15.0 0.8 copy-done.4
  15.8 3.8 %shard_map.83 = (f32[3,128,128]{2,1,0:T(8,128)S(1)}, f32[20,128,128]{2,1,0:T(8,128)S(1)}, bf16[20,3,128,128]{3,2,1,0:T(8,128)(2,1)S(1)}, bf16[256,256]{1,0:T(8,1...) custom-call(s32[8]{0:T(128)S(1)} %stack.39.where_ref, bf16[20,256,128]{2,1,0:T(8,128)(2,1)S(1)} %bitcast.16, ...), custom_call_target="tpu_custom_call" | custom-call | flops 1000000 | bytes 1000000 | tf_op jit(solution)/shard_map/pallas_call | solution.py:130
  19.6 0.3 shard_map.84.own_ref
  19.9 2.1 %collective-permute-start.3 = (f32[72,128]{1,0:T(8,128)S(1)}, f32[72,128]{1,0:T(8,128)S(1)}, u32[]{:S(2)}, u32[]{:S(2)}) collective-permute-start(f32[72,128]{1,0:T(8,128)S(1)} %shard_map.84.own_ref), channel_id=1, source_target_pairs={{1,2},{2,1},{3,4},{4,3},{5,6},{6,5},{7,8},{8,7},{9,10},{10,9},{11,... | collective-permute-start | bytes 110600 | tf_op jit(solution)/shard_map/ppermute | solution.py:483
  22.0 1.0 collective-permute-start.2
  23.1 19.5 %collective-permute-done.3.after_odd.o_ref = f32[72,128]{1,0:T(8,128)S(1)} collective-permute-done((f32[72,128]{1,0:T(8,128)S(1)}, f32[72,128]{1,0:T(8,128)S(1)}, u32[]{:S(2)}, u32[]{:S(2)}) %collective-permute-start.3) | collective-permute-done | bytes 36896 | tf_op jit(solution)/shard_map/ppermute | solution.py:483
  42.6 1.6 %collective-permute-done.2.after_even.e_ref = f32[72,128]{1,0:T(8,128)S(1)} collective-permute-done((f32[72,128]{1,0:T(8,128)S(1)}, f32[72,128]{1,0:T(8,128)S(1)}, u32[]{:S(2)}, u32[]{:S(2)}) %collective-permute-start.2) | collective-permute-done | bytes 36896 | tf_op jit(solution)/shard_map/ppermute | solution.py:479
  44.2 2.9 %shard_map.85 = (f32[3,256,128]{2,1,0:T(8,128)S(1)}, f32[3,32,128]{2,1,0:T(8,128)S(1)}, f32[3,32,128]{2,1,0:T(8,128)S(1)}) custom-call(s32[8]{0:T(128)S(1)} %stack.39.where_ref, f32[20,64,128]{2,1,0:T(8,128)S(1)} %collective-permute-done.first_ref, f32[20,64,128]{2,1,0:T(8,128)S(1)} %collective-permute-done.1.second_ref, ...), custom_call_target="tpu_custom_call" | custom-call | flops 1000000 | bytes 1000000 | tf_op jit(solution)/shard_map/pallas_call | solution.py:214
  47.1 0.1 collective-permute-start.4
  47.2 1.8 %collective-permute-start.5 = (f32[3,32,128]{2,1,0:T(8,128)S(1)}, f32[3,32,128]{2,1,0:T(8,128)S(1)}, u32[]{:S(2)}, u32[]{:S(2)}) collective-permute-start(f32[3,32,128]{2,1,0:T(8,128)S(1)} %get-tuple-element.40), channel_id=1, source_target_pairs={{1,2},{2,1},{3,4},{4,3},{5,6},{6,5},{7,8},{8,7},{9,10},{10,9},{11,... | collective-permute-start | bytes 147464 | tf_op jit(solution)/shard_map/ppermute | solution.py:483
  49.0 1.1 %shard_map.86 = (bf16[3,320,768]{2,1,0:T(8,128)(2,1)S(1)}, bf16[2,3,64,768]{3,2,1,0:T(8,128)(2,1)S(1)}, f32[9,768]{1,0:T(8,128)S(1)}, f32[9,768]{1,0:T(8,128)S(1)}, f32[9,768]{1,0:T(8,128)S(1)}) custom-call(s32[8]{0:T(128)S(1)} %stack.39.where_ref, f32[72,128]{1,0:T(8,128)S(1)} %shard_map.84.own_ref, f32[72,128]{1,0:T(8,128)S(1)} %collective-permute-done.2.after_even.e_ref, ...), custom_call_target="tpu_custom_call" | custom-call | flops 5000000 | bytes 5000000 | tf_op jit(solution)/shard_map/pallas_call | solution.py:270
  50.2 1.7 %shard_map.87.mine_ref = f32[9,768]{1,0:T(8,128)S(1)} custom-call(s32[8]{0:T(128)S(1)} %stack.39.where_ref, f32[3,256,128]{2,1,0:T(8,128)S(1)} %get-tuple-element.35.inc_ref, bf16[3,320,768]{2,1,0:T(8,128)(2,1)S(1)} %get-tuple-element.36.wown_ref, bf16[2,3,64,768]{3,2,1,0:T(8,128)(2,1)S(1)} %get-tuple-element.37.wnear_ref, ...), custom_call_target="tpu_custom_call" | custom-call | flops 1000000 | bytes 1000000 | tf_op jit(solution)/shard_map/pallas_call | solution.py:308
  51.8 0.4 collective-permute-done.4.e_ref
  52.2 5.8 %collective-permute-done.5.o_ref = f32[3,32,128]{2,1,0:T(8,128)S(1)} collective-permute-done((f32[3,32,128]{2,1,0:T(8,128)S(1)}, f32[3,32,128]{2,1,0:T(8,128)S(1)}, u32[]{:S(2)}, u32[]{:S(2)}) %collective-permute-start.5) | collective-permute-done | bytes 49184 | tf_op jit(solution)/shard_map/ppermute | solution.py:483
  58.0 1.1 %shard_map.88.v0 = f32[54,128]{1,0:T(8,128)S(1)} custom-call(f32[9,768]{1,0:T(8,128)S(1)} %shard_map.87.mine_ref, f32[3,32,128]{2,1,0:T(8,128)S(1)} %collective-permute-done.4.e_ref, f32[3,32,128]{2,1,0:T(8,128)S(1)} %collective-permute-done.5.o_ref, bf16[3,320,768]{2,1,0:T(8,128)(2,1)S(1)} %get-tuple-element.36.wown_ref, ...), custom_call_target="tpu_custom_call" | custom-call | flops 1000000 | bytes 1000000 | tf_op jit(solution)/shard_map/pallas_call | solution.py:332
  59.1 0.1 collective-permute-start.8
  59.2 0.9 collective-permute-start.7
  60.1 0.1 collective-permute-start.6
  60.3 0.5 collective-permute-done.8.v3
  60.8 2.5 %collective-permute-done.7.v2 = f32[54,128]{1,0:T(8,128)S(1)} collective-permute-done((f32[54,128]{1,0:T(8,128)S(1)}, f32[54,128]{1,0:T(8,128)S(1)}, u32[]{:S(2)}, u32[]{:S(2)}) %collective-permute-start.7) | collective-permute-done | bytes 27680 | tf_op jit(solution)/shard_map/ppermute | solution.py:497
  63.3 0.2 collective-permute-done.6.v1
  63.5 2.1 %shard_map.89 = (f32[3,256,128]{2,1,0:T(8,128)S(1)}, f32[20,64,128]{2,1,0:T(8,128)S(1)}, f32[20,64,128]{2,1,0:T(8,128)S(1)}) custom-call(s32[8]{0:T(128)S(1)} %stack.39.where_ref, f32[54,128]{1,0:T(8,128)S(1)} %shard_map.88.v0, f32[54,128]{1,0:T(8,128)S(1)} %collective-permute-done.6.v1, f32[54,128]{1,0:T(8,128)S(1)} %collective-permute-done.7.v2, ...), custom_call_target="tpu_custom_call" | custom-call | flops 1000000 | bytes 1000000 | tf_op jit(solution)/shard_map/pallas_call | solution.py:372
  65.6 7.6 %collective-permute-start.9 = (f32[20,64,128]{2,1,0:T(8,128)S(1)}, f32[20,64,128]{2,1,0:T(8,128)S(1)}, u32[]{:S(2)}, u32[]{:S(2)}) collective-permute-start(f32[20,64,128]{2,1,0:T(8,128)S(1)} %get-tuple-element.43), channel_id=1, source_target_pairs={{0,1},{1,0},{2,3},{3,2},{4,5},{5,4},{6,7},{7,6},{8,9},{9,8},{10,11... | collective-permute-start | bytes 1966088 | tf_op jit(solution)/shard_map/ppermute | solution.py:487
  73.2 4.7 %shard_map.90 = (f32[20,256,128]{2,1,0:T(8,128)}, f32[20,128,128]{2,1,0:T(8,128)S(1)}) custom-call(bf16[20,256,128]{2,1,0:T(8,128)(2,1)S(1)} %bitcast.17, bf16[20,3,256,128]{3,2,1,0:T(8,128)(2,1)S(1)} %bitcast.14, f32[3,256,128]{2,1,0:T(8,128)S(1)} %get-tuple-element.45.c_ref, bf16[256,256]{1,0:T(8,128)(2,1)S(1)} %get-tuple-element.46.smat_ref, ...), custom_call_target="tpu_custom_call" | custom-call | flops 1000000 | bytes 1000000 | tf_op jit(solution)/shard_map/pallas_call | solution.py:400
  77.9 23.9 %collective-permute-done.9.first_ref = f32[20,64,128]{2,1,0:T(8,128)S(1)} collective-permute-done((f32[20,64,128]{2,1,0:T(8,128)S(1)}, f32[20,64,128]{2,1,0:T(8,128)S(1)}, u32[]{:S(2)}, u32[]{:S(2)}) %collective-permute-start.9) | collective-permute-done | bytes 655392 | tf_op jit(solution)/shard_map/ppermute | solution.py:487
  101.8 1.1 %collective-permute-done.10.second_ref = f32[20,64,128]{2,1,0:T(8,128)S(1)} collective-permute-done((f32[20,64,128]{2,1,0:T(8,128)S(1)}, f32[20,64,128]{2,1,0:T(8,128)S(1)}, u32[]{:S(2)}, u32[]{:S(2)}) %collective-permute-start.10) | collective-permute-done | bytes 655392 | tf_op jit(solution)/shard_map/ppermute | solution.py:491
  103.0 1.7 %shard_map.91 = f32[20,4,64,128]{3,2,1,0:T(8,128)} custom-call(f32[20,64,128]{2,1,0:T(8,128)S(1)} %collective-permute-done.9.first_ref, f32[20,64,128]{2,1,0:T(8,128)S(1)} %collective-permute-done.10.second_ref, f32[20,128,128]{2,1,0:T(8,128)S(1)} %get-tuple-element.47.edge_ref, ...), custom_call_target="tpu_custom_call", output_to_operand_aliasing={{}: (5, {})} | custom-call | flops 1000000 | bytes 1000000 | tf_op jit(solution)/shard_map/pallas_call | solution.py:441
  (21 shorter events, 0.0 us)
Async XLA Ops:
  0.1 1.3 %copy-start.2 = (bf16[20,8,32,128]{3,2,1,0:T(8,128)(2,1)S(1)}, bf16[20,8,32,128]{3,2,1,0:T(8,128)(2,1)}, u32[]{:S(2)}) copy-start(bf16[20,8,32,128]{3,2,1,0:T(8,128)(2,1)} %param.8) | copy-start | bytes 3932164
  2.1 42.1 %collective-permute-start = (f32[20,64,128]{2,1,0:T(8,128)S(1)}, f32[20,64,128]{2,1,0:T(8,128)S(1)}, u32[]{:S(2)}, u32[]{:S(2)}) collective-permute-start(f32[20,64,128]{2,1,0:T(8,128)S(1)} %get-tuple-element.27), channel_id=1, source_target_pairs={{0,1},{1,0},{2,3},{3,2},{4,5},{5,4},{6,7},{7,6},{8,9},{9,8},{10,11... | collective-permute-start | bytes 1966088 | tf_op jit(solution)/shard_map/ppermute | solution.py:487
  12.2 32.0 %collective-permute-start.1 = (f32[20,64,128]{2,1,0:T(8,128)S(1)}, f32[20,64,128]{2,1,0:T(8,128)S(1)}, u32[]{:S(2)}, u32[]{:S(2)}) collective-permute-start(f32[20,64,128]{2,1,0:T(8,128)S(1)} %get-tuple-element.28), channel_id=1, source_target_pairs={{1,2},{2,1},{3,4},{4,3},{5,6},{6,5},{7,8},{8,7},{9,10},{10,9},{11,... | collective-permute-start | bytes 1966088 | tf_op jit(solution)/shard_map/ppermute | solution.py:491
  12.9 2.1 %copy-start = (bf16[20,3,8,32,128]{4,3,2,1,0:T(8,128)(2,1)S(1)}, bf16[20,3,8,32,128]{4,3,2,1,0:T(8,128)(2,1)}, u32[]{:S(2)}) copy-start(bf16[20,3,8,32,128]{4,3,2,1,0:T(8,128)(2,1)} %param.9) | copy-start | bytes 11796484
  15.0 0.8 copy-start.4
  15.8 3.8 %copy-start.6 = (s32[1,2048]{1,0:T(1,128)S(1)}, s32[1,2048]{1,0:T(1,128)}, u32[]{:S(2)}) copy-start(s32[1,2048]{1,0:T(1,128)} %col_ref.1) | copy-start | bytes 24580
  15.8 3.8 %copy-start.7 = (s32[1,2048]{1,0:T(1,128)S(1)}, s32[1,2048]{1,0:T(1,128)}, u32[]{:S(2)}) copy-start(s32[1,2048]{1,0:T(1,128)} %lev_ref.1) | copy-start | bytes 24580
  15.8 3.8 %copy-start.8 = (f32[1,2048]{1,0:T(1,128)S(1)}, f32[1,2048]{1,0:T(1,128)}, u32[]{:S(2)}) copy-start(f32[1,2048]{1,0:T(1,128)} %innov_ref.1) | copy-start | bytes 24580
  15.8 3.8 %copy-start.9 = (f32[1,2048]{1,0:T(1,128)S(1)}, f32[1,2048]{1,0:T(1,128)}, u32[]{:S(2)}) copy-start(f32[1,2048]{1,0:T(1,128)} %weight_ref.1) | copy-start | bytes 24580
  15.8 28.4 %copy-start.5 = (bf16[128,128]{1,0:T(8,128)(2,1)S(1)}, bf16[128,128]{1,0:T(8,128)(2,1)}, u32[]{:S(2)}) copy-start(bf16[128,128]{1,0:T(8,128)(2,1)} %loc_ref.7) | copy-start | bytes 98308
  19.9 22.7 %collective-permute-start.3 = (f32[72,128]{1,0:T(8,128)S(1)}, f32[72,128]{1,0:T(8,128)S(1)}, u32[]{:S(2)}, u32[]{:S(2)}) collective-permute-start(f32[72,128]{1,0:T(8,128)S(1)} %shard_map.84.own_ref), channel_id=1, source_target_pairs={{1,2},{2,1},{3,4},{4,3},{5,6},{6,5},{7,8},{8,7},{9,10},{10,9},{11,... | collective-permute-start | bytes 110600 | tf_op jit(solution)/shard_map/ppermute | solution.py:483
  22.0 22.2 %collective-permute-start.2 = (f32[72,128]{1,0:T(8,128)S(1)}, f32[72,128]{1,0:T(8,128)S(1)}, u32[]{:S(2)}, u32[]{:S(2)}) collective-permute-start(f32[72,128]{1,0:T(8,128)S(1)} %shard_map.84.own_ref), channel_id=1, source_target_pairs={{0,1},{1,0},{2,3},{3,2},{4,5},{5,4},{6,7},{7,6},{8,9},{9,8},{10,11... | collective-permute-start | bytes 110600 | tf_op jit(solution)/shard_map/ppermute | solution.py:479
  47.1 5.1 %collective-permute-start.4 = (f32[3,32,128]{2,1,0:T(8,128)S(1)}, f32[3,32,128]{2,1,0:T(8,128)S(1)}, u32[]{:S(2)}, u32[]{:S(2)}) collective-permute-start(f32[3,32,128]{2,1,0:T(8,128)S(1)} %get-tuple-element.39), channel_id=1, source_target_pairs={{0,1},{1,0},{2,3},{3,2},{4,5},{5,4},{6,7},{7,6},{8,9},{9,8},{10,11... | collective-permute-start | bytes 147464 | tf_op jit(solution)/shard_map/ppermute | solution.py:479
  47.2 10.8 %collective-permute-start.5 = (f32[3,32,128]{2,1,0:T(8,128)S(1)}, f32[3,32,128]{2,1,0:T(8,128)S(1)}, u32[]{:S(2)}, u32[]{:S(2)}) collective-permute-start(f32[3,32,128]{2,1,0:T(8,128)S(1)} %get-tuple-element.40), channel_id=1, source_target_pairs={{1,2},{2,1},{3,4},{4,3},{5,6},{6,5},{7,8},{8,7},{9,10},{10,9},{11,... | collective-permute-start | bytes 147464 | tf_op jit(solution)/shard_map/ppermute | solution.py:483
  58.0 15.2 %copy-start.3 = (bf16[20,8,32,128]{3,2,1,0:T(8,128)(2,1)S(1)}, bf16[20,8,32,128]{3,2,1,0:T(8,128)(2,1)}, u32[]{:S(2)}) copy-start(bf16[20,8,32,128]{3,2,1,0:T(8,128)(2,1)} %param.8) | copy-start | bytes 3932164
  59.1 1.6 %collective-permute-start.8 = (f32[54,128]{1,0:T(8,128)S(1)}, f32[54,128]{1,0:T(8,128)S(1)}, u32[]{:S(2)}, u32[]{:S(2)}) collective-permute-start(f32[54,128]{1,0:T(8,128)S(1)} %shard_map.88.v0), channel_id=1, source_target_pairs={{0,192},{64,0},{128,64},{192,128},{1,193},{65,1},{129,65},{193,129... | collective-permute-start | bytes 82952 | tf_op jit(solution)/shard_map/ppermute | solution.py:497
  59.2 4.0 %collective-permute-start.7 = (f32[54,128]{1,0:T(8,128)S(1)}, f32[54,128]{1,0:T(8,128)S(1)}, u32[]{:S(2)}, u32[]{:S(2)}) collective-permute-start(f32[54,128]{1,0:T(8,128)S(1)} %shard_map.88.v0), channel_id=1, source_target_pairs={{0,128},{64,192},{128,0},{192,64},{1,129},{65,193},{129,1},{193,65... | collective-permute-start | bytes 82952 | tf_op jit(solution)/shard_map/ppermute | solution.py:497
  60.1 3.4 %collective-permute-start.6 = (f32[54,128]{1,0:T(8,128)S(1)}, f32[54,128]{1,0:T(8,128)S(1)}, u32[]{:S(2)}, u32[]{:S(2)}) collective-permute-start(f32[54,128]{1,0:T(8,128)S(1)} %shard_map.88.v0), channel_id=1, source_target_pairs={{0,64},{64,128},{128,192},{192,0},{1,65},{65,129},{129,193},{193,1... | collective-permute-start | bytes 82952 | tf_op jit(solution)/shard_map/ppermute | solution.py:497
  63.5 9.7 %copy-start.1 = (bf16[20,3,8,32,128]{4,3,2,1,0:T(8,128)(2,1)S(1)}, bf16[20,3,8,32,128]{4,3,2,1,0:T(8,128)(2,1)}, u32[]{:S(2)}) copy-start(bf16[20,3,8,32,128]{4,3,2,1,0:T(8,128)(2,1)} %param.9) | copy-start | bytes 11796484
  65.6 36.2 %collective-permute-start.9 = (f32[20,64,128]{2,1,0:T(8,128)S(1)}, f32[20,64,128]{2,1,0:T(8,128)S(1)}, u32[]{:S(2)}, u32[]{:S(2)}) collective-permute-start(f32[20,64,128]{2,1,0:T(8,128)S(1)} %get-tuple-element.43), channel_id=1, source_target_pairs={{0,1},{1,0},{2,3},{3,2},{4,5},{5,4},{6,7},{7,6},{8,9},{9,8},{10,11... | collective-permute-start | bytes 1966088 | tf_op jit(solution)/shard_map/ppermute | solution.py:487
  73.2 29.8 %collective-permute-start.10 = (f32[20,64,128]{2,1,0:T(8,128)S(1)}, f32[20,64,128]{2,1,0:T(8,128)S(1)}, u32[]{:S(2)}, u32[]{:S(2)}) collective-permute-start(f32[20,64,128]{2,1,0:T(8,128)S(1)} %get-tuple-element.44), channel_id=1, source_target_pairs={{1,2},{2,1},{3,4},{4,3},{5,6},{6,5},{7,8},{8,7},{9,10},{10,9},{11,... | collective-permute-start | bytes 1966088 | tf_op jit(solution)/shard_map/ppermute | solution.py:491

commit v5 on v4

--- a/solution.py
+++ b/solution.py
@@ -1,3 +1,5 @@
+import functools
+
 import jax
 import jax.numpy as jnp
 from jax import lax
@@ -10,14 +12,15 @@
 BF16 = jnp.bfloat16
 SLOTS = 768
 GROUP = 4
+HEAD = 12
 
 TILES = 64
 EVEN = [(i, i ^ 1) for i in range(TILES)]
 ODD = [(i, ((i - 1) ^ 1) + 1) for i in range(1, TILES - 1)] + [(0, TILES - 1), (TILES - 1, 0)]
 
 MEMS = 4
-FIRST = [(TILES * m + a, TILES * m + b) for m in range(MEMS) for a, b in (EVEN if m < MEMS // 2 else ODD)]
-SECOND = [(TILES * m + a, TILES * m + b) for m in range(MEMS) for a, b in (ODD if m < MEMS // 2 else EVEN)]
+FIRST = [(TILES * m + a, TILES * m + b) for m in range(MEMS) for a, b in (ODD if m % 2 else EVEN)]
+SECOND = [(TILES * m + a, TILES * m + b) for m in range(MEMS) for a, b in (EVEN if m % 2 else ODD)]
 
 
 def nn(a, b):
@@ -77,7 +80,8 @@
 
 
 def send_kernel(where_ref, quarters_ref, first_ref, second_ref, token_ref, edges, sems):
-    copies = [pltpu.make_async_copy(quarters_ref.at[:, 3 * n], edges.at[n], sems.at[n]) for n in range(2)]
+    head = pl.ds(0, HEAD)
+    copies = [pltpu.make_async_copy(quarters_ref.at[head, 3 * n], edges.at[n], sems.at[n]) for n in range(2)]
     for copy in copies:
         copy.start()
     token_ref[...] = jnp.zeros_like(token_ref)
@@ -89,7 +93,7 @@
 
 
 def send_part(where, quarters):
-    members = quarters.shape[0]
+    members = HEAD
     return call(
         send_kernel,
         (sds(members, 64, 128), sds(members, 64, 128), sds(8, 128)),
@@ -99,7 +103,7 @@
     )(where, quarters)
 
 
-def own_kernel(where_ref, alpha_ref, ens_ref, loc_ref, after_ref, inner_ref, edge_ref, x_ref, smat_ref, hmat_ref, token_ref):
+def own_kernel(where_ref, alpha_ref, ens_ref, loc_ref, after_ref, inner_ref, edge_ref, x_ref, smat_ref, hmat_ref, token_ref, first_ref, second_ref):
     @pl.when(pl.program_id(0) == 0)
     def _():
         inner_ref[...] = jnp.zeros_like(inner_ref)
@@ -123,10 +127,19 @@
     for v in range(V):
         inner_ref[v] = total[v]
 
+    @pl.when(pl.program_id(0) >= HEAD // GROUP)
+    def _():
+        low = where_ref[7] == 1
+        for k in range(GROUP):
+            rows = [alpha_ref[k, :64].astype(F32), alpha_ref[k, 192:].astype(F32)]
+            first_ref[k] = jnp.where(low, rows[0], rows[1])
+            second_ref[k] = jnp.where(low, rows[1], rows[0])
+
 
 def own_part(where, alpha, ensemble, loc, after):
     members = alpha.shape[0]
     whole = lambda *shape: pl.BlockSpec(shape, lambda i: (0,) * len(shape))
+    rest = pl.BlockSpec((GROUP, 64, 128), lambda i: (jnp.maximum(i - HEAD // GROUP, 0), 0, 0))
     return call(
         own_kernel,
         (
@@ -136,6 +149,8 @@
             sds(256, 256, dtype=BF16),
             sds(128, 128, dtype=BF16),
             sds(8, 128),
+            sds(members - HEAD, 64, 128),
+            sds(members - HEAD, 64, 128),
         ),
         grid=(members // GROUP,),
         ins=[
@@ -152,6 +167,8 @@
             whole(256, 256),
             whole(128, 128),
             whole(8, 128),
+            rest,
+            rest,
         ),
     )(where, alpha, ensemble, loc, after)
 
@@ -193,37 +210,56 @@
     )(count, col, lev, innov, weight, after)
 
 
-def edge_kernel(where_ref, first_ref, second_ref, own_ref, x_ref, hmat_ref, loc_ref, inner_ref, after_even, after_odd, inc_ref, se_ref, so_ref):
+def edge_terms(first_ref, second_ref, own_ref, x_ref, hmat_ref, loc_ref, start, total):
     hmat = hmat_ref[...]
     loc = loc_ref[...]
-    total = [jnp.zeros((128, 128), F32) for v in range(V)]
-    for k in range(own_ref.shape[0]):
+    for k in range(first_ref.shape[0]):
         halo = jnp.concatenate([first_ref[k].astype(BF16), second_ref[k].astype(BF16)], axis=0)
-        lifted = (own_ref[k] + lift(nn(hmat, halo), loc)).astype(BF16).astype(F32)
+        lifted = (own_ref[start + k] + lift(nn(hmat, halo), loc)).astype(BF16).astype(F32)
         for v in range(V):
-            total[v] = total[v] + x_ref[k, v].astype(F32) * lifted
+            total[v] = total[v] + x_ref[start + k, v].astype(F32) * lifted
+    return total
+
+
+def head_kernel(first_ref, second_ref, own_ref, x_ref, hmat_ref, loc_ref, total_ref):
+    zeros = [jnp.zeros((128, 128), F32) for v in range(V)]
+    total = edge_terms(first_ref, second_ref, own_ref, x_ref, hmat_ref, loc_ref, 0, zeros)
+    for v in range(V):
+        total_ref[v] = total[v]
+
+
+def head_part(first, second, own, x, hmat, loc):
+    return call(head_kernel, sds(V, 128, 128), ins=[VMEM] * 6, outs=VMEM)(first, second, own, x, hmat, loc)
+
+
+def edge_kernel(where_ref, first_ref, second_ref, own_ref, x_ref, hmat_ref, loc_ref, inner_ref, head_ref, after_obs, inc_ref, keep_ref, give_ref):
+    total = [head_ref[v] for v in range(V)]
+    total = edge_terms(first_ref, second_ref, own_ref, x_ref, hmat_ref, loc_ref, HEAD, total)
     for v in range(V):
         inc_ref[v, :64] = total[v][:64]
         inc_ref[v, 64:192] = inner_ref[v]
         inc_ref[v, 192:] = total[v][64:]
-        for n, ref in enumerate((se_ref, so_ref)):
-            ref[v] = inc_ref[v, pl.ds(pl.multiple_of(where_ref[n], 32), 32)]
-
-
-def edge_part(where, first, second, own, x, hmat, loc, inner, *after):
+        keep_ref[v] = inc_ref[v, pl.ds(pl.multiple_of(where_ref[8], 32), 32)]
+        give_ref[v] = inc_ref[v, pl.ds(pl.multiple_of(where_ref[9], 32), 32)]
+
+
+def edge_part(where, first, second, own, x, hmat, loc, inner, head, after):
     return call(
         edge_kernel,
         (sds(V, 256, 128), sds(V, 32, 128), sds(V, 32, 128)),
         ins=[SMEM] + [VMEM] * 9,
         outs=(VMEM,) * 3,
-    )(where, first, second, own, x, hmat, loc, inner, *after)
+    )(where, first, second, own, x, hmat, loc, inner, head, after)
 
 
 def tent(distance):
     return jnp.maximum(1.0 - jnp.abs(distance), 0.0)
 
 
-def weights_kernel(where_ref, own_ref, e_ref, o_ref, wown_ref, wnear_ref, lev_ref, innov_ref, weight_ref):
+def weights_kernel(where_ref, own_ref, here_ref, there_ref, wown_ref, wnear_ref, lev_ref, innov_ref, weight_ref, e_ref, o_ref):
+    core_0 = where_ref[10] == 0
+    e_ref[...] = jnp.where(core_0, here_ref[...], there_ref[...])
+    o_ref[...] = jnp.where(core_0, there_ref[...], here_ref[...])
     even_row = where_ref[2].astype(F32)
     odd_row = where_ref[3].astype(F32)
     odd_there = where_ref[4].astype(F32)
@@ -265,8 +301,7 @@
             weight_ref[row] = weight
 
 
-def weights(where, own, even, odd):
-    vmem = pl.BlockSpec(memory_space=pltpu.VMEM)
+def weights(where, own, here, there):
     return call(
         weights_kernel,
         (
@@ -276,9 +311,9 @@
             sds(9, SLOTS),
             sds(9, SLOTS),
         ),
-        ins=[pl.BlockSpec(memory_space=pltpu.SMEM), vmem, vmem, vmem],
-        cost=5000000,
-    )(where, own, even, odd)
+        ins=[SMEM, VMEM, VMEM, VMEM],
+        scratch=[pltpu.VMEM(own.shape, F32), pltpu.VMEM(own.shape, F32)],
+    )(where, own, here, there)
 
 
 def picker(lev_ref):
@@ -288,7 +323,7 @@
         both = jnp.concatenate(halves(cells), axis=1)
         at_all = tn(both, weight)
         at_all = at_all[:128] + at_all[128:]
-        hot = level == lev_ref[row : row + 1, :]
+        hot = level == lev_ref[pl.ds(row, 1), :]
         return jnp.sum(jnp.where(hot, at_all, 0.0), axis=0, keepdims=True)
 
     return pick
@@ -313,28 +348,32 @@
     )(where, inc, wown, wnear, lev)
 
 
-def values_kernel(mine_ref, e_ref, o_ref, wown_ref, wnear_ref, lev_ref, out_ref):
+def values_kernel(where_ref, mine_ref, near_ref, wown_ref, wnear_ref, lev_ref, out_ref):
     pick = picker(lev_ref)
-
-    def put(row, more):
-        line = mine_ref[row : row + 1] + more
+    core = where_ref[10]
+
+    def put(row, line):
         for a in range(6):
-            out_ref[6 * row + a : 6 * row + a + 1] = line[:, 128 * a : 128 * a + 128]
-
-    for v in range(V):
-        put(v, pick(jnp.concatenate([e_ref[v], o_ref[v]], axis=0), wown_ref[v, 256:], v))
-        for n, ref in enumerate((e_ref, o_ref)):
+            out_ref[pl.ds(6 * row + a, 1)] = line[:, 128 * a : 128 * a + 128]
+
+    for v in range(V):
+        for n in range(2):
             row = 3 * n + 3 + v
-            put(row, pick(ref[v], wnear_ref[n, v, 32:], row))
-
-
-def values(mine, even, odd, wown, wnear, lev):
+            put(row, mine_ref[row : row + 1])
+    for v in range(V):
+        halo = pl.ds(pl.multiple_of(256 + 32 * core, 32), 32)
+        put(v, mine_ref[v : v + 1] + pick(near_ref[v], wown_ref[v, halo], v))
+        row = 3 * core + 3 + v
+        put(row, mine_ref[pl.ds(row, 1)] + pick(near_ref[v], wnear_ref[core, v, 32:], row))
+
+
+def values(where, mine, near, wown, wnear, lev):
     return call(
         values_kernel,
         sds(9 * SLOTS // 128, 128),
-        ins=[VMEM] * 6,
+        ins=[SMEM] + [VMEM] * 5,
         outs=VMEM,
-    )(mine, even, odd, wown, wnear, lev)
+    )(where, mine, near, wown, wnear, lev)
 
 
 def adjoint_kernel(where_ref, v0, v1, v2, v3, innov_ref, weight_ref, lev_ref, wown_ref, wnear_ref, x_ref, c_ref, first_ref, second_ref):
@@ -368,7 +407,7 @@
 
 
 def adjoint(where, vals, innov, weight, lev, wown, wnear, x):
-    members = x.shape[0]
+    members = HEAD
     return call(
         adjoint_kernel,
         (sds(V, 256, 128), sds(members, 64, 128), sds(members, 64, 128)),
@@ -382,26 +421,36 @@
     return nn(high, loc) + nn(low, loc)
 
 
-def back_kernel(alpha_ref, ens_ref, c_ref, smat_ref, loc_ref, out_ref, edge_ref):
+def back_kernel(where_ref, alpha_ref, ens_ref, c_ref, smat_ref, loc_ref, out_ref, edge_ref, first_ref, second_ref):
+    low = where_ref[7] == 1
     smat = smat_ref[...]
     loc = loc_ref[...]
     for k in range(GROUP):
         back = ens_ref[k, 0].astype(F32) * c_ref[0]
         for v in range(1, V):
             back = back + ens_ref[k, v].astype(F32) * c_ref[v]
+        first_ref[k] = jnp.where(low, back[:64], back[192:])
+        second_ref[k] = jnp.where(low, back[192:], back[:64])
         full = alpha_ref[k].astype(F32) + drop(smooth(smat, back), loc)
         out_ref[k] = full
         edge_ref[k, :64] = full[:64]
         edge_ref[k, 64:] = full[192:]
 
 
-def back_part(alpha, ensemble, c, smat, loc):
+def back_part(where, alpha, ensemble, c, smat, loc):
     members = alpha.shape[0]
+    rest = pl.BlockSpec((GROUP, 64, 128), lambda i: (jnp.maximum(i - HEAD // GROUP, 0), 0, 0))
     return call(
         back_kernel,
-        (sds(members, 256, 128), sds(members, 128, 128)),
+        (
+            sds(members, 256, 128),
+            sds(members, 128, 128),
+            sds(members - HEAD, 64, 128),
+            sds(members - HEAD, 64, 128),
+        ),
         grid=(members // GROUP,),
         ins=[
+            SMEM,
             pl.BlockSpec((GROUP, 256, 128), lambda i: (i, 0, 0)),
             pl.BlockSpec((GROUP, V, 256, 128), lambda i: (i, 0, 0, 0)),
             pl.BlockSpec((V, 256, 128), lambda i: (0, 0, 0)),
@@ -411,39 +460,40 @@
         outs=(
             pl.BlockSpec((GROUP, 256, 128), lambda i: (i, 0, 0)),
             pl.BlockSpec((GROUP, 128, 128), lambda i: (i, 0, 0)),
+            rest,
+            rest,
         ),
-    )(alpha, ensemble, c, smat, loc)
-
-
-def last_kernel(first_ref, second_ref, edge_ref, hmat_ref, loc_ref, unused_ref, out_ref, held, sems):
-    members = edge_ref.shape[0]
+    )(where, alpha, ensemble, c, smat, loc)
+
+
+def last_kernel(start, first_ref, second_ref, edge_ref, hmat_ref, loc_ref, unused_ref, out_ref, held, sems):
     hmat = hmat_ref[...]
     loc = loc_ref[...]
     copies = []
-    for g in range(members // GROUP):
+    for g in range(first_ref.shape[0] // GROUP):
         for k in range(g * GROUP, (g + 1) * GROUP):
             halo = jnp.concatenate([first_ref[k], second_ref[k]], axis=0)
-            full = edge_ref[k] + drop(smooth(hmat, halo), loc)
+            full = edge_ref[start + k] + drop(smooth(hmat, halo), loc)
             held[k, 0] = full[:64]
             held[k, 1] = full[64:]
-        group = pl.ds(g * GROUP, GROUP)
+        here, there = pl.ds(g * GROUP, GROUP), pl.ds(start + g * GROUP, GROUP)
         for side in range(2):
             copies.append(
-                pltpu.make_async_copy(held.at[group, side], out_ref.at[group, 3 * side], sems.at[g, side])
+                pltpu.make_async_copy(held.at[here, side], out_ref.at[there, 3 * side], sems.at[g, side])
             )
             copies[-1].start()
     for copy in copies:
         copy.wait()
 
 
-def last_part(first, second, edge, hmat, loc, out):
-    members = edge.shape[0]
-    return call(
-        last_kernel,
-        sds(members, 4, 64, 128),
+def last_part(start, first, second, edge, hmat, loc, out):
+    count = first.shape[0]
+    return call(
+        functools.partial(last_kernel, start),
+        sds(*out.shape),
         ins=[VMEM] * 5 + [ANY],
         outs=ANY,
-        scratch=[pltpu.VMEM((members, 2, 64, 128), F32), pltpu.SemaphoreType.DMA((members // GROUP, 2))],
+        scratch=[pltpu.VMEM((count, 2, 64, 128), F32), pltpu.SemaphoreType.DMA((count // GROUP, 2))],
         aliases={5: 0},
     )(first, second, edge, hmat, loc, out)
 
@@ -475,20 +525,16 @@
     return smat, hmat.astype(BF16)
 
 
-def swap_even(x):
-    return lax.ppermute(x, "tile", EVEN)
-
-
-def swap_odd(x):
-    return lax.ppermute(x, "tile", ODD)
-
-
 def swap_first(x):
     return lax.ppermute(x, ("mem", "tile"), FIRST)
 
 
 def swap_second(x):
     return lax.ppermute(x, ("mem", "tile"), SECOND)
+
+
+def swap_core(x):
+    return lax.ppermute(x, "mem", [(m, m ^ 1) for m in range(MEMS)])
 
 
 def round_mem(mine):
@@ -503,7 +549,8 @@
     tile = lax.axis_index("tile")
     tiles = lax.axis_size("tile")
     even = tile % 2 == 0
-    first_low = (tile + lax.axis_index("mem") // (MEMS // 2)) % 2
+    core = lax.axis_index("mem") % 2
+    first_low = (tile + core) % 2
     where = jnp.stack(
         [
             jnp.where(even, 7 * 32, 0),
@@ -514,6 +561,9 @@
             tile % 2,
             tile,
             first_low,
+            7 * 32 * (1 - first_low),
+            7 * 32 * first_low,
+            core,
         ]
     ).astype(jnp.int32)
     flat = alpha.reshape(members, 256, 128)
@@ -521,20 +571,26 @@
 
     send_first, send_second, token = send_part(where, alpha.reshape(members, 4, 64, 128))
     first, second = swap_first(send_first), swap_second(send_second)
-    inner, own_edge, x, smat, hmat, token = own_part(where, flat, flat_ens, loc_vert, token)
+    inner, own_edge, x, smat, hmat, token, send_first, send_second = own_part(where, flat, flat_ens, loc_vert, token)
+    first_rest, second_rest = swap_first(send_first), swap_second(send_second)
     own_obs = observations(obs_count, obs_col, obs_lev, innovation, obs_weight, token)
-    even_obs = swap_even(own_obs)
-    odd_obs = swap_odd(own_obs)
-
-    inc, se, so = edge_part(where, first, second, own_edge, x, hmat, loc_vert, inner, even_obs, odd_obs)
-    near_even, near_odd = swap_even(se), swap_odd(so)
-    wown, wnear, lev, innov, weight = weights(where, own_obs, even_obs, odd_obs)
+    here_obs = swap_first(own_obs)
+
+    head = head_part(first, second, own_edge, x, hmat, loc_vert)
+    inc, keep, give = edge_part(
+        where, first_rest, second_rest, own_edge, x, hmat, loc_vert, inner, head, here_obs
+    )
+    near = swap_first(keep + swap_core(give))
+    there_obs = swap_core(here_obs)
+    wown, wnear, lev, innov, weight = weights(where, own_obs, here_obs, there_obs)
     mine = mine_part(where, inc, wown, wnear, lev)
-    vals = round_mem(values(mine, near_even, near_odd, wown, wnear, lev))
+    vals = round_mem(values(where, mine, near, wown, wnear, lev))
     c, back_first, back_second = adjoint(where, vals, innov, weight, lev, wown, wnear, x)
     halo_first, halo_second = swap_first(back_first), swap_second(back_second)
-    out, edge = back_part(flat, flat_ens, c, smat, loc_vert)
-    out = last_part(halo_first, halo_second, edge, hmat, loc_vert, out.reshape(members, 4, 64, 128))
+    out, edge, back_first, back_second = back_part(where, flat, flat_ens, c, smat, loc_vert)
+    rest_first, rest_second = swap_first(back_first), swap_second(back_second)
+    out = last_part(0, halo_first, halo_second, edge, hmat, loc_vert, out.reshape(members, 4, 64, 128))
+    out = last_part(HEAD, rest_first, rest_second, edge, hmat, loc_vert, out)
     return out.reshape(members, 8, 32, 128)
 
 

time: 105 us -> 103 us (0.981)
  waiting for transfers between devices: 55.6 us -> 41.8 us
  starting transfers between devices: 23.8 us -> 34.1 us
  Pallas kernels: 20.2 us -> 22 us
    ppermute x4 -> x2, waiting for transfers between devices: 27.3 us -> 2.08 us  [swap_core(): return lax.ppermute(x, 'mem', [(m, m ^ 1) for m in range(MEMS)])]
    ppermute x2 -> x4, starting transfers between devices: 0.01 us -> 18.1 us  [swap_second(): return lax.ppermute(x, ('mem', 'tile'), SECOND)]
    ppermute x2 -> x4, waiting for transfers between devices: 1.14 us -> 17.2 us  [swap_second(): return lax.ppermute(x, ('mem', 'tile'), SECOND)]
    ppermute x2 -> x6, starting transfers between devices: 17.7 us -> 5.4 us  [swap_first(): return lax.ppermute(x, ('mem', 'tile'), FIRST)]
    ppermute x2 -> x6, waiting for transfers between devices: 23.9 us -> 18.9 us  [swap_first(): return lax.ppermute(x, ('mem', 'tile'), FIRST)]
    pallas_call x3 -> x5, Pallas kernels: 7.59 us -> 10.8 us  [the longest x1 5.32 us: back_part(): call(back_kernel, (sds(members, 256, 128), sds(members, 128, 128), sds(me...]
    ppermute x4 -> x2, starting transfers between devices: 5.01 us -> 7.34 us  [swap_core(): return lax.ppermute(x, 'mem', [(m, m ^ 1) for m in range(MEMS)])]
    ppermute x3, starting transfers between devices: 1.11 us -> 3.26 us  [round_mem(): lax.ppermute(mine, 'mem', [(i, (i + shift) % size) for i in range(size)])]
  transfers between devices with their start and end apart: 11 -> 15, of which waited for: 9 -> 11; matrix products, arithmetic and copies ran while one was open for 0% -> 0% of each run, Pallas kernels for 11% -> 15%
where the time goes in v5:
time: 103 us
  waiting for transfers between devices  41.8 us (41%)
  starting transfers between devices  34.1 us (33%)
  Pallas kernels  22 us (21%)
  local copies, waits for them, and re-layouts  4.3 us (4%)
    ppermute x6, waiting for transfers between devices, swap_first(): return lax.ppermute(x, ('mem', 'tile'), FIRST)  18.9 us
    ppermute x4, starting transfers between devices, swap_second(): return lax.ppermute(x, ('mem', 'tile'), SECOND)  18.1 us
    ppermute x4, waiting for transfers between devices, swap_second(): return lax.ppermute(x, ('mem', 'tile'), SECOND)  17.2 us
    ppermute x2, starting transfers between devices, swap_core(): return lax.ppermute(x, 'mem', [(m, m ^ 1) for m in range(MEMS)])  7.34 us
    ppermute x6, starting transfers between devices, swap_first(): return lax.ppermute(x, ('mem', 'tile'), FIRST)  5.4 us
    pallas_call x1, Pallas kernels, back_part(): call(back_kernel, (sds(members, 256, 128), sds(members, 128, 128), sds(me...  5.32 us
    unnamed x20, local copies, waits for them, and re-layouts  4.22 us
    pallas_call x1, Pallas kernels, own_part(): call(own_kernel, (sds(V, 128, 128), sds(members, 128, 128), sds(members,...  3.83 us
  transfers between devices with their start and end apart: 15, of which 11 were waited for; matrix products, arithmetic and copies ran while one was open for 0% of the time, Pallas kernels for 15%

profile of v5, /device:TPU:32, one launch (start us, length us, event | category | flops | bytes accessed | tf_op | source)
XLA Modules:
  0.0 103.2 jit_solution(10860204121415354072)
XLA Ops:
  0.1 1.3 %copy-done.2 = bf16[20,8,32,128]{3,2,1,0:T(8,128)(2,1)S(1)} copy-done((bf16[20,8,32,128]{3,2,1,0:T(8,128)(2,1)S(1)}, bf16[20,8,32,128]{3,2,1,0:T(8,128)(2,1)}, u32[]{:S(2)}) %copy-start.2) | copy-done | bytes 1310744
  1.4 0.7 shard_map.82
  2.1 3.4 %collective-permute-start.2 = (f32[12,64,128]{2,1,0:T(8,128)S(1)}, f32[12,64,128]{2,1,0:T(8,128)S(1)}, u32[]{:S(2)}, u32[]{:S(2)}) collective-permute-start(f32[12,64,128]{2,1,0:T(8,128)S(1)} %get-tuple-element.38), channel_id=1, source_target_pairs={{0,1},{1,0},{2,3},{3,2},{4,5},{5,4},{6,7},{7,6},{8,9},{9,8},{10,11... | collective-permute-start | bytes 1179656 | tf_op jit(solution)/shard_map/ppermute | solution.py:529
  5.4 8.2 %collective-permute-start.3 = (f32[12,64,128]{2,1,0:T(8,128)S(1)}, f32[12,64,128]{2,1,0:T(8,128)S(1)}, u32[]{:S(2)}, u32[]{:S(2)}) collective-permute-start(f32[12,64,128]{2,1,0:T(8,128)S(1)} %get-tuple-element.39), channel_id=1, source_target_pairs={{1,2},{2,1},{3,4},{4,3},{5,6},{6,5},{7,8},{8,7},{9,10},{10,9},{11,... | collective-permute-start | bytes 1179656 | tf_op jit(solution)/shard_map/ppermute | solution.py:533
  13.7 2.1 %copy-done = bf16[20,3,8,32,128]{4,3,2,1,0:T(8,128)(2,1)S(1)} copy-done((bf16[20,3,8,32,128]{4,3,2,1,0:T(8,128)(2,1)S(1)}, bf16[20,3,8,32,128]{4,3,2,1,0:T(8,128)(2,1)}, u32[]{:S(2)}) %copy-start) | copy-done | bytes 3932184
  15.8 0.8 copy-done.4
  16.6 3.8 %shard_map.83 = (f32[3,128,128]{2,1,0:T(8,128)S(1)}, f32[20,128,128]{2,1,0:T(8,128)S(1)}, bf16[20,3,128,128]{3,2,1,0:T(8,128)(2,1)S(1)}, bf16[256,256]{1,0:T(8,1...) custom-call(s32[11]{0:T(128)S(1)} %stack.51.where_ref, ...), custom_call_target="tpu_custom_call" | custom-call | flops 1000000 | bytes 1000000 | tf_op jit(solution)/shard_map/pallas_call | solution.py:143
  20.5 1.5 %collective-permute-start.1 = (f32[8,64,128]{2,1,0:T(8,128)S(1)}, f32[8,64,128]{2,1,0:T(8,128)S(1)}, u32[]{:S(2)}, u32[]{:S(2)}) collective-permute-start(f32[8,64,128]{2,1,0:T(8,128)S(1)} %get-tuple-element.33), channel_id=1, source_target_pairs={{1,2},{2,1},{3,4},{4,3},{5,6},{6,5},{7,8},{8,7},{9,10},{10,9},{11,... | collective-permute-start | bytes 786440 | tf_op jit(solution)/shard_map/ppermute | solution.py:533
  23.0 1.5 %collective-permute-start.4 = (f32[72,128]{1,0:T(8,128)S(1)}, f32[72,128]{1,0:T(8,128)S(1)}, u32[]{:S(2)}, u32[]{:S(2)}) collective-permute-start(f32[72,128]{1,0:T(8,128)S(1)} %shard_map.85.own_ref), channel_id=1, source_target_pairs={{0,1},{1,0},{2,3},{3,2},{4,5},{5,4},{6,7},{7,6},{8,9},{9,8},{10,11... | collective-permute-start | bytes 110600 | tf_op jit(solution)/shard_map/ppermute | solution.py:529
  24.5 9.1 %collective-permute-done.3.second_ref = f32[12,64,128]{2,1,0:T(8,128)S(1)} collective-permute-done((f32[12,64,128]{2,1,0:T(8,128)S(1)}, f32[12,64,128]{2,1,0:T(8,128)S(1)}, u32[]{:S(2)}, u32[]{:S(2)}) %collective-permute-start.3) | collective-permute-done | bytes 393248 | tf_op jit(solution)/shard_map/ppermute | solution.py:533
  33.7 1.4 %shard_map.84.head_ref = f32[3,128,128]{2,1,0:T(8,128)S(1)} custom-call(f32[12,64,128]{2,1,0:T(8,128)S(1)} %collective-permute-done.2.first_ref, f32[12,64,128]{2,1,0:T(8,128)S(1)} %collective-permute-done.3.second_ref, f32[20,128,128]{2,1,0:T(8,128)S(1)} %get-tuple-element.34.own_ref, bf16[20,3,128,128]{3,2,1,0:T(8,128)(2,1)S(1)} %get-tuple-element.35.x_ref, ...), custom_call_target="tpu_custom_call" | custom-call | flops 1000000 | bytes 1000000 | tf_op jit(solution)/shard_map/pallas_call | solution.py:232
  35.1 3.0 %collective-permute-done.4.after_obs.here_ref = f32[72,128]{1,0:T(8,128)S(1)} collective-permute-done((f32[72,128]{1,0:T(8,128)S(1)}, f32[72,128]{1,0:T(8,128)S(1)}, u32[]{:S(2)}, u32[]{:S(2)}) %collective-permute-start.4) | collective-permute-done | bytes 36896 | tf_op jit(solution)/shard_map/ppermute | solution.py:529
  38.1 2.3 %collective-permute-done.1.second_ref = f32[8,64,128]{2,1,0:T(8,128)S(1)} collective-permute-done((f32[8,64,128]{2,1,0:T(8,128)S(1)}, f32[8,64,128]{2,1,0:T(8,128)S(1)}, u32[]{:S(2)}, u32[]{:S(2)}) %collective-permute-start.1) | collective-permute-done | bytes 262176 | tf_op jit(solution)/shard_map/ppermute | solution.py:533
  40.4 1.6 %shard_map.86 = (f32[3,256,128]{2,1,0:T(8,128)S(1)}, f32[3,32,128]{2,1,0:T(8,128)S(1)}, f32[3,32,128]{2,1,0:T(8,128)S(1)}) custom-call(s32[11]{0:T(128)S(1)} %stack.51.where_ref, f32[8,64,128]{2,1,0:T(8,128)S(1)} %collective-permute-done.first_ref, f32[8,64,128]{2,1,0:T(8,128)S(1)} %collective-permute-done.1.second_ref, ...), custom_call_target="tpu_custom_call" | custom-call | flops 1000000 | bytes 1000000 | tf_op jit(solution)/shard_map/pallas_call | solution.py:247
  42.1 1.2 %collective-permute-done.6 = f32[3,32,128]{2,1,0:T(8,128)S(1)} collective-permute-done((f32[3,32,128]{2,1,0:T(8,128)S(1)}, f32[3,32,128]{2,1,0:T(8,128)S(1)}, u32[]{:S(2)}, u32[]{:S(2)}) %collective-permute-start.6) | collective-permute-done | bytes 49184 | tf_op jit(solution)/shard_map/ppermute | solution.py:537
  43.7 7.2 %collective-permute-start.5 = (f32[72,128]{1,0:T(8,128)S(1)}, f32[72,128]{1,0:T(8,128)S(1)}, u32[]{:S(2)}, u32[]{:S(2)}) collective-permute-start(f32[72,128]{1,0:T(8,128)S(1)} %collective-permute-done.4.after_obs.here_ref), channel_id=1, source_target_pairs={{0,64},{64,0},{128,192},{192,128},{1,65},{65,1},{129,193},{193,129... | collective-permute-start | bytes 110600 | tf_op jit(solution)/shard_map/ppermute | solution.py:537
  50.9 0.9 collective-permute-done.5.there_ref
  51.8 1.1 %shard_map.87 = (bf16[3,320,768]{2,1,0:T(8,128)(2,1)S(1)}, bf16[2,3,64,768]{3,2,1,0:T(8,128)(2,1)S(1)}, f32[9,768]{1,0:T(8,128)S(1)}, f32[9,768]{1,0:T(8,128)S(1)}, f32[9,768]{1,0:T(8,128)S(1)}) custom-call(s32[11]{0:T(128)S(1)} %stack.51.where_ref, f32[72,128]{1,0:T(8,128)S(1)} %shard_map.85.own_ref, ...), custom_call_target="tpu_custom_call" | custom-call | flops 1000000 | bytes 1000000 | tf_op jit(solution)/shard_map/pallas_call | solution.py:305
  52.9 1.7 %shard_map.88.mine_ref = f32[9,768]{1,0:T(8,128)S(1)} custom-call(s32[11]{0:T(128)S(1)} %stack.51.where_ref, f32[3,256,128]{2,1,0:T(8,128)S(1)} %get-tuple-element.41.inc_ref, bf16[3,320,768]{2,1,0:T(8,128)(2,1)S(1)} %get-tuple-element.42.wown_ref, bf16[2,3,64,768]{3,2,1,0:T(8,128)(2,1)S(1)} %get-tuple-element.43.wnear_ref, ...), custom_call_target="tpu_custom_call" | custom-call | flops 1000000 | bytes 1000000 | tf_op jit(solution)/shard_map/pallas_call | solution.py:343
  54.6 1.4 %shard_map.89.v0 = f32[54,128]{1,0:T(8,128)S(1)} custom-call(s32[11]{0:T(128)S(1)} %stack.51.where_ref, f32[9,768]{1,0:T(8,128)S(1)} %shard_map.88.mine_ref, f32[3,32,128]{2,1,0:T(8,128)S(1)} %collective-permute-done.7.near_ref, bf16[3,320,768]{2,1,0:T(8,128)(2,1)S(1)} %get-tuple-element.42.wown_ref, ...), custom_call_target="tpu_custom_call" | custom-call | flops 1000000 | bytes 1000000 | tf_op jit(solution)/shard_map/pallas_call | solution.py:371
  56.0 3.0 %collective-permute-start.10 = (f32[54,128]{1,0:T(8,128)S(1)}, f32[54,128]{1,0:T(8,128)S(1)}, u32[]{:S(2)}, u32[]{:S(2)}) collective-permute-start(f32[54,128]{1,0:T(8,128)S(1)} %shard_map.89.v0), channel_id=1, source_target_pairs={{0,192},{64,0},{128,64},{192,128},{1,193},{65,1},{129,65},{193,129... | collective-permute-start | bytes 82952 | tf_op jit(solution)/shard_map/ppermute | solution.py:543
  59.2 1.3 %collective-permute-done.10.v3 = f32[54,128]{1,0:T(8,128)S(1)} collective-permute-done((f32[54,128]{1,0:T(8,128)S(1)}, f32[54,128]{1,0:T(8,128)S(1)}, u32[]{:S(2)}, u32[]{:S(2)}) %collective-permute-start.10) | collective-permute-done | bytes 27680 | tf_op jit(solution)/shard_map/ppermute | solution.py:543
  60.5 2.3 %collective-permute-done.9.v2 = f32[54,128]{1,0:T(8,128)S(1)} collective-permute-done((f32[54,128]{1,0:T(8,128)S(1)}, f32[54,128]{1,0:T(8,128)S(1)}, u32[]{:S(2)}, u32[]{:S(2)}) %collective-permute-start.9) | collective-permute-done | bytes 27680 | tf_op jit(solution)/shard_map/ppermute | solution.py:543
  62.8 1.9 %shard_map.90 = (f32[3,256,128]{2,1,0:T(8,128)S(1)}, f32[12,64,128]{2,1,0:T(8,128)S(1)}, f32[12,64,128]{2,1,0:T(8,128)S(1)}) custom-call(s32[11]{0:T(128)S(1)} %stack.51.where_ref, f32[54,128]{1,0:T(8,128)S(1)} %shard_map.89.v0, f32[54,128]{1,0:T(8,128)S(1)} %collective-permute-done.8.v1, f32[54,128]{1,0:T(8,128)S(1)} %collective-permute-done.9.v2, ...), custom_call_target="tpu_custom_call" | custom-call | flops 1000000 | bytes 1000000 | tf_op jit(solution)/shard_map/pallas_call | solution.py:411
  64.8 5.6 %collective-permute-start.14 = (f32[12,64,128]{2,1,0:T(8,128)S(1)}, f32[12,64,128]{2,1,0:T(8,128)S(1)}, u32[]{:S(2)}, u32[]{:S(2)}) collective-permute-start(f32[12,64,128]{2,1,0:T(8,128)S(1)} %get-tuple-element.55), channel_id=1, source_target_pairs={{1,2},{2,1},{3,4},{4,3},{5,6},{6,5},{7,8},{8,7},{9,10},{10,9},{11,... | collective-permute-start | bytes 1179656 | tf_op jit(solution)/shard_map/ppermute | solution.py:533
  70.4 5.3 %shard_map.91 = (f32[20,256,128]{2,1,0:T(8,128)}, f32[20,128,128]{2,1,0:T(8,128)S(1)}, f32[8,64,128]{2,1,0:T(8,128)S(1)}, f32[8,64,128]{2,1,0:T(8,128)S(1)}) custom-call(s32[11]{0:T(128)S(1)} %stack.51.where_ref, bf16[20,256,128]{2,1,0:T(8,128)(2,1)S(1)} %bitcast.20, bf16[20,3,256,128]{3,2,1,0:T(8,128)(2,1)S(1)} %bitcast.17, ...), custom_call_target="tpu_custom_call" | custom-call | flops 1000000 | bytes 1000000 | tf_op jit(solution)/shard_map/pallas_call | solution.py:443
  75.8 2.9 %collective-permute-start.12 = (f32[8,64,128]{2,1,0:T(8,128)S(1)}, f32[8,64,128]{2,1,0:T(8,128)S(1)}, u32[]{:S(2)}, u32[]{:S(2)}) collective-permute-start(f32[8,64,128]{2,1,0:T(8,128)S(1)} %get-tuple-element.52), channel_id=1, source_target_pairs={{1,2},{2,1},{3,4},{4,3},{5,6},{6,5},{7,8},{8,7},{9,10},{10,9},{11,... | collective-permute-start | bytes 786440 | tf_op jit(solution)/shard_map/ppermute | solution.py:533
  78.6 10.1 %collective-permute-done.13.first_ref = f32[12,64,128]{2,1,0:T(8,128)S(1)} collective-permute-done((f32[12,64,128]{2,1,0:T(8,128)S(1)}, f32[12,64,128]{2,1,0:T(8,128)S(1)}, u32[]{:S(2)}, u32[]{:S(2)}) %collective-permute-start.13) | collective-permute-done | bytes 393248 | tf_op jit(solution)/shard_map/ppermute | solution.py:529
  88.9 1.4 %shard_map.92.unused_ref = f32[20,4,64,128]{3,2,1,0:T(8,128)} custom-call(f32[12,64,128]{2,1,0:T(8,128)S(1)} %collective-permute-done.13.first_ref, f32[12,64,128]{2,1,0:T(8,128)S(1)} %collective-permute-done.14.second_ref, f32[20,128,128]{2,1,0:T(8,128)S(1)} %get-tuple-element.53.edge_ref, ...), custom_call_target="tpu_custom_call", output_to_operand_aliasing={{}: (5, {})} | custom-call | flops 1000000 | bytes 1000000 | tf_op jit(solution)/shard_map/pallas_call | solution.py:491
  90.3 5.8 %collective-permute-done.11.first_ref = f32[8,64,128]{2,1,0:T(8,128)S(1)} collective-permute-done((f32[8,64,128]{2,1,0:T(8,128)S(1)}, f32[8,64,128]{2,1,0:T(8,128)S(1)}, u32[]{:S(2)}, u32[]{:S(2)}) %collective-permute-start.11) | collective-permute-done | bytes 262176 | tf_op jit(solution)/shard_map/ppermute | solution.py:529
  96.1 5.6 %collective-permute-done.12.second_ref = f32[8,64,128]{2,1,0:T(8,128)S(1)} collective-permute-done((f32[8,64,128]{2,1,0:T(8,128)S(1)}, f32[8,64,128]{2,1,0:T(8,128)S(1)}, u32[]{:S(2)}, u32[]{:S(2)}) %collective-permute-start.12) | collective-permute-done | bytes 262176 | tf_op jit(solution)/shard_map/ppermute | solution.py:533
  101.7 1.3 %shard_map.93 = f32[20,4,64,128]{3,2,1,0:T(8,128)} custom-call(f32[8,64,128]{2,1,0:T(8,128)S(1)} %collective-permute-done.11.first_ref, f32[8,64,128]{2,1,0:T(8,128)S(1)} %collective-permute-done.12.second_ref, f32[20,128,128]{2,1,0:T(8,128)S(1)} %get-tuple-element.53.edge_ref, ...), custom_call_target="tpu_custom_call", output_to_operand_aliasing={{}: (5, {})} | custom-call | flops 1000000 | bytes 1000000 | tf_op jit(solution)/shard_map/pallas_call | solution.py:491
  (32 shorter events, 1.5 us)
Async XLA Ops:
  0.1 1.3 %copy-start.2 = (bf16[20,8,32,128]{3,2,1,0:T(8,128)(2,1)S(1)}, bf16[20,8,32,128]{3,2,1,0:T(8,128)(2,1)}, u32[]{:S(2)}) copy-start(bf16[20,8,32,128]{3,2,1,0:T(8,128)(2,1)} %param.8) | copy-start | bytes 3932164
  2.1 22.4 %collective-permute-start.2 = (f32[12,64,128]{2,1,0:T(8,128)S(1)}, f32[12,64,128]{2,1,0:T(8,128)S(1)}, u32[]{:S(2)}, u32[]{:S(2)}) collective-permute-start(f32[12,64,128]{2,1,0:T(8,128)S(1)} %get-tuple-element.38), channel_id=1, source_target_pairs={{0,1},{1,0},{2,3},{3,2},{4,5},{5,4},{6,7},{7,6},{8,9},{9,8},{10,11... | collective-permute-start | bytes 1179656 | tf_op jit(solution)/shard_map/ppermute | solution.py:529
  5.4 28.2 %collective-permute-start.3 = (f32[12,64,128]{2,1,0:T(8,128)S(1)}, f32[12,64,128]{2,1,0:T(8,128)S(1)}, u32[]{:S(2)}, u32[]{:S(2)}) collective-permute-start(f32[12,64,128]{2,1,0:T(8,128)S(1)} %get-tuple-element.39), channel_id=1, source_target_pairs={{1,2},{2,1},{3,4},{4,3},{5,6},{6,5},{7,8},{8,7},{9,10},{10,9},{11,... | collective-permute-start | bytes 1179656 | tf_op jit(solution)/shard_map/ppermute | solution.py:533
  13.7 2.1 %copy-start = (bf16[20,3,8,32,128]{4,3,2,1,0:T(8,128)(2,1)S(1)}, bf16[20,3,8,32,128]{4,3,2,1,0:T(8,128)(2,1)}, u32[]{:S(2)}) copy-start(bf16[20,3,8,32,128]{4,3,2,1,0:T(8,128)(2,1)} %param.9) | copy-start | bytes 11796484
  15.8 0.8 copy-start.4
  16.5 6.1 %copy-start.6 = (s32[1,2048]{1,0:T(1,128)S(1)}, s32[1,2048]{1,0:T(1,128)}, u32[]{:S(2)}) copy-start(s32[1,2048]{1,0:T(1,128)} %col_ref.1) | copy-start | bytes 24580
  16.6 6.1 %copy-start.7 = (s32[1,2048]{1,0:T(1,128)S(1)}, s32[1,2048]{1,0:T(1,128)}, u32[]{:S(2)}) copy-start(s32[1,2048]{1,0:T(1,128)} %lev_ref.1) | copy-start | bytes 24580
  16.6 6.1 %copy-start.8 = (f32[1,2048]{1,0:T(1,128)S(1)}, f32[1,2048]{1,0:T(1,128)}, u32[]{:S(2)}) copy-start(f32[1,2048]{1,0:T(1,128)} %innov_ref.1) | copy-start | bytes 24580
  16.6 6.1 %copy-start.9 = (f32[1,2048]{1,0:T(1,128)S(1)}, f32[1,2048]{1,0:T(1,128)}, u32[]{:S(2)}) copy-start(f32[1,2048]{1,0:T(1,128)} %weight_ref.1) | copy-start | bytes 24580
  20.4 17.7 %collective-permute-start = (f32[8,64,128]{2,1,0:T(8,128)S(1)}, f32[8,64,128]{2,1,0:T(8,128)S(1)}, u32[]{:S(2)}, u32[]{:S(2)}) collective-permute-start(f32[8,64,128]{2,1,0:T(8,128)S(1)} %get-tuple-element.32), channel_id=1, source_target_pairs={{0,1},{1,0},{2,3},{3,2},{4,5},{5,4},{6,7},{7,6},{8,9},{9,8},{10,11... | collective-permute-start | bytes 786440 | tf_op jit(solution)/shard_map/ppermute | solution.py:529
  20.5 19.9 %collective-permute-start.1 = (f32[8,64,128]{2,1,0:T(8,128)S(1)}, f32[8,64,128]{2,1,0:T(8,128)S(1)}, u32[]{:S(2)}, u32[]{:S(2)}) collective-permute-start(f32[8,64,128]{2,1,0:T(8,128)S(1)} %get-tuple-element.33), channel_id=1, source_target_pairs={{1,2},{2,1},{3,4},{4,3},{5,6},{6,5},{7,8},{8,7},{9,10},{10,9},{11,... | collective-permute-start | bytes 786440 | tf_op jit(solution)/shard_map/ppermute | solution.py:533
  23.0 15.2 %collective-permute-start.4 = (f32[72,128]{1,0:T(8,128)S(1)}, f32[72,128]{1,0:T(8,128)S(1)}, u32[]{:S(2)}, u32[]{:S(2)}) collective-permute-start(f32[72,128]{1,0:T(8,128)S(1)} %shard_map.85.own_ref), channel_id=1, source_target_pairs={{0,1},{1,0},{2,3},{3,2},{4,5},{5,4},{6,7},{7,6},{8,9},{9,8},{10,11... | collective-permute-start | bytes 110600 | tf_op jit(solution)/shard_map/ppermute | solution.py:529
  42.0 1.3 %collective-permute-start.6 = (f32[3,32,128]{2,1,0:T(8,128)S(1)}, f32[3,32,128]{2,1,0:T(8,128)S(1)}, u32[]{:S(2)}, u32[]{:S(2)}) collective-permute-start(f32[3,32,128]{2,1,0:T(8,128)S(1)} %get-tuple-element.46), channel_id=1, source_target_pairs={{0,64},{64,0},{128,192},{192,128},{1,65},{65,1},{129,193},{193,129... | collective-permute-start | bytes 147464 | tf_op jit(solution)/shard_map/ppermute | solution.py:537
  43.3 11.2 %collective-permute-start.7 = (f32[3,32,128]{2,1,0:T(8,128)S(1)}, f32[3,32,128]{2,1,0:T(8,128)S(1)}, u32[]{:S(2)}, u32[]{:S(2)}) collective-permute-start(f32[3,32,128]{2,1,0:T(8,128)S(1)} %add.21), channel_id=1, source_target_pairs={{0,1},{1,0},{2,3},{3,2},{4,5},{5,4},{6,7},{7,6},{8,9},{9,8},{10,11... | collective-permute-start | bytes 147464 | tf_op jit(solution)/shard_map/ppermute | solution.py:529
  43.7 8.1 %collective-permute-start.5 = (f32[72,128]{1,0:T(8,128)S(1)}, f32[72,128]{1,0:T(8,128)S(1)}, u32[]{:S(2)}, u32[]{:S(2)}) collective-permute-start(f32[72,128]{1,0:T(8,128)S(1)} %collective-permute-done.4.after_obs.here_ref), channel_id=1, source_target_pairs={{0,64},{64,0},{128,192},{192,128},{1,65},{65,1},{129,193},{193,129... | collective-permute-start | bytes 110600 | tf_op jit(solution)/shard_map/ppermute | solution.py:537
  54.6 15.8 %copy-start.3 = (bf16[20,8,32,128]{3,2,1,0:T(8,128)(2,1)S(1)}, bf16[20,8,32,128]{3,2,1,0:T(8,128)(2,1)}, u32[]{:S(2)}) copy-start(bf16[20,8,32,128]{3,2,1,0:T(8,128)(2,1)} %param.8) | copy-start | bytes 3932164
  56.0 4.5 %collective-permute-start.10 = (f32[54,128]{1,0:T(8,128)S(1)}, f32[54,128]{1,0:T(8,128)S(1)}, u32[]{:S(2)}, u32[]{:S(2)}) collective-permute-start(f32[54,128]{1,0:T(8,128)S(1)} %shard_map.89.v0), channel_id=1, source_target_pairs={{0,192},{64,0},{128,64},{192,128},{1,193},{65,1},{129,65},{193,129... | collective-permute-start | bytes 82952 | tf_op jit(solution)/shard_map/ppermute | solution.py:543
  58.9 3.9 %collective-permute-start.9 = (f32[54,128]{1,0:T(8,128)S(1)}, f32[54,128]{1,0:T(8,128)S(1)}, u32[]{:S(2)}, u32[]{:S(2)}) collective-permute-start(f32[54,128]{1,0:T(8,128)S(1)} %shard_map.89.v0), channel_id=1, source_target_pairs={{0,128},{64,192},{128,0},{192,64},{1,129},{65,193},{129,1},{193,65... | collective-permute-start | bytes 82952 | tf_op jit(solution)/shard_map/ppermute | solution.py:543
  59.1 3.7 %collective-permute-start.8 = (f32[54,128]{1,0:T(8,128)S(1)}, f32[54,128]{1,0:T(8,128)S(1)}, u32[]{:S(2)}, u32[]{:S(2)}) collective-permute-start(f32[54,128]{1,0:T(8,128)S(1)} %shard_map.89.v0), channel_id=1, source_target_pairs={{0,64},{64,128},{128,192},{192,0},{1,65},{65,129},{129,193},{193,1... | collective-permute-start | bytes 82952 | tf_op jit(solution)/shard_map/ppermute | solution.py:543
  62.8 7.6 %copy-start.1 = (bf16[20,3,8,32,128]{4,3,2,1,0:T(8,128)(2,1)S(1)}, bf16[20,3,8,32,128]{4,3,2,1,0:T(8,128)(2,1)}, u32[]{:S(2)}) copy-start(bf16[20,3,8,32,128]{4,3,2,1,0:T(8,128)(2,1)} %param.9) | copy-start | bytes 11796484
  62.8 7.6 %copy-start.5 = (bf16[128,128]{1,0:T(8,128)(2,1)S(1)}, bf16[128,128]{1,0:T(8,128)(2,1)}, u32[]{:S(2)}) copy-start(bf16[128,128]{1,0:T(8,128)(2,1)} %loc_ref.11) | copy-start | bytes 98308
  64.7 24.0 %collective-permute-start.13 = (f32[12,64,128]{2,1,0:T(8,128)S(1)}, f32[12,64,128]{2,1,0:T(8,128)S(1)}, u32[]{:S(2)}, u32[]{:S(2)}) collective-permute-start(f32[12,64,128]{2,1,0:T(8,128)S(1)} %get-tuple-element.54), channel_id=1, source_target_pairs={{0,1},{1,0},{2,3},{3,2},{4,5},{5,4},{6,7},{7,6},{8,9},{9,8},{10,11... | collective-permute-start | bytes 1179656 | tf_op jit(solution)/shard_map/ppermute | solution.py:529
  64.8 24.0 %collective-permute-start.14 = (f32[12,64,128]{2,1,0:T(8,128)S(1)}, f32[12,64,128]{2,1,0:T(8,128)S(1)}, u32[]{:S(2)}, u32[]{:S(2)}) collective-permute-start(f32[12,64,128]{2,1,0:T(8,128)S(1)} %get-tuple-element.55), channel_id=1, source_target_pairs={{1,2},{2,1},{3,4},{4,3},{5,6},{6,5},{7,8},{8,7},{9,10},{10,9},{11,... | collective-permute-start | bytes 1179656 | tf_op jit(solution)/shard_map/ppermute | solution.py:533
  75.7 20.3 %collective-permute-start.11 = (f32[8,64,128]{2,1,0:T(8,128)S(1)}, f32[8,64,128]{2,1,0:T(8,128)S(1)}, u32[]{:S(2)}, u32[]{:S(2)}) collective-permute-start(f32[8,64,128]{2,1,0:T(8,128)S(1)} %get-tuple-element.51), channel_id=1, source_target_pairs={{0,1},{1,0},{2,3},{3,2},{4,5},{5,4},{6,7},{7,6},{8,9},{9,8},{10,11... | collective-permute-start | bytes 786440 | tf_op jit(solution)/shard_map/ppermute | solution.py:529
  75.8 26.0 %collective-permute-start.12 = (f32[8,64,128]{2,1,0:T(8,128)S(1)}, f32[8,64,128]{2,1,0:T(8,128)S(1)}, u32[]{:S(2)}, u32[]{:S(2)}) collective-permute-start(f32[8,64,128]{2,1,0:T(8,128)S(1)} %get-tuple-element.52), channel_id=1, source_target_pairs={{1,2},{2,1},{3,4},{4,3},{5,6},{6,5},{7,8},{8,7},{9,10},{10,9},{11,... | collective-permute-start | bytes 786440 | tf_op jit(solution)/shard_map/ppermute | solution.py:533

commit v6 on v5

--- a/solution.py
+++ b/solution.py
@@ -13,10 +13,11 @@
 SLOTS = 768
 GROUP = 4
 HEAD = 12
+OBS = 72
 
 TILES = 64
 EVEN = [(i, i ^ 1) for i in range(TILES)]
-ODD = [(i, ((i - 1) ^ 1) + 1) for i in range(1, TILES - 1)] + [(0, TILES - 1), (TILES - 1, 0)]
+ODD = [(i, ((i - 1) ^ 1) + 1) for i in range(1, TILES - 1)] + [(0, 0), (TILES - 1, TILES - 1)]
 
 MEMS = 4
 FIRST = [(TILES * m + a, TILES * m + b) for m in range(MEMS) for a, b in (ODD if m % 2 else EVEN)]
@@ -79,103 +80,9 @@
     return out[:, :128] + out[:, 128:]
 
 
-def send_kernel(where_ref, quarters_ref, first_ref, second_ref, token_ref, edges, sems):
-    head = pl.ds(0, HEAD)
-    copies = [pltpu.make_async_copy(quarters_ref.at[head, 3 * n], edges.at[n], sems.at[n]) for n in range(2)]
-    for copy in copies:
-        copy.start()
-    token_ref[...] = jnp.zeros_like(token_ref)
-    for copy in copies:
-        copy.wait()
-    low = where_ref[7]
-    first_ref[...] = edges[1 - low].astype(F32)
-    second_ref[...] = edges[low].astype(F32)
-
-
-def send_part(where, quarters):
-    members = HEAD
-    return call(
-        send_kernel,
-        (sds(members, 64, 128), sds(members, 64, 128), sds(8, 128)),
-        ins=[SMEM, ANY],
-        outs=(VMEM,) * 3,
-        scratch=[pltpu.VMEM((2, members, 64, 128), BF16), pltpu.SemaphoreType.DMA((2,))],
-    )(where, quarters)
-
-
-def own_kernel(where_ref, alpha_ref, ens_ref, loc_ref, after_ref, inner_ref, edge_ref, x_ref, smat_ref, hmat_ref, token_ref, first_ref, second_ref):
-    @pl.when(pl.program_id(0) == 0)
-    def _():
-        inner_ref[...] = jnp.zeros_like(inner_ref)
-        token_ref[...] = jnp.zeros_like(token_ref)
-        smat, hmat = matrices(where_ref[6], TILES, where_ref[7] == 0)
-        smat_ref[...] = smat
-        hmat_ref[...] = hmat
-
-    smat = smat_ref[...]
-    loc = loc_ref[...]
-    total = [inner_ref[v] for v in range(V)]
-    for k in range(GROUP):
-        full = lift(nn(smat, alpha_ref[k]), loc)
-        edge_ref[k, :64] = full[:64]
-        edge_ref[k, 64:] = full[192:]
-        lifted = full[64:192].astype(BF16).astype(F32)
-        for v in range(V):
-            total[v] = total[v] + ens_ref[k, v, 64:192].astype(F32) * lifted
-            x_ref[k, v, :64] = ens_ref[k, v, :64]
-            x_ref[k, v, 64:] = ens_ref[k, v, 192:]
-    for v in range(V):
-        inner_ref[v] = total[v]
-
-    @pl.when(pl.program_id(0) >= HEAD // GROUP)
-    def _():
-        low = where_ref[7] == 1
-        for k in range(GROUP):
-            rows = [alpha_ref[k, :64].astype(F32), alpha_ref[k, 192:].astype(F32)]
-            first_ref[k] = jnp.where(low, rows[0], rows[1])
-            second_ref[k] = jnp.where(low, rows[1], rows[0])
-
-
-def own_part(where, alpha, ensemble, loc, after):
-    members = alpha.shape[0]
-    whole = lambda *shape: pl.BlockSpec(shape, lambda i: (0,) * len(shape))
-    rest = pl.BlockSpec((GROUP, 64, 128), lambda i: (jnp.maximum(i - HEAD // GROUP, 0), 0, 0))
-    return call(
-        own_kernel,
-        (
-            sds(V, 128, 128),
-            sds(members, 128, 128),
-            sds(members, V, 128, 128, dtype=BF16),
-            sds(256, 256, dtype=BF16),
-            sds(128, 128, dtype=BF16),
-            sds(8, 128),
-            sds(members - HEAD, 64, 128),
-            sds(members - HEAD, 64, 128),
-        ),
-        grid=(members // GROUP,),
-        ins=[
-            SMEM,
-            pl.BlockSpec((GROUP, 256, 128), lambda i: (i, 0, 0)),
-            pl.BlockSpec((GROUP, V, 256, 128), lambda i: (i, 0, 0, 0)),
-            whole(128, 128),
-            whole(8, 128),
-        ],
-        outs=(
-            whole(V, 128, 128),
-            pl.BlockSpec((GROUP, 128, 128), lambda i: (i, 0, 0)),
-            pl.BlockSpec((GROUP, V, 128, 128), lambda i: (i, 0, 0, 0)),
-            whole(256, 256),
-            whole(128, 128),
-            whole(8, 128),
-            rest,
-            rest,
-        ),
-    )(where, alpha, ensemble, loc, after)
-
-
-def obs_kernel(count_ref, col_ref, lev_ref, innov_ref, weight_ref, after_ref, out_ref):
+def sort_observations(count, col_ref, lev_ref, innov_ref, weight_ref, out_ref):
     slots = col_ref.shape[1]
-    live = lax.broadcasted_iota(jnp.int32, (1, slots), 1) < count_ref[0]
+    live = lax.broadcasted_iota(jnp.int32, (1, slots), 1) < count
     rows = []
     for field in (
         col_ref[...].astype(F32),
@@ -201,38 +108,124 @@
                 out_ref[row : row + 1] = total[6 * f + a : 6 * f + a + 1, 128 * v : 128 * v + 128]
 
 
-def observations(count, col, lev, innov, weight, after):
-    return call(
-        obs_kernel,
-        sds(4 * V * SLOTS // 128, 128),
-        ins=[SMEM] + [VMEM] * 5,
-        outs=VMEM,
-    )(count, col, lev, innov, weight, after)
+def send_kernel(where_ref, count_ref, col_ref, lev_ref, innov_ref, weight_ref, quarters_ref, first_ref, second_ref, obs_ref, edges, sems):
+    head = pl.ds(0, HEAD)
+    copies = [pltpu.make_async_copy(quarters_ref.at[head, 3 * n], edges.at[n], sems.at[n]) for n in range(2)]
+    for copy in copies:
+        copy.start()
+    sort_observations(count_ref[0], col_ref, lev_ref, innov_ref, weight_ref, obs_ref)
+    first_ref[64 * HEAD :] = obs_ref[...]
+    for copy in copies:
+        copy.wait()
+    low = where_ref[7]
+    for k in range(HEAD):
+        first_ref[64 * k : 64 * k + 64] = edges[1 - low, k].astype(F32)
+        second_ref[64 * k : 64 * k + 64] = edges[low, k].astype(F32)
+
+
+def send_part(where, count, col, lev, innov, weight, quarters):
+    return call(
+        send_kernel,
+        (sds(64 * HEAD + OBS, 128), sds(64 * HEAD, 128), sds(OBS, 128)),
+        ins=[SMEM, SMEM] + [VMEM] * 4 + [ANY],
+        outs=(VMEM,) * 3,
+        scratch=[pltpu.VMEM((2, HEAD, 64, 128), BF16), pltpu.SemaphoreType.DMA((2,))],
+    )(where, count, col, lev, innov, weight, quarters)
+
+
+def own_kernel(where_ref, alpha_ref, ens_ref, loc_ref, after_ref, inner_ref, edge_ref, x_ref, smat_ref, hmat_ref, first_ref, second_ref):
+    @pl.when(pl.program_id(0) == 0)
+    def _():
+        inner_ref[...] = jnp.zeros_like(inner_ref)
+        smat, hmat = matrices(where_ref[6], TILES, where_ref[7] == 0)
+        smat_ref[...] = smat
+        hmat_ref[...] = hmat
+
+    smat = smat_ref[...]
+    loc = loc_ref[...]
+    total = [inner_ref[v] for v in range(V)]
+    for k in range(GROUP):
+        full = lift(nn(smat, alpha_ref[k]), loc)
+        edge_ref[k, :64] = full[:64]
+        edge_ref[k, 64:] = full[192:]
+        lifted = full[64:192].astype(BF16).astype(F32)
+        for v in range(V):
+            total[v] = total[v] + ens_ref[k, v, 64:192].astype(F32) * lifted
+            x_ref[k, v, :64] = ens_ref[k, v, :64]
+            x_ref[k, v, 64:] = ens_ref[k, v, 192:]
+    for v in range(V):
+        inner_ref[v] = total[v]
+
+    @pl.when(pl.program_id(0) >= HEAD // GROUP)
+    def _():
+        low = where_ref[7] == 1
+        for k in range(GROUP):
+            rows = [alpha_ref[k, :64].astype(F32), alpha_ref[k, 192:].astype(F32)]
+            first_ref[k] = jnp.where(low, rows[0], rows[1])
+            second_ref[k] = jnp.where(low, rows[1], rows[0])
+
+
+def own_part(where, alpha, ensemble, loc, after):
+    members = alpha.shape[0]
+    whole = lambda *shape: pl.BlockSpec(shape, lambda i: (0,) * len(shape))
+    rest = pl.BlockSpec((GROUP, 64, 128), lambda i: (jnp.maximum(i - HEAD // GROUP, 0), 0, 0))
+    return call(
+        own_kernel,
+        (
+            sds(V, 128, 128),
+            sds(members, 128, 128),
+            sds(members, V, 128, 128, dtype=BF16),
+            sds(256, 256, dtype=BF16),
+            sds(128, 128, dtype=BF16),
+            sds(members - HEAD, 64, 128),
+            sds(members - HEAD, 64, 128),
+        ),
+        grid=(members // GROUP,),
+        ins=[
+            SMEM,
+            pl.BlockSpec((GROUP, 256, 128), lambda i: (i, 0, 0)),
+            pl.BlockSpec((GROUP, V, 256, 128), lambda i: (i, 0, 0, 0)),
+            whole(128, 128),
+            whole(OBS, 128),
+        ],
+        outs=(
+            whole(V, 128, 128),
+            pl.BlockSpec((GROUP, 128, 128), lambda i: (i, 0, 0)),
+            pl.BlockSpec((GROUP, V, 128, 128), lambda i: (i, 0, 0, 0)),
+            whole(256, 256),
+            whole(128, 128),
+            rest,
+            rest,
+        ),
+    )(where, alpha, ensemble, loc, after)
 
 
 def edge_terms(first_ref, second_ref, own_ref, x_ref, hmat_ref, loc_ref, start, total):
     hmat = hmat_ref[...]
     loc = loc_ref[...]
-    for k in range(first_ref.shape[0]):
-        halo = jnp.concatenate([first_ref[k].astype(BF16), second_ref[k].astype(BF16)], axis=0)
+    for k in range(second_ref.shape[0] // 64):
+        rows = slice(64 * k, 64 * k + 64)
+        halo = jnp.concatenate([first_ref[rows].astype(BF16), second_ref[rows].astype(BF16)], axis=0)
         lifted = (own_ref[start + k] + lift(nn(hmat, halo), loc)).astype(BF16).astype(F32)
         for v in range(V):
             total[v] = total[v] + x_ref[start + k, v].astype(F32) * lifted
     return total
 
 
-def head_kernel(first_ref, second_ref, own_ref, x_ref, hmat_ref, loc_ref, total_ref):
+def head_kernel(first_ref, second_ref, own_ref, x_ref, hmat_ref, loc_ref, after_ref, total_ref):
     zeros = [jnp.zeros((128, 128), F32) for v in range(V)]
     total = edge_terms(first_ref, second_ref, own_ref, x_ref, hmat_ref, loc_ref, 0, zeros)
     for v in range(V):
         total_ref[v] = total[v]
 
 
-def head_part(first, second, own, x, hmat, loc):
-    return call(head_kernel, sds(V, 128, 128), ins=[VMEM] * 6, outs=VMEM)(first, second, own, x, hmat, loc)
-
-
-def edge_kernel(where_ref, first_ref, second_ref, own_ref, x_ref, hmat_ref, loc_ref, inner_ref, head_ref, after_obs, inc_ref, keep_ref, give_ref):
+def head_part(first, second, own, x, hmat, loc, after):
+    return call(head_kernel, sds(V, 128, 128), ins=[VMEM] * 7, outs=VMEM)(
+        first, second, own, x, hmat, loc, after
+    )
+
+
+def edge_kernel(where_ref, first_ref, second_ref, own_ref, x_ref, hmat_ref, loc_ref, inner_ref, head_ref, inc_ref, keep_ref, give_ref):
     total = [head_ref[v] for v in range(V)]
     total = edge_terms(first_ref, second_ref, own_ref, x_ref, hmat_ref, loc_ref, HEAD, total)
     for v in range(V):
@@ -243,13 +236,13 @@
         give_ref[v] = inc_ref[v, pl.ds(pl.multiple_of(where_ref[9], 32), 32)]
 
 
-def edge_part(where, first, second, own, x, hmat, loc, inner, head, after):
+def edge_part(where, first, second, own, x, hmat, loc, inner, head):
     return call(
         edge_kernel,
         (sds(V, 256, 128), sds(V, 32, 128), sds(V, 32, 128)),
-        ins=[SMEM] + [VMEM] * 9,
+        ins=[SMEM] + [VMEM] * 8,
         outs=(VMEM,) * 3,
-    )(where, first, second, own, x, hmat, loc, inner, head, after)
+    )(where, first, second, own, x, hmat, loc, inner, head)
 
 
 def tent(distance):
@@ -569,20 +562,19 @@
     flat = alpha.reshape(members, 256, 128)
     flat_ens = ensemble.reshape(members, V, 256, 128)
 
-    send_first, send_second, token = send_part(where, alpha.reshape(members, 4, 64, 128))
+    send_first, send_second, own_obs = send_part(
+        where, obs_count, obs_col, obs_lev, innovation, obs_weight, alpha.reshape(members, 4, 64, 128)
+    )
     first, second = swap_first(send_first), swap_second(send_second)
-    inner, own_edge, x, smat, hmat, token, send_first, send_second = own_part(where, flat, flat_ens, loc_vert, token)
-    first_rest, second_rest = swap_first(send_first), swap_second(send_second)
-    own_obs = observations(obs_count, obs_col, obs_lev, innovation, obs_weight, token)
-    here_obs = swap_first(own_obs)
-
-    head = head_part(first, second, own_edge, x, hmat, loc_vert)
-    inc, keep, give = edge_part(
-        where, first_rest, second_rest, own_edge, x, hmat, loc_vert, inner, head, here_obs
-    )
-    near = swap_first(keep + swap_core(give))
+    inner, own_edge, x, smat, hmat, send_first, send_second = own_part(where, flat, flat_ens, loc_vert, own_obs)
+    rest = send_first.reshape(-1, 128), send_second.reshape(-1, 128)
+    first_rest, second_rest = swap_first(rest[0]), swap_second(rest[1])
+    here_obs = first[64 * HEAD :]
     there_obs = swap_core(here_obs)
     wown, wnear, lev, innov, weight = weights(where, own_obs, here_obs, there_obs)
+    head = head_part(first, second, own_edge, x, hmat, loc_vert, lev)
+    inc, keep, give = edge_part(where, first_rest, second_rest, own_edge, x, hmat, loc_vert, inner, head)
+    near = swap_first(keep + swap_core(give))
     mine = mine_part(where, inc, wown, wnear, lev)
     vals = round_mem(values(where, mine, near, wown, wnear, lev))
     c, back_first, back_second = adjoint(where, vals, innov, weight, lev, wown, wnear, x)

time: 103 us -> 108 us (1.049)
  the two profiles are of different devices: /device:TPU:32 before, /device:TPU:6 now
where the time goes in v6:
time: 108 us; the launch traced here: 107 us
  starting transfers between devices  40.4 us (37%)
  waiting for transfers between devices  36.7 us (34%)
  Pallas kernels  21.9 us (20%)
  local copies, waits for them, and re-layouts  7.07 us (7%)
    ppermute x4, waiting for transfers between devices, swap_second(): return lax.ppermute(x, ('mem', 'tile'), SECOND)  23.6 us
    ppermute x4, starting transfers between devices, swap_second(): return lax.ppermute(x, ('mem', 'tile'), SECOND)  22 us
    ppermute x5, starting transfers between devices, swap_first(): return lax.ppermute(x, ('mem', 'tile'), FIRST)  12.8 us
    ppermute x5, waiting for transfers between devices, swap_first(): return lax.ppermute(x, ('mem', 'tile'), FIRST)  7.76 us
    unnamed x20, local copies, waits for them, and re-layouts  6.98 us
    pallas_call x1, Pallas kernels, back_part(): call(back_kernel, (sds(members, 256, 128), sds(members, 128, 128), sds(me...  5.31 us
    ppermute x3, starting transfers between devices, round_mem(): lax.ppermute(mine, 'mem', [(i, (i + shift) % size) for i in range(size)])  4.83 us
    pallas_call x1, Pallas kernels, own_part(): call(own_kernel, (sds(V, 128, 128), sds(members, 128, 128), sds(members,...  3.78 us
  transfers between devices with their start and end apart: 14, of which 9 were waited for; matrix products, arithmetic and copies ran while one was open for 0% of the time, Pallas kernels for 14%

profile of v6, /device:TPU:6, one launch (start us, length us, event | category | flops | bytes accessed | tf_op | source)
XLA Modules:
  0.0 106.9 jit_solution(2781150293737746130)
XLA Ops:
  0.7 1.3 %copy-done.2 = bf16[20,8,32,128]{3,2,1,0:T(8,128)(2,1)S(1)} copy-done((bf16[20,8,32,128]{3,2,1,0:T(8,128)(2,1)S(1)}, bf16[20,8,32,128]{3,2,1,0:T(8,128)(2,1)}, u32[]{:S(2)}) %copy-start.2) | copy-done | bytes 1310744
  4.9 1.0 shard_map.82
  5.9 5.2 %collective-permute-start.2 = (f32[840,128]{1,0:T(8,128)S(1)}, f32[840,128]{1,0:T(8,128)S(1)}, u32[]{:S(2)}, u32[]{:S(2)}) collective-permute-start(f32[840,128]{1,0:T(8,128)S(1)} %get-tuple-element.37), channel_id=1, source_target_pairs={{0,1},{1,0},{2,3},{3,2},{4,5},{5,4},{6,7},{7,6},{8,9},{9,8},{10,11... | collective-permute-start | bytes 1290248 | tf_op jit(solution)/shard_map/ppermute | solution.py:522
  11.0 9.1 %collective-permute-start.3 = (f32[768,128]{1,0:T(8,128)S(1)}, f32[768,128]{1,0:T(8,128)S(1)}, u32[]{:S(2)}, u32[]{:S(2)}) collective-permute-start(f32[768,128]{1,0:T(8,128)S(1)} %get-tuple-element.38), channel_id=1, source_target_pairs={{1,2},{2,1},{3,4},{4,3},{5,6},{6,5},{7,8},{8,7},{9,10},{10,9},{11,... | collective-permute-start | bytes 1179656 | tf_op jit(solution)/shard_map/ppermute | solution.py:526
  20.2 2.1 %copy-done = bf16[20,3,8,32,128]{4,3,2,1,0:T(8,128)(2,1)S(1)} copy-done((bf16[20,3,8,32,128]{4,3,2,1,0:T(8,128)(2,1)S(1)}, bf16[20,3,8,32,128]{4,3,2,1,0:T(8,128)(2,1)}, u32[]{:S(2)}) %copy-start) | copy-done | bytes 3932184
  23.0 3.8 %shard_map.83 = (f32[3,128,128]{2,1,0:T(8,128)S(1)}, f32[20,128,128]{2,1,0:T(8,128)S(1)}, bf16[20,3,128,128]{3,2,1,0:T(8,128)(2,1)S(1)}, bf16[256,256]{1,0:T(8,1...) custom-call(s32[11]{0:T(128)S(1)} %stack.51.where_ref, ...), custom_call_target="tpu_custom_call" | custom-call | flops 1000000 | bytes 1000000 | tf_op jit(solution)/shard_map/pallas_call | solution.py:172
  26.8 1.9 %collective-permute-start.1 = (f32[512,128]{1,0:T(8,128)S(1)}, f32[512,128]{1,0:T(8,128)S(1)}, u32[]{:S(2)}, u32[]{:S(2)}) collective-permute-start(f32[512,128]{1,0:T(8,128)S(1)} %bitcast.24), channel_id=1, source_target_pairs={{1,2},{2,1},{3,4},{4,3},{5,6},{6,5},{7,8},{8,7},{9,10},{10,9},{11,... | collective-permute-start | bytes 786440 | tf_op jit(solution)/shard_map/ppermute | solution.py:526
  28.8 1.9 %collective-permute-start = (f32[512,128]{1,0:T(8,128)S(1)}, f32[512,128]{1,0:T(8,128)S(1)}, u32[]{:S(2)}, u32[]{:S(2)}) collective-permute-start(f32[512,128]{1,0:T(8,128)S(1)} %bitcast.23), channel_id=1, source_target_pairs={{0,1},{1,0},{2,3},{3,2},{4,5},{5,4},{6,7},{7,6},{8,9},{9,8},{10,11... | collective-permute-start | bytes 786440 | tf_op jit(solution)/shard_map/ppermute | solution.py:522
  32.1 1.1 %shard_map.84 = (bf16[3,320,768]{2,1,0:T(8,128)(2,1)S(1)}, bf16[2,3,64,768]{3,2,1,0:T(8,128)(2,1)S(1)}, f32[9,768]{1,0:T(8,128)S(1)}, f32[9,768]{1,0:T(8,128)S(1)}, f32[9,768]{1,0:T(8,128)S(1)}) custom-call(s32[11]{0:T(128)S(1)} %stack.51.where_ref, f32[72,128]{1,0:T(8,128)S(1)} %get-tuple-element.30.after_ref.own_ref, f32[72,128]{1,0:T(8,128)S(1)} %slice.4.here_ref, ...), custom_call_target="tpu_custom_call" | custom-call | flops 1000000 | bytes 1000000 | tf_op jit(solution)/shard_map/pallas_call | solution.py:298
  33.3 1.4 %shard_map.85.head_ref = f32[3,128,128]{2,1,0:T(8,128)S(1)} custom-call(f32[840,128]{1,0:T(8,128)S(1)} %collective-permute-done.2.first_ref, f32[768,128]{1,0:T(8,128)S(1)} %collective-permute-done.3.second_ref, f32[20,128,128]{2,1,0:T(8,128)S(1)} %get-tuple-element.33.own_ref, bf16[20,3,128,128]{3,2,1,0:T(8,128)(2,1)S(1)} %get-tuple-element.34.x_ref, ...), custom_call_target="tpu_custom_call" | custom-call | flops 1000000 | bytes 1000000 | tf_op jit(solution)/shard_map/pallas_call | solution.py:223
  34.7 14.0 %collective-permute-done.1.second_ref = f32[512,128]{1,0:T(8,128)S(1)} collective-permute-done((f32[512,128]{1,0:T(8,128)S(1)}, f32[512,128]{1,0:T(8,128)S(1)}, u32[]{:S(2)}, u32[]{:S(2)}) %collective-permute-start.1) | collective-permute-done | bytes 262176 | tf_op jit(solution)/shard_map/ppermute | solution.py:526
  48.7 1.6 %shard_map.86 = (f32[3,256,128]{2,1,0:T(8,128)S(1)}, f32[3,32,128]{2,1,0:T(8,128)S(1)}, f32[3,32,128]{2,1,0:T(8,128)S(1)}) custom-call(s32[11]{0:T(128)S(1)} %stack.51.where_ref, f32[512,128]{1,0:T(8,128)S(1)} %collective-permute-done.first_ref, f32[512,128]{1,0:T(8,128)S(1)} %collective-permute-done.1.second_ref, ...), custom_call_target="tpu_custom_call" | custom-call | flops 1000000 | bytes 1000000 | tf_op jit(solution)/shard_map/pallas_call | solution.py:240
  50.5 1.1 %collective-permute-done.5 = f32[3,32,128]{2,1,0:T(8,128)S(1)} collective-permute-done((f32[3,32,128]{2,1,0:T(8,128)S(1)}, f32[3,32,128]{2,1,0:T(8,128)S(1)}, u32[]{:S(2)}, u32[]{:S(2)}) %collective-permute-start.5) | collective-permute-done | bytes 49184 | tf_op jit(solution)/shard_map/ppermute | solution.py:530
  51.7 1.9 %collective-permute-start.6 = (f32[3,32,128]{2,1,0:T(8,128)S(1)}, f32[3,32,128]{2,1,0:T(8,128)S(1)}, u32[]{:S(2)}, u32[]{:S(2)}) collective-permute-start(f32[3,32,128]{2,1,0:T(8,128)S(1)} %add.21), channel_id=1, source_target_pairs={{0,1},{1,0},{2,3},{3,2},{4,5},{5,4},{6,7},{7,6},{8,9},{9,8},{10,11... | collective-permute-start | bytes 147464 | tf_op jit(solution)/shard_map/ppermute | solution.py:522
  53.6 1.7 %shard_map.87.mine_ref = f32[9,768]{1,0:T(8,128)S(1)} custom-call(s32[11]{0:T(128)S(1)} %stack.51.where_ref, f32[3,256,128]{2,1,0:T(8,128)S(1)} %get-tuple-element.40.inc_ref, bf16[3,320,768]{2,1,0:T(8,128)(2,1)S(1)} %get-tuple-element.41.wown_ref, bf16[2,3,64,768]{3,2,1,0:T(8,128)(2,1)S(1)} %get-tuple-element.42.wnear_ref, ...), custom_call_target="tpu_custom_call" | custom-call | flops 1000000 | bytes 1000000 | tf_op jit(solution)/shard_map/pallas_call | solution.py:336
  55.3 3.4 %collective-permute-done.6.near_ref = f32[3,32,128]{2,1,0:T(8,128)S(1)} collective-permute-done((f32[3,32,128]{2,1,0:T(8,128)S(1)}, f32[3,32,128]{2,1,0:T(8,128)S(1)}, u32[]{:S(2)}, u32[]{:S(2)}) %collective-permute-start.6) | collective-permute-done | bytes 49184 | tf_op jit(solution)/shard_map/ppermute | solution.py:522
  58.7 1.4 %shard_map.88.v0 = f32[54,128]{1,0:T(8,128)S(1)} custom-call(s32[11]{0:T(128)S(1)} %stack.51.where_ref, f32[9,768]{1,0:T(8,128)S(1)} %shard_map.87.mine_ref, f32[3,32,128]{2,1,0:T(8,128)S(1)} %collective-permute-done.6.near_ref, bf16[3,320,768]{2,1,0:T(8,128)(2,1)S(1)} %get-tuple-element.41.wown_ref, ...), custom_call_target="tpu_custom_call" | custom-call | flops 1000000 | bytes 1000000 | tf_op jit(solution)/shard_map/pallas_call | solution.py:364
  60.0 2.5 %collective-permute-start.9 = (f32[54,128]{1,0:T(8,128)S(1)}, f32[54,128]{1,0:T(8,128)S(1)}, u32[]{:S(2)}, u32[]{:S(2)}) collective-permute-start(f32[54,128]{1,0:T(8,128)S(1)} %shard_map.88.v0), channel_id=1, source_target_pairs={{0,192},{64,0},{128,64},{192,128},{1,193},{65,1},{129,65},{193,129... | collective-permute-start | bytes 82952 | tf_op jit(solution)/shard_map/ppermute | solution.py:536
  62.5 2.3 %collective-permute-start.8 = (f32[54,128]{1,0:T(8,128)S(1)}, f32[54,128]{1,0:T(8,128)S(1)}, u32[]{:S(2)}, u32[]{:S(2)}) collective-permute-start(f32[54,128]{1,0:T(8,128)S(1)} %shard_map.88.v0), channel_id=1, source_target_pairs={{0,128},{64,192},{128,0},{192,64},{1,129},{65,193},{129,1},{193,65... | collective-permute-start | bytes 82952 | tf_op jit(solution)/shard_map/ppermute | solution.py:536
  64.8 2.1 %collective-permute-done.8.v2 = f32[54,128]{1,0:T(8,128)S(1)} collective-permute-done((f32[54,128]{1,0:T(8,128)S(1)}, f32[54,128]{1,0:T(8,128)S(1)}, u32[]{:S(2)}, u32[]{:S(2)}) %collective-permute-start.8) | collective-permute-done | bytes 27680 | tf_op jit(solution)/shard_map/ppermute | solution.py:536
  67.0 1.1 %collective-permute-done.7.v1 = f32[54,128]{1,0:T(8,128)S(1)} collective-permute-done((f32[54,128]{1,0:T(8,128)S(1)}, f32[54,128]{1,0:T(8,128)S(1)}, u32[]{:S(2)}, u32[]{:S(2)}) %collective-permute-start.7) | collective-permute-done | bytes 27680 | tf_op jit(solution)/shard_map/ppermute | solution.py:536
  68.1 1.9 %shard_map.89 = (f32[3,256,128]{2,1,0:T(8,128)S(1)}, f32[12,64,128]{2,1,0:T(8,128)S(1)}, f32[12,64,128]{2,1,0:T(8,128)S(1)}) custom-call(s32[11]{0:T(128)S(1)} %stack.51.where_ref, f32[54,128]{1,0:T(8,128)S(1)} %shard_map.88.v0, f32[54,128]{1,0:T(8,128)S(1)} %collective-permute-done.7.v1, f32[54,128]{1,0:T(8,128)S(1)} %collective-permute-done.8.v2, ...), custom_call_target="tpu_custom_call" | custom-call | flops 1000000 | bytes 1000000 | tf_op jit(solution)/shard_map/pallas_call | solution.py:404
  70.1 1.9 %collective-permute-start.12 = (f32[12,64,128]{2,1,0:T(8,128)S(1)}, f32[12,64,128]{2,1,0:T(8,128)S(1)}, u32[]{:S(2)}, u32[]{:S(2)}) collective-permute-start(f32[12,64,128]{2,1,0:T(8,128)S(1)} %get-tuple-element.52), channel_id=1, source_target_pairs={{0,1},{1,0},{2,3},{3,2},{4,5},{5,4},{6,7},{7,6},{8,9},{9,8},{10,11... | collective-permute-start | bytes 1179656 | tf_op jit(solution)/shard_map/ppermute | solution.py:522
  72.0 6.1 %collective-permute-start.13 = (f32[12,64,128]{2,1,0:T(8,128)S(1)}, f32[12,64,128]{2,1,0:T(8,128)S(1)}, u32[]{:S(2)}, u32[]{:S(2)}) collective-permute-start(f32[12,64,128]{2,1,0:T(8,128)S(1)} %get-tuple-element.53), channel_id=1, source_target_pairs={{1,2},{2,1},{3,4},{4,3},{5,6},{6,5},{7,8},{8,7},{9,10},{10,9},{11,... | collective-permute-start | bytes 1179656 | tf_op jit(solution)/shard_map/ppermute | solution.py:526
  78.1 5.3 %shard_map.90 = (f32[20,256,128]{2,1,0:T(8,128)}, f32[20,128,128]{2,1,0:T(8,128)S(1)}, f32[8,64,128]{2,1,0:T(8,128)S(1)}, f32[8,64,128]{2,1,0:T(8,128)S(1)}) custom-call(s32[11]{0:T(128)S(1)} %stack.51.where_ref, bf16[20,256,128]{2,1,0:T(8,128)(2,1)S(1)} %bitcast.22, bf16[20,3,256,128]{3,2,1,0:T(8,128)(2,1)S(1)} %bitcast.19, ...), custom_call_target="tpu_custom_call" | custom-call | flops 1000000 | bytes 1000000 | tf_op jit(solution)/shard_map/pallas_call | solution.py:436
  83.4 1.9 %collective-permute-start.10 = (f32[8,64,128]{2,1,0:T(8,128)S(1)}, f32[8,64,128]{2,1,0:T(8,128)S(1)}, u32[]{:S(2)}, u32[]{:S(2)}) collective-permute-start(f32[8,64,128]{2,1,0:T(8,128)S(1)} %get-tuple-element.49), channel_id=1, source_target_pairs={{0,1},{1,0},{2,3},{3,2},{4,5},{5,4},{6,7},{7,6},{8,9},{9,8},{10,11... | collective-permute-start | bytes 786440 | tf_op jit(solution)/shard_map/ppermute | solution.py:522
  85.4 4.9 %collective-permute-start.11 = (f32[8,64,128]{2,1,0:T(8,128)S(1)}, f32[8,64,128]{2,1,0:T(8,128)S(1)}, u32[]{:S(2)}, u32[]{:S(2)}) collective-permute-start(f32[8,64,128]{2,1,0:T(8,128)S(1)} %get-tuple-element.50), channel_id=1, source_target_pairs={{1,2},{2,1},{3,4},{4,3},{5,6},{6,5},{7,8},{8,7},{9,10},{10,9},{11,... | collective-permute-start | bytes 786440 | tf_op jit(solution)/shard_map/ppermute | solution.py:526
  90.2 6.9 %collective-permute-done.13.second_ref = f32[12,64,128]{2,1,0:T(8,128)S(1)} collective-permute-done((f32[12,64,128]{2,1,0:T(8,128)S(1)}, f32[12,64,128]{2,1,0:T(8,128)S(1)}, u32[]{:S(2)}, u32[]{:S(2)}) %collective-permute-start.13) | collective-permute-done | bytes 393248 | tf_op jit(solution)/shard_map/ppermute | solution.py:526
  97.1 1.4 %shard_map.91.unused_ref = f32[20,4,64,128]{3,2,1,0:T(8,128)} custom-call(f32[12,64,128]{2,1,0:T(8,128)S(1)} %collective-permute-done.12.first_ref, f32[12,64,128]{2,1,0:T(8,128)S(1)} %collective-permute-done.13.second_ref, f32[20,128,128]{2,1,0:T(8,128)S(1)} %get-tuple-element.51.edge_ref, ...), custom_call_target="tpu_custom_call", output_to_operand_aliasing={{}: (5, {})} | custom-call | flops 1000000 | bytes 1000000 | tf_op jit(solution)/shard_map/pallas_call | solution.py:484
  98.6 4.4 %collective-permute-done.10.first_ref = f32[8,64,128]{2,1,0:T(8,128)S(1)} collective-permute-done((f32[8,64,128]{2,1,0:T(8,128)S(1)}, f32[8,64,128]{2,1,0:T(8,128)S(1)}, u32[]{:S(2)}, u32[]{:S(2)}) %collective-permute-start.10) | collective-permute-done | bytes 262176 | tf_op jit(solution)/shard_map/ppermute | solution.py:522
  102.9 2.7 %collective-permute-done.11.second_ref = f32[8,64,128]{2,1,0:T(8,128)S(1)} collective-permute-done((f32[8,64,128]{2,1,0:T(8,128)S(1)}, f32[8,64,128]{2,1,0:T(8,128)S(1)}, u32[]{:S(2)}, u32[]{:S(2)}) %collective-permute-start.11) | collective-permute-done | bytes 262176 | tf_op jit(solution)/shard_map/ppermute | solution.py:526
  105.7 1.3 %shard_map.92 = f32[20,4,64,128]{3,2,1,0:T(8,128)} custom-call(f32[8,64,128]{2,1,0:T(8,128)S(1)} %collective-permute-done.10.first_ref, f32[8,64,128]{2,1,0:T(8,128)S(1)} %collective-permute-done.11.second_ref, f32[20,128,128]{2,1,0:T(8,128)S(1)} %get-tuple-element.51.edge_ref, ...), custom_call_target="tpu_custom_call", output_to_operand_aliasing={{}: (5, {})} | custom-call | flops 1000000 | bytes 1000000 | tf_op jit(solution)/shard_map/pallas_call | solution.py:484
  (30 shorter events, 5.3 us)
Async XLA Ops:
  0.7 1.3 %copy-start.2 = (bf16[20,8,32,128]{3,2,1,0:T(8,128)(2,1)S(1)}, bf16[20,8,32,128]{3,2,1,0:T(8,128)(2,1)}, u32[]{:S(2)}) copy-start(bf16[20,8,32,128]{3,2,1,0:T(8,128)(2,1)} %param.8) | copy-start | bytes 3932164
  2.1 0.7 copy-start.6
  2.8 0.7 copy-start.7
  3.5 0.7 copy-start.8
  4.2 0.7 copy-start.9
  4.9 15.3 %copy-start.3 = (bf16[20,8,32,128]{3,2,1,0:T(8,128)(2,1)S(1)}, bf16[20,8,32,128]{3,2,1,0:T(8,128)(2,1)}, u32[]{:S(2)}) copy-start(bf16[20,8,32,128]{3,2,1,0:T(8,128)(2,1)} %param.8) | copy-start | bytes 3932164
  5.9 24.8 %collective-permute-start.2 = (f32[840,128]{1,0:T(8,128)S(1)}, f32[840,128]{1,0:T(8,128)S(1)}, u32[]{:S(2)}, u32[]{:S(2)}) collective-permute-start(f32[840,128]{1,0:T(8,128)S(1)} %get-tuple-element.37), channel_id=1, source_target_pairs={{0,1},{1,0},{2,3},{3,2},{4,5},{5,4},{6,7},{7,6},{8,9},{9,8},{10,11... | collective-permute-start | bytes 1290248 | tf_op jit(solution)/shard_map/ppermute | solution.py:522
  11.0 22.2 %collective-permute-start.3 = (f32[768,128]{1,0:T(8,128)S(1)}, f32[768,128]{1,0:T(8,128)S(1)}, u32[]{:S(2)}, u32[]{:S(2)}) collective-permute-start(f32[768,128]{1,0:T(8,128)S(1)} %get-tuple-element.38), channel_id=1, source_target_pairs={{1,2},{2,1},{3,4},{4,3},{5,6},{6,5},{7,8},{8,7},{9,10},{10,9},{11,... | collective-permute-start | bytes 1179656 | tf_op jit(solution)/shard_map/ppermute | solution.py:526
  20.2 2.1 %copy-start = (bf16[20,3,8,32,128]{4,3,2,1,0:T(8,128)(2,1)S(1)}, bf16[20,3,8,32,128]{4,3,2,1,0:T(8,128)(2,1)}, u32[]{:S(2)}) copy-start(bf16[20,3,8,32,128]{4,3,2,1,0:T(8,128)(2,1)} %param.9) | copy-start | bytes 11796484
  22.3 0.8 copy-start.4
  26.8 21.9 %collective-permute-start.1 = (f32[512,128]{1,0:T(8,128)S(1)}, f32[512,128]{1,0:T(8,128)S(1)}, u32[]{:S(2)}, u32[]{:S(2)}) collective-permute-start(f32[512,128]{1,0:T(8,128)S(1)} %bitcast.24), channel_id=1, source_target_pairs={{1,2},{2,1},{3,4},{4,3},{5,6},{6,5},{7,8},{8,7},{9,10},{10,9},{11,... | collective-permute-start | bytes 786440 | tf_op jit(solution)/shard_map/ppermute | solution.py:526
  28.8 20.0 %collective-permute-start = (f32[512,128]{1,0:T(8,128)S(1)}, f32[512,128]{1,0:T(8,128)S(1)}, u32[]{:S(2)}, u32[]{:S(2)}) collective-permute-start(f32[512,128]{1,0:T(8,128)S(1)} %bitcast.23), channel_id=1, source_target_pairs={{0,1},{1,0},{2,3},{3,2},{4,5},{5,4},{6,7},{7,6},{8,9},{9,8},{10,11... | collective-permute-start | bytes 786440 | tf_op jit(solution)/shard_map/ppermute | solution.py:522
  30.7 1.4 %collective-permute-start.4 = (f32[72,128]{1,0:T(8,128)S(1)}, f32[72,128]{1,0:T(8,128)S(1)}, u32[]{:S(2)}, u32[]{:S(2)}) collective-permute-start(f32[72,128]{1,0:T(8,128)S(1)} %slice.4.here_ref), channel_id=1, source_target_pairs={{0,64},{64,0},{128,192},{192,128},{1,65},{65,1},{129,193},{193,129... | collective-permute-start | bytes 110600 | tf_op jit(solution)/shard_map/ppermute | solution.py:530
  50.3 1.3 %collective-permute-start.5 = (f32[3,32,128]{2,1,0:T(8,128)S(1)}, f32[3,32,128]{2,1,0:T(8,128)S(1)}, u32[]{:S(2)}, u32[]{:S(2)}) collective-permute-start(f32[3,32,128]{2,1,0:T(8,128)S(1)} %get-tuple-element.44), channel_id=1, source_target_pairs={{0,64},{64,0},{128,192},{192,128},{1,65},{65,1},{129,193},{193,129... | collective-permute-start | bytes 147464 | tf_op jit(solution)/shard_map/ppermute | solution.py:530
  51.7 7.0 %collective-permute-start.6 = (f32[3,32,128]{2,1,0:T(8,128)S(1)}, f32[3,32,128]{2,1,0:T(8,128)S(1)}, u32[]{:S(2)}, u32[]{:S(2)}) collective-permute-start(f32[3,32,128]{2,1,0:T(8,128)S(1)} %add.21), channel_id=1, source_target_pairs={{0,1},{1,0},{2,3},{3,2},{4,5},{5,4},{6,7},{7,6},{8,9},{9,8},{10,11... | collective-permute-start | bytes 147464 | tf_op jit(solution)/shard_map/ppermute | solution.py:522
  60.0 4.8 %collective-permute-start.9 = (f32[54,128]{1,0:T(8,128)S(1)}, f32[54,128]{1,0:T(8,128)S(1)}, u32[]{:S(2)}, u32[]{:S(2)}) collective-permute-start(f32[54,128]{1,0:T(8,128)S(1)} %shard_map.88.v0), channel_id=1, source_target_pairs={{0,192},{64,0},{128,64},{192,128},{1,193},{65,1},{129,65},{193,129... | collective-permute-start | bytes 82952 | tf_op jit(solution)/shard_map/ppermute | solution.py:536
  62.5 4.5 %collective-permute-start.8 = (f32[54,128]{1,0:T(8,128)S(1)}, f32[54,128]{1,0:T(8,128)S(1)}, u32[]{:S(2)}, u32[]{:S(2)}) collective-permute-start(f32[54,128]{1,0:T(8,128)S(1)} %shard_map.88.v0), channel_id=1, source_target_pairs={{0,128},{64,192},{128,0},{192,64},{1,129},{65,193},{129,1},{193,65... | collective-permute-start | bytes 82952 | tf_op jit(solution)/shard_map/ppermute | solution.py:536
  64.8 3.3 %collective-permute-start.7 = (f32[54,128]{1,0:T(8,128)S(1)}, f32[54,128]{1,0:T(8,128)S(1)}, u32[]{:S(2)}, u32[]{:S(2)}) collective-permute-start(f32[54,128]{1,0:T(8,128)S(1)} %shard_map.88.v0), channel_id=1, source_target_pairs={{0,64},{64,128},{128,192},{192,0},{1,65},{65,129},{129,193},{193,1... | collective-permute-start | bytes 82952 | tf_op jit(solution)/shard_map/ppermute | solution.py:536
  68.1 10.0 %copy-start.1 = (bf16[20,3,8,32,128]{4,3,2,1,0:T(8,128)(2,1)S(1)}, bf16[20,3,8,32,128]{4,3,2,1,0:T(8,128)(2,1)}, u32[]{:S(2)}) copy-start(bf16[20,3,8,32,128]{4,3,2,1,0:T(8,128)(2,1)} %param.9) | copy-start | bytes 11796484
  68.1 10.0 %copy-start.5 = (bf16[128,128]{1,0:T(8,128)(2,1)S(1)}, bf16[128,128]{1,0:T(8,128)(2,1)}, u32[]{:S(2)}) copy-start(bf16[128,128]{1,0:T(8,128)(2,1)} %loc_ref.11) | copy-start | bytes 98308
  70.1 20.2 %collective-permute-start.12 = (f32[12,64,128]{2,1,0:T(8,128)S(1)}, f32[12,64,128]{2,1,0:T(8,128)S(1)}, u32[]{:S(2)}, u32[]{:S(2)}) collective-permute-start(f32[12,64,128]{2,1,0:T(8,128)S(1)} %get-tuple-element.52), channel_id=1, source_target_pairs={{0,1},{1,0},{2,3},{3,2},{4,5},{5,4},{6,7},{7,6},{8,9},{9,8},{10,11... | collective-permute-start | bytes 1179656 | tf_op jit(solution)/shard_map/ppermute | solution.py:522
  72.0 25.1 %collective-permute-start.13 = (f32[12,64,128]{2,1,0:T(8,128)S(1)}, f32[12,64,128]{2,1,0:T(8,128)S(1)}, u32[]{:S(2)}, u32[]{:S(2)}) collective-permute-start(f32[12,64,128]{2,1,0:T(8,128)S(1)} %get-tuple-element.53), channel_id=1, source_target_pairs={{1,2},{2,1},{3,4},{4,3},{5,6},{6,5},{7,8},{8,7},{9,10},{10,9},{11,... | collective-permute-start | bytes 1179656 | tf_op jit(solution)/shard_map/ppermute | solution.py:526
  83.4 19.5 %collective-permute-start.10 = (f32[8,64,128]{2,1,0:T(8,128)S(1)}, f32[8,64,128]{2,1,0:T(8,128)S(1)}, u32[]{:S(2)}, u32[]{:S(2)}) collective-permute-start(f32[8,64,128]{2,1,0:T(8,128)S(1)} %get-tuple-element.49), channel_id=1, source_target_pairs={{0,1},{1,0},{2,3},{3,2},{4,5},{5,4},{6,7},{7,6},{8,9},{9,8},{10,11... | collective-permute-start | bytes 786440 | tf_op jit(solution)/shard_map/ppermute | solution.py:522
  85.4 20.3 %collective-permute-start.11 = (f32[8,64,128]{2,1,0:T(8,128)S(1)}, f32[8,64,128]{2,1,0:T(8,128)S(1)}, u32[]{:S(2)}, u32[]{:S(2)}) collective-permute-start(f32[8,64,128]{2,1,0:T(8,128)S(1)} %get-tuple-element.50), channel_id=1, source_target_pairs={{1,2},{2,1},{3,4},{4,3},{5,6},{6,5},{7,8},{8,7},{9,10},{10,9},{11,... | collective-permute-start | bytes 786440 | tf_op jit(solution)/shard_map/ppermute | solution.py:526

commit v7 on v6

--- a/solution.py
+++ b/solution.py
@@ -16,12 +16,23 @@
 OBS = 72
 
 TILES = 64
-EVEN = [(i, i ^ 1) for i in range(TILES)]
-ODD = [(i, ((i - 1) ^ 1) + 1) for i in range(1, TILES - 1)] + [(0, 0), (TILES - 1, TILES - 1)]
-
 MEMS = 4
-FIRST = [(TILES * m + a, TILES * m + b) for m in range(MEMS) for a, b in (ODD if m % 2 else EVEN)]
-SECOND = [(TILES * m + a, TILES * m + b) for m in range(MEMS) for a, b in (EVEN if m % 2 else ODD)]
+
+
+def swap_pairs(odd_core):
+    pairs = []
+    for m in range(MEMS):
+        for t in range(TILES):
+            beside = ((t - 1) ^ 1) + 1 if m % 2 == odd_core else t ^ 1
+            if 0 <= beside < TILES:
+                pairs.append((TILES * m + t, TILES * m + beside))
+            else:
+                pairs.append((TILES * m + t, TILES * (m ^ 2) + t))
+    return pairs
+
+
+FIRST = swap_pairs(1)
+SECOND = swap_pairs(0)
 
 
 def nn(a, b):
@@ -47,8 +58,7 @@
     return nt(high, loc) + nt(low, loc)
 
 
-def call(kernel, out, grid=None, ins=None, outs=None, scratch=(), aliases=None, cost=1000000):
-    vmem = pl.BlockSpec(memory_space=pltpu.VMEM)
+def call(kernel, out, grid=None, ins=None, outs=None, scratch=(), aliases=None, cost=1000, vmem=16):
     kw = {}
     if grid is not None:
         kw["grid"] = grid
@@ -56,10 +66,10 @@
         kernel,
         out_shape=out,
         in_specs=ins,
-        out_specs=outs if outs is not None else jax.tree.map(lambda o: vmem, out),
+        out_specs=outs if outs is not None else jax.tree.map(lambda o: VMEM, out),
         scratch_shapes=scratch,
         input_output_aliases=aliases or {},
-        compiler_params=pltpu.CompilerParams(vmem_limit_bytes=16 * 1024 * 1024),
+        compiler_params=pltpu.CompilerParams(vmem_limit_bytes=vmem * 1024 * 1024),
         cost_estimate=pl.CostEstimate(flops=cost, bytes_accessed=cost, transcendentals=0),
         **kw,
     )
@@ -72,6 +82,7 @@
 ANY = pl.BlockSpec(memory_space=pl.ANY)
 SMEM = pl.BlockSpec(memory_space=pltpu.SMEM)
 VMEM = pl.BlockSpec(memory_space=pltpu.VMEM)
+HBM = pl.BlockSpec(memory_space=pltpu.HBM)
 
 
 def smooth(matrix, field):
@@ -108,12 +119,16 @@
                 out_ref[row : row + 1] = total[6 * f + a : 6 * f + a + 1, 128 * v : 128 * v + 128]
 
 
-def send_kernel(where_ref, count_ref, col_ref, lev_ref, innov_ref, weight_ref, quarters_ref, first_ref, second_ref, obs_ref, edges, sems):
+def send_kernel(where_ref, count_ref, *refs):
+    obs_in, (quarters_ref, first_ref, second_ref, obs_ref), obs_here, (edges, sems) = refs[:4], refs[4:8], refs[8:12], refs[12:]
     head = pl.ds(0, HEAD)
     copies = [pltpu.make_async_copy(quarters_ref.at[head, 3 * n], edges.at[n], sems.at[n]) for n in range(2)]
-    for copy in copies:
+    fetches = [pltpu.make_async_copy(obs_in[n], obs_here[n], sems.at[2 + n]) for n in range(4)]
+    for copy in fetches + copies:
         copy.start()
-    sort_observations(count_ref[0], col_ref, lev_ref, innov_ref, weight_ref, obs_ref)
+    for copy in fetches:
+        copy.wait()
+    sort_observations(count_ref[0], *obs_here, obs_ref)
     first_ref[64 * HEAD :] = obs_ref[...]
     for copy in copies:
         copy.wait()
@@ -127,9 +142,11 @@
     return call(
         send_kernel,
         (sds(64 * HEAD + OBS, 128), sds(64 * HEAD, 128), sds(OBS, 128)),
-        ins=[SMEM, SMEM] + [VMEM] * 4 + [ANY],
+        ins=[SMEM, SMEM] + [HBM] * 5,
         outs=(VMEM,) * 3,
-        scratch=[pltpu.VMEM((2, HEAD, 64, 128), BF16), pltpu.SemaphoreType.DMA((2,))],
+        scratch=[pltpu.VMEM(a.shape, a.dtype) for a in (col, lev, innov, weight)]
+        + [pltpu.VMEM((2, HEAD, 64, 128), BF16), pltpu.SemaphoreType.DMA((6,))],
+        vmem=58,
     )(where, count, col, lev, innov, weight, quarters)
 
 

time: 108 us -> 110 us (1.019)
  the two profiles are of different devices: /device:TPU:6 before, /device:TPU:32 now
where the time goes in v7:
time: 110 us; the launch traced here: 109 us
  waiting for transfers between devices  61.9 us (56%)
  Pallas kernels  23.7 us (22%)
  starting transfers between devices  18 us (16%)
  local copies, waits for them, and re-layouts  4.85 us (4%)
    ppermute x4, waiting for transfers between devices, swap_second(): return lax.ppermute(x, ('mem', 'tile'), SECOND)  49.3 us
    ppermute x5, starting transfers between devices, swap_first(): return lax.ppermute(x, ('mem', 'tile'), FIRST)  10.1 us
    ppermute x5, waiting for transfers between devices, swap_first(): return lax.ppermute(x, ('mem', 'tile'), FIRST)  7.3 us
    pallas_call x1, Pallas kernels, back_part(): call(back_kernel, (sds(members, 256, 128), sds(members, 128, 128), sds(me...  5.3 us
    unnamed x14, local copies, waits for them, and re-layouts  4.24 us
    ppermute x4, starting transfers between devices, swap_second(): return lax.ppermute(x, ('mem', 'tile'), SECOND)  4.15 us
    pallas_call x1, Pallas kernels, own_part(): call(own_kernel, (sds(V, 128, 128), sds(members, 128, 128), sds(members,...  3.82 us
    ppermute x3, starting transfers between devices, round_mem(): lax.ppermute(mine, 'mem', [(i, (i + shift) % size) for i in range(size)])  3.39 us
  transfers between devices with their start and end apart: 14, of which 11 were waited for; matrix products, arithmetic and copies ran while one was open for 0% of the time, Pallas kernels for 14%

profile of v7, /device:TPU:32, one launch (start us, length us, event | category | flops | bytes accessed | tf_op | source)
XLA Modules:
  0.0 109.5 jit_solution(11297157811161067369)
XLA Ops:
  0.8 0.6 stack.51.where_ref
  1.4 2.7 %shard_map.82 = (f32[840,128]{1,0:T(8,128)}, f32[768,128]{1,0:T(8,128)}, f32[72,128]{1,0:T(8,128)}) custom-call(s32[11]{0:T(128)} %stack.51.where_ref, s32[1]{0:T(128)S(6)} %copy.13.count_ref, s32[1,2048]{1,0:T(1,128)} %refs_0_.1, s32[1,2048]{1,0:T(1,128)} %refs_1_.1, f32[1,2048]{1,0:T(1,128)} %refs_2_.1, f32[1,2048]{1,0:T(1,128)} %refs_3_.1, ...), custom_call_target="tpu_custom_call" | custom-call | flops 1000 | bytes 1000 | tf_op jit(solution)/shard_map/pallas_call | solution.py:142
  4.1 3.4 %collective-permute-start.2 = (f32[840,128]{1,0:T(8,128)}, f32[840,128]{1,0:T(8,128)S(1)}, u32[]{:S(2)}, u32[]{:S(2)}) collective-permute-start(f32[840,128]{1,0:T(8,128)} %get-tuple-element.37), channel_id=1, source_target_pairs={{0,1},{1,0},{2,3},{3,2},{4,5},{5,4},{6,7},{7,6},{8,9},{9,8},{10,11... | collective-permute-start | bytes 1290248 | tf_op jit(solution)/shard_map/ppermute | solution.py:539
  7.6 2.1 %copy-done = bf16[20,3,8,32,128]{4,3,2,1,0:T(8,128)(2,1)S(1)} copy-done((bf16[20,3,8,32,128]{4,3,2,1,0:T(8,128)(2,1)S(1)}, bf16[20,3,8,32,128]{4,3,2,1,0:T(8,128)(2,1)}, u32[]{:S(2)}) %copy-start) | copy-done | bytes 3932184
  9.7 0.8 copy-done.3
  10.4 0.8 copy-done.5
  11.8 3.8 %shard_map.83 = (f32[3,128,128]{2,1,0:T(8,128)S(1)}, f32[20,128,128]{2,1,0:T(8,128)S(1)}, bf16[20,3,128,128]{3,2,1,0:T(8,128)(2,1)S(1)}, bf16[256,256]{1,0:T(8,1...) custom-call(s32[11]{0:T(128)S(1)} %copy-done.6, ...), custom_call_target="tpu_custom_call" | custom-call | flops 1000 | bytes 1000 | tf_op jit(solution)/shard_map/pallas_call | solution.py:189
  15.6 2.0 %collective-permute-start.1 = (f32[512,128]{1,0:T(8,128)S(1)}, f32[512,128]{1,0:T(8,128)S(1)}, u32[]{:S(2)}, u32[]{:S(2)}) collective-permute-start(f32[512,128]{1,0:T(8,128)S(1)} %bitcast.24), channel_id=1, source_target_pairs={{0,128},{1,2},{2,1},{3,4},{4,3},{5,6},{6,5},{7,8},{8,7},{9,10},{10... | collective-permute-start | bytes 786440 | tf_op jit(solution)/shard_map/ppermute | solution.py:543
  17.6 3.1 %collective-permute-start = (f32[512,128]{1,0:T(8,128)S(1)}, f32[512,128]{1,0:T(8,128)S(1)}, u32[]{:S(2)}, u32[]{:S(2)}) collective-permute-start(f32[512,128]{1,0:T(8,128)S(1)} %bitcast.23), channel_id=1, source_target_pairs={{0,1},{1,0},{2,3},{3,2},{4,5},{5,4},{6,7},{7,6},{8,9},{9,8},{10,11... | collective-permute-start | bytes 786440 | tf_op jit(solution)/shard_map/ppermute | solution.py:539
  20.9 1.2 %collective-permute-done.4.there_ref = f32[72,128]{1,0:T(8,128)S(1)} collective-permute-done((f32[72,128]{1,0:T(8,128)S(1)}, f32[72,128]{1,0:T(8,128)S(1)}, u32[]{:S(2)}, u32[]{:S(2)}) %collective-permute-start.4) | collective-permute-done | bytes 36896 | tf_op jit(solution)/shard_map/ppermute | solution.py:547
  22.1 1.1 %shard_map.84 = (bf16[3,320,768]{2,1,0:T(8,128)(2,1)S(1)}, bf16[2,3,64,768]{3,2,1,0:T(8,128)(2,1)S(1)}, f32[9,768]{1,0:T(8,128)S(1)}, f32[9,768]{1,0:T(8,128)S(1)}, f32[9,768]{1,0:T(8,128)S(1)}) custom-call(s32[11]{0:T(128)S(1)} %copy-done.6, f32[72,128]{1,0:T(8,128)S(1)} %copy-done.5, f32[72,128]{1,0:T(8,128)S(1)} %slice.4.here_ref, ...), custom_call_target="tpu_custom_call" | custom-call | flops 1000 | bytes 1000 | tf_op jit(solution)/shard_map/pallas_call | solution.py:315
  23.3 18.2 %collective-permute-done.3.second_ref = f32[768,128]{1,0:T(8,128)S(1)} collective-permute-done((f32[768,128]{1,0:T(8,128)}, f32[768,128]{1,0:T(8,128)S(1)}, u32[]{:S(2)}, u32[]{:S(2)}) %collective-permute-start.3) | collective-permute-done | bytes 393248 | tf_op jit(solution)/shard_map/ppermute | solution.py:543
  41.5 1.4 %shard_map.85.head_ref = f32[3,128,128]{2,1,0:T(8,128)S(1)} custom-call(f32[840,128]{1,0:T(8,128)S(1)} %collective-permute-done.2.first_ref, f32[768,128]{1,0:T(8,128)S(1)} %collective-permute-done.3.second_ref, f32[20,128,128]{2,1,0:T(8,128)S(1)} %get-tuple-element.33.own_ref, bf16[20,3,128,128]{3,2,1,0:T(8,128)(2,1)S(1)} %get-tuple-element.34.x_ref, ...), custom_call_target="tpu_custom_call" | custom-call | flops 1000 | bytes 1000 | tf_op jit(solution)/shard_map/pallas_call | solution.py:240
  42.9 4.7 %collective-permute-done.1.second_ref = f32[512,128]{1,0:T(8,128)S(1)} collective-permute-done((f32[512,128]{1,0:T(8,128)S(1)}, f32[512,128]{1,0:T(8,128)S(1)}, u32[]{:S(2)}, u32[]{:S(2)}) %collective-permute-start.1) | collective-permute-done | bytes 262176 | tf_op jit(solution)/shard_map/ppermute | solution.py:543
  47.6 1.6 %shard_map.86 = (f32[3,256,128]{2,1,0:T(8,128)S(1)}, f32[3,32,128]{2,1,0:T(8,128)S(1)}, f32[3,32,128]{2,1,0:T(8,128)S(1)}) custom-call(s32[11]{0:T(128)S(1)} %copy-done.6, f32[512,128]{1,0:T(8,128)S(1)} %collective-permute-done.first_ref, f32[512,128]{1,0:T(8,128)S(1)} %collective-permute-done.1.second_ref, f32[20,128,128]{2,1,0:T(8,128)S(1)} %get-tuple-element.33.own_ref, ...), custom_call_target="tpu_custom_call" | custom-call | flops 1000 | bytes 1000 | tf_op jit(solution)/shard_map/pallas_call | solution.py:257
  49.6 0.9 collective-permute-done.5
  50.6 1.7 %shard_map.87.mine_ref = f32[9,768]{1,0:T(8,128)S(1)} custom-call(s32[11]{0:T(128)S(1)} %copy-done.6, f32[3,256,128]{2,1,0:T(8,128)S(1)} %get-tuple-element.40.inc_ref, bf16[3,320,768]{2,1,0:T(8,128)(2,1)S(1)} %get-tuple-element.41.wown_ref, bf16[2,3,64,768]{3,2,1,0:T(8,128)(2,1)S(1)} %get-tuple-element.42.wnear_ref, ...), custom_call_target="tpu_custom_call" | custom-call | flops 1000 | bytes 1000 | tf_op jit(solution)/shard_map/pallas_call | solution.py:353
  52.3 3.3 %collective-permute-done.6.near_ref = f32[3,32,128]{2,1,0:T(8,128)S(1)} collective-permute-done((f32[3,32,128]{2,1,0:T(8,128)S(1)}, f32[3,32,128]{2,1,0:T(8,128)S(1)}, u32[]{:S(2)}, u32[]{:S(2)}) %collective-permute-start.6) | collective-permute-done | bytes 49184 | tf_op jit(solution)/shard_map/ppermute | solution.py:539
  55.6 1.4 %shard_map.88.v0 = f32[54,128]{1,0:T(8,128)S(1)} custom-call(s32[11]{0:T(128)S(1)} %copy-done.6, f32[9,768]{1,0:T(8,128)S(1)} %shard_map.87.mine_ref, f32[3,32,128]{2,1,0:T(8,128)S(1)} %collective-permute-done.6.near_ref, bf16[3,320,768]{2,1,0:T(8,128)(2,1)S(1)} %get-tuple-element.41.wown_ref, bf16[2,3,64,768]{3,2,1,0:T(8,128)(2,1)S(1)} %get-tuple-element.42.wnear_ref, ...), custom_call_target="tpu_custom_call" | custom-call | flops 1000 | bytes 1000 | tf_op jit(solution)/shard_map/pallas_call | solution.py:381
  57.4 2.8 %collective-permute-start.8 = (f32[54,128]{1,0:T(8,128)S(1)}, f32[54,128]{1,0:T(8,128)S(1)}, u32[]{:S(2)}, u32[]{:S(2)}) collective-permute-start(f32[54,128]{1,0:T(8,128)S(1)} %shard_map.88.v0), channel_id=1, source_target_pairs={{0,128},{64,192},{128,0},{192,64},{1,129},{65,193},{129,1},{193,65... | collective-permute-start | bytes 82952 | tf_op jit(solution)/shard_map/ppermute | solution.py:553
  60.4 2.1 %collective-permute-done.8.v2 = f32[54,128]{1,0:T(8,128)S(1)} collective-permute-done((f32[54,128]{1,0:T(8,128)S(1)}, f32[54,128]{1,0:T(8,128)S(1)}, u32[]{:S(2)}, u32[]{:S(2)}) %collective-permute-start.8) | collective-permute-done | bytes 27680 | tf_op jit(solution)/shard_map/ppermute | solution.py:553
  62.5 1.0 collective-permute-done.7.v1
  63.5 1.9 %shard_map.89 = (f32[3,256,128]{2,1,0:T(8,128)S(1)}, f32[12,64,128]{2,1,0:T(8,128)S(1)}, f32[12,64,128]{2,1,0:T(8,128)S(1)}) custom-call(s32[11]{0:T(128)S(1)} %copy-done.6, f32[54,128]{1,0:T(8,128)S(1)} %shard_map.88.v0, f32[54,128]{1,0:T(8,128)S(1)} %collective-permute-done.7.v1, f32[54,128]{1,0:T(8,128)S(1)} %collective-permute-done.8.v2, ...), custom_call_target="tpu_custom_call" | custom-call | flops 1000 | bytes 1000 | tf_op jit(solution)/shard_map/pallas_call | solution.py:421
  65.4 3.5 %collective-permute-start.12 = (f32[12,64,128]{2,1,0:T(8,128)S(1)}, f32[12,64,128]{2,1,0:T(8,128)S(1)}, u32[]{:S(2)}, u32[]{:S(2)}) collective-permute-start(f32[12,64,128]{2,1,0:T(8,128)S(1)} %get-tuple-element.52), channel_id=1, source_target_pairs={{0,1},{1,0},{2,3},{3,2},{4,5},{5,4},{6,7},{7,6},{8,9},{9,8},{10,11... | collective-permute-start | bytes 1179656 | tf_op jit(solution)/shard_map/ppermute | solution.py:539
  68.9 1.4 %collective-permute-start.13 = (f32[12,64,128]{2,1,0:T(8,128)S(1)}, f32[12,64,128]{2,1,0:T(8,128)S(1)}, u32[]{:S(2)}, u32[]{:S(2)}) collective-permute-start(f32[12,64,128]{2,1,0:T(8,128)S(1)} %get-tuple-element.53), channel_id=1, source_target_pairs={{0,128},{1,2},{2,1},{3,4},{4,3},{5,6},{6,5},{7,8},{8,7},{9,10},{10... | collective-permute-start | bytes 1179656 | tf_op jit(solution)/shard_map/ppermute | solution.py:543
  70.4 5.3 %shard_map.90 = (f32[20,256,128]{2,1,0:T(8,128)}, f32[20,128,128]{2,1,0:T(8,128)S(1)}, f32[8,64,128]{2,1,0:T(8,128)S(1)}, f32[8,64,128]{2,1,0:T(8,128)S(1)}) custom-call(s32[11]{0:T(128)S(1)} %copy-done.6, bf16[20,256,128]{2,1,0:T(8,128)(2,1)S(1)} %bitcast.22, bf16[20,3,256,128]{3,2,1,0:T(8,128)(2,1)S(1)} %bitcast.19, ...), custom_call_target="tpu_custom_call" | custom-call | flops 1000 | bytes 1000 | tf_op jit(solution)/shard_map/pallas_call | solution.py:453
  75.7 0.6 collective-permute-start.11
  76.3 3.9 %collective-permute-done.12.first_ref = f32[12,64,128]{2,1,0:T(8,128)S(1)} collective-permute-done((f32[12,64,128]{2,1,0:T(8,128)S(1)}, f32[12,64,128]{2,1,0:T(8,128)S(1)}, u32[]{:S(2)}, u32[]{:S(2)}) %collective-permute-start.12) | collective-permute-done | bytes 393248 | tf_op jit(solution)/shard_map/ppermute | solution.py:539
  80.1 17.7 %collective-permute-done.13.second_ref = f32[12,64,128]{2,1,0:T(8,128)S(1)} collective-permute-done((f32[12,64,128]{2,1,0:T(8,128)S(1)}, f32[12,64,128]{2,1,0:T(8,128)S(1)}, u32[]{:S(2)}, u32[]{:S(2)}) %collective-permute-start.13) | collective-permute-done | bytes 393248 | tf_op jit(solution)/shard_map/ppermute | solution.py:543
  97.8 1.4 %shard_map.91.unused_ref = f32[20,4,64,128]{3,2,1,0:T(8,128)} custom-call(f32[12,64,128]{2,1,0:T(8,128)S(1)} %collective-permute-done.12.first_ref, f32[12,64,128]{2,1,0:T(8,128)S(1)} %collective-permute-done.13.second_ref, f32[20,128,128]{2,1,0:T(8,128)S(1)} %get-tuple-element.51.edge_ref, ...), custom_call_target="tpu_custom_call", output_to_operand_aliasing={{}: (5, {})} | custom-call | flops 1000 | bytes 1000 | tf_op jit(solution)/shard_map/pallas_call | solution.py:501
  99.3 8.8 %collective-permute-done.11.second_ref = f32[8,64,128]{2,1,0:T(8,128)S(1)} collective-permute-done((f32[8,64,128]{2,1,0:T(8,128)S(1)}, f32[8,64,128]{2,1,0:T(8,128)S(1)}, u32[]{:S(2)}, u32[]{:S(2)}) %collective-permute-start.11) | collective-permute-done | bytes 262176 | tf_op jit(solution)/shard_map/ppermute | solution.py:543
  108.0 1.3 %shard_map.92 = f32[20,4,64,128]{3,2,1,0:T(8,128)} custom-call(f32[8,64,128]{2,1,0:T(8,128)S(1)} %collective-permute-done.10.first_ref, f32[8,64,128]{2,1,0:T(8,128)S(1)} %collective-permute-done.11.second_ref, f32[20,128,128]{2,1,0:T(8,128)S(1)} %get-tuple-element.51.edge_ref, ...), custom_call_target="tpu_custom_call", output_to_operand_aliasing={{}: (5, {})} | custom-call | flops 1000 | bytes 1000 | tf_op jit(solution)/shard_map/pallas_call | solution.py:501
  (24 shorter events, 1.9 us)
Async XLA Ops:
  0.0 7.6 %copy-start.2 = (bf16[20,8,32,128]{3,2,1,0:T(8,128)(2,1)S(1)}, bf16[20,8,32,128]{3,2,1,0:T(8,128)(2,1)}, u32[]{:S(2)}) copy-start(bf16[20,8,32,128]{3,2,1,0:T(8,128)(2,1)} %param.8) | copy-start | bytes 3932164
  4.1 16.8 %collective-permute-start.2 = (f32[840,128]{1,0:T(8,128)}, f32[840,128]{1,0:T(8,128)S(1)}, u32[]{:S(2)}, u32[]{:S(2)}) collective-permute-start(f32[840,128]{1,0:T(8,128)} %get-tuple-element.37), channel_id=1, source_target_pairs={{0,1},{1,0},{2,3},{3,2},{4,5},{5,4},{6,7},{7,6},{8,9},{9,8},{10,11... | collective-permute-start | bytes 1290248 | tf_op jit(solution)/shard_map/ppermute | solution.py:539
  7.5 34.0 %collective-permute-start.3 = (f32[768,128]{1,0:T(8,128)}, f32[768,128]{1,0:T(8,128)S(1)}, u32[]{:S(2)}, u32[]{:S(2)}) collective-permute-start(f32[768,128]{1,0:T(8,128)} %get-tuple-element.38), channel_id=1, source_target_pairs={{0,128},{1,2},{2,1},{3,4},{4,3},{5,6},{6,5},{7,8},{8,7},{9,10},{10... | collective-permute-start | bytes 1179656 | tf_op jit(solution)/shard_map/ppermute | solution.py:543
  7.6 2.1 %copy-start = (bf16[20,3,8,32,128]{4,3,2,1,0:T(8,128)(2,1)S(1)}, bf16[20,3,8,32,128]{4,3,2,1,0:T(8,128)(2,1)}, u32[]{:S(2)}) copy-start(bf16[20,3,8,32,128]{4,3,2,1,0:T(8,128)(2,1)} %param.9) | copy-start | bytes 11796484
  9.7 0.8 copy-start.3
  10.4 0.8 copy-start.5
  11.2 0.6 copy-start.6
  15.6 32.0 %collective-permute-start.1 = (f32[512,128]{1,0:T(8,128)S(1)}, f32[512,128]{1,0:T(8,128)S(1)}, u32[]{:S(2)}, u32[]{:S(2)}) collective-permute-start(f32[512,128]{1,0:T(8,128)S(1)} %bitcast.24), channel_id=1, source_target_pairs={{0,128},{1,2},{2,1},{3,4},{4,3},{5,6},{6,5},{7,8},{8,7},{9,10},{10... | collective-permute-start | bytes 786440 | tf_op jit(solution)/shard_map/ppermute | solution.py:543
  17.6 30.0 %collective-permute-start = (f32[512,128]{1,0:T(8,128)S(1)}, f32[512,128]{1,0:T(8,128)S(1)}, u32[]{:S(2)}, u32[]{:S(2)}) collective-permute-start(f32[512,128]{1,0:T(8,128)S(1)} %bitcast.23), channel_id=1, source_target_pairs={{0,1},{1,0},{2,3},{3,2},{4,5},{5,4},{6,7},{7,6},{8,9},{9,8},{10,11... | collective-permute-start | bytes 786440 | tf_op jit(solution)/shard_map/ppermute | solution.py:539
  20.9 1.2 %collective-permute-start.4 = (f32[72,128]{1,0:T(8,128)S(1)}, f32[72,128]{1,0:T(8,128)S(1)}, u32[]{:S(2)}, u32[]{:S(2)}) collective-permute-start(f32[72,128]{1,0:T(8,128)S(1)} %slice.4.here_ref), channel_id=1, source_target_pairs={{0,64},{64,0},{128,192},{192,128},{1,65},{65,1},{129,193},{193,129... | collective-permute-start | bytes 110600 | tf_op jit(solution)/shard_map/ppermute | solution.py:547
  49.2 1.3 %collective-permute-start.5 = (f32[3,32,128]{2,1,0:T(8,128)S(1)}, f32[3,32,128]{2,1,0:T(8,128)S(1)}, u32[]{:S(2)}, u32[]{:S(2)}) collective-permute-start(f32[3,32,128]{2,1,0:T(8,128)S(1)} %get-tuple-element.44), channel_id=1, source_target_pairs={{0,64},{64,0},{128,192},{192,128},{1,65},{65,1},{129,193},{193,129... | collective-permute-start | bytes 147464 | tf_op jit(solution)/shard_map/ppermute | solution.py:547
  50.5 5.1 %collective-permute-start.6 = (f32[3,32,128]{2,1,0:T(8,128)S(1)}, f32[3,32,128]{2,1,0:T(8,128)S(1)}, u32[]{:S(2)}, u32[]{:S(2)}) collective-permute-start(f32[3,32,128]{2,1,0:T(8,128)S(1)} %add.21), channel_id=1, source_target_pairs={{0,1},{1,0},{2,3},{3,2},{4,5},{5,4},{6,7},{7,6},{8,9},{9,8},{10,11... | collective-permute-start | bytes 147464 | tf_op jit(solution)/shard_map/ppermute | solution.py:539
  57.0 3.4 %collective-permute-start.9 = (f32[54,128]{1,0:T(8,128)S(1)}, f32[54,128]{1,0:T(8,128)S(1)}, u32[]{:S(2)}, u32[]{:S(2)}) collective-permute-start(f32[54,128]{1,0:T(8,128)S(1)} %shard_map.88.v0), channel_id=1, source_target_pairs={{0,192},{64,0},{128,64},{192,128},{1,193},{65,1},{129,65},{193,129... | collective-permute-start | bytes 82952 | tf_op jit(solution)/shard_map/ppermute | solution.py:553
  57.4 5.2 %collective-permute-start.8 = (f32[54,128]{1,0:T(8,128)S(1)}, f32[54,128]{1,0:T(8,128)S(1)}, u32[]{:S(2)}, u32[]{:S(2)}) collective-permute-start(f32[54,128]{1,0:T(8,128)S(1)} %shard_map.88.v0), channel_id=1, source_target_pairs={{0,128},{64,192},{128,0},{192,64},{1,129},{65,193},{129,1},{193,65... | collective-permute-start | bytes 82952 | tf_op jit(solution)/shard_map/ppermute | solution.py:553
  60.2 3.3 %collective-permute-start.7 = (f32[54,128]{1,0:T(8,128)S(1)}, f32[54,128]{1,0:T(8,128)S(1)}, u32[]{:S(2)}, u32[]{:S(2)}) collective-permute-start(f32[54,128]{1,0:T(8,128)S(1)} %shard_map.88.v0), channel_id=1, source_target_pairs={{0,64},{64,128},{128,192},{192,0},{1,65},{65,129},{129,193},{193,1... | collective-permute-start | bytes 82952 | tf_op jit(solution)/shard_map/ppermute | solution.py:553
  63.5 6.9 %copy-start.1 = (bf16[20,3,8,32,128]{4,3,2,1,0:T(8,128)(2,1)S(1)}, bf16[20,3,8,32,128]{4,3,2,1,0:T(8,128)(2,1)}, u32[]{:S(2)}) copy-start(bf16[20,3,8,32,128]{4,3,2,1,0:T(8,128)(2,1)} %param.9) | copy-start | bytes 11796484
  63.5 6.9 %copy-start.4 = (bf16[128,128]{1,0:T(8,128)(2,1)S(1)}, bf16[128,128]{1,0:T(8,128)(2,1)}, u32[]{:S(2)}) copy-start(bf16[128,128]{1,0:T(8,128)(2,1)} %loc_ref.11) | copy-start | bytes 98308
  65.4 14.7 %collective-permute-start.12 = (f32[12,64,128]{2,1,0:T(8,128)S(1)}, f32[12,64,128]{2,1,0:T(8,128)S(1)}, u32[]{:S(2)}, u32[]{:S(2)}) collective-permute-start(f32[12,64,128]{2,1,0:T(8,128)S(1)} %get-tuple-element.52), channel_id=1, source_target_pairs={{0,1},{1,0},{2,3},{3,2},{4,5},{5,4},{6,7},{7,6},{8,9},{9,8},{10,11... | collective-permute-start | bytes 1179656 | tf_op jit(solution)/shard_map/ppermute | solution.py:539
  68.9 28.9 %collective-permute-start.13 = (f32[12,64,128]{2,1,0:T(8,128)S(1)}, f32[12,64,128]{2,1,0:T(8,128)S(1)}, u32[]{:S(2)}, u32[]{:S(2)}) collective-permute-start(f32[12,64,128]{2,1,0:T(8,128)S(1)} %get-tuple-element.53), channel_id=1, source_target_pairs={{0,128},{1,2},{2,1},{3,4},{4,3},{5,6},{6,5},{7,8},{8,7},{9,10},{10... | collective-permute-start | bytes 1179656 | tf_op jit(solution)/shard_map/ppermute | solution.py:543
  75.7 23.6 %collective-permute-start.10 = (f32[8,64,128]{2,1,0:T(8,128)S(1)}, f32[8,64,128]{2,1,0:T(8,128)S(1)}, u32[]{:S(2)}, u32[]{:S(2)}) collective-permute-start(f32[8,64,128]{2,1,0:T(8,128)S(1)} %get-tuple-element.49), channel_id=1, source_target_pairs={{0,1},{1,0},{2,3},{3,2},{4,5},{5,4},{6,7},{7,6},{8,9},{9,8},{10,11... | collective-permute-start | bytes 786440 | tf_op jit(solution)/shard_map/ppermute | solution.py:539
  75.7 32.3 %collective-permute-start.11 = (f32[8,64,128]{2,1,0:T(8,128)S(1)}, f32[8,64,128]{2,1,0:T(8,128)S(1)}, u32[]{:S(2)}, u32[]{:S(2)}) collective-permute-start(f32[8,64,128]{2,1,0:T(8,128)S(1)} %get-tuple-element.50), channel_id=1, source_target_pairs={{0,128},{1,2},{2,1},{3,4},{4,3},{5,6},{6,5},{7,8},{8,7},{9,10},{10... | collective-permute-start | bytes 786440 | tf_op jit(solution)/shard_map/ppermute | solution.py:543

commit v8 on v7

--- a/solution.py
+++ b/solution.py
@@ -24,10 +24,7 @@
     for m in range(MEMS):
         for t in range(TILES):
             beside = ((t - 1) ^ 1) + 1 if m % 2 == odd_core else t ^ 1
-            if 0 <= beside < TILES:
-                pairs.append((TILES * m + t, TILES * m + beside))
-            else:
-                pairs.append((TILES * m + t, TILES * (m ^ 2) + t))
+            pairs.append((TILES * m + t, TILES * m + beside % TILES))
     return pairs
 
 
@@ -89,6 +86,10 @@
     both = jnp.concatenate(halves(field), axis=1)
     out = nn(matrix, both)
     return out[:, :128] + out[:, 128:]
+
+
+def side_of_first():
+    return lax.rem(lax.axis_index("tile") + lax.axis_index("mem"), 2)
 
 
 def sort_observations(count, col_ref, lev_ref, innov_ref, weight_ref, out_ref):
@@ -119,7 +120,7 @@
                 out_ref[row : row + 1] = total[6 * f + a : 6 * f + a + 1, 128 * v : 128 * v + 128]
 
 
-def send_kernel(where_ref, count_ref, *refs):
+def send_kernel(count_ref, *refs):
     obs_in, (quarters_ref, first_ref, second_ref, obs_ref), obs_here, (edges, sems) = refs[:4], refs[4:8], refs[8:12], refs[12:]
     head = pl.ds(0, HEAD)
     copies = [pltpu.make_async_copy(quarters_ref.at[head, 3 * n], edges.at[n], sems.at[n]) for n in range(2)]
@@ -132,22 +133,22 @@
     first_ref[64 * HEAD :] = obs_ref[...]
     for copy in copies:
         copy.wait()
-    low = where_ref[7]
+    low = side_of_first()
     for k in range(HEAD):
         first_ref[64 * k : 64 * k + 64] = edges[1 - low, k].astype(F32)
         second_ref[64 * k : 64 * k + 64] = edges[low, k].astype(F32)
 
 
-def send_part(where, count, col, lev, innov, weight, quarters):
+def send_part(count, col, lev, innov, weight, quarters):
     return call(
         send_kernel,
         (sds(64 * HEAD + OBS, 128), sds(64 * HEAD, 128), sds(OBS, 128)),
-        ins=[SMEM, SMEM] + [HBM] * 5,
+        ins=[SMEM] + [HBM] * 5,
         outs=(VMEM,) * 3,
         scratch=[pltpu.VMEM(a.shape, a.dtype) for a in (col, lev, innov, weight)]
         + [pltpu.VMEM((2, HEAD, 64, 128), BF16), pltpu.SemaphoreType.DMA((6,))],
-        vmem=58,
-    )(where, count, col, lev, innov, weight, quarters)
+        vmem=56,
+    )(count, col, lev, innov, weight, quarters)
 
 
 def own_kernel(where_ref, alpha_ref, ens_ref, loc_ref, after_ref, inner_ref, edge_ref, x_ref, smat_ref, hmat_ref, first_ref, second_ref):
@@ -386,9 +387,9 @@
     )(where, mine, near, wown, wnear, lev)
 
 
-def adjoint_kernel(where_ref, v0, v1, v2, v3, innov_ref, weight_ref, lev_ref, wown_ref, wnear_ref, x_ref, c_ref, first_ref, second_ref):
+def adjoint_kernel(where_ref, v0, v1, innov_ref, weight_ref, lev_ref, wown_ref, wnear_ref, x_ref, c_ref, first_ref, second_ref):
     level = lax.broadcasted_iota(jnp.int32, (128, SLOTS), 0).astype(F32)
-    value = v0[...] + v1[...] + v2[...] + v3[...]
+    value = v0[...] + v1[...]
 
     def place(weight, row):
         line = jnp.concatenate([value[6 * row + a : 6 * row + a + 1] for a in range(6)], axis=1)
@@ -421,7 +422,7 @@
     return call(
         adjoint_kernel,
         (sds(V, 256, 128), sds(members, 64, 128), sds(members, 64, 128)),
-        ins=[SMEM] + [VMEM] * 10,
+        ins=[SMEM] + [VMEM] * 8,
         outs=(VMEM,) * 3,
     )(where, *vals, innov, weight, lev, wown, wnear, x)
 
@@ -547,11 +548,8 @@
     return lax.ppermute(x, "mem", [(m, m ^ 1) for m in range(MEMS)])
 
 
-def round_mem(mine):
-    size = lax.axis_size("mem")
-    return [mine] + [
-        lax.ppermute(mine, "mem", [(i, (i + shift) % size) for i in range(size)]) for shift in range(1, size)
-    ]
+def swap_chip(x):
+    return lax.ppermute(x, "mem", [(m, m ^ 2) for m in range(MEMS)])
 
 
 def on_device(alpha, ensemble, loc_vert, obs_col, obs_lev, obs_count, innovation, obs_weight):
@@ -560,7 +558,7 @@
     tiles = lax.axis_size("tile")
     even = tile % 2 == 0
     core = lax.axis_index("mem") % 2
-    first_low = (tile + core) % 2
+    first_low = side_of_first()
     where = jnp.stack(
         [
             jnp.where(even, 7 * 32, 0),
@@ -580,7 +578,7 @@
     flat_ens = ensemble.reshape(members, V, 256, 128)
 
     send_first, send_second, own_obs = send_part(
-        where, obs_count, obs_col, obs_lev, innovation, obs_weight, alpha.reshape(members, 4, 64, 128)
+        obs_count, obs_col, obs_lev, innovation, obs_weight, alpha.reshape(members, 4, 64, 128)
     )
     first, second = swap_first(send_first), swap_second(send_second)
     inner, own_edge, x, smat, hmat, send_first, send_second = own_part(where, flat, flat_ens, loc_vert, own_obs)
@@ -593,7 +591,9 @@
     inc, keep, give = edge_part(where, first_rest, second_rest, own_edge, x, hmat, loc_vert, inner, head)
     near = swap_first(keep + swap_core(give))
     mine = mine_part(where, inc, wown, wnear, lev)
-    vals = round_mem(values(where, mine, near, wown, wnear, lev))
+    vals = values(where, mine, near, wown, wnear, lev)
+    vals = vals + swap_core(vals)
+    vals = vals, swap_chip(vals)
     c, back_first, back_second = adjoint(where, vals, innov, weight, lev, wown, wnear, x)
     halo_first, halo_second = swap_first(back_first), swap_second(back_second)
     out, edge, back_first, back_second = back_part(where, flat, flat_ens, c, smat, loc_vert)

time: 110 us -> 106 us (0.964)
  waiting for transfers between devices: 61.9 us -> 34.7 us
  starting transfers between devices: 18 us -> 43.1 us
  local copies, waits for them, and re-layouts: 4.85 us -> 3.73 us
    ppermute x4, waiting for transfers between devices: 49.3 us -> 14.4 us  [swap_second(): return lax.ppermute(x, ('mem', 'tile'), SECOND)]
    ppermute x2 -> x3, starting transfers between devices: 0.41 us -> 16.6 us  [swap_core(): return lax.ppermute(x, 'mem', [(m, m ^ 1) for m in range(MEMS)])]
    ppermute x4, starting transfers between devices: 4.15 us -> 16.4 us  [swap_second(): return lax.ppermute(x, ('mem', 'tile'), SECOND)]
    ppermute x5, starting transfers between devices: 10.1 us -> 4.18 us  [swap_first(): return lax.ppermute(x, ('mem', 'tile'), FIRST)]
    ppermute x5, waiting for transfers between devices: 7.3 us -> 12.8 us  [swap_first(): return lax.ppermute(x, ('mem', 'tile'), FIRST)]
    ppermute x3 -> x1, starting transfers between devices: 3.39 us -> 5.81 us  [swap_chip(): return lax.ppermute(x, 'mem', [(m, m ^ 2) for m in range(MEMS)])]
    ppermute x3 -> x1, waiting for transfers between devices: 3.15 us -> 4.51 us  [swap_chip(): return lax.ppermute(x, 'mem', [(m, m ^ 2) for m in range(MEMS)])]
    ppermute x2 -> x3, waiting for transfers between devices: 2.12 us -> 2.94 us  [swap_core(): return lax.ppermute(x, 'mem', [(m, m ^ 1) for m in range(MEMS)])]
  transfers between devices with their start and end apart: 14 -> 13, of which waited for: 11 -> 10; matrix products, arithmetic and copies ran while one was open for 0% -> 0% of each run, Pallas kernels for 14% -> 14%
where the time goes in v8:
time: 106 us
  starting transfers between devices  43.1 us (41%)
  waiting for transfers between devices  34.7 us (33%)
  Pallas kernels  23.1 us (22%)
  local copies, waits for them, and re-layouts  3.73 us (4%)
    ppermute x3, starting transfers between devices, swap_core(): return lax.ppermute(x, 'mem', [(m, m ^ 1) for m in range(MEMS)])  16.6 us
    ppermute x4, starting transfers between devices, swap_second(): return lax.ppermute(x, ('mem', 'tile'), SECOND)  16.4 us
    ppermute x4, waiting for transfers between devices, swap_second(): return lax.ppermute(x, ('mem', 'tile'), SECOND)  14.4 us
    ppermute x5, waiting for transfers between devices, swap_first(): return lax.ppermute(x, ('mem', 'tile'), FIRST)  12.8 us
    ppermute x1, starting transfers between devices, swap_chip(): return lax.ppermute(x, 'mem', [(m, m ^ 2) for m in range(MEMS)])  5.81 us
    pallas_call x1, Pallas kernels, back_part(): call(back_kernel, (sds(members, 256, 128), sds(members, 128, 128), sds(me...  5.35 us
    ppermute x1, waiting for transfers between devices, swap_chip(): return lax.ppermute(x, 'mem', [(m, m ^ 2) for m in range(MEMS)])  4.51 us
    ppermute x5, starting transfers between devices, swap_first(): return lax.ppermute(x, ('mem', 'tile'), FIRST)  4.18 us
  transfers between devices with their start and end apart: 13, of which 10 were waited for; matrix products, arithmetic and copies ran while one was open for 0% of the time, Pallas kernels for 14%

profile of v8, /device:TPU:32, one launch (start us, length us, event | category | flops | bytes accessed | tf_op | source)
XLA Modules:
  0.0 105.6 jit_solution(12700514192883059149)
XLA Ops:
  0.8 2.1 %shard_map.82 = (f32[840,128]{1,0:T(8,128)}, f32[768,128]{1,0:T(8,128)}, f32[72,128]{1,0:T(8,128)}) custom-call(s32[1]{0:T(128)S(6)} %copy.13.count_ref, s32[1,2048]{1,0:T(1,128)} %refs_0_.1, s32[1,2048]{1,0:T(1,128)} %refs_1_.1, f32[1,2048]{1,0:T(1,128)} %refs_2_.1, f32[1,2048]{1,0:T(1,128)} %refs_3_.1, bf16[20,4,64,128]{3,2,1,0:T(8,128)(2,1)} %bitcast.20), custom_call_target="tpu_custom_call" | custom-call | flops 1000 | bytes 1000 | tf_op jit(solution)/shard_map/pallas_call | solution.py:143
  2.8 3.4 %collective-permute-start.2 = (f32[840,128]{1,0:T(8,128)}, f32[840,128]{1,0:T(8,128)S(1)}, u32[]{:S(2)}, u32[]{:S(2)}) collective-permute-start(f32[840,128]{1,0:T(8,128)} %get-tuple-element.37), channel_id=1, source_target_pairs={{0,1},{1,0},{2,3},{3,2},{4,5},{5,4},{6,7},{7,6},{8,9},{9,8},{10,11... | collective-permute-start | bytes 1290248 | tf_op jit(solution)/shard_map/ppermute | solution.py:540
  6.2 8.2 %collective-permute-start.3 = (f32[768,128]{1,0:T(8,128)}, f32[768,128]{1,0:T(8,128)S(1)}, u32[]{:S(2)}, u32[]{:S(2)}) collective-permute-start(f32[768,128]{1,0:T(8,128)} %get-tuple-element.38), channel_id=1, source_target_pairs={{0,63},{1,2},{2,1},{3,4},{4,3},{5,6},{6,5},{7,8},{8,7},{9,10},{10,... | collective-permute-start | bytes 1179656 | tf_op jit(solution)/shard_map/ppermute | solution.py:544
  14.5 2.1 %copy-done = bf16[20,3,8,32,128]{4,3,2,1,0:T(8,128)(2,1)S(1)} copy-done((bf16[20,3,8,32,128]{4,3,2,1,0:T(8,128)(2,1)S(1)}, bf16[20,3,8,32,128]{4,3,2,1,0:T(8,128)(2,1)}, u32[]{:S(2)}) %copy-start) | copy-done | bytes 3932184
  16.6 0.8 copy-done.3
  17.4 0.8 copy-done.5
  18.2 3.8 %shard_map.83 = (f32[3,128,128]{2,1,0:T(8,128)S(1)}, f32[20,128,128]{2,1,0:T(8,128)S(1)}, bf16[20,3,128,128]{3,2,1,0:T(8,128)(2,1)S(1)}, bf16[256,256]{1,0:T(8,1...) custom-call(s32[11]{0:T(128)S(1)} %stack.51.where_ref, ...), custom_call_target="tpu_custom_call" | custom-call | flops 1000 | bytes 1000 | tf_op jit(solution)/shard_map/pallas_call | solution.py:190
  22.2 1.6 %collective-permute-done.2.first_ref = f32[840,128]{1,0:T(8,128)S(1)} collective-permute-done((f32[840,128]{1,0:T(8,128)}, f32[840,128]{1,0:T(8,128)S(1)}, u32[]{:S(2)}, u32[]{:S(2)}) %collective-permute-start.2) | collective-permute-done | bytes 430112 | tf_op jit(solution)/shard_map/ppermute | solution.py:540
  23.8 11.1 %collective-permute-start.4 = (f32[72,128]{1,0:T(8,128)S(1)}, f32[72,128]{1,0:T(8,128)S(1)}, u32[]{:S(2)}, u32[]{:S(2)}) collective-permute-start(f32[72,128]{1,0:T(8,128)S(1)} %slice.4.here_ref), channel_id=1, source_target_pairs={{0,64},{64,0},{128,192},{192,128},{1,65},{65,1},{129,193},{193,129... | collective-permute-start | bytes 110600 | tf_op jit(solution)/shard_map/ppermute | solution.py:548
  34.8 0.9 collective-permute-done.4.there_ref
  35.7 1.1 %shard_map.84 = (bf16[3,320,768]{2,1,0:T(8,128)(2,1)S(1)}, bf16[2,3,64,768]{3,2,1,0:T(8,128)(2,1)S(1)}, f32[9,768]{1,0:T(8,128)S(1)}, f32[9,768]{1,0:T(8,128)S(1)}, f32[9,768]{1,0:T(8,128)S(1)}) custom-call(s32[11]{0:T(128)S(1)} %stack.51.where_ref, f32[72,128]{1,0:T(8,128)S(1)} %copy-done.5, f32[72,128]{1,0:T(8,128)S(1)} %slice.4.here_ref, ...), custom_call_target="tpu_custom_call" | custom-call | flops 1000 | bytes 1000 | tf_op jit(solution)/shard_map/pallas_call | solution.py:316
  36.9 1.4 %shard_map.85.head_ref = f32[3,128,128]{2,1,0:T(8,128)S(1)} custom-call(f32[840,128]{1,0:T(8,128)S(1)} %collective-permute-done.2.first_ref, f32[768,128]{1,0:T(8,128)S(1)} %collective-permute-done.3.second_ref, f32[20,128,128]{2,1,0:T(8,128)S(1)} %get-tuple-element.33.own_ref, bf16[20,3,128,128]{3,2,1,0:T(8,128)(2,1)S(1)} %get-tuple-element.34.x_ref, ...), custom_call_target="tpu_custom_call" | custom-call | flops 1000 | bytes 1000 | tf_op jit(solution)/shard_map/pallas_call | solution.py:241
  38.3 2.1 %collective-permute-done.1.second_ref = f32[512,128]{1,0:T(8,128)S(1)} collective-permute-done((f32[512,128]{1,0:T(8,128)S(1)}, f32[512,128]{1,0:T(8,128)S(1)}, u32[]{:S(2)}, u32[]{:S(2)}) %collective-permute-start.1) | collective-permute-done | bytes 262176 | tf_op jit(solution)/shard_map/ppermute | solution.py:544
  40.4 1.6 %shard_map.86 = (f32[3,256,128]{2,1,0:T(8,128)S(1)}, f32[3,32,128]{2,1,0:T(8,128)S(1)}, f32[3,32,128]{2,1,0:T(8,128)S(1)}) custom-call(s32[11]{0:T(128)S(1)} %stack.51.where_ref, f32[512,128]{1,0:T(8,128)S(1)} %collective-permute-done.first_ref, f32[512,128]{1,0:T(8,128)S(1)} %collective-permute-done.1.second_ref, ...), custom_call_target="tpu_custom_call" | custom-call | flops 1000 | bytes 1000 | tf_op jit(solution)/shard_map/pallas_call | solution.py:258
  42.1 1.2 %collective-permute-done.5 = f32[3,32,128]{2,1,0:T(8,128)S(1)} collective-permute-done((f32[3,32,128]{2,1,0:T(8,128)S(1)}, f32[3,32,128]{2,1,0:T(8,128)S(1)}, u32[]{:S(2)}, u32[]{:S(2)}) %collective-permute-start.5) | collective-permute-done | bytes 49184 | tf_op jit(solution)/shard_map/ppermute | solution.py:548
  43.5 1.7 %shard_map.87.mine_ref = f32[9,768]{1,0:T(8,128)S(1)} custom-call(s32[11]{0:T(128)S(1)} %stack.51.where_ref, f32[3,256,128]{2,1,0:T(8,128)S(1)} %get-tuple-element.40.inc_ref, bf16[3,320,768]{2,1,0:T(8,128)(2,1)S(1)} %get-tuple-element.41.wown_ref, bf16[2,3,64,768]{3,2,1,0:T(8,128)(2,1)S(1)} %get-tuple-element.42.wnear_ref, ...), custom_call_target="tpu_custom_call" | custom-call | flops 1000 | bytes 1000 | tf_op jit(solution)/shard_map/pallas_call | solution.py:354
  45.2 3.3 %collective-permute-done.6.near_ref = f32[3,32,128]{2,1,0:T(8,128)S(1)} collective-permute-done((f32[3,32,128]{2,1,0:T(8,128)S(1)}, f32[3,32,128]{2,1,0:T(8,128)S(1)}, u32[]{:S(2)}, u32[]{:S(2)}) %collective-permute-start.6) | collective-permute-done | bytes 49184 | tf_op jit(solution)/shard_map/ppermute | solution.py:540
  48.5 1.4 %shard_map.88 = f32[54,128]{1,0:T(8,128)S(1)} custom-call(s32[11]{0:T(128)S(1)} %stack.51.where_ref, f32[9,768]{1,0:T(8,128)S(1)} %shard_map.87.mine_ref, f32[3,32,128]{2,1,0:T(8,128)S(1)} %collective-permute-done.6.near_ref, bf16[3,320,768]{2,1,0:T(8,128)(2,1)S(1)} %get-tuple-element.41.wown_ref, bf16[2,3,64,768]{3,2,1,0:T(8,128)(2,1)S(1)} %get-tuple-element.42.wnear_ref, ...), custom_call_target="tpu_custom_call" | custom-call | flops 1000 | bytes 1000 | tf_op jit(solution)/shard_map/pallas_call | solution.py:382
  49.8 5.5 %collective-permute-start.7 = (f32[54,128]{1,0:T(8,128)S(1)}, f32[54,128]{1,0:T(8,128)S(1)}, u32[]{:S(2)}, u32[]{:S(2)}) collective-permute-start(f32[54,128]{1,0:T(8,128)S(1)} %shard_map.88), channel_id=1, source_target_pairs={{0,64},{64,0},{128,192},{192,128},{1,65},{65,1},{129,193},{193,129... | collective-permute-start | bytes 82952 | tf_op jit(solution)/shard_map/ppermute | solution.py:548
  55.3 0.9 collective-permute-done.7
  56.1 5.8 %collective-permute-start.8 = (f32[54,128]{1,0:T(8,128)S(1)}, f32[54,128]{1,0:T(8,128)S(1)}, u32[]{:S(2)}, u32[]{:S(2)}) collective-permute-start(f32[54,128]{1,0:T(8,128)S(1)} %add.21.v0), channel_id=1, source_target_pairs={{0,128},{64,192},{128,0},{192,64},{1,129},{65,193},{129,1},{193,65... | collective-permute-start | bytes 82952 | tf_op jit(solution)/shard_map/ppermute | solution.py:552
  62.0 4.5 %collective-permute-done.8.v1 = f32[54,128]{1,0:T(8,128)S(1)} collective-permute-done((f32[54,128]{1,0:T(8,128)S(1)}, f32[54,128]{1,0:T(8,128)S(1)}, u32[]{:S(2)}, u32[]{:S(2)}) %collective-permute-start.8) | collective-permute-done | bytes 27680 | tf_op jit(solution)/shard_map/ppermute | solution.py:552
  66.5 1.9 %shard_map.89 = (f32[3,256,128]{2,1,0:T(8,128)S(1)}, f32[12,64,128]{2,1,0:T(8,128)S(1)}, f32[12,64,128]{2,1,0:T(8,128)S(1)}) custom-call(s32[11]{0:T(128)S(1)} %stack.51.where_ref, f32[54,128]{1,0:T(8,128)S(1)} %add.21.v0, f32[54,128]{1,0:T(8,128)S(1)} %collective-permute-done.8.v1, f32[9,768]{1,0:T(8,128)S(1)} %get-tuple-element.45.innov_ref, ...), custom_call_target="tpu_custom_call" | custom-call | flops 1000 | bytes 1000 | tf_op jit(solution)/shard_map/pallas_call | solution.py:422
  68.5 2.3 %collective-permute-start.12 = (f32[12,64,128]{2,1,0:T(8,128)S(1)}, f32[12,64,128]{2,1,0:T(8,128)S(1)}, u32[]{:S(2)}, u32[]{:S(2)}) collective-permute-start(f32[12,64,128]{2,1,0:T(8,128)S(1)} %get-tuple-element.53), channel_id=1, source_target_pairs={{0,63},{1,2},{2,1},{3,4},{4,3},{5,6},{6,5},{7,8},{8,7},{9,10},{10,... | collective-permute-start | bytes 1179656 | tf_op jit(solution)/shard_map/ppermute | solution.py:544
  70.8 5.3 %shard_map.90 = (f32[20,256,128]{2,1,0:T(8,128)}, f32[20,128,128]{2,1,0:T(8,128)S(1)}, f32[8,64,128]{2,1,0:T(8,128)S(1)}, f32[8,64,128]{2,1,0:T(8,128)S(1)}) custom-call(s32[11]{0:T(128)S(1)} %stack.51.where_ref, bf16[20,256,128]{2,1,0:T(8,128)(2,1)S(1)} %bitcast.22, bf16[20,3,256,128]{3,2,1,0:T(8,128)(2,1)S(1)} %bitcast.19, ...), custom_call_target="tpu_custom_call" | custom-call | flops 1000 | bytes 1000 | tf_op jit(solution)/shard_map/pallas_call | solution.py:454
  76.2 0.6 collective-permute-start.9
  76.8 5.7 %collective-permute-start.10 = (f32[8,64,128]{2,1,0:T(8,128)S(1)}, f32[8,64,128]{2,1,0:T(8,128)S(1)}, u32[]{:S(2)}, u32[]{:S(2)}) collective-permute-start(f32[8,64,128]{2,1,0:T(8,128)S(1)} %get-tuple-element.50), channel_id=1, source_target_pairs={{0,63},{1,2},{2,1},{3,4},{4,3},{5,6},{6,5},{7,8},{8,7},{9,10},{10,... | collective-permute-start | bytes 786440 | tf_op jit(solution)/shard_map/ppermute | solution.py:544
  82.5 7.9 %collective-permute-done.11.first_ref = f32[12,64,128]{2,1,0:T(8,128)S(1)} collective-permute-done((f32[12,64,128]{2,1,0:T(8,128)S(1)}, f32[12,64,128]{2,1,0:T(8,128)S(1)}, u32[]{:S(2)}, u32[]{:S(2)}) %collective-permute-start.11) | collective-permute-done | bytes 393248 | tf_op jit(solution)/shard_map/ppermute | solution.py:540
  90.4 9.5 %collective-permute-done.12.second_ref = f32[12,64,128]{2,1,0:T(8,128)S(1)} collective-permute-done((f32[12,64,128]{2,1,0:T(8,128)S(1)}, f32[12,64,128]{2,1,0:T(8,128)S(1)}, u32[]{:S(2)}, u32[]{:S(2)}) %collective-permute-start.12) | collective-permute-done | bytes 393248 | tf_op jit(solution)/shard_map/ppermute | solution.py:544
  99.9 1.4 %shard_map.91.unused_ref = f32[20,4,64,128]{3,2,1,0:T(8,128)} custom-call(f32[12,64,128]{2,1,0:T(8,128)S(1)} %collective-permute-done.11.first_ref, f32[12,64,128]{2,1,0:T(8,128)S(1)} %collective-permute-done.12.second_ref, f32[20,128,128]{2,1,0:T(8,128)S(1)} %get-tuple-element.51.edge_ref, ...), custom_call_target="tpu_custom_call", output_to_operand_aliasing={{}: (5, {})} | custom-call | flops 1000 | bytes 1000 | tf_op jit(solution)/shard_map/pallas_call | solution.py:502
  101.3 2.8 %collective-permute-done.10.second_ref = f32[8,64,128]{2,1,0:T(8,128)S(1)} collective-permute-done((f32[8,64,128]{2,1,0:T(8,128)S(1)}, f32[8,64,128]{2,1,0:T(8,128)S(1)}, u32[]{:S(2)}, u32[]{:S(2)}) %collective-permute-start.10) | collective-permute-done | bytes 262176 | tf_op jit(solution)/shard_map/ppermute | solution.py:544
  104.2 1.3 %shard_map.92 = f32[20,4,64,128]{3,2,1,0:T(8,128)} custom-call(f32[8,64,128]{2,1,0:T(8,128)S(1)} %collective-permute-done.9.first_ref, f32[8,64,128]{2,1,0:T(8,128)S(1)} %collective-permute-done.10.second_ref, f32[20,128,128]{2,1,0:T(8,128)S(1)} %get-tuple-element.51.edge_ref, ...), custom_call_target="tpu_custom_call", output_to_operand_aliasing={{}: (5, {})} | custom-call | flops 1000 | bytes 1000 | tf_op jit(solution)/shard_map/pallas_call | solution.py:502
  (21 shorter events, 0.6 us)
Async XLA Ops:
  0.0 14.5 %copy-start.2 = (bf16[20,8,32,128]{3,2,1,0:T(8,128)(2,1)S(1)}, bf16[20,8,32,128]{3,2,1,0:T(8,128)(2,1)}, u32[]{:S(2)}) copy-start(bf16[20,8,32,128]{3,2,1,0:T(8,128)(2,1)} %param.8) | copy-start | bytes 3932164
  2.8 20.9 %collective-permute-start.2 = (f32[840,128]{1,0:T(8,128)}, f32[840,128]{1,0:T(8,128)S(1)}, u32[]{:S(2)}, u32[]{:S(2)}) collective-permute-start(f32[840,128]{1,0:T(8,128)} %get-tuple-element.37), channel_id=1, source_target_pairs={{0,1},{1,0},{2,3},{3,2},{4,5},{5,4},{6,7},{7,6},{8,9},{9,8},{10,11... | collective-permute-start | bytes 1290248 | tf_op jit(solution)/shard_map/ppermute | solution.py:540
  6.2 30.7 %collective-permute-start.3 = (f32[768,128]{1,0:T(8,128)}, f32[768,128]{1,0:T(8,128)S(1)}, u32[]{:S(2)}, u32[]{:S(2)}) collective-permute-start(f32[768,128]{1,0:T(8,128)} %get-tuple-element.38), channel_id=1, source_target_pairs={{0,63},{1,2},{2,1},{3,4},{4,3},{5,6},{6,5},{7,8},{8,7},{9,10},{10,... | collective-permute-start | bytes 1179656 | tf_op jit(solution)/shard_map/ppermute | solution.py:544
  14.5 2.1 %copy-start = (bf16[20,3,8,32,128]{4,3,2,1,0:T(8,128)(2,1)S(1)}, bf16[20,3,8,32,128]{4,3,2,1,0:T(8,128)(2,1)}, u32[]{:S(2)}) copy-start(bf16[20,3,8,32,128]{4,3,2,1,0:T(8,128)(2,1)} %param.9) | copy-start | bytes 11796484
  16.6 0.8 copy-start.3
  17.4 0.8 copy-start.5
  22.0 18.4 %collective-permute-start.1 = (f32[512,128]{1,0:T(8,128)S(1)}, f32[512,128]{1,0:T(8,128)S(1)}, u32[]{:S(2)}, u32[]{:S(2)}) collective-permute-start(f32[512,128]{1,0:T(8,128)S(1)} %bitcast.24), channel_id=1, source_target_pairs={{0,63},{1,2},{2,1},{3,4},{4,3},{5,6},{6,5},{7,8},{8,7},{9,10},{10,... | collective-permute-start | bytes 786440 | tf_op jit(solution)/shard_map/ppermute | solution.py:544
  22.2 18.2 %collective-permute-start = (f32[512,128]{1,0:T(8,128)S(1)}, f32[512,128]{1,0:T(8,128)S(1)}, u32[]{:S(2)}, u32[]{:S(2)}) collective-permute-start(f32[512,128]{1,0:T(8,128)S(1)} %bitcast.23), channel_id=1, source_target_pairs={{0,1},{1,0},{2,3},{3,2},{4,5},{5,4},{6,7},{7,6},{8,9},{9,8},{10,11... | collective-permute-start | bytes 786440 | tf_op jit(solution)/shard_map/ppermute | solution.py:540
  23.8 11.9 %collective-permute-start.4 = (f32[72,128]{1,0:T(8,128)S(1)}, f32[72,128]{1,0:T(8,128)S(1)}, u32[]{:S(2)}, u32[]{:S(2)}) collective-permute-start(f32[72,128]{1,0:T(8,128)S(1)} %slice.4.here_ref), channel_id=1, source_target_pairs={{0,64},{64,0},{128,192},{192,128},{1,65},{65,1},{129,193},{193,129... | collective-permute-start | bytes 110600 | tf_op jit(solution)/shard_map/ppermute | solution.py:548
  42.0 1.3 %collective-permute-start.5 = (f32[3,32,128]{2,1,0:T(8,128)S(1)}, f32[3,32,128]{2,1,0:T(8,128)S(1)}, u32[]{:S(2)}, u32[]{:S(2)}) collective-permute-start(f32[3,32,128]{2,1,0:T(8,128)S(1)} %get-tuple-element.44), channel_id=1, source_target_pairs={{0,64},{64,0},{128,192},{192,128},{1,65},{65,1},{129,193},{193,129... | collective-permute-start | bytes 147464 | tf_op jit(solution)/shard_map/ppermute | solution.py:548
  43.4 5.1 %collective-permute-start.6 = (f32[3,32,128]{2,1,0:T(8,128)S(1)}, f32[3,32,128]{2,1,0:T(8,128)S(1)}, u32[]{:S(2)}, u32[]{:S(2)}) collective-permute-start(f32[3,32,128]{2,1,0:T(8,128)S(1)} %add.20), channel_id=1, source_target_pairs={{0,1},{1,0},{2,3},{3,2},{4,5},{5,4},{6,7},{7,6},{8,9},{9,8},{10,11... | collective-permute-start | bytes 147464 | tf_op jit(solution)/shard_map/ppermute | solution.py:540
  49.8 6.3 %collective-permute-start.7 = (f32[54,128]{1,0:T(8,128)S(1)}, f32[54,128]{1,0:T(8,128)S(1)}, u32[]{:S(2)}, u32[]{:S(2)}) collective-permute-start(f32[54,128]{1,0:T(8,128)S(1)} %shard_map.88), channel_id=1, source_target_pairs={{0,64},{64,0},{128,192},{192,128},{1,65},{65,1},{129,193},{193,129... | collective-permute-start | bytes 82952 | tf_op jit(solution)/shard_map/ppermute | solution.py:548
  56.1 10.3 %collective-permute-start.8 = (f32[54,128]{1,0:T(8,128)S(1)}, f32[54,128]{1,0:T(8,128)S(1)}, u32[]{:S(2)}, u32[]{:S(2)}) collective-permute-start(f32[54,128]{1,0:T(8,128)S(1)} %add.21.v0), channel_id=1, source_target_pairs={{0,128},{64,192},{128,0},{192,64},{1,129},{65,193},{129,1},{193,65... | collective-permute-start | bytes 82952 | tf_op jit(solution)/shard_map/ppermute | solution.py:552
  66.5 4.3 %copy-start.1 = (bf16[20,3,8,32,128]{4,3,2,1,0:T(8,128)(2,1)S(1)}, bf16[20,3,8,32,128]{4,3,2,1,0:T(8,128)(2,1)}, u32[]{:S(2)}) copy-start(bf16[20,3,8,32,128]{4,3,2,1,0:T(8,128)(2,1)} %param.9) | copy-start | bytes 11796484
  66.5 4.3 %copy-start.4 = (bf16[128,128]{1,0:T(8,128)(2,1)S(1)}, bf16[128,128]{1,0:T(8,128)(2,1)}, u32[]{:S(2)}) copy-start(bf16[128,128]{1,0:T(8,128)(2,1)} %loc_ref.11) | copy-start | bytes 98308
  68.4 22.0 %collective-permute-start.11 = (f32[12,64,128]{2,1,0:T(8,128)S(1)}, f32[12,64,128]{2,1,0:T(8,128)S(1)}, u32[]{:S(2)}, u32[]{:S(2)}) collective-permute-start(f32[12,64,128]{2,1,0:T(8,128)S(1)} %get-tuple-element.52), channel_id=1, source_target_pairs={{0,1},{1,0},{2,3},{3,2},{4,5},{5,4},{6,7},{7,6},{8,9},{9,8},{10,11... | collective-permute-start | bytes 1179656 | tf_op jit(solution)/shard_map/ppermute | solution.py:540
  68.5 31.4 %collective-permute-start.12 = (f32[12,64,128]{2,1,0:T(8,128)S(1)}, f32[12,64,128]{2,1,0:T(8,128)S(1)}, u32[]{:S(2)}, u32[]{:S(2)}) collective-permute-start(f32[12,64,128]{2,1,0:T(8,128)S(1)} %get-tuple-element.53), channel_id=1, source_target_pairs={{0,63},{1,2},{2,1},{3,4},{4,3},{5,6},{6,5},{7,8},{8,7},{9,10},{10,... | collective-permute-start | bytes 1179656 | tf_op jit(solution)/shard_map/ppermute | solution.py:544
  76.2 25.1 %collective-permute-start.9 = (f32[8,64,128]{2,1,0:T(8,128)S(1)}, f32[8,64,128]{2,1,0:T(8,128)S(1)}, u32[]{:S(2)}, u32[]{:S(2)}) collective-permute-start(f32[8,64,128]{2,1,0:T(8,128)S(1)} %get-tuple-element.49), channel_id=1, source_target_pairs={{0,1},{1,0},{2,3},{3,2},{4,5},{5,4},{6,7},{7,6},{8,9},{9,8},{10,11... | collective-permute-start | bytes 786440 | tf_op jit(solution)/shard_map/ppermute | solution.py:540
  76.8 27.4 %collective-permute-start.10 = (f32[8,64,128]{2,1,0:T(8,128)S(1)}, f32[8,64,128]{2,1,0:T(8,128)S(1)}, u32[]{:S(2)}, u32[]{:S(2)}) collective-permute-start(f32[8,64,128]{2,1,0:T(8,128)S(1)} %get-tuple-element.50), channel_id=1, source_target_pairs={{0,63},{1,2},{2,1},{3,4},{4,3},{5,6},{6,5},{7,8},{8,7},{9,10},{10,... | collective-permute-start | bytes 786440 | tf_op jit(solution)/shard_map/ppermute | solution.py:544

commit v9 on v8

--- a/solution.py
+++ b/solution.py
@@ -19,17 +19,19 @@
 MEMS = 4
 
 
-def swap_pairs(odd_core):
+def partners(odd, spare):
     pairs = []
     for m in range(MEMS):
         for t in range(TILES):
-            beside = ((t - 1) ^ 1) + 1 if m % 2 == odd_core else t ^ 1
-            pairs.append((TILES * m + t, TILES * m + beside % TILES))
+            beside = ((t - 1) ^ 1) + 1 if odd(m) else t ^ 1
+            there = (m, beside) if 0 <= beside < TILES else (m ^ spare, t)
+            pairs.append((TILES * m + t, TILES * there[0] + there[1]))
     return pairs
 
 
-FIRST = swap_pairs(1)
-SECOND = swap_pairs(0)
+FIRST = partners(lambda m: True, 1)
+SECOND = partners(lambda m: False, 1)
+NEAR = partners(lambda m: m % 2 == 1, 2)
 
 
 def nn(a, b):
@@ -89,7 +91,7 @@
 
 
 def side_of_first():
-    return lax.rem(lax.axis_index("tile") + lax.axis_index("mem"), 2)
+    return lax.rem(lax.axis_index("tile") + 1, 2)
 
 
 def sort_observations(count, col_ref, lev_ref, innov_ref, weight_ref, out_ref):
@@ -131,6 +133,7 @@
         copy.wait()
     sort_observations(count_ref[0], *obs_here, obs_ref)
     first_ref[64 * HEAD :] = obs_ref[...]
+    second_ref[64 * HEAD :] = obs_ref[...]
     for copy in copies:
         copy.wait()
     low = side_of_first()
@@ -142,7 +145,7 @@
 def send_part(count, col, lev, innov, weight, quarters):
     return call(
         send_kernel,
-        (sds(64 * HEAD + OBS, 128), sds(64 * HEAD, 128), sds(OBS, 128)),
+        (sds(64 * HEAD + OBS, 128), sds(64 * HEAD + OBS, 128), sds(OBS, 128)),
         ins=[SMEM] + [HBM] * 5,
         outs=(VMEM,) * 3,
         scratch=[pltpu.VMEM(a.shape, a.dtype) for a in (col, lev, innov, weight)]
@@ -218,10 +221,10 @@
     )(where, alpha, ensemble, loc, after)
 
 
-def edge_terms(first_ref, second_ref, own_ref, x_ref, hmat_ref, loc_ref, start, total):
+def edge_terms(first_ref, second_ref, own_ref, x_ref, hmat_ref, loc_ref, start, count, total):
     hmat = hmat_ref[...]
     loc = loc_ref[...]
-    for k in range(second_ref.shape[0] // 64):
+    for k in range(count):
         rows = slice(64 * k, 64 * k + 64)
         halo = jnp.concatenate([first_ref[rows].astype(BF16), second_ref[rows].astype(BF16)], axis=0)
         lifted = (own_ref[start + k] + lift(nn(hmat, halo), loc)).astype(BF16).astype(F32)
@@ -232,7 +235,7 @@
 
 def head_kernel(first_ref, second_ref, own_ref, x_ref, hmat_ref, loc_ref, after_ref, total_ref):
     zeros = [jnp.zeros((128, 128), F32) for v in range(V)]
-    total = edge_terms(first_ref, second_ref, own_ref, x_ref, hmat_ref, loc_ref, 0, zeros)
+    total = edge_terms(first_ref, second_ref, own_ref, x_ref, hmat_ref, loc_ref, 0, HEAD, zeros)
     for v in range(V):
         total_ref[v] = total[v]
 
@@ -245,7 +248,7 @@
 
 def edge_kernel(where_ref, first_ref, second_ref, own_ref, x_ref, hmat_ref, loc_ref, inner_ref, head_ref, inc_ref, keep_ref, give_ref):
     total = [head_ref[v] for v in range(V)]
-    total = edge_terms(first_ref, second_ref, own_ref, x_ref, hmat_ref, loc_ref, HEAD, total)
+    total = edge_terms(first_ref, second_ref, own_ref, x_ref, hmat_ref, loc_ref, HEAD, own_ref.shape[0] - HEAD, total)
     for v in range(V):
         inc_ref[v, :64] = total[v][:64]
         inc_ref[v, 64:192] = inner_ref[v]
@@ -267,17 +270,14 @@
     return jnp.maximum(1.0 - jnp.abs(distance), 0.0)
 
 
-def weights_kernel(where_ref, own_ref, here_ref, there_ref, wown_ref, wnear_ref, lev_ref, innov_ref, weight_ref, e_ref, o_ref):
-    core_0 = where_ref[10] == 0
-    e_ref[...] = jnp.where(core_0, here_ref[...], there_ref[...])
-    o_ref[...] = jnp.where(core_0, there_ref[...], here_ref[...])
+def weights_kernel(where_ref, own_ref, o_ref, e_ref, wown_ref, wnear_ref, lev_ref, innov_ref, weight_ref):
     even_row = where_ref[2].astype(F32)
     odd_row = where_ref[3].astype(F32)
     odd_there = where_ref[4].astype(F32)
     cell = lax.broadcasted_iota(jnp.int32, (32, SLOTS), 0).astype(F32)
 
     def line(ref, field, v):
-        at = 6 * (V * field + v)
+        at = ref.shape[0] - OBS + 6 * (V * field + v)
         return jnp.concatenate([ref[at + a : at + a + 1] for a in range(6)], axis=1)
 
     def columns(code):
@@ -312,7 +312,7 @@
             weight_ref[row] = weight
 
 
-def weights(where, own, here, there):
+def weights(where, own, first, second):
     return call(
         weights_kernel,
         (
@@ -323,8 +323,7 @@
             sds(9, SLOTS),
         ),
         ins=[SMEM, VMEM, VMEM, VMEM],
-        scratch=[pltpu.VMEM(own.shape, F32), pltpu.VMEM(own.shape, F32)],
-    )(where, own, here, there)
+    )(where, own, first, second)
 
 
 def picker(lev_ref):
@@ -544,6 +543,10 @@
     return lax.ppermute(x, ("mem", "tile"), SECOND)
 
 
+def swap_near(x):
+    return lax.ppermute(x, ("mem", "tile"), NEAR)
+
+
 def swap_core(x):
     return lax.ppermute(x, "mem", [(m, m ^ 1) for m in range(MEMS)])
 
@@ -569,8 +572,8 @@
             tile % 2,
             tile,
             first_low,
-            7 * 32 * (1 - first_low),
-            7 * 32 * first_low,
+            7 * 32 * (1 - (tile + core) % 2),
+            7 * 32 * ((tile + core) % 2),
             core,
         ]
     ).astype(jnp.int32)
@@ -584,12 +587,10 @@
     inner, own_edge, x, smat, hmat, send_first, send_second = own_part(where, flat, flat_ens, loc_vert, own_obs)
     rest = send_first.reshape(-1, 128), send_second.reshape(-1, 128)
     first_rest, second_rest = swap_first(rest[0]), swap_second(rest[1])
-    here_obs = first[64 * HEAD :]
-    there_obs = swap_core(here_obs)
-    wown, wnear, lev, innov, weight = weights(where, own_obs, here_obs, there_obs)
+    wown, wnear, lev, innov, weight = weights(where, own_obs, first, second)
     head = head_part(first, second, own_edge, x, hmat, loc_vert, lev)
     inc, keep, give = edge_part(where, first_rest, second_rest, own_edge, x, hmat, loc_vert, inner, head)
-    near = swap_first(keep + swap_core(give))
+    near = swap_near(keep + swap_core(give))
     mine = mine_part(where, inc, wown, wnear, lev)
     vals = values(where, mine, near, wown, wnear, lev)
     vals = vals + swap_core(vals)

time: 106 us -> 101 us (0.953)
  the two profiles are of different devices: /device:TPU:32 before, /device:TPU:6 now
where the time goes in v9:
time: 101 us
  waiting for transfers between devices  49.8 us (49%)
  starting transfers between devices  23.2 us (23%)
  Pallas kernels  23.1 us (23%)
  local copies, waits for them, and re-layouts  3.73 us (4%)
  between operations  1.03 us (1%)
    ppermute x4, waiting for transfers between devices, swap_first(): return lax.ppermute(x, ('mem', 'tile'), FIRST)  26.9 us
    ppermute x4, starting transfers between devices, swap_first(): return lax.ppermute(x, ('mem', 'tile'), FIRST)  16.4 us
    ppermute x4, waiting for transfers between devices, swap_second(): return lax.ppermute(x, ('mem', 'tile'), SECOND)  13.7 us
    pallas_call x1, Pallas kernels, back_part(): call(back_kernel, (sds(members, 256, 128), sds(members, 128, 128), sds(me...  5.38 us
    ppermute x1, waiting for transfers between devices, swap_chip(): return lax.ppermute(x, 'mem', [(m, m ^ 2) for m in range(MEMS)])  3.86 us
    pallas_call x1, Pallas kernels, own_part(): call(own_kernel, (sds(V, 128, 128), sds(members, 128, 128), sds(members,...  3.82 us
    unnamed x12, local copies, waits for them, and re-layouts  3.64 us
    ppermute x2, starting transfers between devices, swap_core(): return lax.ppermute(x, 'mem', [(m, m ^ 1) for m in range(MEMS)])  3.4 us
  transfers between devices with their start and end apart: 12, of which 12 were waited for; matrix products, arithmetic and copies ran while one was open for 0% of the time, Pallas kernels for 15%

profile of v9, /device:TPU:6, one launch (start us, length us, event | category | flops | bytes accessed | tf_op | source)
XLA Modules:
  0.0 100.8 jit_solution(12258136673262573085)
XLA Ops:
  0.8 2.1 %shard_map.82 = (f32[840,128]{1,0:T(8,128)}, f32[840,128]{1,0:T(8,128)}, f32[72,128]{1,0:T(8,128)}) custom-call(s32[1]{0:T(128)S(6)} %copy.13.count_ref, s32[1,2048]{1,0:T(1,128)} %refs_0_.1, s32[1,2048]{1,0:T(1,128)} %refs_1_.1, f32[1,2048]{1,0:T(1,128)} %refs_2_.1, f32[1,2048]{1,0:T(1,128)} %refs_3_.1, bf16[20,4,64,128]{3,2,1,0:T(8,128)(2,1)} %bitcast.20), custom_call_target="tpu_custom_call" | custom-call | flops 1000 | bytes 1000 | tf_op jit(solution)/shard_map/pallas_call | solution.py:146
  2.8 9.1 %collective-permute-start.2 = (f32[840,128]{1,0:T(8,128)}, f32[840,128]{1,0:T(8,128)S(1)}, u32[]{:S(2)}, u32[]{:S(2)}) collective-permute-start(f32[840,128]{1,0:T(8,128)} %get-tuple-element.37), channel_id=1, source_target_pairs={{0,64},{1,2},{2,1},{3,4},{4,3},{5,6},{6,5},{7,8},{8,7},{9,10},{10,... | collective-permute-start | bytes 1290248 | tf_op jit(solution)/shard_map/ppermute | solution.py:539
  12.1 2.1 %copy-done = bf16[20,3,8,32,128]{4,3,2,1,0:T(8,128)(2,1)S(1)} copy-done((bf16[20,3,8,32,128]{4,3,2,1,0:T(8,128)(2,1)S(1)}, bf16[20,3,8,32,128]{4,3,2,1,0:T(8,128)(2,1)}, u32[]{:S(2)}) %copy-start) | copy-done | bytes 3932184
  14.2 0.8 copy-done.3
  14.9 0.8 copy-done.5
  15.7 3.8 %shard_map.83 = (f32[3,128,128]{2,1,0:T(8,128)S(1)}, f32[20,128,128]{2,1,0:T(8,128)S(1)}, bf16[20,3,128,128]{3,2,1,0:T(8,128)(2,1)S(1)}, bf16[256,256]{1,0:T(8,1...) custom-call(s32[11]{0:T(128)S(1)} %stack.51.where_ref, ...), custom_call_target="tpu_custom_call" | custom-call | flops 1000 | bytes 1000 | tf_op jit(solution)/shard_map/pallas_call | solution.py:193
  19.5 3.0 %collective-permute-start.1 = (f32[512,128]{1,0:T(8,128)S(1)}, f32[512,128]{1,0:T(8,128)S(1)}, u32[]{:S(2)}, u32[]{:S(2)}) collective-permute-start(f32[512,128]{1,0:T(8,128)S(1)} %bitcast.24), channel_id=1, source_target_pairs={{0,1},{1,0},{2,3},{3,2},{4,5},{5,4},{6,7},{7,6},{8,9},{9,8},{10,11... | collective-permute-start | bytes 786440 | tf_op jit(solution)/shard_map/ppermute | solution.py:543
  22.6 8.5 %collective-permute-done.2.o_ref.first_ref = f32[840,128]{1,0:T(8,128)S(1)} collective-permute-done((f32[840,128]{1,0:T(8,128)}, f32[840,128]{1,0:T(8,128)S(1)}, u32[]{:S(2)}, u32[]{:S(2)}) %collective-permute-start.2) | collective-permute-done | bytes 430112 | tf_op jit(solution)/shard_map/ppermute | solution.py:539
  31.1 2.5 %collective-permute-done.3.e_ref.second_ref = f32[840,128]{1,0:T(8,128)S(1)} collective-permute-done((f32[840,128]{1,0:T(8,128)}, f32[840,128]{1,0:T(8,128)S(1)}, u32[]{:S(2)}, u32[]{:S(2)}) %collective-permute-start.3) | collective-permute-done | bytes 430112 | tf_op jit(solution)/shard_map/ppermute | solution.py:543
  33.6 1.1 %shard_map.84 = (bf16[3,320,768]{2,1,0:T(8,128)(2,1)S(1)}, bf16[2,3,64,768]{3,2,1,0:T(8,128)(2,1)S(1)}, f32[9,768]{1,0:T(8,128)S(1)}, f32[9,768]{1,0:T(8,128)S(1)}, f32[9,768]{1,0:T(8,128)S(1)}) custom-call(s32[11]{0:T(128)S(1)} %stack.51.where_ref, f32[72,128]{1,0:T(8,128)S(1)} %copy-done.5, f32[840,128]{1,0:T(8,128)S(1)} %collective-permute-done.2.o_ref.first_ref, ...), custom_call_target="tpu_custom_call" | custom-call | flops 1000 | bytes 1000 | tf_op jit(solution)/shard_map/pallas_call | solution.py:316
  34.7 1.4 %shard_map.85.head_ref = f32[3,128,128]{2,1,0:T(8,128)S(1)} custom-call(f32[840,128]{1,0:T(8,128)S(1)} %collective-permute-done.2.o_ref.first_ref, f32[840,128]{1,0:T(8,128)S(1)} %collective-permute-done.3.e_ref.second_ref, f32[20,128,128]{2,1,0:T(8,128)S(1)} %get-tuple-element.33.own_ref, bf16[20,3,128,128]{3,2,1,0:T(8,128)(2,1)S(1)} %get-tuple-element.34.x_ref, ...), custom_call_target="tpu_custom_call" | custom-call | flops 1000 | bytes 1000 | tf_op jit(solution)/shard_map/pallas_call | solution.py:244
  36.1 8.8 %collective-permute-done.1.second_ref = f32[512,128]{1,0:T(8,128)S(1)} collective-permute-done((f32[512,128]{1,0:T(8,128)S(1)}, f32[512,128]{1,0:T(8,128)S(1)}, u32[]{:S(2)}, u32[]{:S(2)}) %collective-permute-start.1) | collective-permute-done | bytes 262176 | tf_op jit(solution)/shard_map/ppermute | solution.py:543
  45.0 0.2 collective-permute-done.first_ref
  45.2 1.6 %shard_map.86 = (f32[3,256,128]{2,1,0:T(8,128)S(1)}, f32[3,32,128]{2,1,0:T(8,128)S(1)}, f32[3,32,128]{2,1,0:T(8,128)S(1)}) custom-call(s32[11]{0:T(128)S(1)} %stack.51.where_ref, f32[512,128]{1,0:T(8,128)S(1)} %collective-permute-done.first_ref, f32[512,128]{1,0:T(8,128)S(1)} %collective-permute-done.1.second_ref, ...), custom_call_target="tpu_custom_call" | custom-call | flops 1000 | bytes 1000 | tf_op jit(solution)/shard_map/pallas_call | solution.py:261
  46.9 1.2 %collective-permute-done.4 = f32[3,32,128]{2,1,0:T(8,128)S(1)} collective-permute-done((f32[3,32,128]{2,1,0:T(8,128)S(1)}, f32[3,32,128]{2,1,0:T(8,128)S(1)}, u32[]{:S(2)}, u32[]{:S(2)}) %collective-permute-start.4) | collective-permute-done | bytes 49184 | tf_op jit(solution)/shard_map/ppermute | solution.py:551
  48.2 1.7 %shard_map.87.mine_ref = f32[9,768]{1,0:T(8,128)S(1)} custom-call(s32[11]{0:T(128)S(1)} %stack.51.where_ref, f32[3,256,128]{2,1,0:T(8,128)S(1)} %get-tuple-element.40.inc_ref, bf16[3,320,768]{2,1,0:T(8,128)(2,1)S(1)} %get-tuple-element.41.wown_ref, bf16[2,3,64,768]{3,2,1,0:T(8,128)(2,1)S(1)} %get-tuple-element.42.wnear_ref, ...), custom_call_target="tpu_custom_call" | custom-call | flops 1000 | bytes 1000 | tf_op jit(solution)/shard_map/pallas_call | solution.py:353
  49.9 3.3 %collective-permute-done.5.near_ref = f32[3,32,128]{2,1,0:T(8,128)S(1)} collective-permute-done((f32[3,32,128]{2,1,0:T(8,128)S(1)}, f32[3,32,128]{2,1,0:T(8,128)S(1)}, u32[]{:S(2)}, u32[]{:S(2)}) %collective-permute-start.5) | collective-permute-done | bytes 49184 | tf_op jit(solution)/shard_map/ppermute | solution.py:547
  53.2 1.4 %shard_map.88 = f32[54,128]{1,0:T(8,128)S(1)} custom-call(s32[11]{0:T(128)S(1)} %stack.51.where_ref, f32[9,768]{1,0:T(8,128)S(1)} %shard_map.87.mine_ref, f32[3,32,128]{2,1,0:T(8,128)S(1)} %collective-permute-done.5.near_ref, bf16[3,320,768]{2,1,0:T(8,128)(2,1)S(1)} %get-tuple-element.41.wown_ref, bf16[2,3,64,768]{3,2,1,0:T(8,128)(2,1)S(1)} %get-tuple-element.42.wnear_ref, ...), custom_call_target="tpu_custom_call" | custom-call | flops 1000 | bytes 1000 | tf_op jit(solution)/shard_map/pallas_call | solution.py:381
  54.5 3.3 %collective-permute-start.6 = (f32[54,128]{1,0:T(8,128)S(1)}, f32[54,128]{1,0:T(8,128)S(1)}, u32[]{:S(2)}, u32[]{:S(2)}) collective-permute-start(f32[54,128]{1,0:T(8,128)S(1)} %shard_map.88), channel_id=1, source_target_pairs={{0,64},{64,0},{128,192},{192,128},{1,65},{65,1},{129,193},{193,129... | collective-permute-start | bytes 82952 | tf_op jit(solution)/shard_map/ppermute | solution.py:551
  57.9 0.9 collective-permute-done.6
  58.7 3.9 %collective-permute-done.7.v1 = f32[54,128]{1,0:T(8,128)S(1)} collective-permute-done((f32[54,128]{1,0:T(8,128)S(1)}, f32[54,128]{1,0:T(8,128)S(1)}, u32[]{:S(2)}, u32[]{:S(2)}) %collective-permute-start.7) | collective-permute-done | bytes 27680 | tf_op jit(solution)/shard_map/ppermute | solution.py:555
  62.6 1.9 %shard_map.89 = (f32[3,256,128]{2,1,0:T(8,128)S(1)}, f32[12,64,128]{2,1,0:T(8,128)S(1)}, f32[12,64,128]{2,1,0:T(8,128)S(1)}) custom-call(s32[11]{0:T(128)S(1)} %stack.51.where_ref, f32[54,128]{1,0:T(8,128)S(1)} %add.31.v0, f32[54,128]{1,0:T(8,128)S(1)} %collective-permute-done.7.v1, f32[9,768]{1,0:T(8,128)S(1)} %get-tuple-element.45.innov_ref, ...), custom_call_target="tpu_custom_call" | custom-call | flops 1000 | bytes 1000 | tf_op jit(solution)/shard_map/pallas_call | solution.py:421
  64.5 4.5 %collective-permute-start.10 = (f32[12,64,128]{2,1,0:T(8,128)S(1)}, f32[12,64,128]{2,1,0:T(8,128)S(1)}, u32[]{:S(2)}, u32[]{:S(2)}) collective-permute-start(f32[12,64,128]{2,1,0:T(8,128)S(1)} %get-tuple-element.52), channel_id=1, source_target_pairs={{0,64},{1,2},{2,1},{3,4},{4,3},{5,6},{6,5},{7,8},{8,7},{9,10},{10,... | collective-permute-start | bytes 1179656 | tf_op jit(solution)/shard_map/ppermute | solution.py:539
  69.1 5.4 %shard_map.90 = (f32[20,256,128]{2,1,0:T(8,128)}, f32[20,128,128]{2,1,0:T(8,128)S(1)}, f32[8,64,128]{2,1,0:T(8,128)S(1)}, f32[8,64,128]{2,1,0:T(8,128)S(1)}) custom-call(s32[11]{0:T(128)S(1)} %stack.51.where_ref, bf16[20,256,128]{2,1,0:T(8,128)(2,1)S(1)} %bitcast.22, bf16[20,3,256,128]{3,2,1,0:T(8,128)(2,1)S(1)} %bitcast.19, ...), custom_call_target="tpu_custom_call" | custom-call | flops 1000 | bytes 1000 | tf_op jit(solution)/shard_map/pallas_call | solution.py:453
  74.4 2.7 %collective-permute-start.8 = (f32[8,64,128]{2,1,0:T(8,128)S(1)}, f32[8,64,128]{2,1,0:T(8,128)S(1)}, u32[]{:S(2)}, u32[]{:S(2)}) collective-permute-start(f32[8,64,128]{2,1,0:T(8,128)S(1)} %get-tuple-element.49), channel_id=1, source_target_pairs={{0,64},{1,2},{2,1},{3,4},{4,3},{5,6},{6,5},{7,8},{8,7},{9,10},{10,... | collective-permute-start | bytes 786440 | tf_op jit(solution)/shard_map/ppermute | solution.py:539
  77.1 0.2 collective-permute-start.9
  77.3 11.7 %collective-permute-done.10.first_ref = f32[12,64,128]{2,1,0:T(8,128)S(1)} collective-permute-done((f32[12,64,128]{2,1,0:T(8,128)S(1)}, f32[12,64,128]{2,1,0:T(8,128)S(1)}, u32[]{:S(2)}, u32[]{:S(2)}) %collective-permute-start.10) | collective-permute-done | bytes 393248 | tf_op jit(solution)/shard_map/ppermute | solution.py:539
  89.1 1.5 %collective-permute-done.11.second_ref = f32[12,64,128]{2,1,0:T(8,128)S(1)} collective-permute-done((f32[12,64,128]{2,1,0:T(8,128)S(1)}, f32[12,64,128]{2,1,0:T(8,128)S(1)}, u32[]{:S(2)}, u32[]{:S(2)}) %collective-permute-start.11) | collective-permute-done | bytes 393248 | tf_op jit(solution)/shard_map/ppermute | solution.py:543
  90.6 1.4 %shard_map.91.unused_ref = f32[20,4,64,128]{3,2,1,0:T(8,128)} custom-call(f32[12,64,128]{2,1,0:T(8,128)S(1)} %collective-permute-done.10.first_ref, f32[12,64,128]{2,1,0:T(8,128)S(1)} %collective-permute-done.11.second_ref, f32[20,128,128]{2,1,0:T(8,128)S(1)} %get-tuple-element.51.edge_ref, ...), custom_call_target="tpu_custom_call", output_to_operand_aliasing={{}: (5, {})} | custom-call | flops 1000 | bytes 1000 | tf_op jit(solution)/shard_map/pallas_call | solution.py:501
  92.0 6.5 %collective-permute-done.8.first_ref = f32[8,64,128]{2,1,0:T(8,128)S(1)} collective-permute-done((f32[8,64,128]{2,1,0:T(8,128)S(1)}, f32[8,64,128]{2,1,0:T(8,128)S(1)}, u32[]{:S(2)}, u32[]{:S(2)}) %collective-permute-start.8) | collective-permute-done | bytes 262176 | tf_op jit(solution)/shard_map/ppermute | solution.py:539
  98.5 0.8 collective-permute-done.9.second_ref
  99.3 1.3 %shard_map.92 = f32[20,4,64,128]{3,2,1,0:T(8,128)} custom-call(f32[8,64,128]{2,1,0:T(8,128)S(1)} %collective-permute-done.8.first_ref, f32[8,64,128]{2,1,0:T(8,128)S(1)} %collective-permute-done.9.second_ref, f32[20,128,128]{2,1,0:T(8,128)S(1)} %get-tuple-element.51.edge_ref, ...), custom_call_target="tpu_custom_call", output_to_operand_aliasing={{}: (5, {})} | custom-call | flops 1000 | bytes 1000 | tf_op jit(solution)/shard_map/pallas_call | solution.py:501
  (18 shorter events, 0.4 us)
Async XLA Ops:
  0.0 12.0 %copy-start.2 = (bf16[20,8,32,128]{3,2,1,0:T(8,128)(2,1)S(1)}, bf16[20,8,32,128]{3,2,1,0:T(8,128)(2,1)}, u32[]{:S(2)}) copy-start(bf16[20,8,32,128]{3,2,1,0:T(8,128)(2,1)} %param.8) | copy-start | bytes 3932164
  2.8 28.2 %collective-permute-start.2 = (f32[840,128]{1,0:T(8,128)}, f32[840,128]{1,0:T(8,128)S(1)}, u32[]{:S(2)}, u32[]{:S(2)}) collective-permute-start(f32[840,128]{1,0:T(8,128)} %get-tuple-element.37), channel_id=1, source_target_pairs={{0,64},{1,2},{2,1},{3,4},{4,3},{5,6},{6,5},{7,8},{8,7},{9,10},{10,... | collective-permute-start | bytes 1290248 | tf_op jit(solution)/shard_map/ppermute | solution.py:539
  11.9 21.6 %collective-permute-start.3 = (f32[840,128]{1,0:T(8,128)}, f32[840,128]{1,0:T(8,128)S(1)}, u32[]{:S(2)}, u32[]{:S(2)}) collective-permute-start(f32[840,128]{1,0:T(8,128)} %get-tuple-element.38), channel_id=1, source_target_pairs={{0,1},{1,0},{2,3},{3,2},{4,5},{5,4},{6,7},{7,6},{8,9},{9,8},{10,11... | collective-permute-start | bytes 1290248 | tf_op jit(solution)/shard_map/ppermute | solution.py:543
  12.0 2.1 %copy-start = (bf16[20,3,8,32,128]{4,3,2,1,0:T(8,128)(2,1)S(1)}, bf16[20,3,8,32,128]{4,3,2,1,0:T(8,128)(2,1)}, u32[]{:S(2)}) copy-start(bf16[20,3,8,32,128]{4,3,2,1,0:T(8,128)(2,1)} %param.9) | copy-start | bytes 11796484
  14.2 0.8 copy-start.3
  14.9 0.8 copy-start.5
  19.5 25.5 %collective-permute-start.1 = (f32[512,128]{1,0:T(8,128)S(1)}, f32[512,128]{1,0:T(8,128)S(1)}, u32[]{:S(2)}, u32[]{:S(2)}) collective-permute-start(f32[512,128]{1,0:T(8,128)S(1)} %bitcast.24), channel_id=1, source_target_pairs={{0,1},{1,0},{2,3},{3,2},{4,5},{5,4},{6,7},{7,6},{8,9},{9,8},{10,11... | collective-permute-start | bytes 786440 | tf_op jit(solution)/shard_map/ppermute | solution.py:543
  22.5 22.7 %collective-permute-start = (f32[512,128]{1,0:T(8,128)S(1)}, f32[512,128]{1,0:T(8,128)S(1)}, u32[]{:S(2)}, u32[]{:S(2)}) collective-permute-start(f32[512,128]{1,0:T(8,128)S(1)} %bitcast.23), channel_id=1, source_target_pairs={{0,64},{1,2},{2,1},{3,4},{4,3},{5,6},{6,5},{7,8},{8,7},{9,10},{10,... | collective-permute-start | bytes 786440 | tf_op jit(solution)/shard_map/ppermute | solution.py:539
  46.8 1.3 %collective-permute-start.4 = (f32[3,32,128]{2,1,0:T(8,128)S(1)}, f32[3,32,128]{2,1,0:T(8,128)S(1)}, u32[]{:S(2)}, u32[]{:S(2)}) collective-permute-start(f32[3,32,128]{2,1,0:T(8,128)S(1)} %get-tuple-element.44), channel_id=1, source_target_pairs={{0,64},{64,0},{128,192},{192,128},{1,65},{65,1},{129,193},{193,129... | collective-permute-start | bytes 147464 | tf_op jit(solution)/shard_map/ppermute | solution.py:551
  48.1 5.1 %collective-permute-start.5 = (f32[3,32,128]{2,1,0:T(8,128)S(1)}, f32[3,32,128]{2,1,0:T(8,128)S(1)}, u32[]{:S(2)}, u32[]{:S(2)}) collective-permute-start(f32[3,32,128]{2,1,0:T(8,128)S(1)} %add.30), channel_id=1, source_target_pairs={{0,1},{1,0},{2,3},{3,2},{4,5},{5,4},{6,7},{7,6},{8,9},{9,8},{10,11... | collective-permute-start | bytes 147464 | tf_op jit(solution)/shard_map/ppermute | solution.py:547
  54.5 4.2 %collective-permute-start.6 = (f32[54,128]{1,0:T(8,128)S(1)}, f32[54,128]{1,0:T(8,128)S(1)}, u32[]{:S(2)}, u32[]{:S(2)}) collective-permute-start(f32[54,128]{1,0:T(8,128)S(1)} %shard_map.88), channel_id=1, source_target_pairs={{0,64},{64,0},{128,192},{192,128},{1,65},{65,1},{129,193},{193,129... | collective-permute-start | bytes 82952 | tf_op jit(solution)/shard_map/ppermute | solution.py:551
  58.7 3.9 %collective-permute-start.7 = (f32[54,128]{1,0:T(8,128)S(1)}, f32[54,128]{1,0:T(8,128)S(1)}, u32[]{:S(2)}, u32[]{:S(2)}) collective-permute-start(f32[54,128]{1,0:T(8,128)S(1)} %add.31.v0), channel_id=1, source_target_pairs={{0,128},{64,192},{128,0},{192,64},{1,129},{65,193},{129,1},{193,65... | collective-permute-start | bytes 82952 | tf_op jit(solution)/shard_map/ppermute | solution.py:555
  62.6 6.5 %copy-start.1 = (bf16[20,3,8,32,128]{4,3,2,1,0:T(8,128)(2,1)S(1)}, bf16[20,3,8,32,128]{4,3,2,1,0:T(8,128)(2,1)}, u32[]{:S(2)}) copy-start(bf16[20,3,8,32,128]{4,3,2,1,0:T(8,128)(2,1)} %param.9) | copy-start | bytes 11796484
  62.6 6.5 %copy-start.4 = (bf16[128,128]{1,0:T(8,128)(2,1)S(1)}, bf16[128,128]{1,0:T(8,128)(2,1)}, u32[]{:S(2)}) copy-start(bf16[128,128]{1,0:T(8,128)(2,1)} %loc_ref.11) | copy-start | bytes 98308
  64.5 24.5 %collective-permute-start.10 = (f32[12,64,128]{2,1,0:T(8,128)S(1)}, f32[12,64,128]{2,1,0:T(8,128)S(1)}, u32[]{:S(2)}, u32[]{:S(2)}) collective-permute-start(f32[12,64,128]{2,1,0:T(8,128)S(1)} %get-tuple-element.52), channel_id=1, source_target_pairs={{0,64},{1,2},{2,1},{3,4},{4,3},{5,6},{6,5},{7,8},{8,7},{9,10},{10,... | collective-permute-start | bytes 1179656 | tf_op jit(solution)/shard_map/ppermute | solution.py:539
  69.1 21.5 %collective-permute-start.11 = (f32[12,64,128]{2,1,0:T(8,128)S(1)}, f32[12,64,128]{2,1,0:T(8,128)S(1)}, u32[]{:S(2)}, u32[]{:S(2)}) collective-permute-start(f32[12,64,128]{2,1,0:T(8,128)S(1)} %get-tuple-element.53), channel_id=1, source_target_pairs={{0,1},{1,0},{2,3},{3,2},{4,5},{5,4},{6,7},{7,6},{8,9},{9,8},{10,11... | collective-permute-start | bytes 1179656 | tf_op jit(solution)/shard_map/ppermute | solution.py:543
  74.4 24.0 %collective-permute-start.8 = (f32[8,64,128]{2,1,0:T(8,128)S(1)}, f32[8,64,128]{2,1,0:T(8,128)S(1)}, u32[]{:S(2)}, u32[]{:S(2)}) collective-permute-start(f32[8,64,128]{2,1,0:T(8,128)S(1)} %get-tuple-element.49), channel_id=1, source_target_pairs={{0,64},{1,2},{2,1},{3,4},{4,3},{5,6},{6,5},{7,8},{8,7},{9,10},{10,... | collective-permute-start | bytes 786440 | tf_op jit(solution)/shard_map/ppermute | solution.py:539
  77.1 22.2 %collective-permute-start.9 = (f32[8,64,128]{2,1,0:T(8,128)S(1)}, f32[8,64,128]{2,1,0:T(8,128)S(1)}, u32[]{:S(2)}, u32[]{:S(2)}) collective-permute-start(f32[8,64,128]{2,1,0:T(8,128)S(1)} %get-tuple-element.50), channel_id=1, source_target_pairs={{0,1},{1,0},{2,3},{3,2},{4,5},{5,4},{6,7},{7,6},{8,9},{9,8},{10,11... | collective-permute-start | bytes 786440 | tf_op jit(solution)/shard_map/ppermute | solution.py:543

commit v10 on v9

--- a/solution.py
+++ b/solution.py
@@ -12,7 +12,8 @@
 BF16 = jnp.bfloat16
 SLOTS = 768
 GROUP = 4
-HEAD = 12
+HEAD = 16
+HEAD_BACK = 12
 OBS = 72
 
 TILES = 64
@@ -122,39 +123,56 @@
                 out_ref[row : row + 1] = total[6 * f + a : 6 * f + a + 1, 128 * v : 128 * v + 128]
 
 
-def send_kernel(count_ref, *refs):
-    obs_in, (quarters_ref, first_ref, second_ref, obs_ref), obs_here, (edges, sems) = refs[:4], refs[4:8], refs[8:12], refs[12:]
-    head = pl.ds(0, HEAD)
-    copies = [pltpu.make_async_copy(quarters_ref.at[head, 3 * n], edges.at[n], sems.at[n]) for n in range(2)]
-    fetches = [pltpu.make_async_copy(obs_in[n], obs_here[n], sems.at[2 + n]) for n in range(4)]
-    for copy in fetches + copies:
+def edge_rows(quarters_ref, start, first_ref, second_ref, edges, sems):
+    count = edges.shape[1]
+    members = pl.ds(start, count)
+    copies = [pltpu.make_async_copy(quarters_ref.at[members, 3 * n], edges.at[n], sems.at[n]) for n in range(2)]
+    for copy in copies:
         copy.start()
-    for copy in fetches:
-        copy.wait()
-    sort_observations(count_ref[0], *obs_here, obs_ref)
-    first_ref[64 * HEAD :] = obs_ref[...]
-    second_ref[64 * HEAD :] = obs_ref[...]
     for copy in copies:
         copy.wait()
     low = side_of_first()
-    for k in range(HEAD):
+    for k in range(count):
         first_ref[64 * k : 64 * k + 64] = edges[1 - low, k].astype(F32)
         second_ref[64 * k : 64 * k + 64] = edges[low, k].astype(F32)
 
 
-def send_part(count, col, lev, innov, weight, quarters):
+def send_kernel(quarters_ref, first_ref, second_ref, token_ref, edges, sems):
+    token_ref[...] = jnp.zeros_like(token_ref)
+    edge_rows(quarters_ref, 0, first_ref, second_ref, edges, sems)
+
+
+def send_part(quarters):
     return call(
         send_kernel,
-        (sds(64 * HEAD + OBS, 128), sds(64 * HEAD + OBS, 128), sds(OBS, 128)),
-        ins=[SMEM] + [HBM] * 5,
+        (sds(64 * HEAD, 128), sds(64 * HEAD, 128), sds(8, 128)),
+        ins=[HBM],
         outs=(VMEM,) * 3,
-        scratch=[pltpu.VMEM(a.shape, a.dtype) for a in (col, lev, innov, weight)]
-        + [pltpu.VMEM((2, HEAD, 64, 128), BF16), pltpu.SemaphoreType.DMA((6,))],
+        scratch=[pltpu.VMEM((2, HEAD, 64, 128), BF16), pltpu.SemaphoreType.DMA((2,))],
         vmem=56,
-    )(count, col, lev, innov, weight, quarters)
-
-
-def own_kernel(where_ref, alpha_ref, ens_ref, loc_ref, after_ref, inner_ref, edge_ref, x_ref, smat_ref, hmat_ref, first_ref, second_ref):
+    )(quarters)
+
+
+def rest_kernel(count_ref, col_ref, lev_ref, innov_ref, weight_ref, quarters_ref, after_ref, first_ref, second_ref, obs_ref, edges, sems):
+    edge_rows(quarters_ref, HEAD, first_ref, second_ref, edges, sems)
+    sort_observations(count_ref[0], col_ref, lev_ref, innov_ref, weight_ref, obs_ref)
+    end = first_ref.shape[0] - OBS
+    first_ref[end:] = obs_ref[...]
+    second_ref[end:] = obs_ref[...]
+
+
+def rest_part(count, col, lev, innov, weight, quarters, after):
+    members = quarters.shape[0] - HEAD
+    return call(
+        rest_kernel,
+        (sds(64 * members + OBS, 128), sds(64 * members + OBS, 128), sds(OBS, 128)),
+        ins=[SMEM] + [VMEM] * 4 + [ANY, VMEM],
+        outs=(VMEM,) * 3,
+        scratch=[pltpu.VMEM((2, members, 64, 128), BF16), pltpu.SemaphoreType.DMA((2,))],
+    )(count, col, lev, innov, weight, quarters, after)
+
+
+def own_kernel(where_ref, alpha_ref, ens_ref, loc_ref, after_ref, inner_ref, edge_ref, x_ref, smat_ref, hmat_ref):
     @pl.when(pl.program_id(0) == 0)
     def _():
         inner_ref[...] = jnp.zeros_like(inner_ref)
@@ -177,19 +195,10 @@
     for v in range(V):
         inner_ref[v] = total[v]
 
-    @pl.when(pl.program_id(0) >= HEAD // GROUP)
-    def _():
-        low = where_ref[7] == 1
-        for k in range(GROUP):
-            rows = [alpha_ref[k, :64].astype(F32), alpha_ref[k, 192:].astype(F32)]
-            first_ref[k] = jnp.where(low, rows[0], rows[1])
-            second_ref[k] = jnp.where(low, rows[1], rows[0])
-
 
 def own_part(where, alpha, ensemble, loc, after):
     members = alpha.shape[0]
     whole = lambda *shape: pl.BlockSpec(shape, lambda i: (0,) * len(shape))
-    rest = pl.BlockSpec((GROUP, 64, 128), lambda i: (jnp.maximum(i - HEAD // GROUP, 0), 0, 0))
     return call(
         own_kernel,
         (
@@ -198,8 +207,6 @@
             sds(members, V, 128, 128, dtype=BF16),
             sds(256, 256, dtype=BF16),
             sds(128, 128, dtype=BF16),
-            sds(members - HEAD, 64, 128),
-            sds(members - HEAD, 64, 128),
         ),
         grid=(members // GROUP,),
         ins=[
@@ -207,7 +214,7 @@
             pl.BlockSpec((GROUP, 256, 128), lambda i: (i, 0, 0)),
             pl.BlockSpec((GROUP, V, 256, 128), lambda i: (i, 0, 0, 0)),
             whole(128, 128),
-            whole(OBS, 128),
+            whole(8, 128),
         ],
         outs=(
             whole(V, 128, 128),
@@ -215,8 +222,6 @@
             pl.BlockSpec((GROUP, V, 128, 128), lambda i: (i, 0, 0, 0)),
             whole(256, 256),
             whole(128, 128),
-            rest,
-            rest,
         ),
     )(where, alpha, ensemble, loc, after)
 
@@ -233,17 +238,15 @@
     return total
 
 
-def head_kernel(first_ref, second_ref, own_ref, x_ref, hmat_ref, loc_ref, after_ref, total_ref):
+def head_kernel(first_ref, second_ref, own_ref, x_ref, hmat_ref, loc_ref, total_ref):
     zeros = [jnp.zeros((128, 128), F32) for v in range(V)]
     total = edge_terms(first_ref, second_ref, own_ref, x_ref, hmat_ref, loc_ref, 0, HEAD, zeros)
     for v in range(V):
         total_ref[v] = total[v]
 
 
-def head_part(first, second, own, x, hmat, loc, after):
-    return call(head_kernel, sds(V, 128, 128), ins=[VMEM] * 7, outs=VMEM)(
-        first, second, own, x, hmat, loc, after
-    )
+def head_part(first, second, own, x, hmat, loc):
+    return call(head_kernel, sds(V, 128, 128), ins=[VMEM] * 6, outs=VMEM)(first, second, own, x, hmat, loc)
 
 
 def edge_kernel(where_ref, first_ref, second_ref, own_ref, x_ref, hmat_ref, loc_ref, inner_ref, head_ref, inc_ref, keep_ref, give_ref):
@@ -270,7 +273,8 @@
     return jnp.maximum(1.0 - jnp.abs(distance), 0.0)
 
 
-def weights_kernel(where_ref, own_ref, o_ref, e_ref, wown_ref, wnear_ref, lev_ref, innov_ref, weight_ref):
+def weights_kernel(where_ref, own_ref, o_ref, e_ref, after_ref, wown_ref, wnear_ref, lev_ref, innov_ref, weight_ref, hot_ref):
+    level = lax.broadcasted_iota(jnp.int32, (128, SLOTS), 0).astype(F32)
     even_row = where_ref[2].astype(F32)
     odd_row = where_ref[3].astype(F32)
     odd_there = where_ref[4].astype(F32)
@@ -300,7 +304,9 @@
     for n, ref in enumerate((own_ref, e_ref, o_ref)):
         for v in range(V):
             row = slice(3 * n + v, 3 * n + v + 1)
-            lev_ref[row] = line(ref, 1, v)
+            lev = line(ref, 1, v)
+            lev_ref[row] = lev
+            hot_ref[3 * n + v] = jnp.where(level == lev, 1.0, 0.0).astype(BF16)
             innov_ref[row] = line(ref, 2, v)
             weight = line(ref, 3, v)
             if n > 0:
@@ -312,7 +318,7 @@
             weight_ref[row] = weight
 
 
-def weights(where, own, first, second):
+def weights(where, own, first, second, after):
     return call(
         weights_kernel,
         (
@@ -321,9 +327,10 @@
             sds(9, SLOTS),
             sds(9, SLOTS),
             sds(9, SLOTS),
+            sds(9, 128, SLOTS, dtype=BF16),
         ),
-        ins=[SMEM, VMEM, VMEM, VMEM],
-    )(where, own, first, second)
+        ins=[SMEM] + [VMEM] * 4,
+    )(where, own, first, second, after)
 
 
 def picker(lev_ref):
@@ -386,16 +393,14 @@
     )(where, mine, near, wown, wnear, lev)
 
 
-def adjoint_kernel(where_ref, v0, v1, innov_ref, weight_ref, lev_ref, wown_ref, wnear_ref, x_ref, c_ref, first_ref, second_ref):
-    level = lax.broadcasted_iota(jnp.int32, (128, SLOTS), 0).astype(F32)
+def adjoint_kernel(where_ref, v0, v1, innov_ref, weight_ref, hot_ref, wown_ref, wnear_ref, x_ref, c_ref, first_ref, second_ref):
     value = v0[...] + v1[...]
 
     def place(weight, row):
         line = jnp.concatenate([value[6 * row + a : 6 * row + a + 1] for a in range(6)], axis=1)
         weighted = weight_ref[row : row + 1] * (line - innov_ref[row : row + 1])
-        hot = level == lev_ref[row : row + 1, :]
-        spread = jnp.where(hot, weighted, 0.0)
-        both = jnp.concatenate(halves(spread), axis=0)
+        hot = hot_ref[row]
+        both = jnp.concatenate([hot * half for half in halves(weighted)], axis=0)
         out = nt(weight, both)
         return out[:, :128] + out[:, 128:]
 
@@ -416,14 +421,14 @@
         second_ref[k] = jnp.where(first_low, high, low)
 
 
-def adjoint(where, vals, innov, weight, lev, wown, wnear, x):
-    members = HEAD
+def adjoint(where, vals, innov, weight, hot, wown, wnear, x):
+    members = HEAD_BACK
     return call(
         adjoint_kernel,
         (sds(V, 256, 128), sds(members, 64, 128), sds(members, 64, 128)),
         ins=[SMEM] + [VMEM] * 8,
         outs=(VMEM,) * 3,
-    )(where, *vals, innov, weight, lev, wown, wnear, x)
+    )(where, *vals, innov, weight, hot, wown, wnear, x)
 
 
 def drop(smoothed, loc):
@@ -449,14 +454,14 @@
 
 def back_part(where, alpha, ensemble, c, smat, loc):
     members = alpha.shape[0]
-    rest = pl.BlockSpec((GROUP, 64, 128), lambda i: (jnp.maximum(i - HEAD // GROUP, 0), 0, 0))
+    rest = pl.BlockSpec((GROUP, 64, 128), lambda i: (jnp.maximum(i - HEAD_BACK // GROUP, 0), 0, 0))
     return call(
         back_kernel,
         (
             sds(members, 256, 128),
             sds(members, 128, 128),
-            sds(members - HEAD, 64, 128),
-            sds(members - HEAD, 64, 128),
+            sds(members - HEAD_BACK, 64, 128),
+            sds(members - HEAD_BACK, 64, 128),
         ),
         grid=(members // GROUP,),
         ins=[
@@ -580,27 +585,29 @@
     flat = alpha.reshape(members, 256, 128)
     flat_ens = ensemble.reshape(members, V, 256, 128)
 
-    send_first, send_second, own_obs = send_part(
-        obs_count, obs_col, obs_lev, innovation, obs_weight, alpha.reshape(members, 4, 64, 128)
+    quarters = alpha.reshape(members, 4, 64, 128)
+    send_first, send_second, token = send_part(quarters)
+    first, second = swap_first(send_first), swap_second(send_second)
+    inner, own_edge, x, smat, hmat = own_part(where, flat, flat_ens, loc_vert, token)
+    send_first, send_second, own_obs = rest_part(
+        obs_count, obs_col, obs_lev, innovation, obs_weight, quarters, hmat
     )
-    first, second = swap_first(send_first), swap_second(send_second)
-    inner, own_edge, x, smat, hmat, send_first, send_second = own_part(where, flat, flat_ens, loc_vert, own_obs)
-    rest = send_first.reshape(-1, 128), send_second.reshape(-1, 128)
-    first_rest, second_rest = swap_first(rest[0]), swap_second(rest[1])
-    wown, wnear, lev, innov, weight = weights(where, own_obs, first, second)
-    head = head_part(first, second, own_edge, x, hmat, loc_vert, lev)
+    first_rest, second_rest = swap_first(send_first), swap_second(send_second)
+    head = head_part(first, second, own_edge, x, hmat, loc_vert)
     inc, keep, give = edge_part(where, first_rest, second_rest, own_edge, x, hmat, loc_vert, inner, head)
-    near = swap_near(keep + swap_core(give))
+    edges = keep + swap_core(give)
+    near = swap_near(edges)
+    wown, wnear, lev, innov, weight, hot = weights(where, own_obs, first_rest, second_rest, edges)
     mine = mine_part(where, inc, wown, wnear, lev)
     vals = values(where, mine, near, wown, wnear, lev)
     vals = vals + swap_core(vals)
     vals = vals, swap_chip(vals)
-    c, back_first, back_second = adjoint(where, vals, innov, weight, lev, wown, wnear, x)
+    c, back_first, back_second = adjoint(where, vals, innov, weight, hot, wown, wnear, x)
     halo_first, halo_second = swap_first(back_first), swap_second(back_second)
     out, edge, back_first, back_second = back_part(where, flat, flat_ens, c, smat, loc_vert)
     rest_first, rest_second = swap_first(back_first), swap_second(back_second)
     out = last_part(0, halo_first, halo_second, edge, hmat, loc_vert, out.reshape(members, 4, 64, 128))
-    out = last_part(HEAD, rest_first, rest_second, edge, hmat, loc_vert, out)
+    out = last_part(HEAD_BACK, rest_first, rest_second, edge, hmat, loc_vert, out)
     return out.reshape(members, 8, 32, 128)
 
 

time: 101 us -> 99.8 us (0.988)
  waiting for transfers between devices: 49.8 us -> 48 us
    ppermute x4, waiting for transfers between devices: 13.7 us -> 7.62 us  [swap_second(): return lax.ppermute(x, ('mem', 'tile'), SECOND)]
    ppermute x4, waiting for transfers between devices: 26.9 us -> 32.4 us  [swap_first(): return lax.ppermute(x, ('mem', 'tile'), FIRST)]
    ppermute x4, starting transfers between devices: 16.4 us -> 18 us  [swap_first(): return lax.ppermute(x, ('mem', 'tile'), FIRST)]
    ppermute x4, starting transfers between devices: 3.22 us -> 1.94 us  [swap_second(): return lax.ppermute(x, ('mem', 'tile'), SECOND)]
    ppermute x1, waiting for transfers between devices: 3.29 us -> 2.08 us  [swap_near(): return lax.ppermute(x, ('mem', 'tile'), NEAR)]
    pallas_call x2 -> x3, Pallas kernels: 3.52 us -> 4.43 us  [the longest x1 2.16 us: send_part(): call(send_kernel, (sds(64 * HEAD, 128), sds(64 * HEAD, 128), sds(8, 128))...]
    unnamed x12 -> x20, local copies, waits for them, and re-layouts: 3.64 us -> 3.56 us
  transfers between devices with their start and end apart: 12 -> 12, of which waited for: 12 -> 12; matrix products, arithmetic and copies ran while one was open for 0% -> 0% of each run, Pallas kernels for 15% -> 16%
where the time goes in v10:
time: 99.8 us; the launch traced here: 99.6 us
  waiting for transfers between devices  48 us (48%)
  Pallas kernels  23.7 us (24%)
  starting transfers between devices  23.2 us (23%)
  local copies, waits for them, and re-layouts  3.65 us (4%)
    ppermute x4, waiting for transfers between devices, swap_first(): return lax.ppermute(x, ('mem', 'tile'), FIRST)  32.4 us
    ppermute x4, starting transfers between devices, swap_first(): return lax.ppermute(x, ('mem', 'tile'), FIRST)  18 us
    ppermute x4, waiting for transfers between devices, swap_second(): return lax.ppermute(x, ('mem', 'tile'), SECOND)  7.62 us
    pallas_call x1, Pallas kernels, back_part(): call(back_kernel, (sds(members, 256, 128), sds(members, 128, 128), sds(me...  5.33 us
    ppermute x1, waiting for transfers between devices, swap_chip(): return lax.ppermute(x, 'mem', [(m, m ^ 2) for m in range(MEMS)])  3.86 us
    pallas_call x1, Pallas kernels, own_part(): call(own_kernel, (sds(V, 128, 128), sds(members, 128, 128), sds(members,...  3.79 us
    unnamed x20, local copies, waits for them, and re-layouts  3.56 us
    ppermute x2, starting transfers between devices, swap_core(): return lax.ppermute(x, 'mem', [(m, m ^ 1) for m in range(MEMS)])  3.22 us
  transfers between devices with their start and end apart: 12, of which 12 were waited for; matrix products, arithmetic and copies ran while one was open for 0% of the time, Pallas kernels for 16%

profile of v10, /device:TPU:6, one launch (start us, length us, event | category | flops | bytes accessed | tf_op | source)
XLA Modules:
  0.0 99.6 jit_solution(4340582676491910092)
XLA Ops:
  0.0 2.2 %shard_map.82 = (f32[1024,128]{1,0:T(8,128)}, f32[1024,128]{1,0:T(8,128)}, f32[8,128]{1,0:T(8,128)}) custom-call(bf16[20,4,64,128]{3,2,1,0:T(8,128)(2,1)} %bitcast.16), custom_call_target="tpu_custom_call" | custom-call | flops 1000 | bytes 1000 | tf_op jit(solution)/shard_map/pallas_call | solution.py:146
  2.2 9.1 %collective-permute-start.2 = (f32[1024,128]{1,0:T(8,128)}, f32[1024,128]{1,0:T(8,128)S(1)}, u32[]{:S(2)}, u32[]{:S(2)}) collective-permute-start(f32[1024,128]{1,0:T(8,128)} %get-tuple-element.39), channel_id=1, source_target_pairs={{0,64},{1,2},{2,1},{3,4},{4,3},{5,6},{6,5},{7,8},{8,7},{9,10},{10,... | collective-permute-start | bytes 1572872 | tf_op jit(solution)/shard_map/ppermute | solution.py:544
  11.4 2.1 %copy-done.1 = bf16[20,3,8,32,128]{4,3,2,1,0:T(8,128)(2,1)S(1)} copy-done((bf16[20,3,8,32,128]{4,3,2,1,0:T(8,128)(2,1)S(1)}, bf16[20,3,8,32,128]{4,3,2,1,0:T(8,128)(2,1)}, u32[]{:S(2)}) %copy-start.1) | copy-done | bytes 3932184
  13.5 0.8 copy-done.3
  14.2 0.7 copy-done.9
  14.9 3.8 %shard_map.83 = (f32[3,128,128]{2,1,0:T(8,128)S(1)}, f32[20,128,128]{2,1,0:T(8,128)S(1)}, bf16[20,3,128,128]{3,2,1,0:T(8,128)(2,1)S(1)}, bf16[256,256]{1,0:T(8,128)(2,1)S(1)}, bf16[128,128]{1,0:T(8,128)(2,1)S(1)}) custom-call(s32[11]{0:T(128)S(1)} %stack.51.where_ref, bf16[20,256,128]{2,1,0:T(8,128)(2,1)S(1)} %bitcast.17, ...), custom_call_target="tpu_custom_call" | custom-call | flops 1000 | bytes 1000 | tf_op jit(solution)/shard_map/pallas_call | solution.py:202
  19.8 1.6 %collective-permute-start = (f32[328,128]{1,0:T(8,128)S(1)}, f32[328,128]{1,0:T(8,128)S(1)}, u32[]{:S(2)}, u32[]{:S(2)}) collective-permute-start(f32[328,128]{1,0:T(8,128)S(1)} %get-tuple-element.34), channel_id=1, source_target_pairs={{0,64},{1,2},{2,1},{3,4},{4,3},{5,6},{6,5},{7,8},{8,7},{9,10},{10,... | collective-permute-start | bytes 503816 | tf_op jit(solution)/shard_map/ppermute | solution.py:544
  21.4 1.5 %collective-permute-start.1 = (f32[328,128]{1,0:T(8,128)S(1)}, f32[328,128]{1,0:T(8,128)S(1)}, u32[]{:S(2)}, u32[]{:S(2)}) collective-permute-start(f32[328,128]{1,0:T(8,128)S(1)} %get-tuple-element.35), channel_id=1, source_target_pairs={{0,1},{1,0},{2,3},{3,2},{4,5},{5,4},{6,7},{7,6},{8,9},{9,8},{10,11... | collective-permute-start | bytes 503816 | tf_op jit(solution)/shard_map/ppermute | solution.py:548
  22.9 12.1 %collective-permute-done.2.first_ref = f32[1024,128]{1,0:T(8,128)S(1)} collective-permute-done((f32[1024,128]{1,0:T(8,128)}, f32[1024,128]{1,0:T(8,128)S(1)}, u32[]{:S(2)}, u32[]{:S(2)}) %collective-permute-start.2) | collective-permute-done | bytes 524320 | tf_op jit(solution)/shard_map/ppermute | solution.py:544
  35.1 1.6 %collective-permute-done.3.second_ref = f32[1024,128]{1,0:T(8,128)S(1)} collective-permute-done((f32[1024,128]{1,0:T(8,128)}, f32[1024,128]{1,0:T(8,128)S(1)}, u32[]{:S(2)}, u32[]{:S(2)}) %collective-permute-start.3) | collective-permute-done | bytes 524320 | tf_op jit(solution)/shard_map/ppermute | solution.py:548
  36.7 1.9 %shard_map.85.head_ref = f32[3,128,128]{2,1,0:T(8,128)S(1)} custom-call(f32[1024,128]{1,0:T(8,128)S(1)} %collective-permute-done.2.first_ref, f32[1024,128]{1,0:T(8,128)S(1)} %collective-permute-done.3.second_ref, f32[20,128,128]{2,1,0:T(8,128)S(1)} %get-tuple-element.36.own_ref, bf16[20,3,128,128]{3,2,1,0:T(8,128)(2,1)S(1)} %get-tuple-element.37.x_ref, ...), custom_call_target="tpu_custom_call" | custom-call | flops 1000 | bytes 1000 | tf_op jit(solution)/shard_map/pallas_call | solution.py:249
  38.5 2.6 %collective-permute-done.first_ref.o_ref = f32[328,128]{1,0:T(8,128)S(1)} collective-permute-done((f32[328,128]{1,0:T(8,128)S(1)}, f32[328,128]{1,0:T(8,128)S(1)}, u32[]{:S(2)}, u32[]{:S(2)}) %collective-permute-start) | collective-permute-done | bytes 167968 | tf_op jit(solution)/shard_map/ppermute | solution.py:544
  41.1 3.1 %collective-permute-done.1.second_ref.e_ref = f32[328,128]{1,0:T(8,128)S(1)} collective-permute-done((f32[328,128]{1,0:T(8,128)S(1)}, f32[328,128]{1,0:T(8,128)S(1)}, u32[]{:S(2)}, u32[]{:S(2)}) %collective-permute-start.1) | collective-permute-done | bytes 167968 | tf_op jit(solution)/shard_map/ppermute | solution.py:548
  44.2 1.2 %shard_map.86 = (f32[3,256,128]{2,1,0:T(8,128)S(1)}, f32[3,32,128]{2,1,0:T(8,128)S(1)}, f32[3,32,128]{2,1,0:T(8,128)S(1)}) custom-call(s32[11]{0:T(128)S(1)} %stack.51.where_ref, f32[328,128]{1,0:T(8,128)S(1)} %collective-permute-done.first_ref.o_ref, f32[328,128]{1,0:T(8,128)S(1)} %collective-permute-done.1.second_ref.e_ref, ...), custom_call_target="tpu_custom_call" | custom-call | flops 1000 | bytes 1000 | tf_op jit(solution)/shard_map/pallas_call | solution.py:264
  45.5 1.2 %collective-permute-done.4 = f32[3,32,128]{2,1,0:T(8,128)S(1)} collective-permute-done((f32[3,32,128]{2,1,0:T(8,128)S(1)}, f32[3,32,128]{2,1,0:T(8,128)S(1)}, u32[]{:S(2)}, u32[]{:S(2)}) %collective-permute-start.4) | collective-permute-done | bytes 49184 | tf_op jit(solution)/shard_map/ppermute | solution.py:556
  46.8 1.4 %shard_map.87 = (bf16[3,320,768]{2,1,0:T(8,128)(2,1)S(1)}, bf16[2,3,64,768]{3,2,1,0:T(8,128)(2,1)S(1)}, f32[9,768]{1,0:T(8,128)S(1)}, f32[9,768]{1,0:T(8,128)S(1...) custom-call(s32[11]{0:T(128)S(1)} %stack.51.where_ref, f32[72,128]{1,0:T(8,128)S(1)} %get-tuple-element.42.own_ref, ...), custom_call_target="tpu_custom_call" | custom-call | flops 1000 | bytes 1000 | tf_op jit(solution)/shard_map/pallas_call | solution.py:322
  48.2 1.7 %shard_map.88.mine_ref = f32[9,768]{1,0:T(8,128)S(1)} custom-call(s32[11]{0:T(128)S(1)} %stack.51.where_ref, f32[3,256,128]{2,1,0:T(8,128)S(1)} %get-tuple-element.41.inc_ref, bf16[3,320,768]{2,1,0:T(8,128)(2,1)S(1)} %get-tuple-element.45.wown_ref, bf16[2,3,64,768]{3,2,1,0:T(8,128)(2,1)S(1)} %get-tuple-element.46.wnear_ref, ...), custom_call_target="tpu_custom_call" | custom-call | flops 1000 | bytes 1000 | tf_op jit(solution)/shard_map/pallas_call | solution.py:360
  49.9 2.1 %collective-permute-done.5.near_ref = f32[3,32,128]{2,1,0:T(8,128)S(1)} collective-permute-done((f32[3,32,128]{2,1,0:T(8,128)S(1)}, f32[3,32,128]{2,1,0:T(8,128)S(1)}, u32[]{:S(2)}, u32[]{:S(2)}) %collective-permute-start.5) | collective-permute-done | bytes 49184 | tf_op jit(solution)/shard_map/ppermute | solution.py:552
  52.0 1.4 %shard_map.89 = f32[54,128]{1,0:T(8,128)S(1)} custom-call(s32[11]{0:T(128)S(1)} %stack.51.where_ref, f32[9,768]{1,0:T(8,128)S(1)} %shard_map.88.mine_ref, f32[3,32,128]{2,1,0:T(8,128)S(1)} %collective-permute-done.5.near_ref, bf16[3,320,768]{2,1,0:T(8,128)(2,1)S(1)} %get-tuple-element.45.wown_ref, bf16[2,3,64,768]{3,2,1,0:T(8,128)(2,1)S(1)} %get-tuple-element.46.wnear_ref, ...), custom_call_target="tpu_custom_call" | custom-call | flops 1000 | bytes 1000 | tf_op jit(solution)/shard_map/pallas_call | solution.py:388
  53.4 3.1 %collective-permute-start.6 = (f32[54,128]{1,0:T(8,128)S(1)}, f32[54,128]{1,0:T(8,128)S(1)}, u32[]{:S(2)}, u32[]{:S(2)}) collective-permute-start(f32[54,128]{1,0:T(8,128)S(1)} %shard_map.89), channel_id=1, source_target_pairs={{0,64},{64,0},{128,192},{192,128},{1,65},{65,1},{129,193},{193,129... | collective-permute-start | bytes 82952 | tf_op jit(solution)/shard_map/ppermute | solution.py:556
  56.5 0.9 collective-permute-done.6
  57.3 3.9 %collective-permute-done.7.v1 = f32[54,128]{1,0:T(8,128)S(1)} collective-permute-done((f32[54,128]{1,0:T(8,128)S(1)}, f32[54,128]{1,0:T(8,128)S(1)}, u32[]{:S(2)}, u32[]{:S(2)}) %collective-permute-start.7) | collective-permute-done | bytes 27680 | tf_op jit(solution)/shard_map/ppermute | solution.py:560
  61.2 1.9 %shard_map.90 = (f32[3,256,128]{2,1,0:T(8,128)S(1)}, f32[12,64,128]{2,1,0:T(8,128)S(1)}, f32[12,64,128]{2,1,0:T(8,128)S(1)}) custom-call(s32[11]{0:T(128)S(1)} %stack.51.where_ref, f32[54,128]{1,0:T(8,128)S(1)} %add.31.v0, f32[54,128]{1,0:T(8,128)S(1)} %collective-permute-done.7.v1, f32[9,768]{1,0:T(8,128)S(1)} %get-tuple-element.48.innov_ref, ...), custom_call_target="tpu_custom_call" | custom-call | flops 1000 | bytes 1000 | tf_op jit(solution)/shard_map/pallas_call | solution.py:426
  63.1 4.8 %collective-permute-start.10 = (f32[12,64,128]{2,1,0:T(8,128)S(1)}, f32[12,64,128]{2,1,0:T(8,128)S(1)}, u32[]{:S(2)}, u32[]{:S(2)}) collective-permute-start(f32[12,64,128]{2,1,0:T(8,128)S(1)} %get-tuple-element.56), channel_id=1, source_target_pairs={{0,64},{1,2},{2,1},{3,4},{4,3},{5,6},{6,5},{7,8},{8,7},{9,10},{10,... | collective-permute-start | bytes 1179656 | tf_op jit(solution)/shard_map/ppermute | solution.py:544
  67.9 5.3 %shard_map.91 = (f32[20,256,128]{2,1,0:T(8,128)}, f32[20,128,128]{2,1,0:T(8,128)S(1)}, f32[8,64,128]{2,1,0:T(8,128)S(1)}, f32[8,64,128]{2,1,0:T(8,128)S(1)}) custom-call(s32[11]{0:T(128)S(1)} %stack.51.where_ref, bf16[20,256,128]{2,1,0:T(8,128)(2,1)S(1)} %bitcast.19, bf16[20,3,256,128]{3,2,1,0:T(8,128)(2,1)S(1)} %bitcast.21, ...), custom_call_target="tpu_custom_call" | custom-call | flops 1000 | bytes 1000 | tf_op jit(solution)/shard_map/pallas_call | solution.py:458
  73.2 2.4 %collective-permute-start.8 = (f32[8,64,128]{2,1,0:T(8,128)S(1)}, f32[8,64,128]{2,1,0:T(8,128)S(1)}, u32[]{:S(2)}, u32[]{:S(2)}) collective-permute-start(f32[8,64,128]{2,1,0:T(8,128)S(1)} %get-tuple-element.53), channel_id=1, source_target_pairs={{0,64},{1,2},{2,1},{3,4},{4,3},{5,6},{6,5},{7,8},{8,7},{9,10},{10,... | collective-permute-start | bytes 786440 | tf_op jit(solution)/shard_map/ppermute | solution.py:544
  76.1 11.5 %collective-permute-done.10.first_ref = f32[12,64,128]{2,1,0:T(8,128)S(1)} collective-permute-done((f32[12,64,128]{2,1,0:T(8,128)S(1)}, f32[12,64,128]{2,1,0:T(8,128)S(1)}, u32[]{:S(2)}, u32[]{:S(2)}) %collective-permute-start.10) | collective-permute-done | bytes 393248 | tf_op jit(solution)/shard_map/ppermute | solution.py:544
  87.6 1.8 %collective-permute-done.11.second_ref = f32[12,64,128]{2,1,0:T(8,128)S(1)} collective-permute-done((f32[12,64,128]{2,1,0:T(8,128)S(1)}, f32[12,64,128]{2,1,0:T(8,128)S(1)}, u32[]{:S(2)}, u32[]{:S(2)}) %collective-permute-start.11) | collective-permute-done | bytes 393248 | tf_op jit(solution)/shard_map/ppermute | solution.py:548
  89.5 1.4 %shard_map.92.unused_ref = f32[20,4,64,128]{3,2,1,0:T(8,128)} custom-call(f32[12,64,128]{2,1,0:T(8,128)S(1)} %collective-permute-done.10.first_ref, f32[12,64,128]{2,1,0:T(8,128)S(1)} %collective-permute-done.11.second_ref, f32[20,128,128]{2,1,0:T(8,128)S(1)} %get-tuple-element.55.edge_ref, ...), custom_call_target="tpu_custom_call", output_to_operand_aliasing={{}: (5, {})} | custom-call | flops 1000 | bytes 1000 | tf_op jit(solution)/shard_map/pallas_call | solution.py:506
  90.9 6.2 %collective-permute-done.8.first_ref = f32[8,64,128]{2,1,0:T(8,128)S(1)} collective-permute-done((f32[8,64,128]{2,1,0:T(8,128)S(1)}, f32[8,64,128]{2,1,0:T(8,128)S(1)}, u32[]{:S(2)}, u32[]{:S(2)}) %collective-permute-start.8) | collective-permute-done | bytes 262176 | tf_op jit(solution)/shard_map/ppermute | solution.py:544
  97.1 1.1 %collective-permute-done.9.second_ref = f32[8,64,128]{2,1,0:T(8,128)S(1)} collective-permute-done((f32[8,64,128]{2,1,0:T(8,128)S(1)}, f32[8,64,128]{2,1,0:T(8,128)S(1)}, u32[]{:S(2)}, u32[]{:S(2)}) %collective-permute-start.9) | collective-permute-done | bytes 262176 | tf_op jit(solution)/shard_map/ppermute | solution.py:548
  98.2 1.3 %shard_map.93 = f32[20,4,64,128]{3,2,1,0:T(8,128)} custom-call(f32[8,64,128]{2,1,0:T(8,128)S(1)} %collective-permute-done.8.first_ref, f32[8,64,128]{2,1,0:T(8,128)S(1)} %collective-permute-done.9.second_ref, f32[20,128,128]{2,1,0:T(8,128)S(1)} %get-tuple-element.55.edge_ref, ...), custom_call_target="tpu_custom_call", output_to_operand_aliasing={{}: (5, {})} | custom-call | flops 1000 | bytes 1000 | tf_op jit(solution)/shard_map/pallas_call | solution.py:506
  (27 shorter events, 1.2 us)
Async XLA Ops:
  0.0 11.4 %copy-start = (bf16[20,8,32,128]{3,2,1,0:T(8,128)(2,1)S(1)}, bf16[20,8,32,128]{3,2,1,0:T(8,128)(2,1)}, u32[]{:S(2)}) copy-start(bf16[20,8,32,128]{3,2,1,0:T(8,128)(2,1)} %param.8) | copy-start | bytes 3932164
  2.2 32.9 %collective-permute-start.2 = (f32[1024,128]{1,0:T(8,128)}, f32[1024,128]{1,0:T(8,128)S(1)}, u32[]{:S(2)}, u32[]{:S(2)}) collective-permute-start(f32[1024,128]{1,0:T(8,128)} %get-tuple-element.39), channel_id=1, source_target_pairs={{0,64},{1,2},{2,1},{3,4},{4,3},{5,6},{6,5},{7,8},{8,7},{9,10},{10,... | collective-permute-start | bytes 1572872 | tf_op jit(solution)/shard_map/ppermute | solution.py:544
  11.3 25.4 %collective-permute-start.3 = (f32[1024,128]{1,0:T(8,128)}, f32[1024,128]{1,0:T(8,128)S(1)}, u32[]{:S(2)}, u32[]{:S(2)}) collective-permute-start(f32[1024,128]{1,0:T(8,128)} %get-tuple-element.40), channel_id=1, source_target_pairs={{0,1},{1,0},{2,3},{3,2},{4,5},{5,4},{6,7},{7,6},{8,9},{9,8},{10,11... | collective-permute-start | bytes 1572872 | tf_op jit(solution)/shard_map/ppermute | solution.py:548
  11.4 2.1 %copy-start.1 = (bf16[20,3,8,32,128]{4,3,2,1,0:T(8,128)(2,1)S(1)}, bf16[20,3,8,32,128]{4,3,2,1,0:T(8,128)(2,1)}, u32[]{:S(2)}) copy-start(bf16[20,3,8,32,128]{4,3,2,1,0:T(8,128)(2,1)} %param.9) | copy-start | bytes 11796484
  13.5 0.8 copy-start.3
  14.2 0.7 copy-start.9
  14.9 4.5 %copy-start.5 = (s32[1,2048]{1,0:T(1,128)S(1)}, s32[1,2048]{1,0:T(1,128)}, u32[]{:S(2)}) copy-start(s32[1,2048]{1,0:T(1,128)} %col_ref.1) | copy-start | bytes 24580
  14.9 4.5 %copy-start.6 = (s32[1,2048]{1,0:T(1,128)S(1)}, s32[1,2048]{1,0:T(1,128)}, u32[]{:S(2)}) copy-start(s32[1,2048]{1,0:T(1,128)} %lev_ref.1) | copy-start | bytes 24580
  14.9 4.5 %copy-start.7 = (f32[1,2048]{1,0:T(1,128)S(1)}, f32[1,2048]{1,0:T(1,128)}, u32[]{:S(2)}) copy-start(f32[1,2048]{1,0:T(1,128)} %innov_ref.1) | copy-start | bytes 24580
  14.9 4.5 %copy-start.8 = (f32[1,2048]{1,0:T(1,128)S(1)}, f32[1,2048]{1,0:T(1,128)}, u32[]{:S(2)}) copy-start(f32[1,2048]{1,0:T(1,128)} %weight_ref.1) | copy-start | bytes 24580
  19.8 21.3 %collective-permute-start = (f32[328,128]{1,0:T(8,128)S(1)}, f32[328,128]{1,0:T(8,128)S(1)}, u32[]{:S(2)}, u32[]{:S(2)}) collective-permute-start(f32[328,128]{1,0:T(8,128)S(1)} %get-tuple-element.34), channel_id=1, source_target_pairs={{0,64},{1,2},{2,1},{3,4},{4,3},{5,6},{6,5},{7,8},{8,7},{9,10},{10,... | collective-permute-start | bytes 503816 | tf_op jit(solution)/shard_map/ppermute | solution.py:544
  21.4 22.8 %collective-permute-start.1 = (f32[328,128]{1,0:T(8,128)S(1)}, f32[328,128]{1,0:T(8,128)S(1)}, u32[]{:S(2)}, u32[]{:S(2)}) collective-permute-start(f32[328,128]{1,0:T(8,128)S(1)} %get-tuple-element.35), channel_id=1, source_target_pairs={{0,1},{1,0},{2,3},{3,2},{4,5},{5,4},{6,7},{7,6},{8,9},{9,8},{10,11... | collective-permute-start | bytes 503816 | tf_op jit(solution)/shard_map/ppermute | solution.py:548
  45.4 1.3 %collective-permute-start.4 = (f32[3,32,128]{2,1,0:T(8,128)S(1)}, f32[3,32,128]{2,1,0:T(8,128)S(1)}, u32[]{:S(2)}, u32[]{:S(2)}) collective-permute-start(f32[3,32,128]{2,1,0:T(8,128)S(1)} %get-tuple-element.44), channel_id=1, source_target_pairs={{0,64},{64,0},{128,192},{192,128},{1,65},{65,1},{129,193},{193,129... | collective-permute-start | bytes 147464 | tf_op jit(solution)/shard_map/ppermute | solution.py:556
  46.7 5.3 %collective-permute-start.5 = (f32[3,32,128]{2,1,0:T(8,128)S(1)}, f32[3,32,128]{2,1,0:T(8,128)S(1)}, u32[]{:S(2)}, u32[]{:S(2)}) collective-permute-start(f32[3,32,128]{2,1,0:T(8,128)S(1)} %add.30.after_ref), channel_id=1, source_target_pairs={{0,1},{1,0},{2,3},{3,2},{4,5},{5,4},{6,7},{7,6},{8,9},{9,8},{10,11... | collective-permute-start | bytes 147464 | tf_op jit(solution)/shard_map/ppermute | solution.py:552
  53.4 4.0 %collective-permute-start.6 = (f32[54,128]{1,0:T(8,128)S(1)}, f32[54,128]{1,0:T(8,128)S(1)}, u32[]{:S(2)}, u32[]{:S(2)}) collective-permute-start(f32[54,128]{1,0:T(8,128)S(1)} %shard_map.89), channel_id=1, source_target_pairs={{0,64},{64,0},{128,192},{192,128},{1,65},{65,1},{129,193},{193,129... | collective-permute-start | bytes 82952 | tf_op jit(solution)/shard_map/ppermute | solution.py:556
  57.3 3.9 %collective-permute-start.7 = (f32[54,128]{1,0:T(8,128)S(1)}, f32[54,128]{1,0:T(8,128)S(1)}, u32[]{:S(2)}, u32[]{:S(2)}) collective-permute-start(f32[54,128]{1,0:T(8,128)S(1)} %add.31.v0), channel_id=1, source_target_pairs={{0,128},{64,192},{128,0},{192,64},{1,129},{65,193},{129,1},{193,65... | collective-permute-start | bytes 82952 | tf_op jit(solution)/shard_map/ppermute | solution.py:560
  61.2 6.7 %copy-start.2 = (bf16[20,3,8,32,128]{4,3,2,1,0:T(8,128)(2,1)S(1)}, bf16[20,3,8,32,128]{4,3,2,1,0:T(8,128)(2,1)}, u32[]{:S(2)}) copy-start(bf16[20,3,8,32,128]{4,3,2,1,0:T(8,128)(2,1)} %param.9) | copy-start | bytes 11796484
  61.2 6.7 %copy-start.4 = (bf16[128,128]{1,0:T(8,128)(2,1)S(1)}, bf16[128,128]{1,0:T(8,128)(2,1)}, u32[]{:S(2)}) copy-start(bf16[128,128]{1,0:T(8,128)(2,1)} %loc_ref.11) | copy-start | bytes 98308
  63.1 24.5 %collective-permute-start.10 = (f32[12,64,128]{2,1,0:T(8,128)S(1)}, f32[12,64,128]{2,1,0:T(8,128)S(1)}, u32[]{:S(2)}, u32[]{:S(2)}) collective-permute-start(f32[12,64,128]{2,1,0:T(8,128)S(1)} %get-tuple-element.56), channel_id=1, source_target_pairs={{0,64},{1,2},{2,1},{3,4},{4,3},{5,6},{6,5},{7,8},{8,7},{9,10},{10,... | collective-permute-start | bytes 1179656 | tf_op jit(solution)/shard_map/ppermute | solution.py:544
  67.9 21.6 %collective-permute-start.11 = (f32[12,64,128]{2,1,0:T(8,128)S(1)}, f32[12,64,128]{2,1,0:T(8,128)S(1)}, u32[]{:S(2)}, u32[]{:S(2)}) collective-permute-start(f32[12,64,128]{2,1,0:T(8,128)S(1)} %get-tuple-element.57), channel_id=1, source_target_pairs={{0,1},{1,0},{2,3},{3,2},{4,5},{5,4},{6,7},{7,6},{8,9},{9,8},{10,11... | collective-permute-start | bytes 1179656 | tf_op jit(solution)/shard_map/ppermute | solution.py:548
  73.2 23.9 %collective-permute-start.8 = (f32[8,64,128]{2,1,0:T(8,128)S(1)}, f32[8,64,128]{2,1,0:T(8,128)S(1)}, u32[]{:S(2)}, u32[]{:S(2)}) collective-permute-start(f32[8,64,128]{2,1,0:T(8,128)S(1)} %get-tuple-element.53), channel_id=1, source_target_pairs={{0,64},{1,2},{2,1},{3,4},{4,3},{5,6},{6,5},{7,8},{8,7},{9,10},{10,... | collective-permute-start | bytes 786440 | tf_op jit(solution)/shard_map/ppermute | solution.py:544
  75.7 22.5 %collective-permute-start.9 = (f32[8,64,128]{2,1,0:T(8,128)S(1)}, f32[8,64,128]{2,1,0:T(8,128)S(1)}, u32[]{:S(2)}, u32[]{:S(2)}) collective-permute-start(f32[8,64,128]{2,1,0:T(8,128)S(1)} %get-tuple-element.54), channel_id=1, source_target_pairs={{0,1},{1,0},{2,3},{3,2},{4,5},{5,4},{6,7},{7,6},{8,9},{9,8},{10,11... | collective-permute-start | bytes 786440 | tf_op jit(solution)/shard_map/ppermute | solution.py:548

commit v11 on v10

--- a/solution.py
+++ b/solution.py
@@ -14,7 +14,8 @@
 GROUP = 4
 HEAD = 16
 HEAD_BACK = 12
-OBS = 72
+OBS = 80
+HALF = OBS // 2
 
 TILES = 64
 MEMS = 4
@@ -116,6 +117,7 @@
         part = rest.astype(BF16)
         rest = rest - part.astype(F32)
         total = total + nn(part, order)
+    out_ref[72:] = jnp.zeros((OBS - 72, 128), F32)
     for f in range(4):
         for a in range(6):
             for v in range(V):
@@ -123,12 +125,59 @@
                 out_ref[row : row + 1] = total[6 * f + a : 6 * f + a + 1, 128 * v : 128 * v + 128]
 
 
-def edge_rows(quarters_ref, start, first_ref, second_ref, edges, sems):
+def send_kernel(quarters_ref, first_ref, second_ref, token_ref, edges, rows, fetched, sent):
+    token_ref[...] = jnp.zeros_like(token_ref)
+    groups = HEAD // GROUP
+    fetches, sends = [], []
+    for g in range(groups):
+        members = pl.ds(g * GROUP, GROUP)
+        for n in range(2):
+            fetches.append(
+                pltpu.make_async_copy(quarters_ref.at[members, 3 * n], edges.at[n, members], fetched.at[g, n])
+            )
+            fetches[-1].start()
+    low = side_of_first()
+    for g in range(groups):
+        for fetch in fetches[2 * g : 2 * g + 2]:
+            fetch.wait()
+        for k in range(g * GROUP, (g + 1) * GROUP):
+            rows[0, 64 * k : 64 * k + 64] = edges[1 - low, k].astype(F32)
+            rows[1, 64 * k : 64 * k + 64] = edges[low, k].astype(F32)
+        part = pl.ds(64 * GROUP * g, 64 * GROUP)
+        for n, ref in enumerate((first_ref, second_ref)):
+            sends.append(pltpu.make_async_copy(rows.at[n, part], ref.at[part], sent.at[g, n]))
+            sends[-1].start()
+    for send in sends:
+        send.wait()
+
+
+def send_part(quarters):
+    return call(
+        send_kernel,
+        (sds(64 * HEAD, 128), sds(64 * HEAD, 128), sds(8, 128)),
+        ins=[HBM],
+        outs=(HBM, HBM, VMEM),
+        scratch=[
+            pltpu.VMEM((2, HEAD, 64, 128), BF16),
+            pltpu.VMEM((2, 64 * HEAD, 128), F32),
+            pltpu.SemaphoreType.DMA((HEAD // GROUP, 2)),
+            pltpu.SemaphoreType.DMA((HEAD // GROUP, 2)),
+        ],
+        vmem=56,
+    )(quarters)
+
+
+def rest_kernel(count_ref, col_ref, lev_ref, innov_ref, weight_ref, quarters_ref, after_ref, first_ref, second_ref, obs_ref, edges, sems):
     count = edges.shape[1]
-    members = pl.ds(start, count)
+    members = pl.ds(HEAD, count)
     copies = [pltpu.make_async_copy(quarters_ref.at[members, 3 * n], edges.at[n], sems.at[n]) for n in range(2)]
     for copy in copies:
         copy.start()
+    sort_observations(count_ref[0], col_ref, lev_ref, innov_ref, weight_ref, obs_ref)
+    core = lax.rem(lax.axis_index("mem"), 2)
+    half = obs_ref[pl.ds(pl.multiple_of(HALF * core, 8), HALF)]
+    first_ref[64 * count :] = half
+    second_ref[64 * count :] = half
     for copy in copies:
         copy.wait()
     low = side_of_first()
@@ -137,35 +186,11 @@
         second_ref[64 * k : 64 * k + 64] = edges[low, k].astype(F32)
 
 
-def send_kernel(quarters_ref, first_ref, second_ref, token_ref, edges, sems):
-    token_ref[...] = jnp.zeros_like(token_ref)
-    edge_rows(quarters_ref, 0, first_ref, second_ref, edges, sems)
-
-
-def send_part(quarters):
-    return call(
-        send_kernel,
-        (sds(64 * HEAD, 128), sds(64 * HEAD, 128), sds(8, 128)),
-        ins=[HBM],
-        outs=(VMEM,) * 3,
-        scratch=[pltpu.VMEM((2, HEAD, 64, 128), BF16), pltpu.SemaphoreType.DMA((2,))],
-        vmem=56,
-    )(quarters)
-
-
-def rest_kernel(count_ref, col_ref, lev_ref, innov_ref, weight_ref, quarters_ref, after_ref, first_ref, second_ref, obs_ref, edges, sems):
-    edge_rows(quarters_ref, HEAD, first_ref, second_ref, edges, sems)
-    sort_observations(count_ref[0], col_ref, lev_ref, innov_ref, weight_ref, obs_ref)
-    end = first_ref.shape[0] - OBS
-    first_ref[end:] = obs_ref[...]
-    second_ref[end:] = obs_ref[...]
-
-
 def rest_part(count, col, lev, innov, weight, quarters, after):
     members = quarters.shape[0] - HEAD
     return call(
         rest_kernel,
-        (sds(64 * members + OBS, 128), sds(64 * members + OBS, 128), sds(OBS, 128)),
+        (sds(64 * members + HALF, 128), sds(64 * members + HALF, 128), sds(OBS, 128)),
         ins=[SMEM] + [VMEM] * 4 + [ANY, VMEM],
         outs=(VMEM,) * 3,
         scratch=[pltpu.VMEM((2, members, 64, 128), BF16), pltpu.SemaphoreType.DMA((2,))],
@@ -256,14 +281,17 @@
         inc_ref[v, :64] = total[v][:64]
         inc_ref[v, 64:192] = inner_ref[v]
         inc_ref[v, 192:] = total[v][64:]
-        keep_ref[v] = inc_ref[v, pl.ds(pl.multiple_of(where_ref[8], 32), 32)]
-        give_ref[v] = inc_ref[v, pl.ds(pl.multiple_of(where_ref[9], 32), 32)]
+        keep_ref[32 * v : 32 * v + 32] = inc_ref[v, pl.ds(pl.multiple_of(where_ref[8], 32), 32)]
+        give_ref[32 * v : 32 * v + 32] = inc_ref[v, pl.ds(pl.multiple_of(where_ref[9], 32), 32)]
+    end = first_ref.shape[0] - HALF
+    give_ref[32 * V : 32 * V + HALF] = first_ref[end:]
+    give_ref[32 * V + HALF :] = second_ref[end:]
 
 
 def edge_part(where, first, second, own, x, hmat, loc, inner, head):
     return call(
         edge_kernel,
-        (sds(V, 256, 128), sds(V, 32, 128), sds(V, 32, 128)),
+        (sds(V, 256, 128), sds(V * 32, 128), sds(V * 32 + OBS, 128)),
         ins=[SMEM] + [VMEM] * 8,
         outs=(VMEM,) * 3,
     )(where, first, second, own, x, hmat, loc, inner, head)
@@ -273,7 +301,12 @@
     return jnp.maximum(1.0 - jnp.abs(distance), 0.0)
 
 
-def weights_kernel(where_ref, own_ref, o_ref, e_ref, after_ref, wown_ref, wnear_ref, lev_ref, innov_ref, weight_ref, hot_ref):
+def weights_kernel(where_ref, own_ref, here_ref, there_ref, after_ref, wown_ref, wnear_ref, lev_ref, innov_ref, weight_ref, hot_ref, o_ref, e_ref):
+    core = where_ref[10]
+    for half, ref in ((core, here_ref), (1 - core, there_ref)):
+        rows = pl.ds(pl.multiple_of(HALF * half, 8), HALF)
+        o_ref[rows] = ref[32 * V : 32 * V + HALF]
+        e_ref[rows] = ref[32 * V + HALF :]
     level = lax.broadcasted_iota(jnp.int32, (128, SLOTS), 0).astype(F32)
     even_row = where_ref[2].astype(F32)
     odd_row = where_ref[3].astype(F32)
@@ -281,7 +314,7 @@
     cell = lax.broadcasted_iota(jnp.int32, (32, SLOTS), 0).astype(F32)
 
     def line(ref, field, v):
-        at = ref.shape[0] - OBS + 6 * (V * field + v)
+        at = 6 * (V * field + v)
         return jnp.concatenate([ref[at + a : at + a + 1] for a in range(6)], axis=1)
 
     def columns(code):
@@ -318,7 +351,7 @@
             weight_ref[row] = weight
 
 
-def weights(where, own, first, second, after):
+def weights(where, own, here, there, after):
     return call(
         weights_kernel,
         (
@@ -330,7 +363,8 @@
             sds(9, 128, SLOTS, dtype=BF16),
         ),
         ins=[SMEM] + [VMEM] * 4,
-    )(where, own, first, second, after)
+        scratch=[pltpu.VMEM((OBS, 128), F32), pltpu.VMEM((OBS, 128), F32)],
+    )(where, own, here, there, after)
 
 
 def picker(lev_ref):
@@ -379,9 +413,9 @@
             put(row, mine_ref[row : row + 1])
     for v in range(V):
         halo = pl.ds(pl.multiple_of(256 + 32 * core, 32), 32)
-        put(v, mine_ref[v : v + 1] + pick(near_ref[v], wown_ref[v, halo], v))
+        put(v, mine_ref[v : v + 1] + pick(near_ref[32 * v : 32 * v + 32], wown_ref[v, halo], v))
         row = 3 * core + 3 + v
-        put(row, mine_ref[pl.ds(row, 1)] + pick(near_ref[v], wnear_ref[core, v, 32:], row))
+        put(row, mine_ref[pl.ds(row, 1)] + pick(near_ref[32 * v : 32 * v + 32], wnear_ref[core, v, 32:], row))
 
 
 def values(where, mine, near, wown, wnear, lev):
@@ -595,9 +629,10 @@
     first_rest, second_rest = swap_first(send_first), swap_second(send_second)
     head = head_part(first, second, own_edge, x, hmat, loc_vert)
     inc, keep, give = edge_part(where, first_rest, second_rest, own_edge, x, hmat, loc_vert, inner, head)
-    edges = keep + swap_core(give)
+    got = swap_core(give)
+    edges = keep + got[: V * 32]
     near = swap_near(edges)
-    wown, wnear, lev, innov, weight, hot = weights(where, own_obs, first_rest, second_rest, edges)
+    wown, wnear, lev, innov, weight, hot = weights(where, own_obs, give, got, edges)
     mine = mine_part(where, inc, wown, wnear, lev)
     vals = values(where, mine, near, wown, wnear, lev)
     vals = vals + swap_core(vals)

time: 99.8 us -> 99.6 us (level)
  no operation moved by 1% of the time
where the time goes in v11:
time: 99.6 us; the launch traced here: 99.4 us
  waiting for transfers between devices  47.2 us (47%)
  Pallas kernels  24.5 us (25%)
  starting transfers between devices  23 us (23%)
  local copies, waits for them, and re-layouts  3.65 us (4%)
    ppermute x4, waiting for transfers between devices, swap_first(): return lax.ppermute(x, ('mem', 'tile'), FIRST)  31.6 us
    ppermute x4, starting transfers between devices, swap_first(): return lax.ppermute(x, ('mem', 'tile'), FIRST)  18 us
    ppermute x4, waiting for transfers between devices, swap_second(): return lax.ppermute(x, ('mem', 'tile'), SECOND)  7.67 us
    pallas_call x1, Pallas kernels, back_part(): call(back_kernel, (sds(members, 256, 128), sds(members, 128, 128), sds(me...  5.35 us
    ppermute x1, waiting for transfers between devices, swap_chip(): return lax.ppermute(x, 'mem', [(m, m ^ 2) for m in range(MEMS)])  3.86 us
    pallas_call x1, Pallas kernels, own_part(): call(own_kernel, (sds(V, 128, 128), sds(members, 128, 128), sds(members,...  3.78 us
    unnamed x20, local copies, waits for them, and re-layouts  3.56 us
    ppermute x2, starting transfers between devices, swap_core(): return lax.ppermute(x, 'mem', [(m, m ^ 1) for m in range(MEMS)])  3.06 us
  transfers between devices with their start and end apart: 12, of which 12 were waited for; matrix products, arithmetic and copies ran while one was open for 0% of the time, Pallas kernels for 16%

profile of v11, /device:TPU:6, one launch (start us, length us, event | category | flops | bytes accessed | tf_op | source)
XLA Modules:
  0.0 99.4 jit_solution(17956895863082861233)
XLA Ops:
  0.0 2.7 %shard_map.82 = (f32[1024,128]{1,0:T(8,128)}, f32[1024,128]{1,0:T(8,128)}, f32[8,128]{1,0:T(8,128)}) custom-call(bf16[20,4,64,128]{3,2,1,0:T(8,128)(2,1)} %bitcast.16), custom_call_target="tpu_custom_call" | custom-call | flops 1000 | bytes 1000 | tf_op jit(solution)/shard_map/pallas_call | solution.py:155
  2.7 9.1 %collective-permute-start.2 = (f32[1024,128]{1,0:T(8,128)}, f32[1024,128]{1,0:T(8,128)S(1)}, u32[]{:S(2)}, u32[]{:S(2)}) collective-permute-start(f32[1024,128]{1,0:T(8,128)} %get-tuple-element.39), channel_id=1, source_target_pairs={{0,64},{1,2},{2,1},{3,4},{4,3},{5,6},{6,5},{7,8},{8,7},{9,10},{10,... | collective-permute-start | bytes 1572872 | tf_op jit(solution)/shard_map/ppermute | solution.py:578
  11.9 2.1 %copy-done.1 = bf16[20,3,8,32,128]{4,3,2,1,0:T(8,128)(2,1)S(1)} copy-done((bf16[20,3,8,32,128]{4,3,2,1,0:T(8,128)(2,1)S(1)}, bf16[20,3,8,32,128]{4,3,2,1,0:T(8,128)(2,1)}, u32[]{:S(2)}) %copy-start.1) | copy-done | bytes 3932184
  14.0 0.8 copy-done.3
  14.8 0.7 copy-done.9
  15.4 3.8 %shard_map.83 = (f32[3,128,128]{2,1,0:T(8,128)S(1)}, f32[20,128,128]{2,1,0:T(8,128)S(1)}, bf16[20,3,128,128]{3,2,1,0:T(8,128)(2,1)S(1)}, bf16[256,256]{1,0:T(8,128)(2,1)S(1)}, bf16[128,128]{1,0:T(8,128)(2,1)S(1)}) custom-call(s32[11]{0:T(128)S(1)} %stack.51.where_ref, bf16[20,256,128]{2,1,0:T(8,128)(2,1)S(1)} %bitcast.17, ...), custom_call_target="tpu_custom_call" | custom-call | flops 1000 | bytes 1000 | tf_op jit(solution)/shard_map/pallas_call | solution.py:227
  20.3 1.6 %collective-permute-start = (f32[296,128]{1,0:T(8,128)S(1)}, f32[296,128]{1,0:T(8,128)S(1)}, u32[]{:S(2)}, u32[]{:S(2)}) collective-permute-start(f32[296,128]{1,0:T(8,128)S(1)} %get-tuple-element.34), channel_id=1, source_target_pairs={{0,64},{1,2},{2,1},{3,4},{4,3},{5,6},{6,5},{7,8},{8,7},{9,10},{10,... | collective-permute-start | bytes 454664 | tf_op jit(solution)/shard_map/ppermute | solution.py:578
  22.0 1.5 %collective-permute-start.1 = (f32[296,128]{1,0:T(8,128)S(1)}, f32[296,128]{1,0:T(8,128)S(1)}, u32[]{:S(2)}, u32[]{:S(2)}) collective-permute-start(f32[296,128]{1,0:T(8,128)S(1)} %get-tuple-element.35), channel_id=1, source_target_pairs={{0,1},{1,0},{2,3},{3,2},{4,5},{5,4},{6,7},{7,6},{8,9},{9,8},{10,11... | collective-permute-start | bytes 454664 | tf_op jit(solution)/shard_map/ppermute | solution.py:582
  23.4 12.1 %collective-permute-done.2.first_ref = f32[1024,128]{1,0:T(8,128)S(1)} collective-permute-done((f32[1024,128]{1,0:T(8,128)}, f32[1024,128]{1,0:T(8,128)S(1)}, u32[]{:S(2)}, u32[]{:S(2)}) %collective-permute-start.2) | collective-permute-done | bytes 524320 | tf_op jit(solution)/shard_map/ppermute | solution.py:578
  35.6 1.6 %collective-permute-done.3.second_ref = f32[1024,128]{1,0:T(8,128)S(1)} collective-permute-done((f32[1024,128]{1,0:T(8,128)}, f32[1024,128]{1,0:T(8,128)S(1)}, u32[]{:S(2)}, u32[]{:S(2)}) %collective-permute-start.3) | collective-permute-done | bytes 524320 | tf_op jit(solution)/shard_map/ppermute | solution.py:582
  37.2 1.9 %shard_map.85.head_ref = f32[3,128,128]{2,1,0:T(8,128)S(1)} custom-call(f32[1024,128]{1,0:T(8,128)S(1)} %collective-permute-done.2.first_ref, f32[1024,128]{1,0:T(8,128)S(1)} %collective-permute-done.3.second_ref, f32[20,128,128]{2,1,0:T(8,128)S(1)} %get-tuple-element.36.own_ref, bf16[20,3,128,128]{3,2,1,0:T(8,128)(2,1)S(1)} %get-tuple-element.37.x_ref, ...), custom_call_target="tpu_custom_call" | custom-call | flops 1000 | bytes 1000 | tf_op jit(solution)/shard_map/pallas_call | solution.py:274
  39.1 1.9 %collective-permute-done.first_ref = f32[296,128]{1,0:T(8,128)S(1)} collective-permute-done((f32[296,128]{1,0:T(8,128)S(1)}, f32[296,128]{1,0:T(8,128)S(1)}, u32[]{:S(2)}, u32[]{:S(2)}) %collective-permute-start) | collective-permute-done | bytes 151584 | tf_op jit(solution)/shard_map/ppermute | solution.py:578
  40.9 3.1 %collective-permute-done.1.second_ref = f32[296,128]{1,0:T(8,128)S(1)} collective-permute-done((f32[296,128]{1,0:T(8,128)S(1)}, f32[296,128]{1,0:T(8,128)S(1)}, u32[]{:S(2)}, u32[]{:S(2)}) %collective-permute-start.1) | collective-permute-done | bytes 151584 | tf_op jit(solution)/shard_map/ppermute | solution.py:582
  44.1 1.2 %shard_map.86 = (f32[3,256,128]{2,1,0:T(8,128)S(1)}, f32[96,128]{1,0:T(8,128)S(1)}, f32[176,128]{1,0:T(8,128)S(1)}) custom-call(s32[11]{0:T(128)S(1)} %stack.51.where_ref, f32[296,128]{1,0:T(8,128)S(1)} %collective-permute-done.first_ref, f32[296,128]{1,0:T(8,128)S(1)} %collective-permute-done.1.second_ref, f32[20,128,128]{2,1,0:T(8,128)S(1)} %get-tuple-element.36.own_ref, ...), custom_call_target="tpu_custom_call" | custom-call | flops 1000 | bytes 1000 | tf_op jit(solution)/shard_map/pallas_call | solution.py:292
  45.3 1.3 %collective-permute-done.4.there_ref = f32[176,128]{1,0:T(8,128)S(1)} collective-permute-done((f32[176,128]{1,0:T(8,128)S(1)}, f32[176,128]{1,0:T(8,128)S(1)}, u32[]{:S(2)}, u32[]{:S(2)}) %collective-permute-start.4) | collective-permute-done | bytes 90144 | tf_op jit(solution)/shard_map/ppermute | solution.py:590
  46.7 1.7 %shard_map.87 = (bf16[3,320,768]{2,1,0:T(8,128)(2,1)S(1)}, bf16[2,3,64,768]{3,2,1,0:T(8,128)(2,1)S(1)}, f32[9,768]{1,0:T(8,128)S(1)}, f32[9,768]{1,0:T(8,128)S(1...) custom-call(s32[11]{0:T(128)S(1)} %stack.51.where_ref, f32[80,128]{1,0:T(8,128)S(1)} %get-tuple-element.42.own_ref, ...), custom_call_target="tpu_custom_call" | custom-call | flops 1000 | bytes 1000 | tf_op jit(solution)/shard_map/pallas_call | solution.py:355
  48.4 1.7 %shard_map.88.mine_ref = f32[9,768]{1,0:T(8,128)S(1)} custom-call(s32[11]{0:T(128)S(1)} %stack.51.where_ref, f32[3,256,128]{2,1,0:T(8,128)S(1)} %get-tuple-element.41.inc_ref, bf16[3,320,768]{2,1,0:T(8,128)(2,1)S(1)} %get-tuple-element.45.wown_ref, bf16[2,3,64,768]{3,2,1,0:T(8,128)(2,1)S(1)} %get-tuple-element.46.wnear_ref, ...), custom_call_target="tpu_custom_call" | custom-call | flops 1000 | bytes 1000 | tf_op jit(solution)/shard_map/pallas_call | solution.py:394
  50.0 1.9 %collective-permute-done.5.near_ref = f32[96,128]{1,0:T(8,128)S(1)} collective-permute-done((f32[96,128]{1,0:T(8,128)S(1)}, f32[96,128]{1,0:T(8,128)S(1)}, u32[]{:S(2)}, u32[]{:S(2)}) %collective-permute-start.5) | collective-permute-done | bytes 49184 | tf_op jit(solution)/shard_map/ppermute | solution.py:586
  51.9 1.4 %shard_map.89 = f32[54,128]{1,0:T(8,128)S(1)} custom-call(s32[11]{0:T(128)S(1)} %stack.51.where_ref, f32[9,768]{1,0:T(8,128)S(1)} %shard_map.88.mine_ref, f32[96,128]{1,0:T(8,128)S(1)} %collective-permute-done.5.near_ref, bf16[3,320,768]{2,1,0:T(8,128)(2,1)S(1)} %get-tuple-element.45.wown_ref, bf16[2,3,64,768]{3,2,1,0:T(8,128)(2,1)S(1)} %get-tuple-element.46.wnear_ref, ...), custom_call_target="tpu_custom_call" | custom-call | flops 1000 | bytes 1000 | tf_op jit(solution)/shard_map/pallas_call | solution.py:422
  53.3 3.0 %collective-permute-start.6 = (f32[54,128]{1,0:T(8,128)S(1)}, f32[54,128]{1,0:T(8,128)S(1)}, u32[]{:S(2)}, u32[]{:S(2)}) collective-permute-start(f32[54,128]{1,0:T(8,128)S(1)} %shard_map.89), channel_id=1, source_target_pairs={{0,64},{64,0},{128,192},{192,128},{1,65},{65,1},{129,193},{193,129... | collective-permute-start | bytes 82952 | tf_op jit(solution)/shard_map/ppermute | solution.py:590
  56.3 0.9 collective-permute-done.6
  57.1 3.9 %collective-permute-done.7.v1 = f32[54,128]{1,0:T(8,128)S(1)} collective-permute-done((f32[54,128]{1,0:T(8,128)S(1)}, f32[54,128]{1,0:T(8,128)S(1)}, u32[]{:S(2)}, u32[]{:S(2)}) %collective-permute-start.7) | collective-permute-done | bytes 27680 | tf_op jit(solution)/shard_map/ppermute | solution.py:594
  61.0 1.9 %shard_map.90 = (f32[3,256,128]{2,1,0:T(8,128)S(1)}, f32[12,64,128]{2,1,0:T(8,128)S(1)}, f32[12,64,128]{2,1,0:T(8,128)S(1)}) custom-call(s32[11]{0:T(128)S(1)} %stack.51.where_ref, f32[54,128]{1,0:T(8,128)S(1)} %add.31.v0, f32[54,128]{1,0:T(8,128)S(1)} %collective-permute-done.7.v1, f32[9,768]{1,0:T(8,128)S(1)} %get-tuple-element.48.innov_ref, ...), custom_call_target="tpu_custom_call" | custom-call | flops 1000 | bytes 1000 | tf_op jit(solution)/shard_map/pallas_call | solution.py:460
  62.9 4.8 %collective-permute-start.10 = (f32[12,64,128]{2,1,0:T(8,128)S(1)}, f32[12,64,128]{2,1,0:T(8,128)S(1)}, u32[]{:S(2)}, u32[]{:S(2)}) collective-permute-start(f32[12,64,128]{2,1,0:T(8,128)S(1)} %get-tuple-element.56), channel_id=1, source_target_pairs={{0,64},{1,2},{2,1},{3,4},{4,3},{5,6},{6,5},{7,8},{8,7},{9,10},{10,... | collective-permute-start | bytes 1179656 | tf_op jit(solution)/shard_map/ppermute | solution.py:578
  67.7 5.3 %shard_map.91 = (f32[20,256,128]{2,1,0:T(8,128)}, f32[20,128,128]{2,1,0:T(8,128)S(1)}, f32[8,64,128]{2,1,0:T(8,128)S(1)}, f32[8,64,128]{2,1,0:T(8,128)S(1)}) custom-call(s32[11]{0:T(128)S(1)} %stack.51.where_ref, bf16[20,256,128]{2,1,0:T(8,128)(2,1)S(1)} %bitcast.19, bf16[20,3,256,128]{3,2,1,0:T(8,128)(2,1)S(1)} %bitcast.21, ...), custom_call_target="tpu_custom_call" | custom-call | flops 1000 | bytes 1000 | tf_op jit(solution)/shard_map/pallas_call | solution.py:492
  73.0 2.4 %collective-permute-start.8 = (f32[8,64,128]{2,1,0:T(8,128)S(1)}, f32[8,64,128]{2,1,0:T(8,128)S(1)}, u32[]{:S(2)}, u32[]{:S(2)}) collective-permute-start(f32[8,64,128]{2,1,0:T(8,128)S(1)} %get-tuple-element.53), channel_id=1, source_target_pairs={{0,64},{1,2},{2,1},{3,4},{4,3},{5,6},{6,5},{7,8},{8,7},{9,10},{10,... | collective-permute-start | bytes 786440 | tf_op jit(solution)/shard_map/ppermute | solution.py:578
  75.9 11.5 %collective-permute-done.10.first_ref = f32[12,64,128]{2,1,0:T(8,128)S(1)} collective-permute-done((f32[12,64,128]{2,1,0:T(8,128)S(1)}, f32[12,64,128]{2,1,0:T(8,128)S(1)}, u32[]{:S(2)}, u32[]{:S(2)}) %collective-permute-start.10) | collective-permute-done | bytes 393248 | tf_op jit(solution)/shard_map/ppermute | solution.py:578
  87.4 1.9 %collective-permute-done.11.second_ref = f32[12,64,128]{2,1,0:T(8,128)S(1)} collective-permute-done((f32[12,64,128]{2,1,0:T(8,128)S(1)}, f32[12,64,128]{2,1,0:T(8,128)S(1)}, u32[]{:S(2)}, u32[]{:S(2)}) %collective-permute-start.11) | collective-permute-done | bytes 393248 | tf_op jit(solution)/shard_map/ppermute | solution.py:582
  89.3 1.4 %shard_map.92.unused_ref = f32[20,4,64,128]{3,2,1,0:T(8,128)} custom-call(f32[12,64,128]{2,1,0:T(8,128)S(1)} %collective-permute-done.10.first_ref, f32[12,64,128]{2,1,0:T(8,128)S(1)} %collective-permute-done.11.second_ref, f32[20,128,128]{2,1,0:T(8,128)S(1)} %get-tuple-element.55.edge_ref, ...), custom_call_target="tpu_custom_call", output_to_operand_aliasing={{}: (5, {})} | custom-call | flops 1000 | bytes 1000 | tf_op jit(solution)/shard_map/pallas_call | solution.py:540
  90.8 6.1 %collective-permute-done.8.first_ref = f32[8,64,128]{2,1,0:T(8,128)S(1)} collective-permute-done((f32[8,64,128]{2,1,0:T(8,128)S(1)}, f32[8,64,128]{2,1,0:T(8,128)S(1)}, u32[]{:S(2)}, u32[]{:S(2)}) %collective-permute-start.8) | collective-permute-done | bytes 262176 | tf_op jit(solution)/shard_map/ppermute | solution.py:578
  96.9 1.1 %collective-permute-done.9.second_ref = f32[8,64,128]{2,1,0:T(8,128)S(1)} collective-permute-done((f32[8,64,128]{2,1,0:T(8,128)S(1)}, f32[8,64,128]{2,1,0:T(8,128)S(1)}, u32[]{:S(2)}, u32[]{:S(2)}) %collective-permute-start.9) | collective-permute-done | bytes 262176 | tf_op jit(solution)/shard_map/ppermute | solution.py:582
  97.9 1.3 %shard_map.93 = f32[20,4,64,128]{3,2,1,0:T(8,128)} custom-call(f32[8,64,128]{2,1,0:T(8,128)S(1)} %collective-permute-done.8.first_ref, f32[8,64,128]{2,1,0:T(8,128)S(1)} %collective-permute-done.9.second_ref, f32[20,128,128]{2,1,0:T(8,128)S(1)} %get-tuple-element.55.edge_ref, ...), custom_call_target="tpu_custom_call", output_to_operand_aliasing={{}: (5, {})} | custom-call | flops 1000 | bytes 1000 | tf_op jit(solution)/shard_map/pallas_call | solution.py:540
  (27 shorter events, 1.2 us)
Async XLA Ops:
  0.0 11.9 %copy-start = (bf16[20,8,32,128]{3,2,1,0:T(8,128)(2,1)S(1)}, bf16[20,8,32,128]{3,2,1,0:T(8,128)(2,1)}, u32[]{:S(2)}) copy-start(bf16[20,8,32,128]{3,2,1,0:T(8,128)(2,1)} %param.8) | copy-start | bytes 3932164
  2.7 32.9 %collective-permute-start.2 = (f32[1024,128]{1,0:T(8,128)}, f32[1024,128]{1,0:T(8,128)S(1)}, u32[]{:S(2)}, u32[]{:S(2)}) collective-permute-start(f32[1024,128]{1,0:T(8,128)} %get-tuple-element.39), channel_id=1, source_target_pairs={{0,64},{1,2},{2,1},{3,4},{4,3},{5,6},{6,5},{7,8},{8,7},{9,10},{10,... | collective-permute-start | bytes 1572872 | tf_op jit(solution)/shard_map/ppermute | solution.py:578
  11.8 25.4 %collective-permute-start.3 = (f32[1024,128]{1,0:T(8,128)}, f32[1024,128]{1,0:T(8,128)S(1)}, u32[]{:S(2)}, u32[]{:S(2)}) collective-permute-start(f32[1024,128]{1,0:T(8,128)} %get-tuple-element.40), channel_id=1, source_target_pairs={{0,1},{1,0},{2,3},{3,2},{4,5},{5,4},{6,7},{7,6},{8,9},{9,8},{10,11... | collective-permute-start | bytes 1572872 | tf_op jit(solution)/shard_map/ppermute | solution.py:582
  11.9 2.1 %copy-start.1 = (bf16[20,3,8,32,128]{4,3,2,1,0:T(8,128)(2,1)S(1)}, bf16[20,3,8,32,128]{4,3,2,1,0:T(8,128)(2,1)}, u32[]{:S(2)}) copy-start(bf16[20,3,8,32,128]{4,3,2,1,0:T(8,128)(2,1)} %param.9) | copy-start | bytes 11796484
  14.0 0.8 copy-start.3
  14.8 0.7 copy-start.9
  15.4 4.5 %copy-start.5 = (s32[1,2048]{1,0:T(1,128)S(1)}, s32[1,2048]{1,0:T(1,128)}, u32[]{:S(2)}) copy-start(s32[1,2048]{1,0:T(1,128)} %col_ref.1) | copy-start | bytes 24580
  15.4 4.5 %copy-start.6 = (s32[1,2048]{1,0:T(1,128)S(1)}, s32[1,2048]{1,0:T(1,128)}, u32[]{:S(2)}) copy-start(s32[1,2048]{1,0:T(1,128)} %lev_ref.1) | copy-start | bytes 24580
  15.4 4.5 %copy-start.7 = (f32[1,2048]{1,0:T(1,128)S(1)}, f32[1,2048]{1,0:T(1,128)}, u32[]{:S(2)}) copy-start(f32[1,2048]{1,0:T(1,128)} %innov_ref.1) | copy-start | bytes 24580
  15.4 4.5 %copy-start.8 = (f32[1,2048]{1,0:T(1,128)S(1)}, f32[1,2048]{1,0:T(1,128)}, u32[]{:S(2)}) copy-start(f32[1,2048]{1,0:T(1,128)} %weight_ref.1) | copy-start | bytes 24580
  20.3 20.6 %collective-permute-start = (f32[296,128]{1,0:T(8,128)S(1)}, f32[296,128]{1,0:T(8,128)S(1)}, u32[]{:S(2)}, u32[]{:S(2)}) collective-permute-start(f32[296,128]{1,0:T(8,128)S(1)} %get-tuple-element.34), channel_id=1, source_target_pairs={{0,64},{1,2},{2,1},{3,4},{4,3},{5,6},{6,5},{7,8},{8,7},{9,10},{10,... | collective-permute-start | bytes 454664 | tf_op jit(solution)/shard_map/ppermute | solution.py:578
  22.0 22.1 %collective-permute-start.1 = (f32[296,128]{1,0:T(8,128)S(1)}, f32[296,128]{1,0:T(8,128)S(1)}, u32[]{:S(2)}, u32[]{:S(2)}) collective-permute-start(f32[296,128]{1,0:T(8,128)S(1)} %get-tuple-element.35), channel_id=1, source_target_pairs={{0,1},{1,0},{2,3},{3,2},{4,5},{5,4},{6,7},{7,6},{8,9},{9,8},{10,11... | collective-permute-start | bytes 454664 | tf_op jit(solution)/shard_map/ppermute | solution.py:582
  45.2 1.4 %collective-permute-start.4 = (f32[176,128]{1,0:T(8,128)S(1)}, f32[176,128]{1,0:T(8,128)S(1)}, u32[]{:S(2)}, u32[]{:S(2)}) collective-permute-start(f32[176,128]{1,0:T(8,128)S(1)} %get-tuple-element.43.here_ref), channel_id=1, source_target_pairs={{0,64},{64,0},{128,192},{192,128},{1,65},{65,1},{129,193},{193,129... | collective-permute-start | bytes 270344 | tf_op jit(solution)/shard_map/ppermute | solution.py:590
  46.6 5.3 %collective-permute-start.5 = (f32[96,128]{1,0:T(8,128)S(1)}, f32[96,128]{1,0:T(8,128)S(1)}, u32[]{:S(2)}, u32[]{:S(2)}) collective-permute-start(f32[96,128]{1,0:T(8,128)S(1)} %slice_add_fusion.after_ref), channel_id=1, source_target_pairs={{0,1},{1,0},{2,3},{3,2},{4,5},{5,4},{6,7},{7,6},{8,9},{9,8},{10,11... | collective-permute-start | bytes 147464 | tf_op jit(solution)/shard_map/ppermute | solution.py:586
  53.3 3.8 %collective-permute-start.6 = (f32[54,128]{1,0:T(8,128)S(1)}, f32[54,128]{1,0:T(8,128)S(1)}, u32[]{:S(2)}, u32[]{:S(2)}) collective-permute-start(f32[54,128]{1,0:T(8,128)S(1)} %shard_map.89), channel_id=1, source_target_pairs={{0,64},{64,0},{128,192},{192,128},{1,65},{65,1},{129,193},{193,129... | collective-permute-start | bytes 82952 | tf_op jit(solution)/shard_map/ppermute | solution.py:590
  57.1 3.9 %collective-permute-start.7 = (f32[54,128]{1,0:T(8,128)S(1)}, f32[54,128]{1,0:T(8,128)S(1)}, u32[]{:S(2)}, u32[]{:S(2)}) collective-permute-start(f32[54,128]{1,0:T(8,128)S(1)} %add.31.v0), channel_id=1, source_target_pairs={{0,128},{64,192},{128,0},{192,64},{1,129},{65,193},{129,1},{193,65... | collective-permute-start | bytes 82952 | tf_op jit(solution)/shard_map/ppermute | solution.py:594
  61.0 6.7 %copy-start.2 = (bf16[20,3,8,32,128]{4,3,2,1,0:T(8,128)(2,1)S(1)}, bf16[20,3,8,32,128]{4,3,2,1,0:T(8,128)(2,1)}, u32[]{:S(2)}) copy-start(bf16[20,3,8,32,128]{4,3,2,1,0:T(8,128)(2,1)} %param.9) | copy-start | bytes 11796484
  61.0 6.7 %copy-start.4 = (bf16[128,128]{1,0:T(8,128)(2,1)S(1)}, bf16[128,128]{1,0:T(8,128)(2,1)}, u32[]{:S(2)}) copy-start(bf16[128,128]{1,0:T(8,128)(2,1)} %loc_ref.11) | copy-start | bytes 98308
  62.9 24.5 %collective-permute-start.10 = (f32[12,64,128]{2,1,0:T(8,128)S(1)}, f32[12,64,128]{2,1,0:T(8,128)S(1)}, u32[]{:S(2)}, u32[]{:S(2)}) collective-permute-start(f32[12,64,128]{2,1,0:T(8,128)S(1)} %get-tuple-element.56), channel_id=1, source_target_pairs={{0,64},{1,2},{2,1},{3,4},{4,3},{5,6},{6,5},{7,8},{8,7},{9,10},{10,... | collective-permute-start | bytes 1179656 | tf_op jit(solution)/shard_map/ppermute | solution.py:578
  67.7 21.6 %collective-permute-start.11 = (f32[12,64,128]{2,1,0:T(8,128)S(1)}, f32[12,64,128]{2,1,0:T(8,128)S(1)}, u32[]{:S(2)}, u32[]{:S(2)}) collective-permute-start(f32[12,64,128]{2,1,0:T(8,128)S(1)} %get-tuple-element.57), channel_id=1, source_target_pairs={{0,1},{1,0},{2,3},{3,2},{4,5},{5,4},{6,7},{7,6},{8,9},{9,8},{10,11... | collective-permute-start | bytes 1179656 | tf_op jit(solution)/shard_map/ppermute | solution.py:582
  73.0 23.8 %collective-permute-start.8 = (f32[8,64,128]{2,1,0:T(8,128)S(1)}, f32[8,64,128]{2,1,0:T(8,128)S(1)}, u32[]{:S(2)}, u32[]{:S(2)}) collective-permute-start(f32[8,64,128]{2,1,0:T(8,128)S(1)} %get-tuple-element.53), channel_id=1, source_target_pairs={{0,64},{1,2},{2,1},{3,4},{4,3},{5,6},{6,5},{7,8},{8,7},{9,10},{10,... | collective-permute-start | bytes 786440 | tf_op jit(solution)/shard_map/ppermute | solution.py:578
  75.5 22.5 %collective-permute-start.9 = (f32[8,64,128]{2,1,0:T(8,128)S(1)}, f32[8,64,128]{2,1,0:T(8,128)S(1)}, u32[]{:S(2)}, u32[]{:S(2)}) collective-permute-start(f32[8,64,128]{2,1,0:T(8,128)S(1)} %get-tuple-element.54), channel_id=1, source_target_pairs={{0,1},{1,0},{2,3},{3,2},{4,5},{5,4},{6,7},{7,6},{8,9},{9,8},{10,11... | collective-permute-start | bytes 786440 | tf_op jit(solution)/shard_map/ppermute | solution.py:582

commit v12 on v11

--- a/solution.py
+++ b/solution.py
@@ -127,26 +127,20 @@
 
 def send_kernel(quarters_ref, first_ref, second_ref, token_ref, edges, rows, fetched, sent):
     token_ref[...] = jnp.zeros_like(token_ref)
-    groups = HEAD // GROUP
-    fetches, sends = [], []
-    for g in range(groups):
-        members = pl.ds(g * GROUP, GROUP)
-        for n in range(2):
-            fetches.append(
-                pltpu.make_async_copy(quarters_ref.at[members, 3 * n], edges.at[n, members], fetched.at[g, n])
-            )
-            fetches[-1].start()
     low = side_of_first()
-    for g in range(groups):
-        for fetch in fetches[2 * g : 2 * g + 2]:
-            fetch.wait()
-        for k in range(g * GROUP, (g + 1) * GROUP):
-            rows[0, 64 * k : 64 * k + 64] = edges[1 - low, k].astype(F32)
-            rows[1, 64 * k : 64 * k + 64] = edges[low, k].astype(F32)
-        part = pl.ds(64 * GROUP * g, 64 * GROUP)
-        for n, ref in enumerate((first_ref, second_ref)):
-            sends.append(pltpu.make_async_copy(rows.at[n, part], ref.at[part], sent.at[g, n]))
-            sends[-1].start()
+    members = pl.ds(0, HEAD)
+    fetches = [
+        pltpu.make_async_copy(quarters_ref.at[members, quarter], edges.at[n], fetched.at[n])
+        for n, quarter in enumerate((3 * (1 - low), 3 * low))
+    ]
+    sends = [pltpu.make_async_copy(rows.at[n], ref, sent.at[n]) for n, ref in enumerate((first_ref, second_ref))]
+    for fetch in fetches:
+        fetch.start()
+    for n in range(2):
+        fetches[n].wait()
+        for k in range(HEAD):
+            rows[n, 64 * k : 64 * k + 64] = edges[n, k].astype(F32)
+        sends[n].start()
     for send in sends:
         send.wait()
 
@@ -160,8 +154,8 @@
         scratch=[
             pltpu.VMEM((2, HEAD, 64, 128), BF16),
             pltpu.VMEM((2, 64 * HEAD, 128), F32),
-            pltpu.SemaphoreType.DMA((HEAD // GROUP, 2)),
-            pltpu.SemaphoreType.DMA((HEAD // GROUP, 2)),
+            pltpu.SemaphoreType.DMA((2,)),
+            pltpu.SemaphoreType.DMA((2,)),
         ],
         vmem=56,
     )(quarters)
@@ -371,9 +365,8 @@
     level = lax.broadcasted_iota(jnp.int32, (128, SLOTS), 0).astype(F32)
 
     def pick(cells, weight, row):
-        both = jnp.concatenate(halves(cells), axis=1)
-        at_all = tn(both, weight)
-        at_all = at_all[:128] + at_all[128:]
+        both = jnp.concatenate(halves(cells), axis=0)
+        at_all = tn(both, jnp.concatenate([weight, weight], axis=0))
         hot = level == lev_ref[pl.ds(row, 1), :]
         return jnp.sum(jnp.where(hot, at_all, 0.0), axis=0, keepdims=True)
 

time: 99.6 us -> 99.3 us (level)
  no operation moved by 1% of the time
where the time goes in v12:
time: 99.3 us; the launch traced here: 99.1 us
  waiting for transfers between devices  47.5 us (48%)
  Pallas kernels  23.9 us (24%)
  starting transfers between devices  23.1 us (23%)
  local copies, waits for them, and re-layouts  3.65 us (4%)
    ppermute x4, waiting for transfers between devices, swap_first(): return lax.ppermute(x, ('mem', 'tile'), FIRST)  31.7 us
    ppermute x4, starting transfers between devices, swap_first(): return lax.ppermute(x, ('mem', 'tile'), FIRST)  18 us
    ppermute x4, waiting for transfers between devices, swap_second(): return lax.ppermute(x, ('mem', 'tile'), SECOND)  7.56 us
    pallas_call x1, Pallas kernels, back_part(): call(back_kernel, (sds(members, 256, 128), sds(members, 128, 128), sds(me...  5.34 us
    ppermute x1, waiting for transfers between devices, swap_chip(): return lax.ppermute(x, 'mem', [(m, m ^ 2) for m in range(MEMS)])  3.86 us
    pallas_call x1, Pallas kernels, own_part(): call(own_kernel, (sds(V, 128, 128), sds(members, 128, 128), sds(members,...  3.78 us
    unnamed x20, local copies, waits for them, and re-layouts  3.56 us
    ppermute x2, starting transfers between devices, swap_core(): return lax.ppermute(x, 'mem', [(m, m ^ 1) for m in range(MEMS)])  3.05 us
  transfers between devices with their start and end apart: 12, of which 12 were waited for; matrix products, arithmetic and copies ran while one was open for 0% of the time, Pallas kernels for 16%

profile of v12, /device:TPU:6, one launch (start us, length us, event | category | flops | bytes accessed | tf_op | source)
XLA Modules:
  0.0 99.1 jit_solution(901335349552186202)
XLA Ops:
  0.0 2.7 %shard_map.82 = (f32[1024,128]{1,0:T(8,128)}, f32[1024,128]{1,0:T(8,128)}, f32[8,128]{1,0:T(8,128)}) custom-call(bf16[20,4,64,128]{3,2,1,0:T(8,128)(2,1)} %bitcast.16), custom_call_target="tpu_custom_call" | custom-call | flops 1000 | bytes 1000 | tf_op jit(solution)/shard_map/pallas_call | solution.py:149
  2.7 9.1 %collective-permute-start.2 = (f32[1024,128]{1,0:T(8,128)}, f32[1024,128]{1,0:T(8,128)S(1)}, u32[]{:S(2)}, u32[]{:S(2)}) collective-permute-start(f32[1024,128]{1,0:T(8,128)} %get-tuple-element.39), channel_id=1, source_target_pairs={{0,64},{1,2},{2,1},{3,4},{4,3},{5,6},{6,5},{7,8},{8,7},{9,10},{10,... | collective-permute-start | bytes 1572872 | tf_op jit(solution)/shard_map/ppermute | solution.py:571
  11.9 2.1 %copy-done.1 = bf16[20,3,8,32,128]{4,3,2,1,0:T(8,128)(2,1)S(1)} copy-done((bf16[20,3,8,32,128]{4,3,2,1,0:T(8,128)(2,1)S(1)}, bf16[20,3,8,32,128]{4,3,2,1,0:T(8,128)(2,1)}, u32[]{:S(2)}) %copy-start.1) | copy-done | bytes 3932184
  14.0 0.8 copy-done.3
  14.8 0.7 copy-done.9
  15.5 3.8 %shard_map.83 = (f32[3,128,128]{2,1,0:T(8,128)S(1)}, f32[20,128,128]{2,1,0:T(8,128)S(1)}, bf16[20,3,128,128]{3,2,1,0:T(8,128)(2,1)S(1)}, bf16[256,256]{1,0:T(8,128)(2,1)S(1)}, bf16[128,128]{1,0:T(8,128)(2,1)S(1)}) custom-call(s32[11]{0:T(128)S(1)} %stack.51.where_ref, bf16[20,256,128]{2,1,0:T(8,128)(2,1)S(1)} %bitcast.17, ...), custom_call_target="tpu_custom_call" | custom-call | flops 1000 | bytes 1000 | tf_op jit(solution)/shard_map/pallas_call | solution.py:221
  20.4 1.6 %collective-permute-start = (f32[296,128]{1,0:T(8,128)S(1)}, f32[296,128]{1,0:T(8,128)S(1)}, u32[]{:S(2)}, u32[]{:S(2)}) collective-permute-start(f32[296,128]{1,0:T(8,128)S(1)} %get-tuple-element.34), channel_id=1, source_target_pairs={{0,64},{1,2},{2,1},{3,4},{4,3},{5,6},{6,5},{7,8},{8,7},{9,10},{10,... | collective-permute-start | bytes 454664 | tf_op jit(solution)/shard_map/ppermute | solution.py:571
  22.0 1.5 %collective-permute-start.1 = (f32[296,128]{1,0:T(8,128)S(1)}, f32[296,128]{1,0:T(8,128)S(1)}, u32[]{:S(2)}, u32[]{:S(2)}) collective-permute-start(f32[296,128]{1,0:T(8,128)S(1)} %get-tuple-element.35), channel_id=1, source_target_pairs={{0,1},{1,0},{2,3},{3,2},{4,5},{5,4},{6,7},{7,6},{8,9},{9,8},{10,11... | collective-permute-start | bytes 454664 | tf_op jit(solution)/shard_map/ppermute | solution.py:575
  23.5 12.1 %collective-permute-done.2.first_ref = f32[1024,128]{1,0:T(8,128)S(1)} collective-permute-done((f32[1024,128]{1,0:T(8,128)}, f32[1024,128]{1,0:T(8,128)S(1)}, u32[]{:S(2)}, u32[]{:S(2)}) %collective-permute-start.2) | collective-permute-done | bytes 524320 | tf_op jit(solution)/shard_map/ppermute | solution.py:571
  35.6 1.6 %collective-permute-done.3.second_ref = f32[1024,128]{1,0:T(8,128)S(1)} collective-permute-done((f32[1024,128]{1,0:T(8,128)}, f32[1024,128]{1,0:T(8,128)S(1)}, u32[]{:S(2)}, u32[]{:S(2)}) %collective-permute-start.3) | collective-permute-done | bytes 524320 | tf_op jit(solution)/shard_map/ppermute | solution.py:575
  37.2 1.9 %shard_map.85.head_ref = f32[3,128,128]{2,1,0:T(8,128)S(1)} custom-call(f32[1024,128]{1,0:T(8,128)S(1)} %collective-permute-done.2.first_ref, f32[1024,128]{1,0:T(8,128)S(1)} %collective-permute-done.3.second_ref, f32[20,128,128]{2,1,0:T(8,128)S(1)} %get-tuple-element.36.own_ref, bf16[20,3,128,128]{3,2,1,0:T(8,128)(2,1)S(1)} %get-tuple-element.37.x_ref, ...), custom_call_target="tpu_custom_call" | custom-call | flops 1000 | bytes 1000 | tf_op jit(solution)/shard_map/pallas_call | solution.py:268
  39.1 1.9 %collective-permute-done.first_ref = f32[296,128]{1,0:T(8,128)S(1)} collective-permute-done((f32[296,128]{1,0:T(8,128)S(1)}, f32[296,128]{1,0:T(8,128)S(1)}, u32[]{:S(2)}, u32[]{:S(2)}) %collective-permute-start) | collective-permute-done | bytes 151584 | tf_op jit(solution)/shard_map/ppermute | solution.py:571
  41.0 3.1 %collective-permute-done.1.second_ref = f32[296,128]{1,0:T(8,128)S(1)} collective-permute-done((f32[296,128]{1,0:T(8,128)S(1)}, f32[296,128]{1,0:T(8,128)S(1)}, u32[]{:S(2)}, u32[]{:S(2)}) %collective-permute-start.1) | collective-permute-done | bytes 151584 | tf_op jit(solution)/shard_map/ppermute | solution.py:575
  44.1 1.2 %shard_map.86 = (f32[3,256,128]{2,1,0:T(8,128)S(1)}, f32[96,128]{1,0:T(8,128)S(1)}, f32[176,128]{1,0:T(8,128)S(1)}) custom-call(s32[11]{0:T(128)S(1)} %stack.51.where_ref, f32[296,128]{1,0:T(8,128)S(1)} %collective-permute-done.first_ref, f32[296,128]{1,0:T(8,128)S(1)} %collective-permute-done.1.second_ref, f32[20,128,128]{2,1,0:T(8,128)S(1)} %get-tuple-element.36.own_ref, ...), custom_call_target="tpu_custom_call" | custom-call | flops 1000 | bytes 1000 | tf_op jit(solution)/shard_map/pallas_call | solution.py:286
  45.3 1.3 %collective-permute-done.4.there_ref = f32[176,128]{1,0:T(8,128)S(1)} collective-permute-done((f32[176,128]{1,0:T(8,128)S(1)}, f32[176,128]{1,0:T(8,128)S(1)}, u32[]{:S(2)}, u32[]{:S(2)}) %collective-permute-start.4) | collective-permute-done | bytes 90144 | tf_op jit(solution)/shard_map/ppermute | solution.py:583
  46.7 1.7 %shard_map.87 = (bf16[3,320,768]{2,1,0:T(8,128)(2,1)S(1)}, bf16[2,3,64,768]{3,2,1,0:T(8,128)(2,1)S(1)}, f32[9,768]{1,0:T(8,128)S(1)}, f32[9,768]{1,0:T(8,128)S(1...) custom-call(s32[11]{0:T(128)S(1)} %stack.51.where_ref, f32[80,128]{1,0:T(8,128)S(1)} %get-tuple-element.42.own_ref, ...), custom_call_target="tpu_custom_call" | custom-call | flops 1000 | bytes 1000 | tf_op jit(solution)/shard_map/pallas_call | solution.py:349
  48.4 1.4 %shard_map.88.mine_ref = f32[9,768]{1,0:T(8,128)S(1)} custom-call(s32[11]{0:T(128)S(1)} %stack.51.where_ref, f32[3,256,128]{2,1,0:T(8,128)S(1)} %get-tuple-element.41.inc_ref, bf16[3,320,768]{2,1,0:T(8,128)(2,1)S(1)} %get-tuple-element.45.wown_ref, bf16[2,3,64,768]{3,2,1,0:T(8,128)(2,1)S(1)} %get-tuple-element.46.wnear_ref, ...), custom_call_target="tpu_custom_call" | custom-call | flops 1000 | bytes 1000 | tf_op jit(solution)/shard_map/pallas_call | solution.py:387
  49.7 2.2 %collective-permute-done.5.near_ref = f32[96,128]{1,0:T(8,128)S(1)} collective-permute-done((f32[96,128]{1,0:T(8,128)S(1)}, f32[96,128]{1,0:T(8,128)S(1)}, u32[]{:S(2)}, u32[]{:S(2)}) %collective-permute-start.5) | collective-permute-done | bytes 49184 | tf_op jit(solution)/shard_map/ppermute | solution.py:579
  52.0 1.1 %shard_map.89 = f32[54,128]{1,0:T(8,128)S(1)} custom-call(s32[11]{0:T(128)S(1)} %stack.51.where_ref, f32[9,768]{1,0:T(8,128)S(1)} %shard_map.88.mine_ref, f32[96,128]{1,0:T(8,128)S(1)} %collective-permute-done.5.near_ref, bf16[3,320,768]{2,1,0:T(8,128)(2,1)S(1)} %get-tuple-element.45.wown_ref, bf16[2,3,64,768]{3,2,1,0:T(8,128)(2,1)S(1)} %get-tuple-element.46.wnear_ref, ...), custom_call_target="tpu_custom_call" | custom-call | flops 1000 | bytes 1000 | tf_op jit(solution)/shard_map/pallas_call | solution.py:415
  53.0 3.0 %collective-permute-start.6 = (f32[54,128]{1,0:T(8,128)S(1)}, f32[54,128]{1,0:T(8,128)S(1)}, u32[]{:S(2)}, u32[]{:S(2)}) collective-permute-start(f32[54,128]{1,0:T(8,128)S(1)} %shard_map.89), channel_id=1, source_target_pairs={{0,64},{64,0},{128,192},{192,128},{1,65},{65,1},{129,193},{193,129... | collective-permute-start | bytes 82952 | tf_op jit(solution)/shard_map/ppermute | solution.py:583
  56.0 0.9 collective-permute-done.6
  56.8 3.9 %collective-permute-done.7.v1 = f32[54,128]{1,0:T(8,128)S(1)} collective-permute-done((f32[54,128]{1,0:T(8,128)S(1)}, f32[54,128]{1,0:T(8,128)S(1)}, u32[]{:S(2)}, u32[]{:S(2)}) %collective-permute-start.7) | collective-permute-done | bytes 27680 | tf_op jit(solution)/shard_map/ppermute | solution.py:587
  60.7 1.9 %shard_map.90 = (f32[3,256,128]{2,1,0:T(8,128)S(1)}, f32[12,64,128]{2,1,0:T(8,128)S(1)}, f32[12,64,128]{2,1,0:T(8,128)S(1)}) custom-call(s32[11]{0:T(128)S(1)} %stack.51.where_ref, f32[54,128]{1,0:T(8,128)S(1)} %add.31.v0, f32[54,128]{1,0:T(8,128)S(1)} %collective-permute-done.7.v1, f32[9,768]{1,0:T(8,128)S(1)} %get-tuple-element.48.innov_ref, ...), custom_call_target="tpu_custom_call" | custom-call | flops 1000 | bytes 1000 | tf_op jit(solution)/shard_map/pallas_call | solution.py:453
  62.6 4.8 %collective-permute-start.10 = (f32[12,64,128]{2,1,0:T(8,128)S(1)}, f32[12,64,128]{2,1,0:T(8,128)S(1)}, u32[]{:S(2)}, u32[]{:S(2)}) collective-permute-start(f32[12,64,128]{2,1,0:T(8,128)S(1)} %get-tuple-element.56), channel_id=1, source_target_pairs={{0,64},{1,2},{2,1},{3,4},{4,3},{5,6},{6,5},{7,8},{8,7},{9,10},{10,... | collective-permute-start | bytes 1179656 | tf_op jit(solution)/shard_map/ppermute | solution.py:571
  67.4 5.3 %shard_map.91 = (f32[20,256,128]{2,1,0:T(8,128)}, f32[20,128,128]{2,1,0:T(8,128)S(1)}, f32[8,64,128]{2,1,0:T(8,128)S(1)}, f32[8,64,128]{2,1,0:T(8,128)S(1)}) custom-call(s32[11]{0:T(128)S(1)} %stack.51.where_ref, bf16[20,256,128]{2,1,0:T(8,128)(2,1)S(1)} %bitcast.19, bf16[20,3,256,128]{3,2,1,0:T(8,128)(2,1)S(1)} %bitcast.21, ...), custom_call_target="tpu_custom_call" | custom-call | flops 1000 | bytes 1000 | tf_op jit(solution)/shard_map/pallas_call | solution.py:485
  72.7 2.4 %collective-permute-start.8 = (f32[8,64,128]{2,1,0:T(8,128)S(1)}, f32[8,64,128]{2,1,0:T(8,128)S(1)}, u32[]{:S(2)}, u32[]{:S(2)}) collective-permute-start(f32[8,64,128]{2,1,0:T(8,128)S(1)} %get-tuple-element.53), channel_id=1, source_target_pairs={{0,64},{1,2},{2,1},{3,4},{4,3},{5,6},{6,5},{7,8},{8,7},{9,10},{10,... | collective-permute-start | bytes 786440 | tf_op jit(solution)/shard_map/ppermute | solution.py:571
  75.6 11.5 %collective-permute-done.10.first_ref = f32[12,64,128]{2,1,0:T(8,128)S(1)} collective-permute-done((f32[12,64,128]{2,1,0:T(8,128)S(1)}, f32[12,64,128]{2,1,0:T(8,128)S(1)}, u32[]{:S(2)}, u32[]{:S(2)}) %collective-permute-start.10) | collective-permute-done | bytes 393248 | tf_op jit(solution)/shard_map/ppermute | solution.py:571
  87.1 1.8 %collective-permute-done.11.second_ref = f32[12,64,128]{2,1,0:T(8,128)S(1)} collective-permute-done((f32[12,64,128]{2,1,0:T(8,128)S(1)}, f32[12,64,128]{2,1,0:T(8,128)S(1)}, u32[]{:S(2)}, u32[]{:S(2)}) %collective-permute-start.11) | collective-permute-done | bytes 393248 | tf_op jit(solution)/shard_map/ppermute | solution.py:575
  88.9 1.4 %shard_map.92.unused_ref = f32[20,4,64,128]{3,2,1,0:T(8,128)} custom-call(f32[12,64,128]{2,1,0:T(8,128)S(1)} %collective-permute-done.10.first_ref, f32[12,64,128]{2,1,0:T(8,128)S(1)} %collective-permute-done.11.second_ref, f32[20,128,128]{2,1,0:T(8,128)S(1)} %get-tuple-element.55.edge_ref, ...), custom_call_target="tpu_custom_call", output_to_operand_aliasing={{}: (5, {})} | custom-call | flops 1000 | bytes 1000 | tf_op jit(solution)/shard_map/pallas_call | solution.py:533
  90.4 6.2 %collective-permute-done.8.first_ref = f32[8,64,128]{2,1,0:T(8,128)S(1)} collective-permute-done((f32[8,64,128]{2,1,0:T(8,128)S(1)}, f32[8,64,128]{2,1,0:T(8,128)S(1)}, u32[]{:S(2)}, u32[]{:S(2)}) %collective-permute-start.8) | collective-permute-done | bytes 262176 | tf_op jit(solution)/shard_map/ppermute | solution.py:571
  96.6 1.1 %collective-permute-done.9.second_ref = f32[8,64,128]{2,1,0:T(8,128)S(1)} collective-permute-done((f32[8,64,128]{2,1,0:T(8,128)S(1)}, f32[8,64,128]{2,1,0:T(8,128)S(1)}, u32[]{:S(2)}, u32[]{:S(2)}) %collective-permute-start.9) | collective-permute-done | bytes 262176 | tf_op jit(solution)/shard_map/ppermute | solution.py:575
  97.7 1.3 %shard_map.93 = f32[20,4,64,128]{3,2,1,0:T(8,128)} custom-call(f32[8,64,128]{2,1,0:T(8,128)S(1)} %collective-permute-done.8.first_ref, f32[8,64,128]{2,1,0:T(8,128)S(1)} %collective-permute-done.9.second_ref, f32[20,128,128]{2,1,0:T(8,128)S(1)} %get-tuple-element.55.edge_ref, ...), custom_call_target="tpu_custom_call", output_to_operand_aliasing={{}: (5, {})} | custom-call | flops 1000 | bytes 1000 | tf_op jit(solution)/shard_map/pallas_call | solution.py:533
  (27 shorter events, 1.2 us)
Async XLA Ops:
  0.0 11.9 %copy-start = (bf16[20,8,32,128]{3,2,1,0:T(8,128)(2,1)S(1)}, bf16[20,8,32,128]{3,2,1,0:T(8,128)(2,1)}, u32[]{:S(2)}) copy-start(bf16[20,8,32,128]{3,2,1,0:T(8,128)(2,1)} %param.8) | copy-start | bytes 3932164
  2.7 32.9 %collective-permute-start.2 = (f32[1024,128]{1,0:T(8,128)}, f32[1024,128]{1,0:T(8,128)S(1)}, u32[]{:S(2)}, u32[]{:S(2)}) collective-permute-start(f32[1024,128]{1,0:T(8,128)} %get-tuple-element.39), channel_id=1, source_target_pairs={{0,64},{1,2},{2,1},{3,4},{4,3},{5,6},{6,5},{7,8},{8,7},{9,10},{10,... | collective-permute-start | bytes 1572872 | tf_op jit(solution)/shard_map/ppermute | solution.py:571
  11.8 25.4 %collective-permute-start.3 = (f32[1024,128]{1,0:T(8,128)}, f32[1024,128]{1,0:T(8,128)S(1)}, u32[]{:S(2)}, u32[]{:S(2)}) collective-permute-start(f32[1024,128]{1,0:T(8,128)} %get-tuple-element.40), channel_id=1, source_target_pairs={{0,1},{1,0},{2,3},{3,2},{4,5},{5,4},{6,7},{7,6},{8,9},{9,8},{10,11... | collective-permute-start | bytes 1572872 | tf_op jit(solution)/shard_map/ppermute | solution.py:575
  11.9 2.1 %copy-start.1 = (bf16[20,3,8,32,128]{4,3,2,1,0:T(8,128)(2,1)S(1)}, bf16[20,3,8,32,128]{4,3,2,1,0:T(8,128)(2,1)}, u32[]{:S(2)}) copy-start(bf16[20,3,8,32,128]{4,3,2,1,0:T(8,128)(2,1)} %param.9) | copy-start | bytes 11796484
  14.0 0.8 copy-start.3
  14.8 0.7 copy-start.9
  15.4 4.5 %copy-start.5 = (s32[1,2048]{1,0:T(1,128)S(1)}, s32[1,2048]{1,0:T(1,128)}, u32[]{:S(2)}) copy-start(s32[1,2048]{1,0:T(1,128)} %col_ref.1) | copy-start | bytes 24580
  15.5 4.5 %copy-start.6 = (s32[1,2048]{1,0:T(1,128)S(1)}, s32[1,2048]{1,0:T(1,128)}, u32[]{:S(2)}) copy-start(s32[1,2048]{1,0:T(1,128)} %lev_ref.1) | copy-start | bytes 24580
  15.5 4.5 %copy-start.7 = (f32[1,2048]{1,0:T(1,128)S(1)}, f32[1,2048]{1,0:T(1,128)}, u32[]{:S(2)}) copy-start(f32[1,2048]{1,0:T(1,128)} %innov_ref.1) | copy-start | bytes 24580
  15.5 4.5 %copy-start.8 = (f32[1,2048]{1,0:T(1,128)S(1)}, f32[1,2048]{1,0:T(1,128)}, u32[]{:S(2)}) copy-start(f32[1,2048]{1,0:T(1,128)} %weight_ref.1) | copy-start | bytes 24580
  20.4 20.6 %collective-permute-start = (f32[296,128]{1,0:T(8,128)S(1)}, f32[296,128]{1,0:T(8,128)S(1)}, u32[]{:S(2)}, u32[]{:S(2)}) collective-permute-start(f32[296,128]{1,0:T(8,128)S(1)} %get-tuple-element.34), channel_id=1, source_target_pairs={{0,64},{1,2},{2,1},{3,4},{4,3},{5,6},{6,5},{7,8},{8,7},{9,10},{10,... | collective-permute-start | bytes 454664 | tf_op jit(solution)/shard_map/ppermute | solution.py:571
  22.0 22.1 %collective-permute-start.1 = (f32[296,128]{1,0:T(8,128)S(1)}, f32[296,128]{1,0:T(8,128)S(1)}, u32[]{:S(2)}, u32[]{:S(2)}) collective-permute-start(f32[296,128]{1,0:T(8,128)S(1)} %get-tuple-element.35), channel_id=1, source_target_pairs={{0,1},{1,0},{2,3},{3,2},{4,5},{5,4},{6,7},{7,6},{8,9},{9,8},{10,11... | collective-permute-start | bytes 454664 | tf_op jit(solution)/shard_map/ppermute | solution.py:575
  45.2 1.4 %collective-permute-start.4 = (f32[176,128]{1,0:T(8,128)S(1)}, f32[176,128]{1,0:T(8,128)S(1)}, u32[]{:S(2)}, u32[]{:S(2)}) collective-permute-start(f32[176,128]{1,0:T(8,128)S(1)} %get-tuple-element.43.here_ref), channel_id=1, source_target_pairs={{0,64},{64,0},{128,192},{192,128},{1,65},{65,1},{129,193},{193,129... | collective-permute-start | bytes 270344 | tf_op jit(solution)/shard_map/ppermute | solution.py:583
  46.6 5.3 %collective-permute-start.5 = (f32[96,128]{1,0:T(8,128)S(1)}, f32[96,128]{1,0:T(8,128)S(1)}, u32[]{:S(2)}, u32[]{:S(2)}) collective-permute-start(f32[96,128]{1,0:T(8,128)S(1)} %slice_add_fusion.after_ref), channel_id=1, source_target_pairs={{0,1},{1,0},{2,3},{3,2},{4,5},{5,4},{6,7},{7,6},{8,9},{9,8},{10,11... | collective-permute-start | bytes 147464 | tf_op jit(solution)/shard_map/ppermute | solution.py:579
  53.0 3.8 %collective-permute-start.6 = (f32[54,128]{1,0:T(8,128)S(1)}, f32[54,128]{1,0:T(8,128)S(1)}, u32[]{:S(2)}, u32[]{:S(2)}) collective-permute-start(f32[54,128]{1,0:T(8,128)S(1)} %shard_map.89), channel_id=1, source_target_pairs={{0,64},{64,0},{128,192},{192,128},{1,65},{65,1},{129,193},{193,129... | collective-permute-start | bytes 82952 | tf_op jit(solution)/shard_map/ppermute | solution.py:583
  56.8 3.9 %collective-permute-start.7 = (f32[54,128]{1,0:T(8,128)S(1)}, f32[54,128]{1,0:T(8,128)S(1)}, u32[]{:S(2)}, u32[]{:S(2)}) collective-permute-start(f32[54,128]{1,0:T(8,128)S(1)} %add.31.v0), channel_id=1, source_target_pairs={{0,128},{64,192},{128,0},{192,64},{1,129},{65,193},{129,1},{193,65... | collective-permute-start | bytes 82952 | tf_op jit(solution)/shard_map/ppermute | solution.py:587
  60.7 6.7 %copy-start.2 = (bf16[20,3,8,32,128]{4,3,2,1,0:T(8,128)(2,1)S(1)}, bf16[20,3,8,32,128]{4,3,2,1,0:T(8,128)(2,1)}, u32[]{:S(2)}) copy-start(bf16[20,3,8,32,128]{4,3,2,1,0:T(8,128)(2,1)} %param.9) | copy-start | bytes 11796484
  60.7 6.7 %copy-start.4 = (bf16[128,128]{1,0:T(8,128)(2,1)S(1)}, bf16[128,128]{1,0:T(8,128)(2,1)}, u32[]{:S(2)}) copy-start(bf16[128,128]{1,0:T(8,128)(2,1)} %loc_ref.11) | copy-start | bytes 98308
  62.6 24.5 %collective-permute-start.10 = (f32[12,64,128]{2,1,0:T(8,128)S(1)}, f32[12,64,128]{2,1,0:T(8,128)S(1)}, u32[]{:S(2)}, u32[]{:S(2)}) collective-permute-start(f32[12,64,128]{2,1,0:T(8,128)S(1)} %get-tuple-element.56), channel_id=1, source_target_pairs={{0,64},{1,2},{2,1},{3,4},{4,3},{5,6},{6,5},{7,8},{8,7},{9,10},{10,... | collective-permute-start | bytes 1179656 | tf_op jit(solution)/shard_map/ppermute | solution.py:571
  67.4 21.5 %collective-permute-start.11 = (f32[12,64,128]{2,1,0:T(8,128)S(1)}, f32[12,64,128]{2,1,0:T(8,128)S(1)}, u32[]{:S(2)}, u32[]{:S(2)}) collective-permute-start(f32[12,64,128]{2,1,0:T(8,128)S(1)} %get-tuple-element.57), channel_id=1, source_target_pairs={{0,1},{1,0},{2,3},{3,2},{4,5},{5,4},{6,7},{7,6},{8,9},{9,8},{10,11... | collective-permute-start | bytes 1179656 | tf_op jit(solution)/shard_map/ppermute | solution.py:575
  72.7 23.8 %collective-permute-start.8 = (f32[8,64,128]{2,1,0:T(8,128)S(1)}, f32[8,64,128]{2,1,0:T(8,128)S(1)}, u32[]{:S(2)}, u32[]{:S(2)}) collective-permute-start(f32[8,64,128]{2,1,0:T(8,128)S(1)} %get-tuple-element.53), channel_id=1, source_target_pairs={{0,64},{1,2},{2,1},{3,4},{4,3},{5,6},{6,5},{7,8},{8,7},{9,10},{10,... | collective-permute-start | bytes 786440 | tf_op jit(solution)/shard_map/ppermute | solution.py:571
  75.2 22.5 %collective-permute-start.9 = (f32[8,64,128]{2,1,0:T(8,128)S(1)}, f32[8,64,128]{2,1,0:T(8,128)S(1)}, u32[]{:S(2)}, u32[]{:S(2)}) collective-permute-start(f32[8,64,128]{2,1,0:T(8,128)S(1)} %get-tuple-element.54), channel_id=1, source_target_pairs={{0,1},{1,0},{2,3},{3,2},{4,5},{5,4},{6,7},{7,6},{8,9},{9,8},{10,11... | collective-permute-start | bytes 786440 | tf_op jit(solution)/shard_map/ppermute | solution.py:575

commit v13 on v12

--- a/solution.py
+++ b/solution.py
@@ -125,24 +125,18 @@
                 out_ref[row : row + 1] = total[6 * f + a : 6 * f + a + 1, 128 * v : 128 * v + 128]
 
 
-def send_kernel(quarters_ref, first_ref, second_ref, token_ref, edges, rows, fetched, sent):
+def send_kernel(quarters_ref, first_ref, second_ref, token_ref, edges, sems):
+    members = pl.ds(0, HEAD)
+    copies = [pltpu.make_async_copy(quarters_ref.at[members, 3 * n], edges.at[n], sems.at[n]) for n in range(2)]
+    for copy in copies:
+        copy.start()
     token_ref[...] = jnp.zeros_like(token_ref)
+    for copy in copies:
+        copy.wait()
     low = side_of_first()
-    members = pl.ds(0, HEAD)
-    fetches = [
-        pltpu.make_async_copy(quarters_ref.at[members, quarter], edges.at[n], fetched.at[n])
-        for n, quarter in enumerate((3 * (1 - low), 3 * low))
-    ]
-    sends = [pltpu.make_async_copy(rows.at[n], ref, sent.at[n]) for n, ref in enumerate((first_ref, second_ref))]
-    for fetch in fetches:
-        fetch.start()
-    for n in range(2):
-        fetches[n].wait()
-        for k in range(HEAD):
-            rows[n, 64 * k : 64 * k + 64] = edges[n, k].astype(F32)
-        sends[n].start()
-    for send in sends:
-        send.wait()
+    for k in range(HEAD):
+        first_ref[64 * k : 64 * k + 64] = edges[1 - low, k].astype(F32)
+        second_ref[64 * k : 64 * k + 64] = edges[low, k].astype(F32)
 
 
 def send_part(quarters):
@@ -150,13 +144,8 @@
         send_kernel,
         (sds(64 * HEAD, 128), sds(64 * HEAD, 128), sds(8, 128)),
         ins=[HBM],
-        outs=(HBM, HBM, VMEM),
-        scratch=[
-            pltpu.VMEM((2, HEAD, 64, 128), BF16),
-            pltpu.VMEM((2, 64 * HEAD, 128), F32),
-            pltpu.SemaphoreType.DMA((2,)),
-            pltpu.SemaphoreType.DMA((2,)),
-        ],
+        outs=(VMEM,) * 3,
+        scratch=[pltpu.VMEM((2, HEAD, 64, 128), BF16), pltpu.SemaphoreType.DMA((2,))],
         vmem=56,
     )(quarters)
 
@@ -423,20 +412,27 @@
 def adjoint_kernel(where_ref, v0, v1, innov_ref, weight_ref, hot_ref, wown_ref, wnear_ref, x_ref, c_ref, first_ref, second_ref):
     value = v0[...] + v1[...]
 
+    def weighted(row):
+        line = jnp.concatenate([value[6 * row + a : 6 * row + a + 1] for a in range(6)], axis=1)
+        return weight_ref[row : row + 1] * (line - innov_ref[row : row + 1])
+
     def place(weight, row):
-        line = jnp.concatenate([value[6 * row + a : 6 * row + a + 1] for a in range(6)], axis=1)
-        weighted = weight_ref[row : row + 1] * (line - innov_ref[row : row + 1])
         hot = hot_ref[row]
-        both = jnp.concatenate([hot * half for half in halves(weighted)], axis=0)
+        both = jnp.concatenate([hot * half for half in halves(weighted(row))], axis=0)
         out = nt(weight, both)
         return out[:, :128] + out[:, 128:]
+
+    def place_near(weight, row):
+        both = jnp.concatenate(halves(weight.astype(F32) * weighted(row)), axis=0)
+        out = nt(both, hot_ref[row])
+        return out[:32] + out[32:]
 
     adj = []
     for v in range(V):
         c_ref[v] = place(wown_ref[v, :256], v)
         for n in range(2):
             rows = pl.ds(pl.multiple_of(where_ref[n], 32), 32)
-            c_ref[v, rows] = c_ref[v, rows] + place(wnear_ref[n, v, :32], 3 * n + 3 + v)
+            c_ref[v, rows] = c_ref[v, rows] + place_near(wnear_ref[n, v, :32], 3 * n + 3 + v)
         adj.append(jnp.concatenate([c_ref[v, :64], c_ref[v, 192:]], axis=0))
     first_low = where_ref[7] == 1
     for k in range(first_ref.shape[0]):

time: 99.3 us -> 98.4 us (level)
  no operation moved by 1% of the time
where the time goes in v13:
time: 98.4 us; the launch traced here: 98.2 us
  waiting for transfers between devices  47.5 us (48%)
  Pallas kernels  23.1 us (23%)
  starting transfers between devices  23 us (23%)
  local copies, waits for them, and re-layouts  3.65 us (4%)
    ppermute x4, waiting for transfers between devices, swap_first(): return lax.ppermute(x, ('mem', 'tile'), FIRST)  31.7 us
    ppermute x4, starting transfers between devices, swap_first(): return lax.ppermute(x, ('mem', 'tile'), FIRST)  18 us
    ppermute x4, waiting for transfers between devices, swap_second(): return lax.ppermute(x, ('mem', 'tile'), SECOND)  7.61 us
    pallas_call x1, Pallas kernels, back_part(): call(back_kernel, (sds(members, 256, 128), sds(members, 128, 128), sds(me...  5.35 us
    ppermute x1, waiting for transfers between devices, swap_chip(): return lax.ppermute(x, 'mem', [(m, m ^ 2) for m in range(MEMS)])  3.86 us
    pallas_call x1, Pallas kernels, own_part(): call(own_kernel, (sds(V, 128, 128), sds(members, 128, 128), sds(members,...  3.78 us
    unnamed x20, local copies, waits for them, and re-layouts  3.56 us
    ppermute x2, starting transfers between devices, swap_core(): return lax.ppermute(x, 'mem', [(m, m ^ 1) for m in range(MEMS)])  3.05 us
  transfers between devices with their start and end apart: 12, of which 12 were waited for; matrix products, arithmetic and copies ran while one was open for 0% of the time, Pallas kernels for 16%

profile of v13, /device:TPU:6, one launch (start us, length us, event | category | flops | bytes accessed | tf_op | source)
XLA Modules:
  0.0 98.2 jit_solution(16774458391376240876)
XLA Ops:
  0.0 2.2 %shard_map.82 = (f32[1024,128]{1,0:T(8,128)}, f32[1024,128]{1,0:T(8,128)}, f32[8,128]{1,0:T(8,128)}) custom-call(bf16[20,4,64,128]{3,2,1,0:T(8,128)(2,1)} %bitcast.16), custom_call_target="tpu_custom_call" | custom-call | flops 1000 | bytes 1000 | tf_op jit(solution)/shard_map/pallas_call | solution.py:143
  2.2 9.1 %collective-permute-start.2 = (f32[1024,128]{1,0:T(8,128)}, f32[1024,128]{1,0:T(8,128)S(1)}, u32[]{:S(2)}, u32[]{:S(2)}) collective-permute-start(f32[1024,128]{1,0:T(8,128)} %get-tuple-element.39), channel_id=1, source_target_pairs={{0,64},{1,2},{2,1},{3,4},{4,3},{5,6},{6,5},{7,8},{8,7},{9,10},{10,... | collective-permute-start | bytes 1572872 | tf_op jit(solution)/shard_map/ppermute | solution.py:567
  11.4 2.1 %copy-done.1 = bf16[20,3,8,32,128]{4,3,2,1,0:T(8,128)(2,1)S(1)} copy-done((bf16[20,3,8,32,128]{4,3,2,1,0:T(8,128)(2,1)S(1)}, bf16[20,3,8,32,128]{4,3,2,1,0:T(8,128)(2,1)}, u32[]{:S(2)}) %copy-start.1) | copy-done | bytes 3932184
  13.5 0.8 copy-done.3
  14.2 0.7 copy-done.9
  14.9 3.8 %shard_map.83 = (f32[3,128,128]{2,1,0:T(8,128)S(1)}, f32[20,128,128]{2,1,0:T(8,128)S(1)}, bf16[20,3,128,128]{3,2,1,0:T(8,128)(2,1)S(1)}, bf16[256,256]{1,0:T(8,128)(2,1)S(1)}, bf16[128,128]{1,0:T(8,128)(2,1)S(1)}) custom-call(s32[11]{0:T(128)S(1)} %stack.51.where_ref, bf16[20,256,128]{2,1,0:T(8,128)(2,1)S(1)} %bitcast.17, ...), custom_call_target="tpu_custom_call" | custom-call | flops 1000 | bytes 1000 | tf_op jit(solution)/shard_map/pallas_call | solution.py:210
  19.8 1.6 %collective-permute-start = (f32[296,128]{1,0:T(8,128)S(1)}, f32[296,128]{1,0:T(8,128)S(1)}, u32[]{:S(2)}, u32[]{:S(2)}) collective-permute-start(f32[296,128]{1,0:T(8,128)S(1)} %get-tuple-element.34), channel_id=1, source_target_pairs={{0,64},{1,2},{2,1},{3,4},{4,3},{5,6},{6,5},{7,8},{8,7},{9,10},{10,... | collective-permute-start | bytes 454664 | tf_op jit(solution)/shard_map/ppermute | solution.py:567
  21.5 1.5 %collective-permute-start.1 = (f32[296,128]{1,0:T(8,128)S(1)}, f32[296,128]{1,0:T(8,128)S(1)}, u32[]{:S(2)}, u32[]{:S(2)}) collective-permute-start(f32[296,128]{1,0:T(8,128)S(1)} %get-tuple-element.35), channel_id=1, source_target_pairs={{0,1},{1,0},{2,3},{3,2},{4,5},{5,4},{6,7},{7,6},{8,9},{9,8},{10,11... | collective-permute-start | bytes 454664 | tf_op jit(solution)/shard_map/ppermute | solution.py:571
  22.9 12.1 %collective-permute-done.2.first_ref = f32[1024,128]{1,0:T(8,128)S(1)} collective-permute-done((f32[1024,128]{1,0:T(8,128)}, f32[1024,128]{1,0:T(8,128)S(1)}, u32[]{:S(2)}, u32[]{:S(2)}) %collective-permute-start.2) | collective-permute-done | bytes 524320 | tf_op jit(solution)/shard_map/ppermute | solution.py:567
  35.1 1.6 %collective-permute-done.3.second_ref = f32[1024,128]{1,0:T(8,128)S(1)} collective-permute-done((f32[1024,128]{1,0:T(8,128)}, f32[1024,128]{1,0:T(8,128)S(1)}, u32[]{:S(2)}, u32[]{:S(2)}) %collective-permute-start.3) | collective-permute-done | bytes 524320 | tf_op jit(solution)/shard_map/ppermute | solution.py:571
  36.6 1.9 %shard_map.85.head_ref = f32[3,128,128]{2,1,0:T(8,128)S(1)} custom-call(f32[1024,128]{1,0:T(8,128)S(1)} %collective-permute-done.2.first_ref, f32[1024,128]{1,0:T(8,128)S(1)} %collective-permute-done.3.second_ref, f32[20,128,128]{2,1,0:T(8,128)S(1)} %get-tuple-element.36.own_ref, bf16[20,3,128,128]{3,2,1,0:T(8,128)(2,1)S(1)} %get-tuple-element.37.x_ref, ...), custom_call_target="tpu_custom_call" | custom-call | flops 1000 | bytes 1000 | tf_op jit(solution)/shard_map/pallas_call | solution.py:257
  38.5 1.9 %collective-permute-done.first_ref = f32[296,128]{1,0:T(8,128)S(1)} collective-permute-done((f32[296,128]{1,0:T(8,128)S(1)}, f32[296,128]{1,0:T(8,128)S(1)}, u32[]{:S(2)}, u32[]{:S(2)}) %collective-permute-start) | collective-permute-done | bytes 151584 | tf_op jit(solution)/shard_map/ppermute | solution.py:567
  40.4 3.1 %collective-permute-done.1.second_ref = f32[296,128]{1,0:T(8,128)S(1)} collective-permute-done((f32[296,128]{1,0:T(8,128)S(1)}, f32[296,128]{1,0:T(8,128)S(1)}, u32[]{:S(2)}, u32[]{:S(2)}) %collective-permute-start.1) | collective-permute-done | bytes 151584 | tf_op jit(solution)/shard_map/ppermute | solution.py:571
  43.5 1.2 %shard_map.86 = (f32[3,256,128]{2,1,0:T(8,128)S(1)}, f32[96,128]{1,0:T(8,128)S(1)}, f32[176,128]{1,0:T(8,128)S(1)}) custom-call(s32[11]{0:T(128)S(1)} %stack.51.where_ref, f32[296,128]{1,0:T(8,128)S(1)} %collective-permute-done.first_ref, f32[296,128]{1,0:T(8,128)S(1)} %collective-permute-done.1.second_ref, f32[20,128,128]{2,1,0:T(8,128)S(1)} %get-tuple-element.36.own_ref, ...), custom_call_target="tpu_custom_call" | custom-call | flops 1000 | bytes 1000 | tf_op jit(solution)/shard_map/pallas_call | solution.py:275
  44.8 1.3 %collective-permute-done.4.there_ref = f32[176,128]{1,0:T(8,128)S(1)} collective-permute-done((f32[176,128]{1,0:T(8,128)S(1)}, f32[176,128]{1,0:T(8,128)S(1)}, u32[]{:S(2)}, u32[]{:S(2)}) %collective-permute-start.4) | collective-permute-done | bytes 90144 | tf_op jit(solution)/shard_map/ppermute | solution.py:579
  46.2 1.7 %shard_map.87 = (bf16[3,320,768]{2,1,0:T(8,128)(2,1)S(1)}, bf16[2,3,64,768]{3,2,1,0:T(8,128)(2,1)S(1)}, f32[9,768]{1,0:T(8,128)S(1)}, f32[9,768]{1,0:T(8,128)S(1...) custom-call(s32[11]{0:T(128)S(1)} %stack.51.where_ref, f32[80,128]{1,0:T(8,128)S(1)} %get-tuple-element.42.own_ref, ...), custom_call_target="tpu_custom_call" | custom-call | flops 1000 | bytes 1000 | tf_op jit(solution)/shard_map/pallas_call | solution.py:338
  47.8 1.4 %shard_map.88.mine_ref = f32[9,768]{1,0:T(8,128)S(1)} custom-call(s32[11]{0:T(128)S(1)} %stack.51.where_ref, f32[3,256,128]{2,1,0:T(8,128)S(1)} %get-tuple-element.41.inc_ref, bf16[3,320,768]{2,1,0:T(8,128)(2,1)S(1)} %get-tuple-element.45.wown_ref, bf16[2,3,64,768]{3,2,1,0:T(8,128)(2,1)S(1)} %get-tuple-element.46.wnear_ref, ...), custom_call_target="tpu_custom_call" | custom-call | flops 1000 | bytes 1000 | tf_op jit(solution)/shard_map/pallas_call | solution.py:376
  49.2 2.2 %collective-permute-done.5.near_ref = f32[96,128]{1,0:T(8,128)S(1)} collective-permute-done((f32[96,128]{1,0:T(8,128)S(1)}, f32[96,128]{1,0:T(8,128)S(1)}, u32[]{:S(2)}, u32[]{:S(2)}) %collective-permute-start.5) | collective-permute-done | bytes 49184 | tf_op jit(solution)/shard_map/ppermute | solution.py:575
  51.4 1.1 %shard_map.89 = f32[54,128]{1,0:T(8,128)S(1)} custom-call(s32[11]{0:T(128)S(1)} %stack.51.where_ref, f32[9,768]{1,0:T(8,128)S(1)} %shard_map.88.mine_ref, f32[96,128]{1,0:T(8,128)S(1)} %collective-permute-done.5.near_ref, bf16[3,320,768]{2,1,0:T(8,128)(2,1)S(1)} %get-tuple-element.45.wown_ref, bf16[2,3,64,768]{3,2,1,0:T(8,128)(2,1)S(1)} %get-tuple-element.46.wnear_ref, ...), custom_call_target="tpu_custom_call" | custom-call | flops 1000 | bytes 1000 | tf_op jit(solution)/shard_map/pallas_call | solution.py:404
  52.5 3.0 %collective-permute-start.6 = (f32[54,128]{1,0:T(8,128)S(1)}, f32[54,128]{1,0:T(8,128)S(1)}, u32[]{:S(2)}, u32[]{:S(2)}) collective-permute-start(f32[54,128]{1,0:T(8,128)S(1)} %shard_map.89), channel_id=1, source_target_pairs={{0,64},{64,0},{128,192},{192,128},{1,65},{65,1},{129,193},{193,129... | collective-permute-start | bytes 82952 | tf_op jit(solution)/shard_map/ppermute | solution.py:579
  55.4 0.9 collective-permute-done.6
  56.3 3.9 %collective-permute-done.7.v1 = f32[54,128]{1,0:T(8,128)S(1)} collective-permute-done((f32[54,128]{1,0:T(8,128)S(1)}, f32[54,128]{1,0:T(8,128)S(1)}, u32[]{:S(2)}, u32[]{:S(2)}) %collective-permute-start.7) | collective-permute-done | bytes 27680 | tf_op jit(solution)/shard_map/ppermute | solution.py:583
  60.2 1.6 %shard_map.90 = (f32[3,256,128]{2,1,0:T(8,128)S(1)}, f32[12,64,128]{2,1,0:T(8,128)S(1)}, f32[12,64,128]{2,1,0:T(8,128)S(1)}) custom-call(s32[11]{0:T(128)S(1)} %stack.51.where_ref, f32[54,128]{1,0:T(8,128)S(1)} %add.31.v0, f32[54,128]{1,0:T(8,128)S(1)} %collective-permute-done.7.v1, f32[9,768]{1,0:T(8,128)S(1)} %get-tuple-element.48.innov_ref, ...), custom_call_target="tpu_custom_call" | custom-call | flops 1000 | bytes 1000 | tf_op jit(solution)/shard_map/pallas_call | solution.py:449
  61.8 4.8 %collective-permute-start.10 = (f32[12,64,128]{2,1,0:T(8,128)S(1)}, f32[12,64,128]{2,1,0:T(8,128)S(1)}, u32[]{:S(2)}, u32[]{:S(2)}) collective-permute-start(f32[12,64,128]{2,1,0:T(8,128)S(1)} %get-tuple-element.56), channel_id=1, source_target_pairs={{0,64},{1,2},{2,1},{3,4},{4,3},{5,6},{6,5},{7,8},{8,7},{9,10},{10,... | collective-permute-start | bytes 1179656 | tf_op jit(solution)/shard_map/ppermute | solution.py:567
  66.6 5.3 %shard_map.91 = (f32[20,256,128]{2,1,0:T(8,128)}, f32[20,128,128]{2,1,0:T(8,128)S(1)}, f32[8,64,128]{2,1,0:T(8,128)S(1)}, f32[8,64,128]{2,1,0:T(8,128)S(1)}) custom-call(s32[11]{0:T(128)S(1)} %stack.51.where_ref, bf16[20,256,128]{2,1,0:T(8,128)(2,1)S(1)} %bitcast.19, bf16[20,3,256,128]{3,2,1,0:T(8,128)(2,1)S(1)} %bitcast.21, ...), custom_call_target="tpu_custom_call" | custom-call | flops 1000 | bytes 1000 | tf_op jit(solution)/shard_map/pallas_call | solution.py:481
  72.0 2.4 %collective-permute-start.8 = (f32[8,64,128]{2,1,0:T(8,128)S(1)}, f32[8,64,128]{2,1,0:T(8,128)S(1)}, u32[]{:S(2)}, u32[]{:S(2)}) collective-permute-start(f32[8,64,128]{2,1,0:T(8,128)S(1)} %get-tuple-element.53), channel_id=1, source_target_pairs={{0,64},{1,2},{2,1},{3,4},{4,3},{5,6},{6,5},{7,8},{8,7},{9,10},{10,... | collective-permute-start | bytes 786440 | tf_op jit(solution)/shard_map/ppermute | solution.py:567
  74.9 11.5 %collective-permute-done.10.first_ref = f32[12,64,128]{2,1,0:T(8,128)S(1)} collective-permute-done((f32[12,64,128]{2,1,0:T(8,128)S(1)}, f32[12,64,128]{2,1,0:T(8,128)S(1)}, u32[]{:S(2)}, u32[]{:S(2)}) %collective-permute-start.10) | collective-permute-done | bytes 393248 | tf_op jit(solution)/shard_map/ppermute | solution.py:567
  86.3 1.8 %collective-permute-done.11.second_ref = f32[12,64,128]{2,1,0:T(8,128)S(1)} collective-permute-done((f32[12,64,128]{2,1,0:T(8,128)S(1)}, f32[12,64,128]{2,1,0:T(8,128)S(1)}, u32[]{:S(2)}, u32[]{:S(2)}) %collective-permute-start.11) | collective-permute-done | bytes 393248 | tf_op jit(solution)/shard_map/ppermute | solution.py:571
  88.2 1.4 %shard_map.92.unused_ref = f32[20,4,64,128]{3,2,1,0:T(8,128)} custom-call(f32[12,64,128]{2,1,0:T(8,128)S(1)} %collective-permute-done.10.first_ref, f32[12,64,128]{2,1,0:T(8,128)S(1)} %collective-permute-done.11.second_ref, f32[20,128,128]{2,1,0:T(8,128)S(1)} %get-tuple-element.55.edge_ref, ...), custom_call_target="tpu_custom_call", output_to_operand_aliasing={{}: (5, {})} | custom-call | flops 1000 | bytes 1000 | tf_op jit(solution)/shard_map/pallas_call | solution.py:529
  89.6 6.2 %collective-permute-done.8.first_ref = f32[8,64,128]{2,1,0:T(8,128)S(1)} collective-permute-done((f32[8,64,128]{2,1,0:T(8,128)S(1)}, f32[8,64,128]{2,1,0:T(8,128)S(1)}, u32[]{:S(2)}, u32[]{:S(2)}) %collective-permute-start.8) | collective-permute-done | bytes 262176 | tf_op jit(solution)/shard_map/ppermute | solution.py:567
  95.8 1.1 %collective-permute-done.9.second_ref = f32[8,64,128]{2,1,0:T(8,128)S(1)} collective-permute-done((f32[8,64,128]{2,1,0:T(8,128)S(1)}, f32[8,64,128]{2,1,0:T(8,128)S(1)}, u32[]{:S(2)}, u32[]{:S(2)}) %collective-permute-start.9) | collective-permute-done | bytes 262176 | tf_op jit(solution)/shard_map/ppermute | solution.py:571
  96.9 1.3 %shard_map.93 = f32[20,4,64,128]{3,2,1,0:T(8,128)} custom-call(f32[8,64,128]{2,1,0:T(8,128)S(1)} %collective-permute-done.8.first_ref, f32[8,64,128]{2,1,0:T(8,128)S(1)} %collective-permute-done.9.second_ref, f32[20,128,128]{2,1,0:T(8,128)S(1)} %get-tuple-element.55.edge_ref, ...), custom_call_target="tpu_custom_call", output_to_operand_aliasing={{}: (5, {})} | custom-call | flops 1000 | bytes 1000 | tf_op jit(solution)/shard_map/pallas_call | solution.py:529
  (27 shorter events, 1.2 us)
Async XLA Ops:
  0.0 11.4 %copy-start = (bf16[20,8,32,128]{3,2,1,0:T(8,128)(2,1)S(1)}, bf16[20,8,32,128]{3,2,1,0:T(8,128)(2,1)}, u32[]{:S(2)}) copy-start(bf16[20,8,32,128]{3,2,1,0:T(8,128)(2,1)} %param.8) | copy-start | bytes 3932164
  2.2 32.9 %collective-permute-start.2 = (f32[1024,128]{1,0:T(8,128)}, f32[1024,128]{1,0:T(8,128)S(1)}, u32[]{:S(2)}, u32[]{:S(2)}) collective-permute-start(f32[1024,128]{1,0:T(8,128)} %get-tuple-element.39), channel_id=1, source_target_pairs={{0,64},{1,2},{2,1},{3,4},{4,3},{5,6},{6,5},{7,8},{8,7},{9,10},{10,... | collective-permute-start | bytes 1572872 | tf_op jit(solution)/shard_map/ppermute | solution.py:567
  11.3 25.4 %collective-permute-start.3 = (f32[1024,128]{1,0:T(8,128)}, f32[1024,128]{1,0:T(8,128)S(1)}, u32[]{:S(2)}, u32[]{:S(2)}) collective-permute-start(f32[1024,128]{1,0:T(8,128)} %get-tuple-element.40), channel_id=1, source_target_pairs={{0,1},{1,0},{2,3},{3,2},{4,5},{5,4},{6,7},{7,6},{8,9},{9,8},{10,11... | collective-permute-start | bytes 1572872 | tf_op jit(solution)/shard_map/ppermute | solution.py:571
  11.4 2.1 %copy-start.1 = (bf16[20,3,8,32,128]{4,3,2,1,0:T(8,128)(2,1)S(1)}, bf16[20,3,8,32,128]{4,3,2,1,0:T(8,128)(2,1)}, u32[]{:S(2)}) copy-start(bf16[20,3,8,32,128]{4,3,2,1,0:T(8,128)(2,1)} %param.9) | copy-start | bytes 11796484
  13.5 0.8 copy-start.3
  14.2 0.7 copy-start.9
  14.9 4.5 %copy-start.5 = (s32[1,2048]{1,0:T(1,128)S(1)}, s32[1,2048]{1,0:T(1,128)}, u32[]{:S(2)}) copy-start(s32[1,2048]{1,0:T(1,128)} %col_ref.1) | copy-start | bytes 24580
  14.9 4.5 %copy-start.6 = (s32[1,2048]{1,0:T(1,128)S(1)}, s32[1,2048]{1,0:T(1,128)}, u32[]{:S(2)}) copy-start(s32[1,2048]{1,0:T(1,128)} %lev_ref.1) | copy-start | bytes 24580
  14.9 4.5 %copy-start.7 = (f32[1,2048]{1,0:T(1,128)S(1)}, f32[1,2048]{1,0:T(1,128)}, u32[]{:S(2)}) copy-start(f32[1,2048]{1,0:T(1,128)} %innov_ref.1) | copy-start | bytes 24580
  14.9 4.5 %copy-start.8 = (f32[1,2048]{1,0:T(1,128)S(1)}, f32[1,2048]{1,0:T(1,128)}, u32[]{:S(2)}) copy-start(f32[1,2048]{1,0:T(1,128)} %weight_ref.1) | copy-start | bytes 24580
  19.8 20.6 %collective-permute-start = (f32[296,128]{1,0:T(8,128)S(1)}, f32[296,128]{1,0:T(8,128)S(1)}, u32[]{:S(2)}, u32[]{:S(2)}) collective-permute-start(f32[296,128]{1,0:T(8,128)S(1)} %get-tuple-element.34), channel_id=1, source_target_pairs={{0,64},{1,2},{2,1},{3,4},{4,3},{5,6},{6,5},{7,8},{8,7},{9,10},{10,... | collective-permute-start | bytes 454664 | tf_op jit(solution)/shard_map/ppermute | solution.py:567
  21.5 22.1 %collective-permute-start.1 = (f32[296,128]{1,0:T(8,128)S(1)}, f32[296,128]{1,0:T(8,128)S(1)}, u32[]{:S(2)}, u32[]{:S(2)}) collective-permute-start(f32[296,128]{1,0:T(8,128)S(1)} %get-tuple-element.35), channel_id=1, source_target_pairs={{0,1},{1,0},{2,3},{3,2},{4,5},{5,4},{6,7},{7,6},{8,9},{9,8},{10,11... | collective-permute-start | bytes 454664 | tf_op jit(solution)/shard_map/ppermute | solution.py:571
  44.7 1.4 %collective-permute-start.4 = (f32[176,128]{1,0:T(8,128)S(1)}, f32[176,128]{1,0:T(8,128)S(1)}, u32[]{:S(2)}, u32[]{:S(2)}) collective-permute-start(f32[176,128]{1,0:T(8,128)S(1)} %get-tuple-element.43.here_ref), channel_id=1, source_target_pairs={{0,64},{64,0},{128,192},{192,128},{1,65},{65,1},{129,193},{193,129... | collective-permute-start | bytes 270344 | tf_op jit(solution)/shard_map/ppermute | solution.py:579
  46.1 5.3 %collective-permute-start.5 = (f32[96,128]{1,0:T(8,128)S(1)}, f32[96,128]{1,0:T(8,128)S(1)}, u32[]{:S(2)}, u32[]{:S(2)}) collective-permute-start(f32[96,128]{1,0:T(8,128)S(1)} %slice_add_fusion.after_ref), channel_id=1, source_target_pairs={{0,1},{1,0},{2,3},{3,2},{4,5},{5,4},{6,7},{7,6},{8,9},{9,8},{10,11... | collective-permute-start | bytes 147464 | tf_op jit(solution)/shard_map/ppermute | solution.py:575
  52.5 3.8 %collective-permute-start.6 = (f32[54,128]{1,0:T(8,128)S(1)}, f32[54,128]{1,0:T(8,128)S(1)}, u32[]{:S(2)}, u32[]{:S(2)}) collective-permute-start(f32[54,128]{1,0:T(8,128)S(1)} %shard_map.89), channel_id=1, source_target_pairs={{0,64},{64,0},{128,192},{192,128},{1,65},{65,1},{129,193},{193,129... | collective-permute-start | bytes 82952 | tf_op jit(solution)/shard_map/ppermute | solution.py:579
  56.3 3.9 %collective-permute-start.7 = (f32[54,128]{1,0:T(8,128)S(1)}, f32[54,128]{1,0:T(8,128)S(1)}, u32[]{:S(2)}, u32[]{:S(2)}) collective-permute-start(f32[54,128]{1,0:T(8,128)S(1)} %add.31.v0), channel_id=1, source_target_pairs={{0,128},{64,192},{128,0},{192,64},{1,129},{65,193},{129,1},{193,65... | collective-permute-start | bytes 82952 | tf_op jit(solution)/shard_map/ppermute | solution.py:583
  60.2 6.4 %copy-start.2 = (bf16[20,3,8,32,128]{4,3,2,1,0:T(8,128)(2,1)S(1)}, bf16[20,3,8,32,128]{4,3,2,1,0:T(8,128)(2,1)}, u32[]{:S(2)}) copy-start(bf16[20,3,8,32,128]{4,3,2,1,0:T(8,128)(2,1)} %param.9) | copy-start | bytes 11796484
  60.2 6.4 %copy-start.4 = (bf16[128,128]{1,0:T(8,128)(2,1)S(1)}, bf16[128,128]{1,0:T(8,128)(2,1)}, u32[]{:S(2)}) copy-start(bf16[128,128]{1,0:T(8,128)(2,1)} %loc_ref.11) | copy-start | bytes 98308
  61.8 24.5 %collective-permute-start.10 = (f32[12,64,128]{2,1,0:T(8,128)S(1)}, f32[12,64,128]{2,1,0:T(8,128)S(1)}, u32[]{:S(2)}, u32[]{:S(2)}) collective-permute-start(f32[12,64,128]{2,1,0:T(8,128)S(1)} %get-tuple-element.56), channel_id=1, source_target_pairs={{0,64},{1,2},{2,1},{3,4},{4,3},{5,6},{6,5},{7,8},{8,7},{9,10},{10,... | collective-permute-start | bytes 1179656 | tf_op jit(solution)/shard_map/ppermute | solution.py:567
  66.6 21.6 %collective-permute-start.11 = (f32[12,64,128]{2,1,0:T(8,128)S(1)}, f32[12,64,128]{2,1,0:T(8,128)S(1)}, u32[]{:S(2)}, u32[]{:S(2)}) collective-permute-start(f32[12,64,128]{2,1,0:T(8,128)S(1)} %get-tuple-element.57), channel_id=1, source_target_pairs={{0,1},{1,0},{2,3},{3,2},{4,5},{5,4},{6,7},{7,6},{8,9},{9,8},{10,11... | collective-permute-start | bytes 1179656 | tf_op jit(solution)/shard_map/ppermute | solution.py:571
  72.0 23.8 %collective-permute-start.8 = (f32[8,64,128]{2,1,0:T(8,128)S(1)}, f32[8,64,128]{2,1,0:T(8,128)S(1)}, u32[]{:S(2)}, u32[]{:S(2)}) collective-permute-start(f32[8,64,128]{2,1,0:T(8,128)S(1)} %get-tuple-element.53), channel_id=1, source_target_pairs={{0,64},{1,2},{2,1},{3,4},{4,3},{5,6},{6,5},{7,8},{8,7},{9,10},{10,... | collective-permute-start | bytes 786440 | tf_op jit(solution)/shard_map/ppermute | solution.py:567
  74.4 22.5 %collective-permute-start.9 = (f32[8,64,128]{2,1,0:T(8,128)S(1)}, f32[8,64,128]{2,1,0:T(8,128)S(1)}, u32[]{:S(2)}, u32[]{:S(2)}) collective-permute-start(f32[8,64,128]{2,1,0:T(8,128)S(1)} %get-tuple-element.54), channel_id=1, source_target_pairs={{0,1},{1,0},{2,3},{3,2},{4,5},{5,4},{6,7},{7,6},{8,9},{9,8},{10,11... | collective-permute-start | bytes 786440 | tf_op jit(solution)/shard_map/ppermute | solution.py:571

commit v14 on v13

--- a/solution.py
+++ b/solution.py
@@ -13,7 +13,7 @@
 SLOTS = 768
 GROUP = 4
 HEAD = 16
-HEAD_BACK = 12
+HEAD_BACK = 16
 OBS = 80
 HALF = OBS // 2
 
@@ -381,9 +381,14 @@
     )(where, inc, wown, wnear, lev)
 
 
-def values_kernel(where_ref, mine_ref, near_ref, wown_ref, wnear_ref, lev_ref, out_ref):
-    pick = picker(lev_ref)
+def values_kernel(where_ref, mine_ref, near_ref, wown_ref, wnear_ref, hot_ref, out_ref):
     core = where_ref[10]
+
+    def pick(cells, weight, row):
+        both = jnp.concatenate(halves(cells), axis=0)
+        at_level = nn(both, hot_ref[row])
+        at_level = at_level[:32] + at_level[32:]
+        return jnp.sum(weight.astype(F32) * at_level, axis=0, keepdims=True)
 
     def put(row, line):
         for a in range(6):
@@ -400,13 +405,13 @@
         put(row, mine_ref[pl.ds(row, 1)] + pick(near_ref[32 * v : 32 * v + 32], wnear_ref[core, v, 32:], row))
 
 
-def values(where, mine, near, wown, wnear, lev):
+def values(where, mine, near, wown, wnear, hot):
     return call(
         values_kernel,
         sds(9 * SLOTS // 128, 128),
         ins=[SMEM] + [VMEM] * 5,
         outs=VMEM,
-    )(where, mine, near, wown, wnear, lev)
+    )(where, mine, near, wown, wnear, hot)
 
 
 def adjoint_kernel(where_ref, v0, v1, innov_ref, weight_ref, hot_ref, wown_ref, wnear_ref, x_ref, c_ref, first_ref, second_ref):
@@ -623,7 +628,7 @@
     near = swap_near(edges)
     wown, wnear, lev, innov, weight, hot = weights(where, own_obs, give, got, edges)
     mine = mine_part(where, inc, wown, wnear, lev)
-    vals = values(where, mine, near, wown, wnear, lev)
+    vals = values(where, mine, near, wown, wnear, hot)
     vals = vals + swap_core(vals)
     vals = vals, swap_chip(vals)
     c, back_first, back_second = adjoint(where, vals, innov, weight, hot, wown, wnear, x)

time: 98.4 us -> 98.1 us (level)
    ppermute x4, waiting for transfers between devices: 7.61 us -> 5.79 us  [swap_second(): return lax.ppermute(x, ('mem', 'tile'), SECOND)]
    ppermute x4, waiting for transfers between devices: 31.7 us -> 33.4 us  [swap_first(): return lax.ppermute(x, ('mem', 'tile'), FIRST)]
  transfers between devices with their start and end apart: 12 -> 12, of which waited for: 12 -> 11; matrix products, arithmetic and copies ran while one was open for 0% -> 0% of each run, Pallas kernels for 16% -> 16%
where the time goes in v14:
time: 98.1 us; the launch traced here: 97.9 us
  waiting for transfers between devices  47.4 us (48%)
  starting transfers between devices  23.1 us (24%)
  Pallas kernels  23 us (23%)
  local copies, waits for them, and re-layouts  3.65 us (4%)
    ppermute x4, waiting for transfers between devices, swap_first(): return lax.ppermute(x, ('mem', 'tile'), FIRST)  33.4 us
    ppermute x4, starting transfers between devices, swap_first(): return lax.ppermute(x, ('mem', 'tile'), FIRST)  18 us
    ppermute x4, waiting for transfers between devices, swap_second(): return lax.ppermute(x, ('mem', 'tile'), SECOND)  5.79 us
    pallas_call x1, Pallas kernels, back_part(): call(back_kernel, (sds(members, 256, 128), sds(members, 128, 128), sds(me...  5.3 us
    ppermute x1, waiting for transfers between devices, swap_chip(): return lax.ppermute(x, 'mem', [(m, m ^ 2) for m in range(MEMS)])  3.86 us
    pallas_call x1, Pallas kernels, own_part(): call(own_kernel, (sds(V, 128, 128), sds(members, 128, 128), sds(members,...  3.79 us
    unnamed x20, local copies, waits for them, and re-layouts  3.56 us
    ppermute x2, starting transfers between devices, swap_core(): return lax.ppermute(x, 'mem', [(m, m ^ 1) for m in range(MEMS)])  3.06 us
  transfers between devices with their start and end apart: 12, of which 11 were waited for; matrix products, arithmetic and copies ran while one was open for 0% of the time, Pallas kernels for 16%

profile of v14, /device:TPU:6, one launch (start us, length us, event | category | flops | bytes accessed | tf_op | source)
XLA Modules:
  0.0 97.9 jit_solution(3568877434751970886)
XLA Ops:
  0.0 2.2 %shard_map.82 = (f32[1024,128]{1,0:T(8,128)}, f32[1024,128]{1,0:T(8,128)}, f32[8,128]{1,0:T(8,128)}) custom-call(bf16[20,4,64,128]{3,2,1,0:T(8,128)(2,1)} %bitcast.16), custom_call_target="tpu_custom_call" | custom-call | flops 1000 | bytes 1000 | tf_op jit(solution)/shard_map/pallas_call | solution.py:143
  2.2 9.1 %collective-permute-start.2 = (f32[1024,128]{1,0:T(8,128)}, f32[1024,128]{1,0:T(8,128)S(1)}, u32[]{:S(2)}, u32[]{:S(2)}) collective-permute-start(f32[1024,128]{1,0:T(8,128)} %get-tuple-element.39), channel_id=1, source_target_pairs={{0,64},{1,2},{2,1},{3,4},{4,3},{5,6},{6,5},{7,8},{8,7},{9,10},{10,... | collective-permute-start | bytes 1572872 | tf_op jit(solution)/shard_map/ppermute | solution.py:572
  11.4 2.1 %copy-done.1 = bf16[20,3,8,32,128]{4,3,2,1,0:T(8,128)(2,1)S(1)} copy-done((bf16[20,3,8,32,128]{4,3,2,1,0:T(8,128)(2,1)S(1)}, bf16[20,3,8,32,128]{4,3,2,1,0:T(8,128)(2,1)}, u32[]{:S(2)}) %copy-start.1) | copy-done | bytes 3932184
  13.5 0.8 copy-done.3
  14.2 0.7 copy-done.9
  14.9 3.8 %shard_map.83 = (f32[3,128,128]{2,1,0:T(8,128)S(1)}, f32[20,128,128]{2,1,0:T(8,128)S(1)}, bf16[20,3,128,128]{3,2,1,0:T(8,128)(2,1)S(1)}, bf16[256,256]{1,0:T(8,128)(2,1)S(1)}, bf16[128,128]{1,0:T(8,128)(2,1)S(1)}) custom-call(s32[11]{0:T(128)S(1)} %stack.51.where_ref, bf16[20,256,128]{2,1,0:T(8,128)(2,1)S(1)} %bitcast.17, ...), custom_call_target="tpu_custom_call" | custom-call | flops 1000 | bytes 1000 | tf_op jit(solution)/shard_map/pallas_call | solution.py:210
  19.8 1.6 %collective-permute-start = (f32[296,128]{1,0:T(8,128)S(1)}, f32[296,128]{1,0:T(8,128)S(1)}, u32[]{:S(2)}, u32[]{:S(2)}) collective-permute-start(f32[296,128]{1,0:T(8,128)S(1)} %get-tuple-element.34), channel_id=1, source_target_pairs={{0,64},{1,2},{2,1},{3,4},{4,3},{5,6},{6,5},{7,8},{8,7},{9,10},{10,... | collective-permute-start | bytes 454664 | tf_op jit(solution)/shard_map/ppermute | solution.py:572
  21.5 1.5 %collective-permute-start.1 = (f32[296,128]{1,0:T(8,128)S(1)}, f32[296,128]{1,0:T(8,128)S(1)}, u32[]{:S(2)}, u32[]{:S(2)}) collective-permute-start(f32[296,128]{1,0:T(8,128)S(1)} %get-tuple-element.35), channel_id=1, source_target_pairs={{0,1},{1,0},{2,3},{3,2},{4,5},{5,4},{6,7},{7,6},{8,9},{9,8},{10,11... | collective-permute-start | bytes 454664 | tf_op jit(solution)/shard_map/ppermute | solution.py:576
  22.9 12.1 %collective-permute-done.2.first_ref = f32[1024,128]{1,0:T(8,128)S(1)} collective-permute-done((f32[1024,128]{1,0:T(8,128)}, f32[1024,128]{1,0:T(8,128)S(1)}, u32[]{:S(2)}, u32[]{:S(2)}) %collective-permute-start.2) | collective-permute-done | bytes 524320 | tf_op jit(solution)/shard_map/ppermute | solution.py:572
  35.0 1.6 %collective-permute-done.3.second_ref = f32[1024,128]{1,0:T(8,128)S(1)} collective-permute-done((f32[1024,128]{1,0:T(8,128)}, f32[1024,128]{1,0:T(8,128)S(1)}, u32[]{:S(2)}, u32[]{:S(2)}) %collective-permute-start.3) | collective-permute-done | bytes 524320 | tf_op jit(solution)/shard_map/ppermute | solution.py:576
  36.6 1.9 %shard_map.85.head_ref = f32[3,128,128]{2,1,0:T(8,128)S(1)} custom-call(f32[1024,128]{1,0:T(8,128)S(1)} %collective-permute-done.2.first_ref, f32[1024,128]{1,0:T(8,128)S(1)} %collective-permute-done.3.second_ref, f32[20,128,128]{2,1,0:T(8,128)S(1)} %get-tuple-element.36.own_ref, bf16[20,3,128,128]{3,2,1,0:T(8,128)(2,1)S(1)} %get-tuple-element.37.x_ref, ...), custom_call_target="tpu_custom_call" | custom-call | flops 1000 | bytes 1000 | tf_op jit(solution)/shard_map/pallas_call | solution.py:257
  38.5 1.9 %collective-permute-done.first_ref = f32[296,128]{1,0:T(8,128)S(1)} collective-permute-done((f32[296,128]{1,0:T(8,128)S(1)}, f32[296,128]{1,0:T(8,128)S(1)}, u32[]{:S(2)}, u32[]{:S(2)}) %collective-permute-start) | collective-permute-done | bytes 151584 | tf_op jit(solution)/shard_map/ppermute | solution.py:572
  40.4 3.1 %collective-permute-done.1.second_ref = f32[296,128]{1,0:T(8,128)S(1)} collective-permute-done((f32[296,128]{1,0:T(8,128)S(1)}, f32[296,128]{1,0:T(8,128)S(1)}, u32[]{:S(2)}, u32[]{:S(2)}) %collective-permute-start.1) | collective-permute-done | bytes 151584 | tf_op jit(solution)/shard_map/ppermute | solution.py:576
  43.5 1.2 %shard_map.86 = (f32[3,256,128]{2,1,0:T(8,128)S(1)}, f32[96,128]{1,0:T(8,128)S(1)}, f32[176,128]{1,0:T(8,128)S(1)}) custom-call(s32[11]{0:T(128)S(1)} %stack.51.where_ref, f32[296,128]{1,0:T(8,128)S(1)} %collective-permute-done.first_ref, f32[296,128]{1,0:T(8,128)S(1)} %collective-permute-done.1.second_ref, f32[20,128,128]{2,1,0:T(8,128)S(1)} %get-tuple-element.36.own_ref, ...), custom_call_target="tpu_custom_call" | custom-call | flops 1000 | bytes 1000 | tf_op jit(solution)/shard_map/pallas_call | solution.py:275
  44.8 1.3 %collective-permute-done.4.there_ref = f32[176,128]{1,0:T(8,128)S(1)} collective-permute-done((f32[176,128]{1,0:T(8,128)S(1)}, f32[176,128]{1,0:T(8,128)S(1)}, u32[]{:S(2)}, u32[]{:S(2)}) %collective-permute-start.4) | collective-permute-done | bytes 90144 | tf_op jit(solution)/shard_map/ppermute | solution.py:584
  46.2 1.7 %shard_map.87 = (bf16[3,320,768]{2,1,0:T(8,128)(2,1)S(1)}, bf16[2,3,64,768]{3,2,1,0:T(8,128)(2,1)S(1)}, f32[9,768]{1,0:T(8,128)S(1)}, f32[9,768]{1,0:T(8,128)S(1...) custom-call(s32[11]{0:T(128)S(1)} %stack.51.where_ref, f32[80,128]{1,0:T(8,128)S(1)} %get-tuple-element.42.own_ref, ...), custom_call_target="tpu_custom_call" | custom-call | flops 1000 | bytes 1000 | tf_op jit(solution)/shard_map/pallas_call | solution.py:338
  47.8 1.4 %shard_map.88.mine_ref = f32[9,768]{1,0:T(8,128)S(1)} custom-call(s32[11]{0:T(128)S(1)} %stack.51.where_ref, f32[3,256,128]{2,1,0:T(8,128)S(1)} %get-tuple-element.41.inc_ref, bf16[3,320,768]{2,1,0:T(8,128)(2,1)S(1)} %get-tuple-element.45.wown_ref, bf16[2,3,64,768]{3,2,1,0:T(8,128)(2,1)S(1)} %get-tuple-element.46.wnear_ref, ...), custom_call_target="tpu_custom_call" | custom-call | flops 1000 | bytes 1000 | tf_op jit(solution)/shard_map/pallas_call | solution.py:376
  49.2 2.2 %collective-permute-done.5.near_ref = f32[96,128]{1,0:T(8,128)S(1)} collective-permute-done((f32[96,128]{1,0:T(8,128)S(1)}, f32[96,128]{1,0:T(8,128)S(1)}, u32[]{:S(2)}, u32[]{:S(2)}) %collective-permute-start.5) | collective-permute-done | bytes 49184 | tf_op jit(solution)/shard_map/ppermute | solution.py:580
  51.4 0.9 shard_map.89
  52.3 3.0 %collective-permute-start.6 = (f32[54,128]{1,0:T(8,128)S(1)}, f32[54,128]{1,0:T(8,128)S(1)}, u32[]{:S(2)}, u32[]{:S(2)}) collective-permute-start(f32[54,128]{1,0:T(8,128)S(1)} %shard_map.89), channel_id=1, source_target_pairs={{0,64},{64,0},{128,192},{192,128},{1,65},{65,1},{129,193},{193,129... | collective-permute-start | bytes 82952 | tf_op jit(solution)/shard_map/ppermute | solution.py:584
  55.3 0.9 collective-permute-done.6
  56.1 3.9 %collective-permute-done.7.v1 = f32[54,128]{1,0:T(8,128)S(1)} collective-permute-done((f32[54,128]{1,0:T(8,128)S(1)}, f32[54,128]{1,0:T(8,128)S(1)}, u32[]{:S(2)}, u32[]{:S(2)}) %collective-permute-start.7) | collective-permute-done | bytes 27680 | tf_op jit(solution)/shard_map/ppermute | solution.py:588
  60.0 1.7 %shard_map.90 = (f32[3,256,128]{2,1,0:T(8,128)S(1)}, f32[16,64,128]{2,1,0:T(8,128)S(1)}, f32[16,64,128]{2,1,0:T(8,128)S(1)}) custom-call(s32[11]{0:T(128)S(1)} %stack.51.where_ref, f32[54,128]{1,0:T(8,128)S(1)} %add.31.v0, f32[54,128]{1,0:T(8,128)S(1)} %collective-permute-done.7.v1, f32[9,768]{1,0:T(8,128)S(1)} %get-tuple-element.49.innov_ref, ...), custom_call_target="tpu_custom_call" | custom-call | flops 1000 | bytes 1000 | tf_op jit(solution)/shard_map/pallas_call | solution.py:454
  61.7 4.8 %collective-permute-start.10 = (f32[16,64,128]{2,1,0:T(8,128)S(1)}, f32[16,64,128]{2,1,0:T(8,128)S(1)}, u32[]{:S(2)}, u32[]{:S(2)}) collective-permute-start(f32[16,64,128]{2,1,0:T(8,128)S(1)} %get-tuple-element.56), channel_id=1, source_target_pairs={{0,64},{1,2},{2,1},{3,4},{4,3},{5,6},{6,5},{7,8},{8,7},{9,10},{10,... | collective-permute-start | bytes 1572872 | tf_op jit(solution)/shard_map/ppermute | solution.py:572
  66.5 5.3 %shard_map.91 = (f32[20,256,128]{2,1,0:T(8,128)}, f32[20,128,128]{2,1,0:T(8,128)S(1)}, f32[4,64,128]{2,1,0:T(8,128)S(1)}, f32[4,64,128]{2,1,0:T(8,128)S(1)}) custom-call(s32[11]{0:T(128)S(1)} %stack.51.where_ref, bf16[20,256,128]{2,1,0:T(8,128)(2,1)S(1)} %bitcast.19, bf16[20,3,256,128]{3,2,1,0:T(8,128)(2,1)S(1)} %bitcast.21, ...), custom_call_target="tpu_custom_call" | custom-call | flops 1000 | bytes 1000 | tf_op jit(solution)/shard_map/pallas_call | solution.py:486
  71.8 2.4 %collective-permute-start.8 = (f32[4,64,128]{2,1,0:T(8,128)S(1)}, f32[4,64,128]{2,1,0:T(8,128)S(1)}, u32[]{:S(2)}, u32[]{:S(2)}) collective-permute-start(f32[4,64,128]{2,1,0:T(8,128)S(1)} %get-tuple-element.53), channel_id=1, source_target_pairs={{0,64},{1,2},{2,1},{3,4},{4,3},{5,6},{6,5},{7,8},{8,7},{9,10},{10,... | collective-permute-start | bytes 393224 | tf_op jit(solution)/shard_map/ppermute | solution.py:572
  74.2 0.5 collective-permute-start.9
  74.7 17.2 %collective-permute-done.10.first_ref = f32[16,64,128]{2,1,0:T(8,128)S(1)} collective-permute-done((f32[16,64,128]{2,1,0:T(8,128)S(1)}, f32[16,64,128]{2,1,0:T(8,128)S(1)}, u32[]{:S(2)}, u32[]{:S(2)}) %collective-permute-start.10) | collective-permute-done | bytes 524320 | tf_op jit(solution)/shard_map/ppermute | solution.py:572
  91.9 1.6 %shard_map.92.unused_ref = f32[20,4,64,128]{3,2,1,0:T(8,128)} custom-call(f32[16,64,128]{2,1,0:T(8,128)S(1)} %collective-permute-done.10.first_ref, f32[16,64,128]{2,1,0:T(8,128)S(1)} %collective-permute-done.11.second_ref, f32[20,128,128]{2,1,0:T(8,128)S(1)} %get-tuple-element.55.edge_ref, ...), custom_call_target="tpu_custom_call", output_to_operand_aliasing={{}: (5, {})} | custom-call | flops 1000 | bytes 1000 | tf_op jit(solution)/shard_map/pallas_call | solution.py:534
  93.5 2.2 %collective-permute-done.8.first_ref = f32[4,64,128]{2,1,0:T(8,128)S(1)} collective-permute-done((f32[4,64,128]{2,1,0:T(8,128)S(1)}, f32[4,64,128]{2,1,0:T(8,128)S(1)}, u32[]{:S(2)}, u32[]{:S(2)}) %collective-permute-start.8) | collective-permute-done | bytes 131104 | tf_op jit(solution)/shard_map/ppermute | solution.py:572
  95.7 1.1 %collective-permute-done.9.second_ref = f32[4,64,128]{2,1,0:T(8,128)S(1)} collective-permute-done((f32[4,64,128]{2,1,0:T(8,128)S(1)}, f32[4,64,128]{2,1,0:T(8,128)S(1)}, u32[]{:S(2)}, u32[]{:S(2)}) %collective-permute-start.9) | collective-permute-done | bytes 131104 | tf_op jit(solution)/shard_map/ppermute | solution.py:576
  96.7 1.1 %shard_map.93 = f32[20,4,64,128]{3,2,1,0:T(8,128)} custom-call(f32[4,64,128]{2,1,0:T(8,128)S(1)} %collective-permute-done.8.first_ref, f32[4,64,128]{2,1,0:T(8,128)S(1)} %collective-permute-done.9.second_ref, f32[20,128,128]{2,1,0:T(8,128)S(1)} %get-tuple-element.55.edge_ref, ...), custom_call_target="tpu_custom_call", output_to_operand_aliasing={{}: (5, {})} | custom-call | flops 1000 | bytes 1000 | tf_op jit(solution)/shard_map/pallas_call | solution.py:534
  (27 shorter events, 0.7 us)
Async XLA Ops:
  0.0 11.4 %copy-start = (bf16[20,8,32,128]{3,2,1,0:T(8,128)(2,1)S(1)}, bf16[20,8,32,128]{3,2,1,0:T(8,128)(2,1)}, u32[]{:S(2)}) copy-start(bf16[20,8,32,128]{3,2,1,0:T(8,128)(2,1)} %param.8) | copy-start | bytes 3932164
  2.2 32.9 %collective-permute-start.2 = (f32[1024,128]{1,0:T(8,128)}, f32[1024,128]{1,0:T(8,128)S(1)}, u32[]{:S(2)}, u32[]{:S(2)}) collective-permute-start(f32[1024,128]{1,0:T(8,128)} %get-tuple-element.39), channel_id=1, source_target_pairs={{0,64},{1,2},{2,1},{3,4},{4,3},{5,6},{6,5},{7,8},{8,7},{9,10},{10,... | collective-permute-start | bytes 1572872 | tf_op jit(solution)/shard_map/ppermute | solution.py:572
  11.3 25.4 %collective-permute-start.3 = (f32[1024,128]{1,0:T(8,128)}, f32[1024,128]{1,0:T(8,128)S(1)}, u32[]{:S(2)}, u32[]{:S(2)}) collective-permute-start(f32[1024,128]{1,0:T(8,128)} %get-tuple-element.40), channel_id=1, source_target_pairs={{0,1},{1,0},{2,3},{3,2},{4,5},{5,4},{6,7},{7,6},{8,9},{9,8},{10,11... | collective-permute-start | bytes 1572872 | tf_op jit(solution)/shard_map/ppermute | solution.py:576
  11.4 2.1 %copy-start.1 = (bf16[20,3,8,32,128]{4,3,2,1,0:T(8,128)(2,1)S(1)}, bf16[20,3,8,32,128]{4,3,2,1,0:T(8,128)(2,1)}, u32[]{:S(2)}) copy-start(bf16[20,3,8,32,128]{4,3,2,1,0:T(8,128)(2,1)} %param.9) | copy-start | bytes 11796484
  13.5 0.8 copy-start.3
  14.2 0.7 copy-start.9
  14.9 4.5 %copy-start.5 = (s32[1,2048]{1,0:T(1,128)S(1)}, s32[1,2048]{1,0:T(1,128)}, u32[]{:S(2)}) copy-start(s32[1,2048]{1,0:T(1,128)} %col_ref.1) | copy-start | bytes 24580
  14.9 4.5 %copy-start.6 = (s32[1,2048]{1,0:T(1,128)S(1)}, s32[1,2048]{1,0:T(1,128)}, u32[]{:S(2)}) copy-start(s32[1,2048]{1,0:T(1,128)} %lev_ref.1) | copy-start | bytes 24580
  14.9 4.5 %copy-start.7 = (f32[1,2048]{1,0:T(1,128)S(1)}, f32[1,2048]{1,0:T(1,128)}, u32[]{:S(2)}) copy-start(f32[1,2048]{1,0:T(1,128)} %innov_ref.1) | copy-start | bytes 24580
  14.9 4.5 %copy-start.8 = (f32[1,2048]{1,0:T(1,128)S(1)}, f32[1,2048]{1,0:T(1,128)}, u32[]{:S(2)}) copy-start(f32[1,2048]{1,0:T(1,128)} %weight_ref.1) | copy-start | bytes 24580
  19.8 20.6 %collective-permute-start = (f32[296,128]{1,0:T(8,128)S(1)}, f32[296,128]{1,0:T(8,128)S(1)}, u32[]{:S(2)}, u32[]{:S(2)}) collective-permute-start(f32[296,128]{1,0:T(8,128)S(1)} %get-tuple-element.34), channel_id=1, source_target_pairs={{0,64},{1,2},{2,1},{3,4},{4,3},{5,6},{6,5},{7,8},{8,7},{9,10},{10,... | collective-permute-start | bytes 454664 | tf_op jit(solution)/shard_map/ppermute | solution.py:572
  21.5 22.1 %collective-permute-start.1 = (f32[296,128]{1,0:T(8,128)S(1)}, f32[296,128]{1,0:T(8,128)S(1)}, u32[]{:S(2)}, u32[]{:S(2)}) collective-permute-start(f32[296,128]{1,0:T(8,128)S(1)} %get-tuple-element.35), channel_id=1, source_target_pairs={{0,1},{1,0},{2,3},{3,2},{4,5},{5,4},{6,7},{7,6},{8,9},{9,8},{10,11... | collective-permute-start | bytes 454664 | tf_op jit(solution)/shard_map/ppermute | solution.py:576
  44.7 1.4 %collective-permute-start.4 = (f32[176,128]{1,0:T(8,128)S(1)}, f32[176,128]{1,0:T(8,128)S(1)}, u32[]{:S(2)}, u32[]{:S(2)}) collective-permute-start(f32[176,128]{1,0:T(8,128)S(1)} %get-tuple-element.43.here_ref), channel_id=1, source_target_pairs={{0,64},{64,0},{128,192},{192,128},{1,65},{65,1},{129,193},{193,129... | collective-permute-start | bytes 270344 | tf_op jit(solution)/shard_map/ppermute | solution.py:584
  46.1 5.3 %collective-permute-start.5 = (f32[96,128]{1,0:T(8,128)S(1)}, f32[96,128]{1,0:T(8,128)S(1)}, u32[]{:S(2)}, u32[]{:S(2)}) collective-permute-start(f32[96,128]{1,0:T(8,128)S(1)} %slice_add_fusion.after_ref), channel_id=1, source_target_pairs={{0,1},{1,0},{2,3},{3,2},{4,5},{5,4},{6,7},{7,6},{8,9},{9,8},{10,11... | collective-permute-start | bytes 147464 | tf_op jit(solution)/shard_map/ppermute | solution.py:580
  52.3 3.8 %collective-permute-start.6 = (f32[54,128]{1,0:T(8,128)S(1)}, f32[54,128]{1,0:T(8,128)S(1)}, u32[]{:S(2)}, u32[]{:S(2)}) collective-permute-start(f32[54,128]{1,0:T(8,128)S(1)} %shard_map.89), channel_id=1, source_target_pairs={{0,64},{64,0},{128,192},{192,128},{1,65},{65,1},{129,193},{193,129... | collective-permute-start | bytes 82952 | tf_op jit(solution)/shard_map/ppermute | solution.py:584
  56.1 3.9 %collective-permute-start.7 = (f32[54,128]{1,0:T(8,128)S(1)}, f32[54,128]{1,0:T(8,128)S(1)}, u32[]{:S(2)}, u32[]{:S(2)}) collective-permute-start(f32[54,128]{1,0:T(8,128)S(1)} %add.31.v0), channel_id=1, source_target_pairs={{0,128},{64,192},{128,0},{192,64},{1,129},{65,193},{129,1},{193,65... | collective-permute-start | bytes 82952 | tf_op jit(solution)/shard_map/ppermute | solution.py:588
  60.0 6.5 %copy-start.2 = (bf16[20,3,8,32,128]{4,3,2,1,0:T(8,128)(2,1)S(1)}, bf16[20,3,8,32,128]{4,3,2,1,0:T(8,128)(2,1)}, u32[]{:S(2)}) copy-start(bf16[20,3,8,32,128]{4,3,2,1,0:T(8,128)(2,1)} %param.9) | copy-start | bytes 11796484
  60.0 6.5 %copy-start.4 = (bf16[128,128]{1,0:T(8,128)(2,1)S(1)}, bf16[128,128]{1,0:T(8,128)(2,1)}, u32[]{:S(2)}) copy-start(bf16[128,128]{1,0:T(8,128)(2,1)} %loc_ref.11) | copy-start | bytes 98308
  61.7 30.2 %collective-permute-start.10 = (f32[16,64,128]{2,1,0:T(8,128)S(1)}, f32[16,64,128]{2,1,0:T(8,128)S(1)}, u32[]{:S(2)}, u32[]{:S(2)}) collective-permute-start(f32[16,64,128]{2,1,0:T(8,128)S(1)} %get-tuple-element.56), channel_id=1, source_target_pairs={{0,64},{1,2},{2,1},{3,4},{4,3},{5,6},{6,5},{7,8},{8,7},{9,10},{10,... | collective-permute-start | bytes 1572872 | tf_op jit(solution)/shard_map/ppermute | solution.py:572
  66.5 25.4 %collective-permute-start.11 = (f32[16,64,128]{2,1,0:T(8,128)S(1)}, f32[16,64,128]{2,1,0:T(8,128)S(1)}, u32[]{:S(2)}, u32[]{:S(2)}) collective-permute-start(f32[16,64,128]{2,1,0:T(8,128)S(1)} %get-tuple-element.57), channel_id=1, source_target_pairs={{0,1},{1,0},{2,3},{3,2},{4,5},{5,4},{6,7},{7,6},{8,9},{9,8},{10,11... | collective-permute-start | bytes 1572872 | tf_op jit(solution)/shard_map/ppermute | solution.py:576
  71.8 23.9 %collective-permute-start.8 = (f32[4,64,128]{2,1,0:T(8,128)S(1)}, f32[4,64,128]{2,1,0:T(8,128)S(1)}, u32[]{:S(2)}, u32[]{:S(2)}) collective-permute-start(f32[4,64,128]{2,1,0:T(8,128)S(1)} %get-tuple-element.53), channel_id=1, source_target_pairs={{0,64},{1,2},{2,1},{3,4},{4,3},{5,6},{6,5},{7,8},{8,7},{9,10},{10,... | collective-permute-start | bytes 393224 | tf_op jit(solution)/shard_map/ppermute | solution.py:572
  74.2 22.5 %collective-permute-start.9 = (f32[4,64,128]{2,1,0:T(8,128)S(1)}, f32[4,64,128]{2,1,0:T(8,128)S(1)}, u32[]{:S(2)}, u32[]{:S(2)}) collective-permute-start(f32[4,64,128]{2,1,0:T(8,128)S(1)} %get-tuple-element.54), channel_id=1, source_target_pairs={{0,1},{1,0},{2,3},{3,2},{4,5},{5,4},{6,7},{7,6},{8,9},{9,8},{10,11... | collective-permute-start | bytes 393224 | tf_op jit(solution)/shard_map/ppermute | solution.py:576

commit v15 on v14

--- a/solution.py
+++ b/solution.py
@@ -13,7 +13,7 @@
 SLOTS = 768
 GROUP = 4
 HEAD = 16
-HEAD_BACK = 16
+HEAD_BACK = 12
 OBS = 80
 HALF = OBS // 2
 

time: 98.1 us -> 98.2 us (level)
    ppermute x4, waiting for transfers between devices: 5.79 us -> 7.61 us  [swap_second(): return lax.ppermute(x, ('mem', 'tile'), SECOND)]
    ppermute x4, waiting for transfers between devices: 33.4 us -> 31.7 us  [swap_first(): return lax.ppermute(x, ('mem', 'tile'), FIRST)]
  transfers between devices with their start and end apart: 12 -> 12, of which waited for: 11 -> 12; matrix products, arithmetic and copies ran while one was open for 0% -> 0% of each run, Pallas kernels for 16% -> 16%
where the time goes in v15:
time: 98.2 us; the launch traced here: 98 us
  waiting for transfers between devices  47.5 us (48%)
  starting transfers between devices  23.1 us (24%)
  Pallas kernels  22.9 us (23%)
  local copies, waits for them, and re-layouts  3.65 us (4%)
    ppermute x4, waiting for transfers between devices, swap_first(): return lax.ppermute(x, ('mem', 'tile'), FIRST)  31.7 us
    ppermute x4, starting transfers between devices, swap_first(): return lax.ppermute(x, ('mem', 'tile'), FIRST)  18 us
    ppermute x4, waiting for transfers between devices, swap_second(): return lax.ppermute(x, ('mem', 'tile'), SECOND)  7.61 us
    pallas_call x1, Pallas kernels, back_part(): call(back_kernel, (sds(members, 256, 128), sds(members, 128, 128), sds(me...  5.3 us
    ppermute x1, waiting for transfers between devices, swap_chip(): return lax.ppermute(x, 'mem', [(m, m ^ 2) for m in range(MEMS)])  3.86 us
    pallas_call x1, Pallas kernels, own_part(): call(own_kernel, (sds(V, 128, 128), sds(members, 128, 128), sds(members,...  3.79 us
    unnamed x20, local copies, waits for them, and re-layouts  3.56 us
    ppermute x2, starting transfers between devices, swap_core(): return lax.ppermute(x, 'mem', [(m, m ^ 1) for m in range(MEMS)])  3.06 us
  transfers between devices with their start and end apart: 12, of which 12 were waited for; matrix products, arithmetic and copies ran while one was open for 0% of the time, Pallas kernels for 16%

profile of v15, /device:TPU:6, one launch (start us, length us, event | category | flops | bytes accessed | tf_op | source)
XLA Modules:
  0.0 98.0 jit_solution(4559187923263837299)
XLA Ops:
  0.0 2.2 %shard_map.82 = (f32[1024,128]{1,0:T(8,128)}, f32[1024,128]{1,0:T(8,128)}, f32[8,128]{1,0:T(8,128)}) custom-call(bf16[20,4,64,128]{3,2,1,0:T(8,128)(2,1)} %bitcast.16), custom_call_target="tpu_custom_call" | custom-call | flops 1000 | bytes 1000 | tf_op jit(solution)/shard_map/pallas_call | solution.py:143
  2.2 9.1 %collective-permute-start.2 = (f32[1024,128]{1,0:T(8,128)}, f32[1024,128]{1,0:T(8,128)S(1)}, u32[]{:S(2)}, u32[]{:S(2)}) collective-permute-start(f32[1024,128]{1,0:T(8,128)} %get-tuple-element.39), channel_id=1, source_target_pairs={{0,64},{1,2},{2,1},{3,4},{4,3},{5,6},{6,5},{7,8},{8,7},{9,10},{10,... | collective-permute-start | bytes 1572872 | tf_op jit(solution)/shard_map/ppermute | solution.py:572
  11.4 2.1 %copy-done.1 = bf16[20,3,8,32,128]{4,3,2,1,0:T(8,128)(2,1)S(1)} copy-done((bf16[20,3,8,32,128]{4,3,2,1,0:T(8,128)(2,1)S(1)}, bf16[20,3,8,32,128]{4,3,2,1,0:T(8,128)(2,1)}, u32[]{:S(2)}) %copy-start.1) | copy-done | bytes 3932184
  13.5 0.8 copy-done.3
  14.2 0.7 copy-done.9
  14.9 3.8 %shard_map.83 = (f32[3,128,128]{2,1,0:T(8,128)S(1)}, f32[20,128,128]{2,1,0:T(8,128)S(1)}, bf16[20,3,128,128]{3,2,1,0:T(8,128)(2,1)S(1)}, bf16[256,256]{1,0:T(8,128)(2,1)S(1)}, bf16[128,128]{1,0:T(8,128)(2,1)S(1)}) custom-call(s32[11]{0:T(128)S(1)} %stack.51.where_ref, bf16[20,256,128]{2,1,0:T(8,128)(2,1)S(1)} %bitcast.17, ...), custom_call_target="tpu_custom_call" | custom-call | flops 1000 | bytes 1000 | tf_op jit(solution)/shard_map/pallas_call | solution.py:210
  19.8 1.6 %collective-permute-start = (f32[296,128]{1,0:T(8,128)S(1)}, f32[296,128]{1,0:T(8,128)S(1)}, u32[]{:S(2)}, u32[]{:S(2)}) collective-permute-start(f32[296,128]{1,0:T(8,128)S(1)} %get-tuple-element.34), channel_id=1, source_target_pairs={{0,64},{1,2},{2,1},{3,4},{4,3},{5,6},{6,5},{7,8},{8,7},{9,10},{10,... | collective-permute-start | bytes 454664 | tf_op jit(solution)/shard_map/ppermute | solution.py:572
  21.5 1.5 %collective-permute-start.1 = (f32[296,128]{1,0:T(8,128)S(1)}, f32[296,128]{1,0:T(8,128)S(1)}, u32[]{:S(2)}, u32[]{:S(2)}) collective-permute-start(f32[296,128]{1,0:T(8,128)S(1)} %get-tuple-element.35), channel_id=1, source_target_pairs={{0,1},{1,0},{2,3},{3,2},{4,5},{5,4},{6,7},{7,6},{8,9},{9,8},{10,11... | collective-permute-start | bytes 454664 | tf_op jit(solution)/shard_map/ppermute | solution.py:576
  22.9 12.1 %collective-permute-done.2.first_ref = f32[1024,128]{1,0:T(8,128)S(1)} collective-permute-done((f32[1024,128]{1,0:T(8,128)}, f32[1024,128]{1,0:T(8,128)S(1)}, u32[]{:S(2)}, u32[]{:S(2)}) %collective-permute-start.2) | collective-permute-done | bytes 524320 | tf_op jit(solution)/shard_map/ppermute | solution.py:572
  35.0 1.6 %collective-permute-done.3.second_ref = f32[1024,128]{1,0:T(8,128)S(1)} collective-permute-done((f32[1024,128]{1,0:T(8,128)}, f32[1024,128]{1,0:T(8,128)S(1)}, u32[]{:S(2)}, u32[]{:S(2)}) %collective-permute-start.3) | collective-permute-done | bytes 524320 | tf_op jit(solution)/shard_map/ppermute | solution.py:576
  36.6 1.9 %shard_map.85.head_ref = f32[3,128,128]{2,1,0:T(8,128)S(1)} custom-call(f32[1024,128]{1,0:T(8,128)S(1)} %collective-permute-done.2.first_ref, f32[1024,128]{1,0:T(8,128)S(1)} %collective-permute-done.3.second_ref, f32[20,128,128]{2,1,0:T(8,128)S(1)} %get-tuple-element.36.own_ref, bf16[20,3,128,128]{3,2,1,0:T(8,128)(2,1)S(1)} %get-tuple-element.37.x_ref, ...), custom_call_target="tpu_custom_call" | custom-call | flops 1000 | bytes 1000 | tf_op jit(solution)/shard_map/pallas_call | solution.py:257
  38.5 1.9 %collective-permute-done.first_ref = f32[296,128]{1,0:T(8,128)S(1)} collective-permute-done((f32[296,128]{1,0:T(8,128)S(1)}, f32[296,128]{1,0:T(8,128)S(1)}, u32[]{:S(2)}, u32[]{:S(2)}) %collective-permute-start) | collective-permute-done | bytes 151584 | tf_op jit(solution)/shard_map/ppermute | solution.py:572
  40.4 3.1 %collective-permute-done.1.second_ref = f32[296,128]{1,0:T(8,128)S(1)} collective-permute-done((f32[296,128]{1,0:T(8,128)S(1)}, f32[296,128]{1,0:T(8,128)S(1)}, u32[]{:S(2)}, u32[]{:S(2)}) %collective-permute-start.1) | collective-permute-done | bytes 151584 | tf_op jit(solution)/shard_map/ppermute | solution.py:576
  43.5 1.2 %shard_map.86 = (f32[3,256,128]{2,1,0:T(8,128)S(1)}, f32[96,128]{1,0:T(8,128)S(1)}, f32[176,128]{1,0:T(8,128)S(1)}) custom-call(s32[11]{0:T(128)S(1)} %stack.51.where_ref, f32[296,128]{1,0:T(8,128)S(1)} %collective-permute-done.first_ref, f32[296,128]{1,0:T(8,128)S(1)} %collective-permute-done.1.second_ref, f32[20,128,128]{2,1,0:T(8,128)S(1)} %get-tuple-element.36.own_ref, ...), custom_call_target="tpu_custom_call" | custom-call | flops 1000 | bytes 1000 | tf_op jit(solution)/shard_map/pallas_call | solution.py:275
  44.8 1.3 %collective-permute-done.4.there_ref = f32[176,128]{1,0:T(8,128)S(1)} collective-permute-done((f32[176,128]{1,0:T(8,128)S(1)}, f32[176,128]{1,0:T(8,128)S(1)}, u32[]{:S(2)}, u32[]{:S(2)}) %collective-permute-start.4) | collective-permute-done | bytes 90144 | tf_op jit(solution)/shard_map/ppermute | solution.py:584
  46.2 1.7 %shard_map.87 = (bf16[3,320,768]{2,1,0:T(8,128)(2,1)S(1)}, bf16[2,3,64,768]{3,2,1,0:T(8,128)(2,1)S(1)}, f32[9,768]{1,0:T(8,128)S(1)}, f32[9,768]{1,0:T(8,128)S(1...) custom-call(s32[11]{0:T(128)S(1)} %stack.51.where_ref, f32[80,128]{1,0:T(8,128)S(1)} %get-tuple-element.42.own_ref, ...), custom_call_target="tpu_custom_call" | custom-call | flops 1000 | bytes 1000 | tf_op jit(solution)/shard_map/pallas_call | solution.py:338
  47.8 1.4 %shard_map.88.mine_ref = f32[9,768]{1,0:T(8,128)S(1)} custom-call(s32[11]{0:T(128)S(1)} %stack.51.where_ref, f32[3,256,128]{2,1,0:T(8,128)S(1)} %get-tuple-element.41.inc_ref, bf16[3,320,768]{2,1,0:T(8,128)(2,1)S(1)} %get-tuple-element.45.wown_ref, bf16[2,3,64,768]{3,2,1,0:T(8,128)(2,1)S(1)} %get-tuple-element.46.wnear_ref, ...), custom_call_target="tpu_custom_call" | custom-call | flops 1000 | bytes 1000 | tf_op jit(solution)/shard_map/pallas_call | solution.py:376
  49.2 2.2 %collective-permute-done.5.near_ref = f32[96,128]{1,0:T(8,128)S(1)} collective-permute-done((f32[96,128]{1,0:T(8,128)S(1)}, f32[96,128]{1,0:T(8,128)S(1)}, u32[]{:S(2)}, u32[]{:S(2)}) %collective-permute-start.5) | collective-permute-done | bytes 49184 | tf_op jit(solution)/shard_map/ppermute | solution.py:580
  51.4 0.9 shard_map.89
  52.3 3.0 %collective-permute-start.6 = (f32[54,128]{1,0:T(8,128)S(1)}, f32[54,128]{1,0:T(8,128)S(1)}, u32[]{:S(2)}, u32[]{:S(2)}) collective-permute-start(f32[54,128]{1,0:T(8,128)S(1)} %shard_map.89), channel_id=1, source_target_pairs={{0,64},{64,0},{128,192},{192,128},{1,65},{65,1},{129,193},{193,129... | collective-permute-start | bytes 82952 | tf_op jit(solution)/shard_map/ppermute | solution.py:584
  55.3 0.9 collective-permute-done.6
  56.1 3.9 %collective-permute-done.7.v1 = f32[54,128]{1,0:T(8,128)S(1)} collective-permute-done((f32[54,128]{1,0:T(8,128)S(1)}, f32[54,128]{1,0:T(8,128)S(1)}, u32[]{:S(2)}, u32[]{:S(2)}) %collective-permute-start.7) | collective-permute-done | bytes 27680 | tf_op jit(solution)/shard_map/ppermute | solution.py:588
  60.0 1.6 %shard_map.90 = (f32[3,256,128]{2,1,0:T(8,128)S(1)}, f32[12,64,128]{2,1,0:T(8,128)S(1)}, f32[12,64,128]{2,1,0:T(8,128)S(1)}) custom-call(s32[11]{0:T(128)S(1)} %stack.51.where_ref, f32[54,128]{1,0:T(8,128)S(1)} %add.31.v0, f32[54,128]{1,0:T(8,128)S(1)} %collective-permute-done.7.v1, f32[9,768]{1,0:T(8,128)S(1)} %get-tuple-element.49.innov_ref, ...), custom_call_target="tpu_custom_call" | custom-call | flops 1000 | bytes 1000 | tf_op jit(solution)/shard_map/pallas_call | solution.py:454
  61.6 4.8 %collective-permute-start.10 = (f32[12,64,128]{2,1,0:T(8,128)S(1)}, f32[12,64,128]{2,1,0:T(8,128)S(1)}, u32[]{:S(2)}, u32[]{:S(2)}) collective-permute-start(f32[12,64,128]{2,1,0:T(8,128)S(1)} %get-tuple-element.56), channel_id=1, source_target_pairs={{0,64},{1,2},{2,1},{3,4},{4,3},{5,6},{6,5},{7,8},{8,7},{9,10},{10,... | collective-permute-start | bytes 1179656 | tf_op jit(solution)/shard_map/ppermute | solution.py:572
  66.4 5.3 %shard_map.91 = (f32[20,256,128]{2,1,0:T(8,128)}, f32[20,128,128]{2,1,0:T(8,128)S(1)}, f32[8,64,128]{2,1,0:T(8,128)S(1)}, f32[8,64,128]{2,1,0:T(8,128)S(1)}) custom-call(s32[11]{0:T(128)S(1)} %stack.51.where_ref, bf16[20,256,128]{2,1,0:T(8,128)(2,1)S(1)} %bitcast.19, bf16[20,3,256,128]{3,2,1,0:T(8,128)(2,1)S(1)} %bitcast.21, ...), custom_call_target="tpu_custom_call" | custom-call | flops 1000 | bytes 1000 | tf_op jit(solution)/shard_map/pallas_call | solution.py:486
  71.7 2.4 %collective-permute-start.8 = (f32[8,64,128]{2,1,0:T(8,128)S(1)}, f32[8,64,128]{2,1,0:T(8,128)S(1)}, u32[]{:S(2)}, u32[]{:S(2)}) collective-permute-start(f32[8,64,128]{2,1,0:T(8,128)S(1)} %get-tuple-element.53), channel_id=1, source_target_pairs={{0,64},{1,2},{2,1},{3,4},{4,3},{5,6},{6,5},{7,8},{8,7},{9,10},{10,... | collective-permute-start | bytes 786440 | tf_op jit(solution)/shard_map/ppermute | solution.py:572
  74.6 11.5 %collective-permute-done.10.first_ref = f32[12,64,128]{2,1,0:T(8,128)S(1)} collective-permute-done((f32[12,64,128]{2,1,0:T(8,128)S(1)}, f32[12,64,128]{2,1,0:T(8,128)S(1)}, u32[]{:S(2)}, u32[]{:S(2)}) %collective-permute-start.10) | collective-permute-done | bytes 393248 | tf_op jit(solution)/shard_map/ppermute | solution.py:572
  86.2 1.8 %collective-permute-done.11.second_ref = f32[12,64,128]{2,1,0:T(8,128)S(1)} collective-permute-done((f32[12,64,128]{2,1,0:T(8,128)S(1)}, f32[12,64,128]{2,1,0:T(8,128)S(1)}, u32[]{:S(2)}, u32[]{:S(2)}) %collective-permute-start.11) | collective-permute-done | bytes 393248 | tf_op jit(solution)/shard_map/ppermute | solution.py:576
  88.0 1.4 %shard_map.92.unused_ref = f32[20,4,64,128]{3,2,1,0:T(8,128)} custom-call(f32[12,64,128]{2,1,0:T(8,128)S(1)} %collective-permute-done.10.first_ref, f32[12,64,128]{2,1,0:T(8,128)S(1)} %collective-permute-done.11.second_ref, f32[20,128,128]{2,1,0:T(8,128)S(1)} %get-tuple-element.55.edge_ref, ...), custom_call_target="tpu_custom_call", output_to_operand_aliasing={{}: (5, {})} | custom-call | flops 1000 | bytes 1000 | tf_op jit(solution)/shard_map/pallas_call | solution.py:534
  89.5 6.2 %collective-permute-done.8.first_ref = f32[8,64,128]{2,1,0:T(8,128)S(1)} collective-permute-done((f32[8,64,128]{2,1,0:T(8,128)S(1)}, f32[8,64,128]{2,1,0:T(8,128)S(1)}, u32[]{:S(2)}, u32[]{:S(2)}) %collective-permute-start.8) | collective-permute-done | bytes 262176 | tf_op jit(solution)/shard_map/ppermute | solution.py:572
  95.6 1.1 %collective-permute-done.9.second_ref = f32[8,64,128]{2,1,0:T(8,128)S(1)} collective-permute-done((f32[8,64,128]{2,1,0:T(8,128)S(1)}, f32[8,64,128]{2,1,0:T(8,128)S(1)}, u32[]{:S(2)}, u32[]{:S(2)}) %collective-permute-start.9) | collective-permute-done | bytes 262176 | tf_op jit(solution)/shard_map/ppermute | solution.py:576
  96.7 1.3 %shard_map.93 = f32[20,4,64,128]{3,2,1,0:T(8,128)} custom-call(f32[8,64,128]{2,1,0:T(8,128)S(1)} %collective-permute-done.8.first_ref, f32[8,64,128]{2,1,0:T(8,128)S(1)} %collective-permute-done.9.second_ref, f32[20,128,128]{2,1,0:T(8,128)S(1)} %get-tuple-element.55.edge_ref, ...), custom_call_target="tpu_custom_call", output_to_operand_aliasing={{}: (5, {})} | custom-call | flops 1000 | bytes 1000 | tf_op jit(solution)/shard_map/pallas_call | solution.py:534
  (27 shorter events, 1.2 us)
Async XLA Ops:
  0.0 11.4 %copy-start = (bf16[20,8,32,128]{3,2,1,0:T(8,128)(2,1)S(1)}, bf16[20,8,32,128]{3,2,1,0:T(8,128)(2,1)}, u32[]{:S(2)}) copy-start(bf16[20,8,32,128]{3,2,1,0:T(8,128)(2,1)} %param.8) | copy-start | bytes 3932164
  2.2 32.9 %collective-permute-start.2 = (f32[1024,128]{1,0:T(8,128)}, f32[1024,128]{1,0:T(8,128)S(1)}, u32[]{:S(2)}, u32[]{:S(2)}) collective-permute-start(f32[1024,128]{1,0:T(8,128)} %get-tuple-element.39), channel_id=1, source_target_pairs={{0,64},{1,2},{2,1},{3,4},{4,3},{5,6},{6,5},{7,8},{8,7},{9,10},{10,... | collective-permute-start | bytes 1572872 | tf_op jit(solution)/shard_map/ppermute | solution.py:572
  11.3 25.4 %collective-permute-start.3 = (f32[1024,128]{1,0:T(8,128)}, f32[1024,128]{1,0:T(8,128)S(1)}, u32[]{:S(2)}, u32[]{:S(2)}) collective-permute-start(f32[1024,128]{1,0:T(8,128)} %get-tuple-element.40), channel_id=1, source_target_pairs={{0,1},{1,0},{2,3},{3,2},{4,5},{5,4},{6,7},{7,6},{8,9},{9,8},{10,11... | collective-permute-start | bytes 1572872 | tf_op jit(solution)/shard_map/ppermute | solution.py:576
  11.4 2.1 %copy-start.1 = (bf16[20,3,8,32,128]{4,3,2,1,0:T(8,128)(2,1)S(1)}, bf16[20,3,8,32,128]{4,3,2,1,0:T(8,128)(2,1)}, u32[]{:S(2)}) copy-start(bf16[20,3,8,32,128]{4,3,2,1,0:T(8,128)(2,1)} %param.9) | copy-start | bytes 11796484
  13.5 0.8 copy-start.3
  14.2 0.7 copy-start.9
  14.9 4.5 %copy-start.5 = (s32[1,2048]{1,0:T(1,128)S(1)}, s32[1,2048]{1,0:T(1,128)}, u32[]{:S(2)}) copy-start(s32[1,2048]{1,0:T(1,128)} %col_ref.1) | copy-start | bytes 24580
  14.9 4.5 %copy-start.6 = (s32[1,2048]{1,0:T(1,128)S(1)}, s32[1,2048]{1,0:T(1,128)}, u32[]{:S(2)}) copy-start(s32[1,2048]{1,0:T(1,128)} %lev_ref.1) | copy-start | bytes 24580
  14.9 4.5 %copy-start.7 = (f32[1,2048]{1,0:T(1,128)S(1)}, f32[1,2048]{1,0:T(1,128)}, u32[]{:S(2)}) copy-start(f32[1,2048]{1,0:T(1,128)} %innov_ref.1) | copy-start | bytes 24580
  14.9 4.5 %copy-start.8 = (f32[1,2048]{1,0:T(1,128)S(1)}, f32[1,2048]{1,0:T(1,128)}, u32[]{:S(2)}) copy-start(f32[1,2048]{1,0:T(1,128)} %weight_ref.1) | copy-start | bytes 24580
  19.8 20.6 %collective-permute-start = (f32[296,128]{1,0:T(8,128)S(1)}, f32[296,128]{1,0:T(8,128)S(1)}, u32[]{:S(2)}, u32[]{:S(2)}) collective-permute-start(f32[296,128]{1,0:T(8,128)S(1)} %get-tuple-element.34), channel_id=1, source_target_pairs={{0,64},{1,2},{2,1},{3,4},{4,3},{5,6},{6,5},{7,8},{8,7},{9,10},{10,... | collective-permute-start | bytes 454664 | tf_op jit(solution)/shard_map/ppermute | solution.py:572
  21.5 22.1 %collective-permute-start.1 = (f32[296,128]{1,0:T(8,128)S(1)}, f32[296,128]{1,0:T(8,128)S(1)}, u32[]{:S(2)}, u32[]{:S(2)}) collective-permute-start(f32[296,128]{1,0:T(8,128)S(1)} %get-tuple-element.35), channel_id=1, source_target_pairs={{0,1},{1,0},{2,3},{3,2},{4,5},{5,4},{6,7},{7,6},{8,9},{9,8},{10,11... | collective-permute-start | bytes 454664 | tf_op jit(solution)/shard_map/ppermute | solution.py:576
  44.7 1.4 %collective-permute-start.4 = (f32[176,128]{1,0:T(8,128)S(1)}, f32[176,128]{1,0:T(8,128)S(1)}, u32[]{:S(2)}, u32[]{:S(2)}) collective-permute-start(f32[176,128]{1,0:T(8,128)S(1)} %get-tuple-element.43.here_ref), channel_id=1, source_target_pairs={{0,64},{64,0},{128,192},{192,128},{1,65},{65,1},{129,193},{193,129... | collective-permute-start | bytes 270344 | tf_op jit(solution)/shard_map/ppermute | solution.py:584
  46.1 5.3 %collective-permute-start.5 = (f32[96,128]{1,0:T(8,128)S(1)}, f32[96,128]{1,0:T(8,128)S(1)}, u32[]{:S(2)}, u32[]{:S(2)}) collective-permute-start(f32[96,128]{1,0:T(8,128)S(1)} %slice_add_fusion.after_ref), channel_id=1, source_target_pairs={{0,1},{1,0},{2,3},{3,2},{4,5},{5,4},{6,7},{7,6},{8,9},{9,8},{10,11... | collective-permute-start | bytes 147464 | tf_op jit(solution)/shard_map/ppermute | solution.py:580
  52.3 3.8 %collective-permute-start.6 = (f32[54,128]{1,0:T(8,128)S(1)}, f32[54,128]{1,0:T(8,128)S(1)}, u32[]{:S(2)}, u32[]{:S(2)}) collective-permute-start(f32[54,128]{1,0:T(8,128)S(1)} %shard_map.89), channel_id=1, source_target_pairs={{0,64},{64,0},{128,192},{192,128},{1,65},{65,1},{129,193},{193,129... | collective-permute-start | bytes 82952 | tf_op jit(solution)/shard_map/ppermute | solution.py:584
  56.1 3.9 %collective-permute-start.7 = (f32[54,128]{1,0:T(8,128)S(1)}, f32[54,128]{1,0:T(8,128)S(1)}, u32[]{:S(2)}, u32[]{:S(2)}) collective-permute-start(f32[54,128]{1,0:T(8,128)S(1)} %add.31.v0), channel_id=1, source_target_pairs={{0,128},{64,192},{128,0},{192,64},{1,129},{65,193},{129,1},{193,65... | collective-permute-start | bytes 82952 | tf_op jit(solution)/shard_map/ppermute | solution.py:588
  60.0 6.5 %copy-start.2 = (bf16[20,3,8,32,128]{4,3,2,1,0:T(8,128)(2,1)S(1)}, bf16[20,3,8,32,128]{4,3,2,1,0:T(8,128)(2,1)}, u32[]{:S(2)}) copy-start(bf16[20,3,8,32,128]{4,3,2,1,0:T(8,128)(2,1)} %param.9) | copy-start | bytes 11796484
  60.0 6.5 %copy-start.4 = (bf16[128,128]{1,0:T(8,128)(2,1)S(1)}, bf16[128,128]{1,0:T(8,128)(2,1)}, u32[]{:S(2)}) copy-start(bf16[128,128]{1,0:T(8,128)(2,1)} %loc_ref.11) | copy-start | bytes 98308
  61.6 24.5 %collective-permute-start.10 = (f32[12,64,128]{2,1,0:T(8,128)S(1)}, f32[12,64,128]{2,1,0:T(8,128)S(1)}, u32[]{:S(2)}, u32[]{:S(2)}) collective-permute-start(f32[12,64,128]{2,1,0:T(8,128)S(1)} %get-tuple-element.56), channel_id=1, source_target_pairs={{0,64},{1,2},{2,1},{3,4},{4,3},{5,6},{6,5},{7,8},{8,7},{9,10},{10,... | collective-permute-start | bytes 1179656 | tf_op jit(solution)/shard_map/ppermute | solution.py:572
  66.4 21.6 %collective-permute-start.11 = (f32[12,64,128]{2,1,0:T(8,128)S(1)}, f32[12,64,128]{2,1,0:T(8,128)S(1)}, u32[]{:S(2)}, u32[]{:S(2)}) collective-permute-start(f32[12,64,128]{2,1,0:T(8,128)S(1)} %get-tuple-element.57), channel_id=1, source_target_pairs={{0,1},{1,0},{2,3},{3,2},{4,5},{5,4},{6,7},{7,6},{8,9},{9,8},{10,11... | collective-permute-start | bytes 1179656 | tf_op jit(solution)/shard_map/ppermute | solution.py:576
  71.7 23.9 %collective-permute-start.8 = (f32[8,64,128]{2,1,0:T(8,128)S(1)}, f32[8,64,128]{2,1,0:T(8,128)S(1)}, u32[]{:S(2)}, u32[]{:S(2)}) collective-permute-start(f32[8,64,128]{2,1,0:T(8,128)S(1)} %get-tuple-element.53), channel_id=1, source_target_pairs={{0,64},{1,2},{2,1},{3,4},{4,3},{5,6},{6,5},{7,8},{8,7},{9,10},{10,... | collective-permute-start | bytes 786440 | tf_op jit(solution)/shard_map/ppermute | solution.py:572
  74.2 22.5 %collective-permute-start.9 = (f32[8,64,128]{2,1,0:T(8,128)S(1)}, f32[8,64,128]{2,1,0:T(8,128)S(1)}, u32[]{:S(2)}, u32[]{:S(2)}) collective-permute-start(f32[8,64,128]{2,1,0:T(8,128)S(1)} %get-tuple-element.54), channel_id=1, source_target_pairs={{0,1},{1,0},{2,3},{3,2},{4,5},{5,4},{6,7},{7,6},{8,9},{9,8},{10,11... | collective-permute-start | bytes 786440 | tf_op jit(solution)/shard_map/ppermute | solution.py:576

commit v16 on v15

--- a/solution.py
+++ b/solution.py
@@ -31,8 +31,8 @@
     return pairs
 
 
-FIRST = partners(lambda m: True, 1)
-SECOND = partners(lambda m: False, 1)
+FIRST = partners(lambda m: False, 1)
+SECOND = partners(lambda m: True, 1)
 NEAR = partners(lambda m: m % 2 == 1, 2)
 
 
@@ -93,7 +93,7 @@
 
 
 def side_of_first():
-    return lax.rem(lax.axis_index("tile") + 1, 2)
+    return lax.rem(lax.axis_index("tile"), 2)
 
 
 def sort_observations(count, col_ref, lev_ref, innov_ref, weight_ref, out_ref):
@@ -267,8 +267,8 @@
         keep_ref[32 * v : 32 * v + 32] = inc_ref[v, pl.ds(pl.multiple_of(where_ref[8], 32), 32)]
         give_ref[32 * v : 32 * v + 32] = inc_ref[v, pl.ds(pl.multiple_of(where_ref[9], 32), 32)]
     end = first_ref.shape[0] - HALF
-    give_ref[32 * V : 32 * V + HALF] = first_ref[end:]
-    give_ref[32 * V + HALF :] = second_ref[end:]
+    give_ref[32 * V : 32 * V + HALF] = second_ref[end:]
+    give_ref[32 * V + HALF :] = first_ref[end:]
 
 
 def edge_part(where, first, second, own, x, hmat, loc, inner, head):

time: 98.2 us -> 98.1 us (level)
  waiting for transfers between devices: 47.5 us -> 44.9 us
  starting transfers between devices: 23.1 us -> 25.6 us
    ppermute x4, waiting for transfers between devices: 31.7 us -> 12.7 us  [swap_first(): return lax.ppermute(x, ('mem', 'tile'), FIRST)]
    ppermute x4, waiting for transfers between devices: 7.61 us -> 24.3 us  [swap_second(): return lax.ppermute(x, ('mem', 'tile'), SECOND)]
    ppermute x4, starting transfers between devices: 1.94 us -> 16.9 us  [swap_second(): return lax.ppermute(x, ('mem', 'tile'), SECOND)]
    ppermute x4, starting transfers between devices: 18 us -> 3.55 us  [swap_first(): return lax.ppermute(x, ('mem', 'tile'), FIRST)]
    ppermute x2, starting transfers between devices: 3.06 us -> 4.93 us  [swap_core(): return lax.ppermute(x, 'mem', [(m, m ^ 1) for m in range(MEMS)])]
  transfers between devices with their start and end apart: 12 -> 12, of which waited for: 12 -> 10; matrix products, arithmetic and copies ran while one was open for 0% -> 0% of each run, Pallas kernels for 16% -> 16%
where the time goes in v16:
time: 98.1 us; the launch traced here: 97.8 us
  waiting for transfers between devices  44.9 us (46%)
  starting transfers between devices  25.6 us (26%)
  Pallas kernels  22.9 us (23%)
  local copies, waits for them, and re-layouts  3.65 us (4%)
    ppermute x4, waiting for transfers between devices, swap_second(): return lax.ppermute(x, ('mem', 'tile'), SECOND)  24.3 us
    ppermute x4, starting transfers between devices, swap_second(): return lax.ppermute(x, ('mem', 'tile'), SECOND)  16.9 us
    ppermute x4, waiting for transfers between devices, swap_first(): return lax.ppermute(x, ('mem', 'tile'), FIRST)  12.7 us
    pallas_call x1, Pallas kernels, back_part(): call(back_kernel, (sds(members, 256, 128), sds(members, 128, 128), sds(me...  5.27 us
    ppermute x2, starting transfers between devices, swap_core(): return lax.ppermute(x, 'mem', [(m, m ^ 1) for m in range(MEMS)])  4.93 us
    pallas_call x1, Pallas kernels, own_part(): call(own_kernel, (sds(V, 128, 128), sds(members, 128, 128), sds(members,...  3.79 us
    ppermute x1, waiting for transfers between devices, swap_chip(): return lax.ppermute(x, 'mem', [(m, m ^ 2) for m in range(MEMS)])  3.78 us
    unnamed x20, local copies, waits for them, and re-layouts  3.56 us
  transfers between devices with their start and end apart: 12, of which 10 were waited for; matrix products, arithmetic and copies ran while one was open for 0% of the time, Pallas kernels for 16%

profile of v16, /device:TPU:6, one launch (start us, length us, event | category | flops | bytes accessed | tf_op | source)
XLA Modules:
  0.0 97.8 jit_solution(14727753323497945938)
XLA Ops:
  0.0 2.2 %shard_map.82 = (f32[1024,128]{1,0:T(8,128)}, f32[1024,128]{1,0:T(8,128)}, f32[8,128]{1,0:T(8,128)}) custom-call(bf16[20,4,64,128]{3,2,1,0:T(8,128)(2,1)} %bitcast.16), custom_call_target="tpu_custom_call" | custom-call | flops 1000 | bytes 1000 | tf_op jit(solution)/shard_map/pallas_call | solution.py:143
  2.2 3.4 %collective-permute-start.2 = (f32[1024,128]{1,0:T(8,128)}, f32[1024,128]{1,0:T(8,128)S(1)}, u32[]{:S(2)}, u32[]{:S(2)}) collective-permute-start(f32[1024,128]{1,0:T(8,128)} %get-tuple-element.39), channel_id=1, source_target_pairs={{0,1},{1,0},{2,3},{3,2},{4,5},{5,4},{6,7},{7,6},{8,9},{9,8},{10,11... | collective-permute-start | bytes 1572872 | tf_op jit(solution)/shard_map/ppermute | solution.py:572
  5.5 7.2 %collective-permute-start.3 = (f32[1024,128]{1,0:T(8,128)}, f32[1024,128]{1,0:T(8,128)S(1)}, u32[]{:S(2)}, u32[]{:S(2)}) collective-permute-start(f32[1024,128]{1,0:T(8,128)} %get-tuple-element.40), channel_id=1, source_target_pairs={{0,64},{1,2},{2,1},{3,4},{4,3},{5,6},{6,5},{7,8},{8,7},{9,10},{10,... | collective-permute-start | bytes 1572872 | tf_op jit(solution)/shard_map/ppermute | solution.py:576
  12.8 2.1 %copy-done.1 = bf16[20,3,8,32,128]{4,3,2,1,0:T(8,128)(2,1)S(1)} copy-done((bf16[20,3,8,32,128]{4,3,2,1,0:T(8,128)(2,1)S(1)}, bf16[20,3,8,32,128]{4,3,2,1,0:T(8,128)(2,1)}, u32[]{:S(2)}) %copy-start.1) | copy-done | bytes 3932184
  14.9 0.8 copy-done.3
  15.7 0.7 copy-done.9
  16.4 3.8 %shard_map.83 = (f32[3,128,128]{2,1,0:T(8,128)S(1)}, f32[20,128,128]{2,1,0:T(8,128)S(1)}, bf16[20,3,128,128]{3,2,1,0:T(8,128)(2,1)S(1)}, bf16[256,256]{1,0:T(8,128)(2,1)S(1)}, bf16[128,128]{1,0:T(8,128)(2,1)S(1)}) custom-call(s32[11]{0:T(128)S(1)} %stack.51.where_ref, bf16[20,256,128]{2,1,0:T(8,128)(2,1)S(1)} %bitcast.17, ...), custom_call_target="tpu_custom_call" | custom-call | flops 1000 | bytes 1000 | tf_op jit(solution)/shard_map/pallas_call | solution.py:210
  20.9 0.4 shard_map.84
  21.4 1.5 %collective-permute-start.1 = (f32[296,128]{1,0:T(8,128)S(1)}, f32[296,128]{1,0:T(8,128)S(1)}, u32[]{:S(2)}, u32[]{:S(2)}) collective-permute-start(f32[296,128]{1,0:T(8,128)S(1)} %get-tuple-element.35), channel_id=1, source_target_pairs={{0,64},{1,2},{2,1},{3,4},{4,3},{5,6},{6,5},{7,8},{8,7},{9,10},{10,... | collective-permute-start | bytes 454664 | tf_op jit(solution)/shard_map/ppermute | solution.py:576
  22.8 8.3 %collective-permute-done.2.first_ref = f32[1024,128]{1,0:T(8,128)S(1)} collective-permute-done((f32[1024,128]{1,0:T(8,128)}, f32[1024,128]{1,0:T(8,128)S(1)}, u32[]{:S(2)}, u32[]{:S(2)}) %collective-permute-start.2) | collective-permute-done | bytes 524320 | tf_op jit(solution)/shard_map/ppermute | solution.py:572
  31.2 0.9 collective-permute-done.3.second_ref
  32.0 1.9 %shard_map.85.head_ref = f32[3,128,128]{2,1,0:T(8,128)S(1)} custom-call(f32[1024,128]{1,0:T(8,128)S(1)} %collective-permute-done.2.first_ref, f32[1024,128]{1,0:T(8,128)S(1)} %collective-permute-done.3.second_ref, f32[20,128,128]{2,1,0:T(8,128)S(1)} %get-tuple-element.36.own_ref, bf16[20,3,128,128]{3,2,1,0:T(8,128)(2,1)S(1)} %get-tuple-element.37.x_ref, ...), custom_call_target="tpu_custom_call" | custom-call | flops 1000 | bytes 1000 | tf_op jit(solution)/shard_map/pallas_call | solution.py:257
  33.9 8.4 %collective-permute-done.1.second_ref = f32[296,128]{1,0:T(8,128)S(1)} collective-permute-done((f32[296,128]{1,0:T(8,128)S(1)}, f32[296,128]{1,0:T(8,128)S(1)}, u32[]{:S(2)}, u32[]{:S(2)}) %collective-permute-start.1) | collective-permute-done | bytes 151584 | tf_op jit(solution)/shard_map/ppermute | solution.py:576
  42.3 1.2 %shard_map.86 = (f32[3,256,128]{2,1,0:T(8,128)S(1)}, f32[96,128]{1,0:T(8,128)S(1)}, f32[176,128]{1,0:T(8,128)S(1)}) custom-call(s32[11]{0:T(128)S(1)} %stack.51.where_ref, f32[296,128]{1,0:T(8,128)S(1)} %collective-permute-done.first_ref, f32[296,128]{1,0:T(8,128)S(1)} %collective-permute-done.1.second_ref, f32[20,128,128]{2,1,0:T(8,128)S(1)} %get-tuple-element.36.own_ref, ...), custom_call_target="tpu_custom_call" | custom-call | flops 1000 | bytes 1000 | tf_op jit(solution)/shard_map/pallas_call | solution.py:275
  43.6 1.3 %collective-permute-done.4.there_ref = f32[176,128]{1,0:T(8,128)S(1)} collective-permute-done((f32[176,128]{1,0:T(8,128)S(1)}, f32[176,128]{1,0:T(8,128)S(1)}, u32[]{:S(2)}, u32[]{:S(2)}) %collective-permute-start.4) | collective-permute-done | bytes 90144 | tf_op jit(solution)/shard_map/ppermute | solution.py:584
  45.0 1.7 %shard_map.87 = (bf16[3,320,768]{2,1,0:T(8,128)(2,1)S(1)}, bf16[2,3,64,768]{3,2,1,0:T(8,128)(2,1)S(1)}, f32[9,768]{1,0:T(8,128)S(1)}, f32[9,768]{1,0:T(8,128)S(1...) custom-call(s32[11]{0:T(128)S(1)} %stack.51.where_ref, f32[80,128]{1,0:T(8,128)S(1)} %get-tuple-element.42.own_ref, ...), custom_call_target="tpu_custom_call" | custom-call | flops 1000 | bytes 1000 | tf_op jit(solution)/shard_map/pallas_call | solution.py:338
  46.6 1.4 %shard_map.88.mine_ref = f32[9,768]{1,0:T(8,128)S(1)} custom-call(s32[11]{0:T(128)S(1)} %stack.51.where_ref, f32[3,256,128]{2,1,0:T(8,128)S(1)} %get-tuple-element.41.inc_ref, bf16[3,320,768]{2,1,0:T(8,128)(2,1)S(1)} %get-tuple-element.45.wown_ref, bf16[2,3,64,768]{3,2,1,0:T(8,128)(2,1)S(1)} %get-tuple-element.46.wnear_ref, ...), custom_call_target="tpu_custom_call" | custom-call | flops 1000 | bytes 1000 | tf_op jit(solution)/shard_map/pallas_call | solution.py:376
  48.0 2.0 %collective-permute-done.5.near_ref = f32[96,128]{1,0:T(8,128)S(1)} collective-permute-done((f32[96,128]{1,0:T(8,128)S(1)}, f32[96,128]{1,0:T(8,128)S(1)}, u32[]{:S(2)}, u32[]{:S(2)}) %collective-permute-start.5) | collective-permute-done | bytes 49184 | tf_op jit(solution)/shard_map/ppermute | solution.py:580
  50.0 0.9 shard_map.89
  50.8 4.8 %collective-permute-start.6 = (f32[54,128]{1,0:T(8,128)S(1)}, f32[54,128]{1,0:T(8,128)S(1)}, u32[]{:S(2)}, u32[]{:S(2)}) collective-permute-start(f32[54,128]{1,0:T(8,128)S(1)} %shard_map.89), channel_id=1, source_target_pairs={{0,64},{64,0},{128,192},{192,128},{1,65},{65,1},{129,193},{193,129... | collective-permute-start | bytes 82952 | tf_op jit(solution)/shard_map/ppermute | solution.py:584
  55.7 0.9 collective-permute-done.6
  56.5 0.1 collective-permute-start.7
  56.6 3.8 %collective-permute-done.7.v1 = f32[54,128]{1,0:T(8,128)S(1)} collective-permute-done((f32[54,128]{1,0:T(8,128)S(1)}, f32[54,128]{1,0:T(8,128)S(1)}, u32[]{:S(2)}, u32[]{:S(2)}) %collective-permute-start.7) | collective-permute-done | bytes 27680 | tf_op jit(solution)/shard_map/ppermute | solution.py:588
  60.4 1.6 %shard_map.90 = (f32[3,256,128]{2,1,0:T(8,128)S(1)}, f32[12,64,128]{2,1,0:T(8,128)S(1)}, f32[12,64,128]{2,1,0:T(8,128)S(1)}) custom-call(s32[11]{0:T(128)S(1)} %stack.51.where_ref, f32[54,128]{1,0:T(8,128)S(1)} %add.27.v0, f32[54,128]{1,0:T(8,128)S(1)} %collective-permute-done.7.v1, f32[9,768]{1,0:T(8,128)S(1)} %get-tuple-element.49.innov_ref, ...), custom_call_target="tpu_custom_call" | custom-call | flops 1000 | bytes 1000 | tf_op jit(solution)/shard_map/pallas_call | solution.py:454
  62.1 5.4 %collective-permute-start.11 = (f32[12,64,128]{2,1,0:T(8,128)S(1)}, f32[12,64,128]{2,1,0:T(8,128)S(1)}, u32[]{:S(2)}, u32[]{:S(2)}) collective-permute-start(f32[12,64,128]{2,1,0:T(8,128)S(1)} %get-tuple-element.57), channel_id=1, source_target_pairs={{0,64},{1,2},{2,1},{3,4},{4,3},{5,6},{6,5},{7,8},{8,7},{9,10},{10,... | collective-permute-start | bytes 1179656 | tf_op jit(solution)/shard_map/ppermute | solution.py:576
  67.5 5.3 %shard_map.91 = (f32[20,256,128]{2,1,0:T(8,128)}, f32[20,128,128]{2,1,0:T(8,128)S(1)}, f32[8,64,128]{2,1,0:T(8,128)S(1)}, f32[8,64,128]{2,1,0:T(8,128)S(1)}) custom-call(s32[11]{0:T(128)S(1)} %stack.51.where_ref, bf16[20,256,128]{2,1,0:T(8,128)(2,1)S(1)} %bitcast.19, bf16[20,3,256,128]{3,2,1,0:T(8,128)(2,1)S(1)} %bitcast.21, ...), custom_call_target="tpu_custom_call" | custom-call | flops 1000 | bytes 1000 | tf_op jit(solution)/shard_map/pallas_call | solution.py:486
  72.8 2.9 %collective-permute-start.9 = (f32[8,64,128]{2,1,0:T(8,128)S(1)}, f32[8,64,128]{2,1,0:T(8,128)S(1)}, u32[]{:S(2)}, u32[]{:S(2)}) collective-permute-start(f32[8,64,128]{2,1,0:T(8,128)S(1)} %get-tuple-element.54), channel_id=1, source_target_pairs={{0,64},{1,2},{2,1},{3,4},{4,3},{5,6},{6,5},{7,8},{8,7},{9,10},{10,... | collective-permute-start | bytes 786440 | tf_op jit(solution)/shard_map/ppermute | solution.py:576
  75.7 4.4 %collective-permute-done.10.first_ref = f32[12,64,128]{2,1,0:T(8,128)S(1)} collective-permute-done((f32[12,64,128]{2,1,0:T(8,128)S(1)}, f32[12,64,128]{2,1,0:T(8,128)S(1)}, u32[]{:S(2)}, u32[]{:S(2)}) %collective-permute-start.10) | collective-permute-done | bytes 393248 | tf_op jit(solution)/shard_map/ppermute | solution.py:572
  80.1 12.2 %collective-permute-done.11.second_ref = f32[12,64,128]{2,1,0:T(8,128)S(1)} collective-permute-done((f32[12,64,128]{2,1,0:T(8,128)S(1)}, f32[12,64,128]{2,1,0:T(8,128)S(1)}, u32[]{:S(2)}, u32[]{:S(2)}) %collective-permute-start.11) | collective-permute-done | bytes 393248 | tf_op jit(solution)/shard_map/ppermute | solution.py:576
  92.2 1.4 %shard_map.92.unused_ref = f32[20,4,64,128]{3,2,1,0:T(8,128)} custom-call(f32[12,64,128]{2,1,0:T(8,128)S(1)} %collective-permute-done.10.first_ref, f32[12,64,128]{2,1,0:T(8,128)S(1)} %collective-permute-done.11.second_ref, f32[20,128,128]{2,1,0:T(8,128)S(1)} %get-tuple-element.55.edge_ref, ...), custom_call_target="tpu_custom_call", output_to_operand_aliasing={{}: (5, {})} | custom-call | flops 1000 | bytes 1000 | tf_op jit(solution)/shard_map/pallas_call | solution.py:534
  93.7 2.9 %collective-permute-done.9.second_ref = f32[8,64,128]{2,1,0:T(8,128)S(1)} collective-permute-done((f32[8,64,128]{2,1,0:T(8,128)S(1)}, f32[8,64,128]{2,1,0:T(8,128)S(1)}, u32[]{:S(2)}, u32[]{:S(2)}) %collective-permute-start.9) | collective-permute-done | bytes 262176 | tf_op jit(solution)/shard_map/ppermute | solution.py:576
  96.5 1.3 %shard_map.93 = f32[20,4,64,128]{3,2,1,0:T(8,128)} custom-call(f32[8,64,128]{2,1,0:T(8,128)S(1)} %collective-permute-done.8.first_ref, f32[8,64,128]{2,1,0:T(8,128)S(1)} %collective-permute-done.9.second_ref, f32[20,128,128]{2,1,0:T(8,128)S(1)} %get-tuple-element.55.edge_ref, ...), custom_call_target="tpu_custom_call", output_to_operand_aliasing={{}: (5, {})} | custom-call | flops 1000 | bytes 1000 | tf_op jit(solution)/shard_map/pallas_call | solution.py:534
  (27 shorter events, 0.5 us)
Async XLA Ops:
  0.0 12.8 %copy-start = (bf16[20,8,32,128]{3,2,1,0:T(8,128)(2,1)S(1)}, bf16[20,8,32,128]{3,2,1,0:T(8,128)(2,1)}, u32[]{:S(2)}) copy-start(bf16[20,8,32,128]{3,2,1,0:T(8,128)(2,1)} %param.8) | copy-start | bytes 3932164
  2.2 29.0 %collective-permute-start.2 = (f32[1024,128]{1,0:T(8,128)}, f32[1024,128]{1,0:T(8,128)S(1)}, u32[]{:S(2)}, u32[]{:S(2)}) collective-permute-start(f32[1024,128]{1,0:T(8,128)} %get-tuple-element.39), channel_id=1, source_target_pairs={{0,1},{1,0},{2,3},{3,2},{4,5},{5,4},{6,7},{7,6},{8,9},{9,8},{10,11... | collective-permute-start | bytes 1572872 | tf_op jit(solution)/shard_map/ppermute | solution.py:572
  5.5 26.5 %collective-permute-start.3 = (f32[1024,128]{1,0:T(8,128)}, f32[1024,128]{1,0:T(8,128)S(1)}, u32[]{:S(2)}, u32[]{:S(2)}) collective-permute-start(f32[1024,128]{1,0:T(8,128)} %get-tuple-element.40), channel_id=1, source_target_pairs={{0,64},{1,2},{2,1},{3,4},{4,3},{5,6},{6,5},{7,8},{8,7},{9,10},{10,... | collective-permute-start | bytes 1572872 | tf_op jit(solution)/shard_map/ppermute | solution.py:576
  12.8 2.1 %copy-start.1 = (bf16[20,3,8,32,128]{4,3,2,1,0:T(8,128)(2,1)S(1)}, bf16[20,3,8,32,128]{4,3,2,1,0:T(8,128)(2,1)}, u32[]{:S(2)}) copy-start(bf16[20,3,8,32,128]{4,3,2,1,0:T(8,128)(2,1)} %param.9) | copy-start | bytes 11796484
  14.9 0.8 copy-start.3
  15.7 0.7 copy-start.9
  16.4 4.5 %copy-start.5 = (s32[1,2048]{1,0:T(1,128)S(1)}, s32[1,2048]{1,0:T(1,128)}, u32[]{:S(2)}) copy-start(s32[1,2048]{1,0:T(1,128)} %col_ref.1) | copy-start | bytes 24580
  16.4 4.5 %copy-start.6 = (s32[1,2048]{1,0:T(1,128)S(1)}, s32[1,2048]{1,0:T(1,128)}, u32[]{:S(2)}) copy-start(s32[1,2048]{1,0:T(1,128)} %lev_ref.1) | copy-start | bytes 24580
  16.4 4.5 %copy-start.7 = (f32[1,2048]{1,0:T(1,128)S(1)}, f32[1,2048]{1,0:T(1,128)}, u32[]{:S(2)}) copy-start(f32[1,2048]{1,0:T(1,128)} %innov_ref.1) | copy-start | bytes 24580
  16.4 4.5 %copy-start.8 = (f32[1,2048]{1,0:T(1,128)S(1)}, f32[1,2048]{1,0:T(1,128)}, u32[]{:S(2)}) copy-start(f32[1,2048]{1,0:T(1,128)} %weight_ref.1) | copy-start | bytes 24580
  21.3 12.7 %collective-permute-start = (f32[296,128]{1,0:T(8,128)S(1)}, f32[296,128]{1,0:T(8,128)S(1)}, u32[]{:S(2)}, u32[]{:S(2)}) collective-permute-start(f32[296,128]{1,0:T(8,128)S(1)} %get-tuple-element.34), channel_id=1, source_target_pairs={{0,1},{1,0},{2,3},{3,2},{4,5},{5,4},{6,7},{7,6},{8,9},{9,8},{10,11... | collective-permute-start | bytes 454664 | tf_op jit(solution)/shard_map/ppermute | solution.py:572
  21.4 21.0 %collective-permute-start.1 = (f32[296,128]{1,0:T(8,128)S(1)}, f32[296,128]{1,0:T(8,128)S(1)}, u32[]{:S(2)}, u32[]{:S(2)}) collective-permute-start(f32[296,128]{1,0:T(8,128)S(1)} %get-tuple-element.35), channel_id=1, source_target_pairs={{0,64},{1,2},{2,1},{3,4},{4,3},{5,6},{6,5},{7,8},{8,7},{9,10},{10,... | collective-permute-start | bytes 454664 | tf_op jit(solution)/shard_map/ppermute | solution.py:576
  43.5 1.4 %collective-permute-start.4 = (f32[176,128]{1,0:T(8,128)S(1)}, f32[176,128]{1,0:T(8,128)S(1)}, u32[]{:S(2)}, u32[]{:S(2)}) collective-permute-start(f32[176,128]{1,0:T(8,128)S(1)} %get-tuple-element.43.here_ref), channel_id=1, source_target_pairs={{0,64},{64,0},{128,192},{192,128},{1,65},{65,1},{129,193},{193,129... | collective-permute-start | bytes 270344 | tf_op jit(solution)/shard_map/ppermute | solution.py:584
  44.9 5.1 %collective-permute-start.5 = (f32[96,128]{1,0:T(8,128)S(1)}, f32[96,128]{1,0:T(8,128)S(1)}, u32[]{:S(2)}, u32[]{:S(2)}) collective-permute-start(f32[96,128]{1,0:T(8,128)S(1)} %slice_add_fusion.after_ref), channel_id=1, source_target_pairs={{0,1},{1,0},{2,3},{3,2},{4,5},{5,4},{6,7},{7,6},{8,9},{9,8},{10,11... | collective-permute-start | bytes 147464 | tf_op jit(solution)/shard_map/ppermute | solution.py:580
  50.8 5.7 %collective-permute-start.6 = (f32[54,128]{1,0:T(8,128)S(1)}, f32[54,128]{1,0:T(8,128)S(1)}, u32[]{:S(2)}, u32[]{:S(2)}) collective-permute-start(f32[54,128]{1,0:T(8,128)S(1)} %shard_map.89), channel_id=1, source_target_pairs={{0,64},{64,0},{128,192},{192,128},{1,65},{65,1},{129,193},{193,129... | collective-permute-start | bytes 82952 | tf_op jit(solution)/shard_map/ppermute | solution.py:584
  56.5 3.9 %collective-permute-start.7 = (f32[54,128]{1,0:T(8,128)S(1)}, f32[54,128]{1,0:T(8,128)S(1)}, u32[]{:S(2)}, u32[]{:S(2)}) collective-permute-start(f32[54,128]{1,0:T(8,128)S(1)} %add.27.v0), channel_id=1, source_target_pairs={{0,128},{64,192},{128,0},{192,64},{1,129},{65,193},{129,1},{193,65... | collective-permute-start | bytes 82952 | tf_op jit(solution)/shard_map/ppermute | solution.py:588
  60.4 7.1 %copy-start.2 = (bf16[20,3,8,32,128]{4,3,2,1,0:T(8,128)(2,1)S(1)}, bf16[20,3,8,32,128]{4,3,2,1,0:T(8,128)(2,1)}, u32[]{:S(2)}) copy-start(bf16[20,3,8,32,128]{4,3,2,1,0:T(8,128)(2,1)} %param.9) | copy-start | bytes 11796484
  60.4 7.1 %copy-start.4 = (bf16[128,128]{1,0:T(8,128)(2,1)S(1)}, bf16[128,128]{1,0:T(8,128)(2,1)}, u32[]{:S(2)}) copy-start(bf16[128,128]{1,0:T(8,128)(2,1)} %loc_ref.11) | copy-start | bytes 98308
  62.0 18.0 %collective-permute-start.10 = (f32[12,64,128]{2,1,0:T(8,128)S(1)}, f32[12,64,128]{2,1,0:T(8,128)S(1)}, u32[]{:S(2)}, u32[]{:S(2)}) collective-permute-start(f32[12,64,128]{2,1,0:T(8,128)S(1)} %get-tuple-element.56), channel_id=1, source_target_pairs={{0,1},{1,0},{2,3},{3,2},{4,5},{5,4},{6,7},{7,6},{8,9},{9,8},{10,11... | collective-permute-start | bytes 1179656 | tf_op jit(solution)/shard_map/ppermute | solution.py:572
  62.1 30.1 %collective-permute-start.11 = (f32[12,64,128]{2,1,0:T(8,128)S(1)}, f32[12,64,128]{2,1,0:T(8,128)S(1)}, u32[]{:S(2)}, u32[]{:S(2)}) collective-permute-start(f32[12,64,128]{2,1,0:T(8,128)S(1)} %get-tuple-element.57), channel_id=1, source_target_pairs={{0,64},{1,2},{2,1},{3,4},{4,3},{5,6},{6,5},{7,8},{8,7},{9,10},{10,... | collective-permute-start | bytes 1179656 | tf_op jit(solution)/shard_map/ppermute | solution.py:576
  72.8 20.8 %collective-permute-start.8 = (f32[8,64,128]{2,1,0:T(8,128)S(1)}, f32[8,64,128]{2,1,0:T(8,128)S(1)}, u32[]{:S(2)}, u32[]{:S(2)}) collective-permute-start(f32[8,64,128]{2,1,0:T(8,128)S(1)} %get-tuple-element.53), channel_id=1, source_target_pairs={{0,1},{1,0},{2,3},{3,2},{4,5},{5,4},{6,7},{7,6},{8,9},{9,8},{10,11... | collective-permute-start | bytes 786440 | tf_op jit(solution)/shard_map/ppermute | solution.py:572
  72.8 23.7 %collective-permute-start.9 = (f32[8,64,128]{2,1,0:T(8,128)S(1)}, f32[8,64,128]{2,1,0:T(8,128)S(1)}, u32[]{:S(2)}, u32[]{:S(2)}) collective-permute-start(f32[8,64,128]{2,1,0:T(8,128)S(1)} %get-tuple-element.54), channel_id=1, source_target_pairs={{0,64},{1,2},{2,1},{3,4},{4,3},{5,6},{6,5},{7,8},{8,7},{9,10},{10,... | collective-permute-start | bytes 786440 | tf_op jit(solution)/shard_map/ppermute | solution.py:576
